TPU v7x, 32 devices: a whole 2x2x4 slice. The times are simulated.
32 devices in a mesh: section: 2 (over y), fsdp: 16 (over z, x, core).
Axes of the slice: x: 2, y: 2, z: 4, core: 2. Of those that a mesh axis runs over, the one named last changes fastest.
Arguments:
- tokens: bfloat16 [2, 1536, 1024], P(None, 'fsdp'), may hold values from -6 to 6
- cotangent: bfloat16 [2, 1536, 1024], P(None, 'fsdp'), may hold values from -6 to 6
- routes: int32 [2, 2, 1536, 8], P('section', None, 'fsdp'), may hold values from 0 to 31, all different within a row; in each aligned block of 96 rows (0 to 95, 96 to 191, ..., all dimensions but the last counted through in order) at most 28 rows name the same one
- picture_start: int32 [2, 16], P(None, 'fsdp'), may hold values from 0 to 32
- w_qkv: bfloat16 [2, 1024, 2048], P('section', 'fsdp'), may hold values from -0.1875 to 0.1875
- w_out: bfloat16 [2, 1024, 1024], P('section', 'fsdp'), may hold values from -1 to 1
- w_router: bfloat16 [2, 1024, 32], P('section', 'fsdp'), may hold values from -0.09375 to 0.09375
- gain_attn: bfloat16 [2, 1024], P('section', 'fsdp'), may hold values from 0.099609375 to 1.8984375
- gain_moe: bfloat16 [2, 1024], P('section', 'fsdp'), may hold values from 0.099609375 to 1.8984375
- w_gate_up: bfloat16 [2, 16384, 2048], P('section', 'fsdp'), may hold values from -0.1875 to 0.1875
- w_down: bfloat16 [2, 16384, 1024], P('section', 'fsdp'), may hold values from -0.75 to 0.75
Outputs:
- section_out: bfloat16 [2, 2, 1536, 1024], P('section', None, 'fsdp')
- section_grad: bfloat16 [2, 2, 1536, 1024], P('section', None, 'fsdp')
- grad_qkv: float32 [2, 1024, 2048], P('section', 'fsdp')
- grad_out: float32 [2, 1024, 1024], P('section', 'fsdp')
- grad_router: float32 [2, 1024, 32], P('section', 'fsdp')
- grad_gain_attn: float32 [2, 1024], P('section', 'fsdp')
- grad_gain_moe: float32 [2, 1024], P('section', 'fsdp')
- grad_gate_up: float32 [2, 16384, 2048], P('section', 'fsdp')
- grad_down: float32 [2, 16384, 1024], P('section', 'fsdp')
Inputs may be any that keep to these rules, and one draw needn't show every extreme that they name: `routes`: each token names 8 different experts. In each layer and micro-batch no expert is named by more than 28 tokens of one sequence, and in some sequence one expert is named by exactly 28.
All inputs are finite; a program needn't handle non-finite values.
Results may differ from a plain program's by a relative error of at most 0.034.
Values may be sent and summed in bfloat16 or wider, within the bound.
No kernel may reach another device: no remote copies, remote signals or barrier semaphores. Data moves between devices by JAX's collectives and lax.ppermute only.
A program may use at most 256 MiB of HBM per device.

v0:
```python
import jax
import jax.numpy as jnp
from jax import lax
from jax.sharding import PartitionSpec as P

D = 1024
QUERY_HEADS = 16
KEY_VALUE_HEADS = 8
HEAD_SIZE = 64
EXPERTS = 32
TOP = 8
PIC = 64
CAP = 28


highest = lax.Precision.HIGHEST
epsilon = 1e-05


def from_behind(block, axis, distance):
    devices = range(lax.axis_size(axis))
    route = [(i - distance, i) for i in devices if i - distance in devices]
    return lax.ppermute(block, axis, route)


def norm_rows(values, gain_vec):
    return (
        values * lax.rsqrt(jnp.mean(values * values, axis=-1, keepdims=True) + epsilon) * gain_vec
    )


def apply_rotary(values):
    half_width = HEAD_SIZE // 2
    token_length = values.shape[0]
    frequency = 10000.0 ** (-2.0 * jnp.arange(half_width, dtype=jnp.float32) / HEAD_SIZE)
    angles = jnp.arange(token_length, dtype=jnp.float32)[:, None] * frequency[None, :]
    cosine = jnp.cos(angles)[:, None, :]
    sine_table = jnp.sin(angles)[:, None, :]
    first_half = values[..., :half_width]
    second_half = values[..., half_width:]
    return jnp.concatenate(
        [
            first_half * cosine - second_half * sine_table,
            second_half * cosine + first_half * sine_table,
        ],
        axis=-1,
    )


def visible(start_pos, token_length):
    row_pos = jnp.arange(token_length, dtype=jnp.int32)[:, None]
    col_pos = jnp.arange(token_length, dtype=jnp.int32)[None, :]
    row_inside = (row_pos >= start_pos) & (row_pos < start_pos + PIC)
    col_inside = (col_pos >= start_pos) & (col_pos < start_pos + PIC)
    return (col_pos <= row_pos) | row_inside & col_inside


def slot_table(route_rows):
    token_length = route_rows.shape[0]
    flat_routes = route_rows.reshape(-1)
    onehot = (flat_routes[:, None] == jnp.arange(EXPERTS, dtype=jnp.int32)[None, :]).astype(
        jnp.int32
    )
    before = jnp.cumsum(onehot, axis=0) - onehot
    place_index = jnp.sum(before * onehot, axis=1)
    slot_index = flat_routes * CAP + place_index
    slot_owner = (
        jnp.full((EXPERTS * CAP,), token_length * TOP, jnp.int32)
        .at[slot_index]
        .set(jnp.arange(token_length * TOP, dtype=jnp.int32))
    )
    return (slot_index.reshape(token_length, TOP), slot_owner)


def to_slots(per_expert, devices):
    repeat_count = max(1, devices // EXPERTS)
    spread = jnp.repeat(per_expert, repeat_count, axis=0) if repeat_count > 1 else per_expert
    return spread.reshape(devices, -1, CAP, D)


def from_slots(returned):
    repeat_count = max(1, returned.shape[0] // EXPERTS)
    return jnp.sum(returned.reshape(EXPERTS, repeat_count, CAP, D), axis=1)


def expert_mats(w_gate_up, w_down, per_device):
    gate_w = w_gate_up[:, :D].reshape(per_device, -1, D)
    up_w = w_gate_up[:, D:].reshape(per_device, -1, D)
    down_w = w_down.reshape(per_device, -1, D)
    return (gate_w, up_w, down_w)


def expert_front(arrived, gate_w, up_w):
    gate_val = jnp.einsum("necd,ehd->nech", arrived, gate_w, preferred_element_type=jnp.float32)
    up_val = jnp.einsum("necd,ehd->nech", arrived, up_w, preferred_element_type=jnp.float32)
    return (gate_val, up_val)


def routed_rows(normed_moe, slot_owner):
    padded = jnp.concatenate([normed_moe, jnp.zeros((1, D), jnp.bfloat16)], axis=0)
    return padded[slot_owner // TOP].reshape(EXPERTS, CAP, D)


def attention_front(layer_in, start_pos, gathered):
    w_qkv, w_out, w_router, gain_attn, gain_moe = gathered
    token_length = layer_in.shape[0]
    query_width = QUERY_HEADS * HEAD_SIZE
    key_width = KEY_VALUE_HEADS * HEAD_SIZE
    inputs = layer_in.astype(jnp.float32)
    normed = norm_rows(inputs, gain_attn.astype(jnp.float32)).astype(jnp.bfloat16)
    query_key_value = jnp.dot(normed, w_qkv, preferred_element_type=jnp.float32)
    unrotated_query = query_key_value[:, :query_width].reshape(token_length, QUERY_HEADS, HEAD_SIZE)
    unrotated_key = query_key_value[:, query_width : query_width + key_width].reshape(
        token_length, KEY_VALUE_HEADS, HEAD_SIZE
    )
    query_matrix_rows = (
        apply_rotary(unrotated_query)
        .astype(jnp.bfloat16)
        .reshape(token_length, KEY_VALUE_HEADS, QUERY_HEADS // KEY_VALUE_HEADS, HEAD_SIZE)
    )
    key_matrix_rows = apply_rotary(unrotated_key).astype(jnp.bfloat16)
    value_matrix_rows = (
        query_key_value[:, query_width + key_width :]
        .reshape(token_length, KEY_VALUE_HEADS, HEAD_SIZE)
        .astype(jnp.bfloat16)
    )
    scores = jnp.einsum(
        "qngd,knd->ngqk", query_matrix_rows, key_matrix_rows, preferred_element_type=jnp.float32
    ) * HEAD_SIZE ** (-0.5)
    scores = jnp.where(visible(start_pos, token_length)[None, None], scores, -1e30)
    exponent = jnp.exp(scores - jnp.max(scores, axis=-1, keepdims=True))
    probs = exponent / jnp.sum(exponent, axis=-1, keepdims=True)
    probs_low = probs.astype(jnp.bfloat16)
    mixed_heads = (
        jnp.einsum(
            "ngqk,knd->qngd", probs_low, value_matrix_rows, preferred_element_type=jnp.float32
        )
        .reshape(token_length, query_width)
        .astype(jnp.bfloat16)
    )
    residual = inputs + jnp.dot(mixed_heads, w_out, preferred_element_type=jnp.float32)
    normed_moe = norm_rows(residual, gain_moe.astype(jnp.float32)).astype(jnp.bfloat16)
    logits = jnp.dot(normed_moe, w_router, preferred_element_type=jnp.float32)
    return (
        inputs,
        normed,
        unrotated_query,
        unrotated_key,
        query_matrix_rows,
        key_matrix_rows,
        value_matrix_rows,
        probs,
        probs_low,
        mixed_heads,
        residual,
        normed_moe,
        logits,
    )


def forward_tick(layer_in, route_rows, start_pos, gathered, w_gate_up, w_down):
    front = attention_front(layer_in, start_pos, gathered)
    residual, normed_moe, logits = (front[10], front[11], front[12])
    slot_index, slot_owner = slot_table(route_rows)
    outgoing = to_slots(routed_rows(normed_moe, slot_owner), lax.axis_size("fsdp"))
    gate_w, up_w, down_w = expert_mats(w_gate_up, w_down, outgoing.shape[1])
    gate_val, up_val = expert_front(
        lax.all_to_all(outgoing, "fsdp", split_axis=0, concat_axis=0, tiled=True), gate_w, up_w
    )
    activation = (jax.nn.silu(gate_val) * up_val).astype(jnp.bfloat16)
    partial_out = jnp.einsum(
        "nech,ehd->necd", activation, down_w, preferred_element_type=jnp.float32
    )
    returned = lax.all_to_all(
        partial_out.astype(jnp.bfloat16), "fsdp", split_axis=0, concat_axis=0, tiled=True
    ).astype(partial_out.dtype)
    result = returned
    returned, arrived = (result, None)
    expert_out = from_slots(returned).astype(jnp.bfloat16)
    picked = expert_out.reshape(EXPERTS * CAP, D)[slot_index].astype(jnp.float32)
    gate_weights = jax.nn.softmax(jnp.take_along_axis(logits, route_rows, axis=1), axis=-1)
    mixture = jnp.einsum("tk,tkd->td", gate_weights, picked, precision=highest)
    return (residual + mixture, expert_out, arrived)


def backward_tick(
    layer_in, route_rows, start_pos, gathered, w_gate_up, w_down, expert_out, grad_out
):
    w_qkv, w_out, w_router, gain_attn, gain_moe = gathered
    front = attention_front(layer_in, start_pos, gathered)
    (
        inputs,
        normed,
        unrotated_query,
        unrotated_key,
        query_matrix_rows,
        key_matrix_rows,
        value_matrix_rows,
        probs,
        probs_low,
        mixed_heads,
        residual,
        normed_moe,
        logits,
    ) = front
    token_length = inputs.shape[0]
    slot_index, slot_owner = slot_table(route_rows)
    gate_weights = jax.nn.softmax(jnp.take_along_axis(logits, route_rows, axis=1), axis=-1)
    picked = expert_out.reshape(EXPERTS * CAP, D)[slot_index].astype(jnp.float32)
    grad_gate_weights = jnp.einsum("td,tkd->tk", grad_out, picked, precision=highest)
    grad_chosen = gate_weights * (
        grad_gate_weights - jnp.sum(gate_weights * grad_gate_weights, axis=-1, keepdims=True)
    )
    onehot = (route_rows[:, :, None] == jnp.arange(EXPERTS, dtype=jnp.int32)[None, None, :]).astype(
        jnp.float32
    )
    grad_logits = jnp.einsum("tk,tke->te", grad_chosen, onehot, precision=highest)
    pair_grad = (
        (gate_weights[:, :, None] * grad_out[:, None, :])
        .astype(jnp.bfloat16)
        .reshape(token_length * TOP, D)
    )
    pair_grad = jnp.concatenate([pair_grad, jnp.zeros((1, D), jnp.bfloat16)], axis=0)
    devices = lax.axis_size("fsdp")
    grad_slots = to_slots(pair_grad[slot_owner].reshape(EXPERTS, CAP, D), devices)
    token_slots = to_slots(routed_rows(normed_moe, slot_owner), devices)
    grad_arrived, token_arrived = (
        lax.all_to_all(grad_slots, "fsdp", split_axis=0, concat_axis=0, tiled=True),
        lax.all_to_all(token_slots, "fsdp", split_axis=0, concat_axis=0, tiled=True),
    )
    gate_w, up_w, down_w = expert_mats(w_gate_up, w_down, grad_slots.shape[1])
    gate_val, up_val = expert_front(token_arrived, gate_w, up_w)
    sigmoid_val = jax.nn.sigmoid(gate_val)
    silu_val = gate_val * sigmoid_val
    activation = (silu_val * up_val).astype(jnp.bfloat16)
    grad_act = jnp.einsum(
        "necd,ehd->nech", grad_arrived, down_w, preferred_element_type=jnp.float32
    )
    grad_down_w = jnp.einsum(
        "nech,necd->ehd", activation, grad_arrived, preferred_element_type=jnp.float32
    )
    grad_gate = (grad_act * up_val * sigmoid_val * (1.0 + gate_val * (1.0 - sigmoid_val))).astype(
        jnp.bfloat16
    )
    grad_up = (grad_act * silu_val).astype(jnp.bfloat16)
    grad_gate_w = jnp.einsum(
        "nech,necd->ehd", grad_gate, token_arrived, preferred_element_type=jnp.float32
    )
    grad_up_w = jnp.einsum(
        "nech,necd->ehd", grad_up, token_arrived, preferred_element_type=jnp.float32
    )
    partial_in = jnp.einsum("nech,ehd->necd", grad_gate, gate_w, preferred_element_type=jnp.float32)
    partial_in = partial_in + jnp.einsum(
        "nech,ehd->necd", grad_up, up_w, preferred_element_type=jnp.float32
    )
    returned = lax.all_to_all(
        partial_in.astype(jnp.bfloat16), "fsdp", split_axis=0, concat_axis=0, tiled=True
    ).astype(partial_in.dtype)
    grad_slot_rows = from_slots(returned).reshape(EXPERTS * CAP, D)
    grad_normed_moe = jnp.sum(grad_slot_rows[slot_index], axis=1)
    grad_normed_moe = grad_normed_moe + jnp.dot(
        grad_logits, w_router.astype(jnp.float32).T, precision=highest
    )
    grad_router_w = jnp.dot(normed_moe.astype(jnp.float32).T, grad_logits, precision=highest)
    moe_value, pull_moe = jax.vjp(norm_rows, residual, gain_moe.astype(jnp.float32))
    grad_resid_norm, grad_gain_moe = pull_moe(grad_normed_moe)
    grad_residual = grad_out + grad_resid_norm
    grad_branch = grad_residual.astype(jnp.bfloat16)
    grad_w_out = jnp.dot(mixed_heads.T, grad_branch, preferred_element_type=jnp.float32)
    gradient_mixed_heads = jnp.dot(grad_branch, w_out.T, preferred_element_type=jnp.float32).astype(
        jnp.bfloat16
    )
    gradient_mixed_heads = gradient_mixed_heads.reshape(
        token_length, KEY_VALUE_HEADS, QUERY_HEADS // KEY_VALUE_HEADS, HEAD_SIZE
    )
    grad_probs = jnp.einsum(
        "qngd,knd->ngqk",
        gradient_mixed_heads,
        value_matrix_rows,
        preferred_element_type=jnp.float32,
    )
    grad_values = jnp.einsum(
        "ngqk,qngd->knd", probs_low, gradient_mixed_heads, preferred_element_type=jnp.float32
    )
    grad_scores = (
        probs * (grad_probs - jnp.sum(probs * grad_probs, axis=-1, keepdims=True))
    ).astype(jnp.bfloat16)
    grad_query = jnp.einsum(
        "ngqk,knd->qngd", grad_scores, key_matrix_rows, preferred_element_type=jnp.float32
    ) * HEAD_SIZE ** (-0.5)
    grad_keys = jnp.einsum(
        "ngqk,qngd->knd", grad_scores, query_matrix_rows, preferred_element_type=jnp.float32
    ) * HEAD_SIZE ** (-0.5)
    query_value, pull_query = jax.vjp(apply_rotary, unrotated_query)
    key_value, pull_key = jax.vjp(apply_rotary, unrotated_key)
    grad_query_raw = pull_query(grad_query.reshape(token_length, QUERY_HEADS, HEAD_SIZE))[0]
    grad_key_raw = pull_key(grad_keys)[0]
    grad_qkv_rows = jnp.concatenate(
        [
            grad_query_raw.reshape(token_length, -1),
            grad_key_raw.reshape(token_length, -1),
            grad_values.reshape(token_length, -1),
        ],
        axis=1,
    ).astype(jnp.bfloat16)
    grad_w_qkv = jnp.dot(normed.T, grad_qkv_rows, preferred_element_type=jnp.float32)
    grad_normed = jnp.dot(grad_qkv_rows, w_qkv.T, preferred_element_type=jnp.float32)
    attn_value, pull_attn = jax.vjp(norm_rows, inputs, gain_attn.astype(jnp.float32))
    grad_in_norm, grad_gain_attn = pull_attn(grad_normed)
    grad_in = grad_residual + grad_in_norm
    shared = (grad_w_qkv, grad_w_out, grad_router_w, grad_gain_attn, grad_gain_moe)
    local_grads = (
        jnp.concatenate([grad_gate_w.reshape(-1, D), grad_up_w.reshape(-1, D)], axis=1),
        grad_down_w.reshape(-1, D),
    )
    return (grad_in, shared, local_grads)


def on_device(
    tokens,
    cotangent,
    routes,
    picture_start,
    w_qkv,
    w_out,
    w_router,
    gain_attn,
    gain_moe,
    w_gate_up,
    w_down,
):
    first_section = lax.axis_index("section") == 0
    micro_count = tokens.shape[0]
    own_routes = routes[0]
    local_gate_up = w_gate_up[0]
    local_down = w_down[0]

    def fetch():
        return (
            lax.all_gather(w_qkv[0], "fsdp", axis=0, tiled=True),
            lax.all_gather(w_out[0], "fsdp", axis=0, tiled=True),
            lax.all_gather(w_router[0], "fsdp", axis=0, tiled=True),
            lax.all_gather(gain_attn[0], "fsdp", axis=0, tiled=True),
            lax.all_gather(gain_moe[0], "fsdp", axis=0, tiled=True),
        )

    def weights_now():
        return fetch()

    passed = jnp.zeros_like(tokens[0])
    layer_inputs = []
    route_list = []
    start_list = []
    outputs = []
    experts_kept = []
    arrivals = []
    for tick_index in range(micro_count + 1):
        earlier = min(tick_index, micro_count - 1)
        later = max(tick_index - 1, 0)
        layer_in = jnp.where(first_section, tokens[earlier], passed)
        route_rows = jnp.where(first_section, own_routes[earlier], own_routes[later])
        start_pos = jnp.where(first_section, picture_start[earlier, 0], picture_start[later, 0])
        result_out, expert_out, arrived = forward_tick(
            layer_in, route_rows, start_pos, weights_now(), local_gate_up, local_down
        )
        out_low = result_out.astype(jnp.bfloat16)
        layer_inputs.append(layer_in)
        route_list.append(route_rows)
        start_list.append(start_pos)
        outputs.append(out_low)
        experts_kept.append(expert_out)
        arrivals.append(arrived)
        if tick_index < micro_count:
            passed = from_behind(out_low, "section", 1)
    section_out = jnp.stack(
        [
            jnp.where(first_section, outputs[index_mb], outputs[index_mb + 1])
            for index_mb in range(micro_count)
        ]
    )
    passed_grad = jnp.zeros_like(tokens[0])
    grads_list = []
    shared_total = None
    local_total = None
    for back_index in range(micro_count + 1):
        tick_index = micro_count - back_index
        later_mb = max(micro_count - 1 - back_index, 0)
        grad_out = jnp.where(first_section, passed_grad, cotangent[later_mb]).astype(jnp.float32)
        active = jnp.where(
            first_section, 1.0 if back_index >= 1 else 0.0, 1.0 if back_index < micro_count else 0.0
        )
        grad_in, shared, local_grads = backward_tick(
            layer_inputs[tick_index],
            route_list[tick_index],
            start_list[tick_index],
            weights_now(),
            local_gate_up,
            local_down,
            experts_kept[tick_index],
            grad_out,
        )
        shared = jax.tree.map(lambda array_piece: active * array_piece, shared)
        local_grads = jax.tree.map(lambda array_piece: active * array_piece, local_grads)
        if shared_total is None:
            shared_total = shared
            local_total = local_grads
        else:
            shared_total = jax.tree.map(jnp.add, shared_total, shared)
            local_total = jax.tree.map(jnp.add, local_total, local_grads)
        grad_low = grad_in.astype(jnp.bfloat16)
        grads_list.append(grad_low)
        if back_index < micro_count:
            passed_grad = from_behind(grad_low, "section", -1)
    section_grad = jnp.stack(
        [
            jnp.where(
                first_section,
                grads_list[micro_count - index_mb],
                grads_list[micro_count - 1 - index_mb],
            )
            for index_mb in range(micro_count)
        ]
    )
    summed = lax.psum_scatter(shared_total, "fsdp", scatter_dimension=0, tiled=True)
    grad_gate_up_rows = local_total[0]
    grad_down_rows = local_total[1]
    return (
        section_out[None],
        section_grad[None],
        summed[0][None],
        summed[1][None],
        summed[2][None],
        summed[3][None],
        summed[4][None],
        grad_gate_up_rows[None],
        grad_down_rows[None],
    )


def solution(mesh):
    return jax.shard_map(
        on_device,
        mesh=mesh,
        in_specs=(
            P(None, "fsdp", None),
            P(None, "fsdp", None),
            P("section", None, "fsdp", None),
            P(None, "fsdp"),
            P("section", "fsdp", None),
            P("section", "fsdp", None),
            P("section", "fsdp", None),
            P("section", "fsdp"),
            P("section", "fsdp"),
            P("section", "fsdp", None),
            P("section", "fsdp", None),
        ),
        out_specs=(
            P("section", None, "fsdp", None),
            P("section", None, "fsdp", None),
            P("section", "fsdp", None),
            P("section", "fsdp", None),
            P("section", "fsdp", None),
            P("section", "fsdp"),
            P("section", "fsdp"),
            P("section", "fsdp", None),
            P("section", "fsdp", None),
        ),
        check_vma=False,
    )
```

profile of v0, /device:TPU:0, one launch (start us, length us, event | category | flops | bytes accessed | tf_op | source)
XLA Modules:
  0.0 1251.9 jit_solution(11201600705683137713)
XLA Ops:
  13.4 35.3 %all-reduce.23 = (bf16[1024]{0:T(1024)(128)(2,1)S(1)}, bf16[1024]{0:T(1024)(128)(2,1)S(1)}) all-reduce(bf16[1024]{0:T(1024)(128)(2,1)S(1)} %dynamic-update-slice, bf16[1024]{0:T(1024)(128)(2,1)S(1)} %dynamic-update-slice.1), channel_id=2, replica_groups=mesh['section'=2,'fsdp'=16] {'fsdp'}, use_global_device_ids=true, to_apply=%add.18 | all-reduce | flops 2048 | bytes 8192
  72.5 33.2 %all-gather.10.cloned.1.call-done = bf16[1,1024,1024]{2,1,0:T(8,128)(2,1)} async-done(((bf16[1,64,1024]{2,1,0:T(8,128)(2,1)}), bf16[1,1024,1024]{2,1,0:T(8,128)(2,1)}) %all-gather.10.cloned.1.call-update) | async-done | bytes 2097168 | tf_op jit(solution)/shard_map/all_gather | solution.py:341
  130.1 31.9 %all-to-all-done = bf16[16,2,28,1024]{3,1,2,0:T(2,128)(2,1)} async-done(((bf16[16,2,28,1024]{3,1,2,0:T(2,128)(2,1)}), bf16[16,2,28,1024]{3,1,2,0:T(2,128)(2,1)}, u32[]{:S(2)}, u32[]{:S(2)}) %all-to-all-start) | async-done | bytes 1835040 | tf_op jit(solution)/shard_map/all_to_all | solution.py:168
  176.0 10.3 all-to-all-start.1
  186.8 51.6 %all-gather.4 = bf16[1,1024,32]{2,0,1:T(2,128)(2,1)} all-gather(bf16[1,64,32]{2,0,1:T(2,128)(2,1)S(1)} %copy.250), channel_id=6, replica_groups=mesh['section'=2,'fsdp'=16] {'fsdp'}, dimensions={1}, use_global_device_ids=true | all-gather | bytes 69632 | tf_op jit(solution)/shard_map/all_gather | solution.py:342
  265.3 6.3 gather_fusion.1
  308.3 50.1 %all_to_all.63 = bf16[16,2,28,1024]{3,1,2,0:T(2,128)(2,1)S(1)} all-to-all(bf16[16,2,28,1024]{3,1,2,0:T(2,128)(2,1)S(1)} %copy.264), channel_id=1, replica_groups=mesh['section'=2,'fsdp'=16] {'fsdp'}, dimensions={0} | all-to-all | bytes 3670016 | tf_op jit(solution)/shard_map/all_to_all | solution.py:168
  384.0 25.0 %all-to-all-done.3 = bf16[16,2,28,1024]{3,1,2,0:T(2,128)(2,1)} async-done(((bf16[16,2,28,1024]{3,1,2,0:T(2,128)(2,1)}), bf16[16,2,28,1024]{3,1,2,0:T(2,128)(2,1)}, u32[]{:S(2)}, u32[]{:S(2)}) %all-to-all-start.3) | async-done | bytes 1835040 | tf_op jit(solution)/shard_map/all_to_all | solution.py:174
  416.2 6.3 gather_fusion.3
  461.2 52.3 %all_to_all.64 = bf16[16,2,28,1024]{3,1,2,0:T(2,128)(2,1)S(1)} all-to-all(bf16[16,2,28,1024]{3,1,2,0:T(2,128)(2,1)S(1)} %copy.274), channel_id=1, replica_groups=mesh['section'=2,'fsdp'=16] {'fsdp'}, dimensions={0} | all-to-all | bytes 3670016 | tf_op jit(solution)/shard_map/all_to_all | solution.py:168
  535.5 28.8 %all-to-all-done.5 = bf16[16,2,28,1024]{3,1,2,0:T(2,128)(2,1)} async-done(((bf16[16,2,28,1024]{3,1,2,0:T(2,128)(2,1)}), bf16[16,2,28,1024]{3,1,2,0:T(2,128)(2,1)}, u32[]{:S(2)}, u32[]{:S(2)}) %all-to-all-start.5) | async-done | bytes 1835040 | tf_op jit(solution)/shard_map/all_to_all | solution.py:174
  571.4 6.3 gather_fusion.5
  582.5 7.2 gather_fusion.6
  597.0 52.8 %all_to_all.65 = bf16[16,2,28,1024]{3,1,2,0:T(2,128)(2,1)S(1)} all-to-all(bf16[16,2,28,1024]{3,1,2,0:T(2,128)(2,1)S(1)} %copy.279), channel_id=1, replica_groups=mesh['section'=2,'fsdp'=16] {'fsdp'}, dimensions={0} | all-to-all | bytes 3670016 | tf_op jit(solution)/shard_map/all_to_all | solution.py:228
  664.1 35.9 %all-to-all-done.7 = bf16[16,2,28,1024]{3,1,2,0:T(2,128)(2,1)} async-done(((bf16[16,2,28,1024]{3,1,2,0:T(2,128)(2,1)}), bf16[16,2,28,1024]{3,1,2,0:T(2,128)(2,1)}, u32[]{:S(2)}, u32[]{:S(2)}) %all-to-all-start.7) | async-done | bytes 1835040 | tf_op jit(solution)/shard_map/all_to_all | solution.py:256
  711.6 6.7 gather_fusion.7
  735.7 8.1 collective-permute-done.2
  747.1 7.2 gather_fusion.8
  761.6 52.3 %all_to_all.66 = bf16[16,2,28,1024]{3,1,2,0:T(2,128)(2,1)S(1)} all-to-all(bf16[16,2,28,1024]{3,1,2,0:T(2,128)(2,1)S(1)} %copy.288), channel_id=1, replica_groups=mesh['section'=2,'fsdp'=16] {'fsdp'}, dimensions={0} | all-to-all | bytes 3670016 | tf_op jit(solution)/shard_map/all_to_all | solution.py:228
  830.7 33.3 %all-to-all-done.9 = bf16[16,2,28,1024]{3,1,2,0:T(2,128)(2,1)} async-done(((bf16[16,2,28,1024]{3,1,2,0:T(2,128)(2,1)}), bf16[16,2,28,1024]{3,1,2,0:T(2,128)(2,1)}, u32[]{:S(2)}, u32[]{:S(2)}) %all-to-all-start.9) | async-done | bytes 1835040 | tf_op jit(solution)/shard_map/all_to_all | solution.py:256
  875.5 6.7 gather_fusion.9
  901.3 6.8 collective-permute-done.3
  912.0 7.3 gather_fusion.10
  926.6 52.3 %all_to_all.67 = bf16[16,2,28,1024]{3,1,2,0:T(2,128)(2,1)S(1)} all-to-all(bf16[16,2,28,1024]{3,1,2,0:T(2,128)(2,1)S(1)} %copy.297), channel_id=1, replica_groups=mesh['section'=2,'fsdp'=16] {'fsdp'}, dimensions={0} | all-to-all | bytes 3670016 | tf_op jit(solution)/shard_map/all_to_all | solution.py:228
  1003.8 25.0 %all-to-all-done.11 = bf16[16,2,28,1024]{3,1,2,0:T(2,128)(2,1)} async-done(((bf16[16,2,28,1024]{3,1,2,0:T(2,128)(2,1)}), bf16[16,2,28,1024]{3,1,2,0:T(2,128)(2,1)}, u32[]{:S(2)}, u32[]{:S(2)}) %all-to-all-start.11) | async-done | bytes 1835040 | tf_op jit(solution)/shard_map/all_to_all | solution.py:256
  1040.5 6.8 gather_fusion.11
  1058.2 5.8 fusion.187
  1076.0 11.7 multiply_add_fusion
  1125.9 11.9 fusion.4
  1137.9 7.5 fusion.5
  1147.9 40.3 %all-reduce.22 = (f32[1024]{0:T(1024)S(1)}, f32[1024]{0:T(1024)S(1)}) all-reduce(f32[1024]{0:T(1024)S(1)} %multiply_add_fusion.15, f32[1024]{0:T(1024)S(1)} %multiply_add_fusion.14), channel_id=10, replica_groups=mesh['section'=2,'fsdp'=16] {'fsdp'}, use_global_device_ids=true, to_apply=%region_51.53.clone | all-reduce | flops 2048 | bytes 16384
  1191.4 53.7 %reduce-scatter.6.cloned.1.call-done = f32[64,2048]{1,0:T(8,128)} async-done(((f32[1024,2048]{1,0:T(8,128)}), f32[64,2048]{1,0:T(8,128)}) %reduce-scatter.6.cloned.1.call-update) | async-done | bytes 524304 | tf_op jit(solution)/shard_map/reduce_scatter | solution.py:424
  (803 shorter events, 453.9 us)
Async XLA Ops:
  7.2 163.5 %copy-start = (bf16[1,1024,1024]{2,1,0:T(8,128)(2,1)S(1)}, bf16[1,1024,1024]{2,1,0:T(8,128)(2,1)}, u32[]{:S(2)}) copy-start(bf16[1,1024,1024]{2,1,0:T(8,128)(2,1)} %param.23) | copy-start | bytes 6291460
  7.2 56.4 %all-gather.8.cloned.1.call-start = ((), (), s32[]{:S(2)}) async-start(), calls=%async_computation.17 | async-start | bytes 4456448 | tf_op jit(solution)/shard_map/all_gather | solution.py:340
  7.9 97.8 %all-gather.10.cloned.1.call-start = ((), (), s32[]{:S(2)}) async-start(), calls=%async_computation.18 | async-start | bytes 2228224 | tf_op jit(solution)/shard_map/all_gather | solution.py:341
  9.5 248.5 %copy-start.32 = (s32[1,1,96,8]{3,2,1,0:T(8,128)}, s32[1,1,96,8]{3,2,1,0:T(8,128)S(1)}, u32[]{:S(2)}) copy-start(s32[1,1,96,8]{3,2,1,0:T(8,128)S(1)} %copy.371) | copy-start | bytes 9220
  9.6 57.2 %copy-start.169 = (s32[768]{0:T(1024)}, s32[768]{0:T(1024)S(1)}, u32[]{:S(2)}) copy-start(s32[768]{0:T(1024)S(1)} %eq.131) | copy-start | bytes 9220
  48.7 59.4 %copy-start.131 = (f32[1024]{0:T(1024)}, f32[1024]{0:T(1024)S(1)}, u32[]{:S(2)}) copy-start(f32[1024]{0:T(1024)S(1)} %convert_element_type.414) | copy-start | bytes 12292
  59.0 231.5 %copy-start.42 = (f32[96,32]{0,1:T(8,128)}, f32[96,32]{0,1:T(8,128)S(1)}, u32[]{:S(2)}) copy-start(f32[96,32]{0,1:T(8,128)S(1)} %get-tuple-element.100) | copy-start | bytes 36868
  59.0 231.5 %copy-start.45 = (f32[96,32]{0,1:T(8,128)}, f32[96,32]{0,1:T(8,128)S(1)}, u32[]{:S(2)}) copy-start(f32[96,32]{0,1:T(8,128)S(1)} %get-tuple-element.101) | copy-start | bytes 36868
  108.1 166.3 %copy-start.19 = (f32[96,1024]{1,0:T(8,128)}, f32[96,1024]{1,0:T(8,128)S(1)}, u32[]{:S(2)}) copy-start(f32[96,1024]{1,0:T(8,128)S(1)} %get-tuple-element.105) | copy-start | bytes 1179652
  108.2 144.1 %copy-start.37 = (bf16[96,1024]{1,0:T(8,128)(2,1)}, bf16[96,1024]{1,0:T(8,128)(2,1)S(1)}, u32[]{:S(2)}) copy-start(bf16[96,1024]{1,0:T(8,128)(2,1)S(1)} %multiply_convert_fusion.5) | copy-start | bytes 589828
  120.8 41.1 %all-to-all-start = ((bf16[16,2,28,1024]{3,1,2,0:T(2,128)(2,1)}), bf16[16,2,28,1024]{3,1,2,0:T(2,128)(2,1)}, u32[]{:S(2)}, u32[]{:S(2)}) async-start(bf16[16,2,28,1024]{3,1,2,0:T(2,128)(2,1)} %copy.253), calls=%async_computation | async-start | bytes 3670016 | tf_op jit(solution)/shard_map/all_to_all | solution.py:168
  176.0 66.5 %copy-start.174 = (s32[6,128]{1,0:T(8,128)S(1)}, s32[6,128]{1,0:T(8,128)}, u32[]{:S(2)}) copy-start(s32[6,128]{1,0:T(8,128)} %copy-done.173) | copy-start | bytes 9220
  176.0 82.1 %all-to-all-start.1 = ((bf16[16,2,28,1024]{3,1,2,0:T(2,128)(2,1)}), bf16[16,2,28,1024]{3,1,2,0:T(2,128)(2,1)}, u32[]{:S(2)}, u32[]{:S(2)}) async-start(bf16[16,2,28,1024]{3,1,2,0:T(2,128)(2,1)} %copy.256), calls=%async_computation.1 | async-start | bytes 3670016 | tf_op jit(solution)/shard_map/all_to_all | solution.py:174
  186.3 58.2 %copy-start.170 = (s32[768]{0:T(1024)S(1)}, s32[768]{0:T(1024)}, u32[]{:S(2)}) copy-start(s32[768]{0:T(1024)} %copy-done.169) | copy-start | bytes 9220
  186.4 59.9 %copy-start.34 = (s32[1,1,96,8]{3,2,1,0:T(8,128)}, s32[1,1,96,8]{3,2,1,0:T(8,128)S(1)}, u32[]{:S(2)}) copy-start(s32[1,1,96,8]{3,2,1,0:T(8,128)S(1)} %copy.372) | copy-start | bytes 9220
  274.5 8.0 collective-permute-start
  296.9 81.3 %copy-start.40 = (bf16[96,1024]{1,0:T(8,128)(2,1)}, bf16[96,1024]{1,0:T(8,128)(2,1)S(1)}, u32[]{:S(2)}) copy-start(bf16[96,1024]{1,0:T(8,128)(2,1)S(1)} %multiply_convert_fusion.4) | copy-start | bytes 589828
  367.9 41.1 %all-to-all-start.3 = ((bf16[16,2,28,1024]{3,1,2,0:T(2,128)(2,1)}), bf16[16,2,28,1024]{3,1,2,0:T(2,128)(2,1)}, u32[]{:S(2)}, u32[]{:S(2)}) async-start(bf16[16,2,28,1024]{3,1,2,0:T(2,128)(2,1)} %copy.267), calls=%async_computation.3 | async-start | bytes 3670016 | tf_op jit(solution)/shard_map/all_to_all | solution.py:174
  426.1 9.5 collective-permute-start.1
  449.8 79.9 %copy-start.39 = (bf16[96,1024]{1,0:T(8,128)(2,1)}, bf16[96,1024]{1,0:T(8,128)(2,1)S(1)}, u32[]{:S(2)}) copy-start(bf16[96,1024]{1,0:T(8,128)(2,1)S(1)} %multiply_convert_fusion.3) | copy-start | bytes 589828
  523.0 41.3 %all-to-all-start.5 = ((bf16[16,2,28,1024]{3,1,2,0:T(2,128)(2,1)}), bf16[16,2,28,1024]{3,1,2,0:T(2,128)(2,1)}, u32[]{:S(2)}, u32[]{:S(2)}) async-start(bf16[16,2,28,1024]{3,1,2,0:T(2,128)(2,1)} %copy.277), calls=%async_computation.5 | async-start | bytes 3670016 | tf_op jit(solution)/shard_map/all_to_all | solution.py:174
  580.9 82.6 %copy-start.110 = (f32[96,8]{1,0:T(8,128)}, f32[96,8]{1,0:T(8,128)S(1)}, u32[]{:S(2)}) copy-start(f32[96,8]{1,0:T(8,128)S(1)} %get-tuple-element.33) | copy-start | bytes 9220
  593.3 56.5 %copy-start.234 = (f32[2,16,28,512]{3,2,1,0:T(8,128)S(1)}, f32[2,16,28,512]{3,2,1,0:T(8,128)}, u32[]{:S(2)}) copy-start(f32[2,16,28,512]{3,2,1,0:T(8,128)} %get-tuple-element.119) | copy-start | bytes 5505028
  658.7 41.3 %all-to-all-start.7 = ((bf16[16,2,28,1024]{3,1,2,0:T(2,128)(2,1)}), bf16[16,2,28,1024]{3,1,2,0:T(2,128)(2,1)}, u32[]{:S(2)}, u32[]{:S(2)}) async-start(bf16[16,2,28,1024]{3,1,2,0:T(2,128)(2,1)} %copy.281), calls=%async_computation.7 | async-start | bytes 3670016 | tf_op jit(solution)/shard_map/all_to_all | solution.py:256
  664.1 56.9 %copy-start.153 = (f32[96,1,32]{2,1,0:T(1,128)}, f32[96,1,32]{2,1,0:T(1,128)S(1)}, u32[]{:S(2)}) copy-start(f32[96,1,32]{2,1,0:T(1,128)S(1)} %fusion.183) | copy-start | bytes 36868
  733.9 9.9 collective-permute-start.2
  822.8 41.1 %all-to-all-start.9 = ((bf16[16,2,28,1024]{3,1,2,0:T(2,128)(2,1)}), bf16[16,2,28,1024]{3,1,2,0:T(2,128)(2,1)}, u32[]{:S(2)}, u32[]{:S(2)}) async-start(bf16[16,2,28,1024]{3,1,2,0:T(2,128)(2,1)} %copy.290), calls=%async_computation.9 | async-start | bytes 3670016 | tf_op jit(solution)/shard_map/all_to_all | solution.py:256
  898.3 9.8 collective-permute-start.3
  987.9 40.9 %all-to-all-start.11 = ((bf16[16,2,28,1024]{3,1,2,0:T(2,128)(2,1)}), bf16[16,2,28,1024]{3,1,2,0:T(2,128)(2,1)}, u32[]{:S(2)}, u32[]{:S(2)}) async-start(bf16[16,2,28,1024]{3,1,2,0:T(2,128)(2,1)} %copy.299), calls=%async_computation.11 | async-start | bytes 3670016 | tf_op jit(solution)/shard_map/all_to_all | solution.py:256
  992.3 121.7 %reduce-scatter.10.cloned.1.call-start = ((), (), s32[]{:S(2)}) async-start(), calls=%async_computation.19 | async-start | bytes 557056
  1003.8 187.6 %reduce-scatter.8.cloned.1.call-start = ((), (), s32[]{:S(2)}) async-start(), calls=%async_computation.16 | async-start | bytes 4456448 | tf_op jit(solution)/shard_map/reduce_scatter | solution.py:424
  1057.3 187.9 %reduce-scatter.6.cloned.1.call-start = ((), (), s32[]{:S(2)}) async-start(), calls=%async_computation.15 | async-start | bytes 8912896 | tf_op jit(solution)/shard_map/reduce_scatter | solution.py:424
  (221 other events, 1478.0 us)
Sparse Core Ops, SparseCore 0:
  10.2 53.3 all-gather.7
  65.8 39.9 all-gather.9
  1003.9 56.4 reduce-scatter.9
  1065.1 71.7 reduce-scatter.7
  1141.4 103.7 reduce-scatter.5
where the time goes:
time: 1260 us; the launch traced here: 1250 us
  blocking collectives  387 us (31%)
  waiting for transfers between devices  297 us (24%)
  local copies, waits for them, and re-layouts  258 us (20%)
  matrix products  178 us (14%)
  other arithmetic  60.8 us (5%)
  starting transfers between devices  50.1 us (4%)
  between operations  21.3 us (2%)
    all_to_all x3, blocking collectives, backward_tick(): lax.all_to_all(grad_slots, 'fsdp', split_axis=0, concat_axis=0, tiled=True)  157 us
    all_to_all x2, blocking collectives, forward_tick(): lax.all_to_all(outgoing, 'fsdp', split_axis=0, concat_axis=0, tiled=True)  102 us
    all_to_all x3, waiting for transfers between devices, backward_tick(): lax.all_to_all(partial_in.astype(jnp.bfloat16), 'fsdp', split_axis=0, con...  94.1 us
    unnamed x2, blocking collectives  75.6 us
    all_to_all x3, waiting for transfers between devices, forward_tick(): lax.all_to_all(partial_out.astype(jnp.bfloat16), 'fsdp', split_axis=0, co...  53.8 us
    reduce_scatter x2, waiting for transfers between devices, on_device(): lax.psum_scatter(shared_total, 'fsdp', scatter_dimension=0, tiled=True)  53.7 us
    all_gather x1, blocking collectives, fetch(): lax.all_gather(w_router[0], 'fsdp', axis=0, tiled=True)  51.6 us
    another operation x12, local copies, waits for them, and re-layouts, to_slots(): return spread.reshape(devices, -1, CAP, D)  44.6 us
  transfers between devices with their start and end apart: 16, of which 13 were waited for; matrix products, arithmetic and copies ran while one was open for 16% of the time, Pallas kernels for 0%

commit v1 on v0

v1 whole, which is shorter than its diff:
```python
import functools

import jax
import jax.numpy as jnp
import numpy as np
from jax import lax
from jax.experimental import pallas as pl
from jax.experimental.pallas import tpu as pltpu
from jax.sharding import PartitionSpec as P

D = 1024
QUERY_HEADS = 16
KEY_VALUE_HEADS = 8
HEAD_SIZE = 64
EXPERTS = 32
TOP = 8
PIC = 64
SLOTS = 32
LANES = 128
QKV = 2048
WIDE = D + LANES
WCOLS = QKV + D + LANES
epsilon = 1e-05
scale = HEAD_SIZE ** (-0.5)
f32 = jnp.float32
bf16 = jnp.bfloat16
VMEM_LIMIT = 56 * 1024 * 1024

PATH = (0, 2, 4, 6, 7, 5, 3, 1)
PLACE = tuple(PATH.index(c) for c in range(8))


def dot(a, b, ca, cb):
    return lax.dot_general(a, b, (((ca,), (cb,)), ((), ())), preferred_element_type=f32)


def nn(a, b):
    return dot(a, b, 1, 0)


def nt(a, b):
    return dot(a, b, 1, 1)


def tn(a, b):
    return dot(a, b, 0, 0)


def lanes_of(shape):
    return lax.broadcasted_iota(jnp.int32, shape, len(shape) - 1)


def rms(values):
    return lax.rsqrt(jnp.mean(values * values, axis=-1, keepdims=True) + epsilon)


def norm_back(values, inv, gain, grad):
    scaled = grad * gain
    inner = jnp.mean(scaled * values, axis=-1, keepdims=True)
    return inv * scaled - values * (inv * inv * inv * inner)


def turn(chunk, cosine, sine, back):
    first = (lanes_of(chunk.shape) & 63) < 32
    ahead = pltpu.roll(chunk, 96, 1)
    behind = pltpu.roll(chunk, 32, 1)
    if back:
        swapped = jnp.where(first, ahead, -behind)
    else:
        swapped = jnp.where(first, -ahead, behind)
    return chunk * cosine + swapped * sine


def halves(chunk):
    low = lanes_of(chunk.shape) < 64
    return jnp.concatenate([jnp.where(low, chunk, 0.0), jnp.where(low, 0.0, chunk)], axis=0)


def join(stacked):
    rows = stacked.shape[0] // 2
    low = lanes_of((rows, LANES)) < 64
    return jnp.where(low, stacked[:rows], stacked[rows:])


def doubled(chunk, odd):
    low = lanes_of(chunk.shape) < 64
    other = pltpu.roll(chunk, 64, 1)
    return jnp.where(low, other, chunk) if odd else jnp.where(low, chunk, other)


def load_weights(order, w_hbm, w_vmem, sems):
    copies = []
    for k in range(8):
        for b in range(2):
            copies.append(
                pltpu.make_async_copy(
                    w_hbm.at[k, b], w_vmem.at[order[0, k] * 2 + (order[1, 0] ^ b)], sems.at[k * 2 + b]
                )
            )
    for copy in copies:
        copy.start()
    return copies


def gains_of(w_vmem):
    pieces = ([], [])
    for c in range(8):
        even = w_vmem[2 * c, 0:16, QKV + D :].astype(f32)
        odd = w_vmem[2 * c + 1, 0:16, QKV + D :].astype(f32)
        even = pltpu.roll(even, 64, 1)
        both = jnp.where(lanes_of(even.shape) < 64, even, odd)
        for i in range(2):
            pieces[i].append(both[i : i + 1])
    return jnp.concatenate(pieces[0], axis=1), jnp.concatenate(pieces[1], axis=1)


def attn_forward_kernel(
    save, order, starts, x_ref, pos_ref, cos_ref, sin_ref, w_hbm, *rest
):
    if save:
        (out_ref, resid_ref, gate_ref, normed_ref, q_ref, k_ref, v_ref, probs_ref, mixed_ref) = rest[:9]
        w_vmem, sems = rest[9:]
    else:
        out_ref, resid_ref, w_vmem, sems, mixed_ref = rest
    copies = load_weights(order, w_hbm, w_vmem, sems)
    seqs, length = x_ref.shape[0], x_ref.shape[1]
    rows = seqs * length
    for copy in copies:
        copy.wait()
    gain_attn, gain_moe = gains_of(w_vmem)
    x = x_ref[...].reshape(rows, D).astype(f32)
    normed = (x * rms(x) * gain_attn).astype(bf16)
    w_qkv = w_vmem[:, :, :QKV].reshape(D, QKV)
    qkv = nn(normed, w_qkv)
    cosine, sine = cos_ref[...], sin_ref[...]
    row_pos = lax.broadcasted_iota(jnp.int32, (length, length), 0)
    col_pos = lax.broadcasted_iota(jnp.int32, (length, length), 1)
    for s in range(seqs):
        top = slice(s * length, (s + 1) * length)
        start = starts[s]
        both = (
            (row_pos >= start) & (row_pos < start + PIC) & (col_pos >= start) & (col_pos < start + PIC)
        )
        bias = jnp.where((col_pos <= row_pos) | both, 0.0, -1e30)
        bias = jnp.concatenate([bias, bias], axis=0)
        keys, values = [], []
        for c in range(4):
            key = turn(qkv[top, D + c * LANES : D + (c + 1) * LANES], cosine, sine, False)
            value = qkv[top, D + 512 + c * LANES : D + 512 + (c + 1) * LANES]
            keys.append(key)
            values.append(value)
            if save:
                k_ref[top, c * LANES : (c + 1) * LANES] = key.astype(bf16)
                v_ref[top, c * LANES : (c + 1) * LANES] = value.astype(bf16)
        for j in range(KEY_VALUE_HEADS):
            query = turn(qkv[top, j * LANES : (j + 1) * LANES], cosine, sine, False)
            if save:
                q_ref[top, j * LANES : (j + 1) * LANES] = query.astype(bf16)
            key = doubled(keys[j // 2], j % 2 == 1).astype(bf16)
            value = doubled(values[j // 2], j % 2 == 1).astype(bf16)
            scores = nt(halves(query).astype(bf16), key) * scale + bias
            exponent = jnp.exp(scores - jnp.max(scores, axis=-1, keepdims=True))
            probs = exponent / jnp.sum(exponent, axis=-1, keepdims=True)
            if save:
                probs_ref[s * KEY_VALUE_HEADS + j] = probs
            mixed = join(nn(probs.astype(bf16), value))
            mixed_ref[top, j * LANES : (j + 1) * LANES] = mixed.astype(bf16)
    w_out = w_vmem[:, :, QKV : QKV + D].reshape(D, D)
    resid = x + nn(mixed_ref[...], w_out)
    normed_moe = (resid * rms(resid) * gain_moe).astype(bf16)
    w_small = w_vmem[:, :, QKV + D :].reshape(D, LANES)
    logits = nn(normed_moe, w_small)
    pos = pos_ref[...]
    routed = pos < 64.0
    logits = jnp.where(routed, logits, -1e30)
    exponent = jnp.where(routed, jnp.exp(logits - jnp.max(logits, axis=-1, keepdims=True)), 0.0)
    gate = exponent / jnp.sum(exponent, axis=-1, keepdims=True)
    high = gate.astype(bf16).astype(f32)
    low = gate - high
    lane = lanes_of(gate.shape)
    columns = jnp.where(
        lane < 32,
        high,
        jnp.where(
            lane < 64,
            pltpu.roll(low, 32, 1),
            jnp.where(lane < 96, pltpu.roll(pos, 64, 1), 0.0),
        ),
    )
    out_ref[:, :, :D] = normed_moe.reshape(seqs, length, D)
    out_ref[:, :, D:] = columns.astype(bf16).reshape(seqs, length, LANES)
    resid_ref[...] = resid
    if save:
        gate_ref[...] = gate
        normed_ref[...] = normed


def vmem():
    return pl.BlockSpec(memory_space=pltpu.VMEM)


def smem():
    return pl.BlockSpec(memory_space=pltpu.SMEM)


def anywhere():
    return pl.BlockSpec(memory_space=pl.ANY)


def attn_forward(save, order, starts, x, pos, cosine, sine, w_all):
    seqs, length = x.shape[0], x.shape[1]
    rows = seqs * length
    shape = jax.ShapeDtypeStruct
    outs = [shape((seqs, length, WIDE), bf16), shape((rows, D), f32)]
    scratch = [pltpu.VMEM((16, 64, WCOLS), bf16), pltpu.SemaphoreType.DMA((16,))]
    if save:
        outs += [
            shape((rows, LANES), f32),
            shape((rows, D), bf16),
            shape((rows, D), bf16),
            shape((rows, 512), bf16),
            shape((rows, 512), bf16),
            shape((seqs * KEY_VALUE_HEADS, 2 * length, length), f32),
            shape((rows, D), bf16),
        ]
    else:
        scratch.append(pltpu.VMEM((rows, D), bf16))
    return pl.pallas_call(
        functools.partial(attn_forward_kernel, save),
        out_shape=outs,
        in_specs=[smem(), smem(), vmem(), vmem(), vmem(), vmem(), anywhere()],
        out_specs=[vmem()] * len(outs),
        scratch_shapes=scratch,
        compiler_params=pltpu.CompilerParams(vmem_limit_bytes=VMEM_LIMIT),
        cost_estimate=pl.CostEstimate(
            flops=2 * rows * D * 3400, bytes_accessed=12_000_000, transcendentals=rows * 2048
        ),
        name="attn_forward",
    )(order, starts, x, pos, cosine, sine, w_all)


def attn_backward_kernel(
    with_grads,
    order,
    sum_ref,
    g_ref,
    x_ref,
    wide_ref,
    resid_ref,
    gate_ref,
    normed_ref,
    q_ref,
    k_ref,
    v_ref,
    probs_ref,
    mixed_ref,
    cos_ref,
    sin_ref,
    w_hbm,
    *rest,
):
    if with_grads:
        grad_ref, big_ref, w_vmem, sems, back_ref, gains_ref = rest
    else:
        grad_ref, w_vmem, sems, back_ref = rest
    copies = load_weights(order, w_hbm, w_vmem, sems)
    seqs, length = x_ref.shape[0], x_ref.shape[1]
    rows = seqs * length
    for copy in copies:
        copy.wait()
    gain_attn, gain_moe = gains_of(w_vmem)
    gate = gate_ref[...]
    high_low = sum_ref[:, D:]
    grad_gate = high_low + pltpu.roll(high_low, 96, 1)
    inner = jnp.sum(gate * grad_gate, axis=-1, keepdims=True)
    grad_logits = jnp.where(lanes_of(gate.shape) < 32, gate * (grad_gate - inner), 0.0)
    grad_logits = grad_logits.astype(bf16)
    w_small = w_vmem[:, :, QKV + D :].reshape(D, LANES)
    grad_normed_moe = sum_ref[:, :D] + nt(grad_logits, w_small)
    resid = resid_ref[...]
    inv_moe = rms(resid)
    grad_resid = g_ref[...].reshape(rows, D).astype(f32) + norm_back(
        resid, inv_moe, gain_moe, grad_normed_moe
    )
    grad_branch = grad_resid.astype(bf16)
    w_out = w_vmem[:, :, QKV : QKV + D].reshape(D, D)
    grad_mixed = nt(grad_branch, w_out)
    cosine, sine = cos_ref[...], sin_ref[...]
    low = lanes_of((length, LANES)) < 64
    for s in range(seqs):
        top = slice(s * length, (s + 1) * length)
        key_parts, value_parts = [], []
        for j in range(KEY_VALUE_HEADS):
            here = slice(j * LANES, (j + 1) * LANES)
            pair = slice((j // 2) * LANES, (j // 2 + 1) * LANES)
            query = halves(q_ref[top, here].astype(f32)).astype(bf16)
            key = doubled(k_ref[top, pair].astype(f32), j % 2 == 1).astype(bf16)
            value = doubled(v_ref[top, pair].astype(f32), j % 2 == 1).astype(bf16)
            grad_heads = halves(grad_mixed[top, here]).astype(bf16)
            probs = probs_ref[s * KEY_VALUE_HEADS + j]
            grad_probs = nt(grad_heads, value)
            grad_value = tn(probs.astype(bf16), grad_heads)
            grad_scores = probs * (grad_probs - jnp.sum(probs * grad_probs, axis=-1, keepdims=True))
            grad_scores = grad_scores.astype(bf16)
            grad_query = join(nn(grad_scores, key)) * scale
            grad_key = tn(grad_scores, query) * scale
            back_ref[top, here] = turn(grad_query, cosine, sine, True).astype(bf16)
            key_parts.append(grad_key + pltpu.roll(grad_key, 64, 1))
            value_parts.append(grad_value + pltpu.roll(grad_value, 64, 1))
        for c in range(4):
            grad_key = jnp.where(low, key_parts[2 * c], key_parts[2 * c + 1])
            grad_value = jnp.where(low, value_parts[2 * c], value_parts[2 * c + 1])
            back_ref[top, D + c * LANES : D + (c + 1) * LANES] = turn(
                grad_key, cosine, sine, True
            ).astype(bf16)
            back_ref[top, D + 512 + c * LANES : D + 512 + (c + 1) * LANES] = grad_value.astype(bf16)
    w_qkv = w_vmem[:, :, :QKV].reshape(D, QKV)
    grad_rows = back_ref[...]
    grad_normed = nt(grad_rows, w_qkv)
    x = x_ref[...].reshape(rows, D).astype(f32)
    inv_attn = rms(x)
    grad_in = grad_resid + norm_back(x, inv_attn, gain_attn, grad_normed)
    grad_ref[...] = grad_in.astype(bf16).reshape(seqs, length, D)
    if with_grads:
        gains_ref[0:1] = jnp.sum(grad_normed * x * inv_attn, axis=0, keepdims=True)
        gains_ref[1:2] = jnp.sum(grad_normed_moe * resid * inv_moe, axis=0, keepdims=True)
        row = lax.broadcasted_iota(jnp.int32, (LANES, LANES), 0)
        lane = lanes_of((LANES, LANES))
        for k in range(8):
            columns = pl.ds(pl.multiple_of(order[0, k] * LANES, LANES), LANES)
            part_qkv = tn(normed_ref[:, columns], grad_rows)
            part_out = tn(mixed_ref[:, columns], grad_branch)
            moe_rows = jnp.concatenate(
                [wide_ref[s, :, columns] for s in range(seqs)], axis=0
            )
            part_small = tn(moe_rows, grad_logits)
            for i in range(2):
                piece = gains_ref[i : i + 1, columns]
                turned = pltpu.roll(piece, 64, 1)
                part_small = part_small + jnp.where((row == i) & (lane >= 64), turned, 0.0)
                part_small = part_small + jnp.where((row == 64 + i) & (lane >= 64), piece, 0.0)
            for b in range(2):
                half = slice(b * 64, (b + 1) * 64)
                slot = order[1, 0] ^ b
                big_ref[k, slot, :, :QKV] = part_qkv[half].astype(bf16)
                big_ref[k, slot, :, QKV : QKV + D] = part_out[half].astype(bf16)
                big_ref[k, slot, :, QKV + D :] = part_small[half].astype(bf16)


def attn_backward(with_grads, order, sums, g, x, saved, cosine, sine, w_all):
    seqs, length = x.shape[0], x.shape[1]
    rows = seqs * length
    shape = jax.ShapeDtypeStruct
    outs = [shape((seqs, length, D), bf16)]
    scratch = [
        pltpu.VMEM((16, 64, WCOLS), bf16),
        pltpu.SemaphoreType.DMA((16,)),
        pltpu.VMEM((rows, QKV), bf16),
    ]
    if with_grads:
        outs.append(shape((8, 2, 64, WCOLS), bf16))
        scratch.append(pltpu.VMEM((8, D), f32))
    return pl.pallas_call(
        functools.partial(attn_backward_kernel, with_grads),
        out_shape=outs,
        in_specs=[smem()] + [vmem()] * 14 + [anywhere()],
        out_specs=[vmem()] * len(outs),
        scratch_shapes=scratch,
        compiler_params=pltpu.CompilerParams(vmem_limit_bytes=VMEM_LIMIT),
        cost_estimate=pl.CostEstimate(
            flops=4 * rows * D * 3400, bytes_accessed=20_000_000, transcendentals=0
        ),
        name="attn_backward",
    )(order, sums, g, x, *saved, cosine, sine, w_all)


def expert_kernel(mode, parts, which, *refs):
    refs = list(refs)
    take = lambda count: [refs.pop(0) for _ in range(count)]
    x_refs = take(parts)
    g_refs = take(parts) if mode else []
    w_in, w_down = take(2)
    out_refs = take(parts)
    if mode == 2:
        x_rows, g_rows, act_rows, gate_rows, up_rows = take(5)
    elif mode == 1:
        x_rows, g_rows = take(2)
    else:
        (x_rows,) = take(1)
    hot_ref, scale_ref, result_ref = take(3)
    per = x_rows.shape[0]
    hid = w_down.shape[0] // per
    first = which[0]
    spots = [(i, s) for i in range(parts) for s in range(x_refs[i].shape[0])]
    length = x_refs[0].shape[1]
    row8 = lax.broadcasted_iota(jnp.int32, (8, LANES), 0)
    lane8 = lanes_of((8, LANES))
    pick = jnp.where((lane8 == 64 + first + row8) & (row8 < per), 1.0, 0.0).astype(bf16)
    slot = lax.broadcasted_iota(jnp.int32, (SLOTS, length), 0).astype(f32)
    lane = lanes_of((SLOTS, LANES))
    for n, (i, s) in enumerate(spots):
        columns = x_refs[i][s, :, D:]
        places = nt(pick, columns)
        hot = jnp.concatenate(
            [jnp.where(places[j : j + 1] == slot, 1.0, 0.0) for j in range(per)], axis=0
        ).astype(bf16)
        hot_ref[n] = hot
        taken = nn(hot, x_refs[i][s])
        here = slice(n * SLOTS, (n + 1) * SLOTS)
        for j in range(per):
            block = taken[j * SLOTS : (j + 1) * SLOTS]
            x_rows[j, here] = block[:, :D].astype(bf16)
            own = (lane == first + j) | (lane == 32 + first + j)
            gate = jnp.sum(jnp.where(own, block[:, D:], 0.0), axis=-1, keepdims=True)
            scale_ref[j, here] = jnp.broadcast_to(gate, (SLOTS, LANES))
        if mode:
            taken = nn(hot, g_refs[i][s])
            for j in range(per):
                g_rows[j, here] = taken[j * SLOTS : (j + 1) * SLOTS].astype(bf16)
    total = len(spots) * SLOTS
    lane = lanes_of((total, LANES))
    for j in range(per):
        own_rows = slice(j * hid, (j + 1) * hid)
        rows = x_rows[j]
        gate_val = nt(rows, w_in[own_rows, :D])
        up_val = nt(rows, w_in[own_rows, D:])
        sig = jax.nn.sigmoid(gate_val)
        silu = gate_val * sig
        act = silu * up_val
        gate = scale_ref[j][:, 0:1]

        def forward():
            result_ref[j, :, :D] = (nn(act.astype(bf16), w_down[own_rows]) * gate).astype(bf16)

        def backward():
            inner = nt(g_rows[j], w_down[own_rows])
            grad_gw = jnp.sum(act.astype(bf16).astype(f32) * inner, axis=-1, keepdims=True)
            inner = inner * gate
            grad_gate = (inner * up_val * sig * (1.0 + gate_val * (1.0 - sig))).astype(bf16)
            grad_up = (inner * silu).astype(bf16)
            if mode == 2:
                act_rows[j] = (act * gate).astype(bf16)
                gate_rows[j] = grad_gate
                up_rows[j] = grad_up
            grad_in = nn(grad_gate, w_in[own_rows, :D]) + nn(grad_up, w_in[own_rows, D:])
            high = grad_gw.astype(bf16).astype(f32)
            extra = jnp.where(
                lane == first + j, high, jnp.where(lane == 32 + first + j, grad_gw - high, 0.0)
            )
            result_ref[j, :, :D] = grad_in.astype(bf16)
            result_ref[j, :, D:] = extra.astype(bf16)

        if mode == 0:
            forward()
        else:
            backward()
            if mode == 2:

                @pl.when(which[1] != 0)
                def _():
                    forward()

    for n, (i, s) in enumerate(spots):
        here = slice(n * SLOTS, (n + 1) * SLOTS)
        block = jnp.concatenate([result_ref[j, here] for j in range(per)], axis=0)
        out_refs[i][s] = tn(hot_ref[n], block).astype(bf16)


def expert_call(mode, which, x_parts, g_parts, w_in, w_down, per):
    parts = len(x_parts)
    seqs = sum(x.shape[0] for x in x_parts)
    length = x_parts[0].shape[1]
    hid = w_down.shape[0] // per
    total = seqs * SLOTS
    out_width = WIDE if mode else D
    shape = jax.ShapeDtypeStruct
    outs = [shape((x.shape[0], length, out_width), bf16) for x in x_parts]
    rows = (per, total, D)
    scratch = [
        pltpu.VMEM((seqs, per * SLOTS, length), bf16),
        pltpu.VMEM((per, total, LANES), f32),
        pltpu.VMEM((per, total, out_width), bf16),
    ]
    if mode == 2:
        outs += [shape(rows, bf16), shape(rows, bf16)] + [shape((per, total, hid), bf16)] * 3
    else:
        scratch = [pltpu.VMEM(rows, bf16)] * (2 if mode else 1) + scratch
    units = (3, 5, 7)[mode]
    whole = lambda a: pl.BlockSpec(a.shape, lambda i, *_: (0,) * len(a.shape))
    prefetch = [which]
    g_specs = []
    g_args = []
    if mode:
        if isinstance(g_parts, tuple):
            g_all, picks = g_parts
            prefetch.append(jnp.stack([p[0] for p in picks]))
            for n, (x, pick) in enumerate(zip(x_parts, picks)):
                count = x.shape[0]
                g_specs.append(
                    pl.BlockSpec(
                        (None, count, length, D),
                        functools.partial(
                            lambda n, m, i, which, index: (index[n], m, 0, 0), n, pick[1]
                        ),
                    )
                )
                g_args.append(g_all)
        else:
            g_specs = [whole(g) for g in g_parts]
            g_args = list(g_parts)
    body = functools.partial(expert_kernel, mode, parts)
    if len(prefetch) == 2:
        inner_body = body
        body = lambda which, index, *refs: inner_body(which, *refs)
    return pl.pallas_call(
        body,
        out_shape=outs,
        grid_spec=pltpu.PrefetchScalarGridSpec(
            num_scalar_prefetch=len(prefetch),
            grid=(1,),
            in_specs=[whole(x) for x in x_parts] + g_specs + [whole(w_in), whole(w_down)],
            out_specs=[whole(o) for o in outs],
            scratch_shapes=scratch,
        ),
        compiler_params=pltpu.CompilerParams(vmem_limit_bytes=VMEM_LIMIT),
        cost_estimate=pl.CostEstimate(
            flops=2 * units * per * total * D * hid,
            bytes_accessed=6_000_000 + 4 * seqs * length * WIDE,
            transcendentals=per * total * hid,
        ),
        name="experts_%d" % mode,
    )(*prefetch, *x_parts, *g_args, w_in, w_down)


def weight_grad_kernel(groups, *refs):
    refs = list(refs)
    sets = [[refs.pop(0) for _ in range(5)] for _ in range(groups)]
    in_ref, down_ref = refs
    for half in range(2):
        total = None
        for x_rows, g_rows, act, gate, up in sets:
            term = tn((up if half else gate)[0], x_rows[0])
            total = term if total is None else total + term
        in_ref[:, half * D : (half + 1) * D] = total
    total = None
    for x_rows, g_rows, act, gate, up in sets:
        term = tn(act[0], g_rows[0])
        total = term if total is None else total + term
    down_ref[...] = total


def weight_grads(saved, hid, per):
    tile = min(hid, 256)
    tiles = hid // tile
    specs, args = [], []
    for group in saved:
        for n, a in enumerate(group):
            if n < 2:
                specs.append(pl.BlockSpec((1,) + a.shape[1:], lambda j, h: (j, 0, 0)))
            else:
                specs.append(pl.BlockSpec((1, a.shape[1], tile), lambda j, h: (j, 0, h)))
            args.append(a)
    shape = jax.ShapeDtypeStruct
    count = sum(group[0].shape[1] for group in saved)
    return pl.pallas_call(
        functools.partial(weight_grad_kernel, len(saved)),
        out_shape=[shape((per * hid, 2 * D), f32), shape((per * hid, D), f32)],
        grid=(per, tiles),
        in_specs=specs,
        out_specs=[
            pl.BlockSpec((tile, 2 * D), lambda j, h: (j * tiles + h, 0)),
            pl.BlockSpec((tile, D), lambda j, h: (j * tiles + h, 0)),
        ],
        compiler_params=pltpu.CompilerParams(vmem_limit_bytes=VMEM_LIMIT),
        cost_estimate=pl.CostEstimate(
            flops=6 * per * count * D * hid, bytes_accessed=27_000_000, transcendentals=0
        ),
        name="weight_grads",
    )(*args)


class Ring:
    def __init__(self):
        self.ahead, self.behind, self.core = [], [], [(i, i ^ 1) for i in range(16)]
        for p, chip in enumerate(PATH):
            for b in range(2):
                here = chip * 2 + b
                self.ahead.append((here, PATH[(p + 1) % 8] * 2 + b))
                self.behind.append((here, PATH[(p - 1) % 8] * 2 + b))
        index = lax.axis_index("fsdp")
        place = jnp.asarray(PLACE, jnp.int32)[index // 2]
        chips = jnp.asarray(PATH, jnp.int32)[(place + jnp.arange(8)) % 8]
        self.chips = chips
        self.order = jnp.stack([chips, jnp.broadcast_to(index % 2, (8,))]).astype(jnp.int32)

    def plus(self, a):
        return lax.ppermute(a, "fsdp", self.ahead)

    def minus(self, a):
        return lax.ppermute(a, "fsdp", self.behind)

    def swap(self, a):
        return lax.ppermute(a, "fsdp", self.core)

    def gather(self, own):
        half = own.shape[0] // 2
        groups = [[own]]
        before = after = own
        for _ in range(3):
            before, after = self.plus(before), self.minus(after)
            groups.append([before, after])
        groups.append([self.plus(before[:half]), self.minus(after[half:])])
        return [group + [self.swap(a) for a in group] for group in groups]

    def picks(self):
        core = self.order[1, 0]
        out = []
        for k in range(5):
            chips = [self.chips[0]] if k == 0 else [self.chips[8 - k], self.chips[k]]
            out.append([(chip * 2 + (core ^ b), m if k == 4 else 0) for b in range(2) for m, chip in enumerate(chips)])
        return out

    def scatter(self, groups):
        kept = []
        for group in groups:
            count = len(group) // 2
            came = [self.swap(a) for a in group[count:]]
            kept.append([a.astype(f32) + b.astype(f32) for a, b in zip(group[:count], came)])
        up = self.minus(kept[4][0].astype(bf16))
        down = self.plus(kept[4][1].astype(bf16))
        for k in (3, 2, 1):
            to_before, to_after = kept[k]
            if k == 3:
                half = up.shape[0]
                to_before = jnp.concatenate([to_before[:half] + up, to_before[half:]])
                to_after = jnp.concatenate([to_after[:half], to_after[half:] + down])
            else:
                to_before, to_after = to_before + up, to_after + down
            up, down = self.minus(to_before.astype(bf16)), self.plus(to_after.astype(bf16))
        return kept[0][0] + up.astype(f32) + down.astype(f32)


def on_device(
    tokens,
    cotangent,
    routes,
    picture_start,
    w_qkv,
    w_out,
    w_router,
    gain_attn,
    gain_moe,
    w_gate_up,
    w_down,
):
    section = lax.axis_index("section")
    first_section = section == 0
    index = lax.axis_index("fsdp")
    devices = lax.axis_size("fsdp")
    seqs, length = tokens.shape[0], tokens.shape[1]
    rows = seqs * length
    w_in, w_down = w_gate_up[0], w_down[0]
    per = max(1, EXPERTS // devices)
    hid = w_down.shape[0] // per
    first_expert = index * EXPERTS // devices
    which = jnp.stack([first_expert, section]).astype(jnp.int32)
    ringed = devices == 16

    angles = np.arange(length)[:, None] * 10000.0 ** (-2.0 * (np.arange(LANES) % 32) / HEAD_SIZE)
    cosine = jnp.asarray(np.cos(angles), f32)
    sine = jnp.asarray(np.sin(angles), f32)
    starts = picture_start[:, 0]

    named = jnp.any(routes[0][..., None] == jnp.arange(LANES, dtype=jnp.int32), axis=2)
    earlier = jnp.asarray(np.tril(np.ones((length, length)), -1), bf16)
    place = jnp.einsum("ts,mse->mte", earlier, named.astype(bf16), preferred_element_type=f32)
    pos = jnp.where(named, place, 255.0).reshape(rows, LANES)

    if ringed:
        ring = Ring()
        order = ring.order
        gains = jnp.concatenate([gain_attn, gain_moe])
        side = jnp.concatenate([gains, jnp.zeros((62, 64), bf16)])
        small = jnp.concatenate([w_router[0], jnp.zeros((64, 32), bf16), side], axis=1)
        groups = ring.gather(jnp.concatenate([w_qkv[0], w_out[0], small], axis=1))
        near = [jnp.concatenate(groups[4][:2]), jnp.concatenate(groups[4][2:])]
        blocks = [[groups[0][0], groups[0][1]]]
        blocks += [[groups[k][1], groups[k][3]] for k in (1, 2, 3)]
        blocks += [[jnp.concatenate(groups[4][0:2]), jnp.concatenate(groups[4][2:4])]]
        blocks += [[groups[k][0], groups[k][2]] for k in (3, 2, 1)]
        w_all = jnp.stack([b for pair in blocks for b in pair]).reshape(8, 2, 64, WCOLS)
    else:
        order = jnp.stack([jnp.arange(8), jnp.zeros((8,))]).astype(jnp.int32)
        gather = lambda a: lax.all_gather(a[0], "fsdp", axis=0, tiled=True)
        big = jnp.concatenate([gather(w_qkv), gather(w_out)], axis=1).reshape(16, 64, QKV + D)
        gains = jnp.stack([gather(gain_attn), gather(gain_moe)]).reshape(2, 16, 64)
        side = jnp.concatenate(
            [jnp.moveaxis(gains, 0, 1), jnp.zeros((16, 62, 64), bf16)], axis=1
        )
        router = gather(w_router).reshape(16, 64, EXPERTS)
        small = jnp.concatenate([router, jnp.zeros((16, 64, 32), bf16), side], axis=2)
        w_all = jnp.concatenate([big, small], axis=2).reshape(8, 2, 64, WCOLS)

    def gather_rows(own):
        if ringed:
            return ring.gather(own)
        every = lax.all_gather(own, "fsdp", axis=0, tiled=True)
        return every.reshape(-1, 8, length, own.shape[-1])

    def scatter_rows(groups):
        if ringed:
            return ring.scatter(groups)
        every = groups.reshape((devices * seqs,) + groups.shape[2:])
        return lax.psum_scatter(every, "fsdp", scatter_dimension=0, tiled=True).astype(f32)

    def experts(mode, x_groups, g_groups):
        if ringed:
            payload, kept = [], []
            for n, group in enumerate(x_groups):
                g = None
                if mode:
                    g = (g_groups[0], g_groups[1][n]) if isinstance(g_groups, tuple) else g_groups[n]
                out = expert_call(mode, which, group, g, w_in, w_down, per)
                payload.append(out[: len(group)])
                kept.append(out[len(group) :])
            return payload, (weight_grads(kept, hid, per) if mode == 2 else None)

        def step(total, both):
            out = expert_call(
                mode, which, [both[0]], [both[1]] if mode else None, w_in, w_down, per
            )
            if mode == 2:
                total = jax.tree.map(jnp.add, total, list(weight_grads([out[1:]], hid, per)))
            return total, out[0]

        zero = [jnp.zeros((per * hid, 2 * D), f32), jnp.zeros((per * hid, D), f32)]
        total, payload = lax.scan(
            step, zero if mode == 2 else None, (x_groups, g_groups if mode else x_groups)
        )
        return payload, total

    payload, resid = attn_forward(False, order, starts, tokens, pos, cosine, sine, w_all)
    mixture = scatter_rows(experts(0, gather_rows(payload), None)[0])
    first_out = (resid.reshape(seqs, length, D) + mixture).astype(bf16)
    passed = lax.ppermute(first_out, "section", [(0, 1)])
    if ringed:
        g_all = lax.all_gather(cotangent, "fsdp", axis=0)
        g_second = (g_all, ring.picks())
    else:
        g_second = gather_rows(cotangent)

    layer_in = jnp.where(first_section, tokens, passed)
    payload, resid, *saved = attn_forward(True, order, starts, layer_in, pos, cosine, sine, w_all)
    saved = [payload, resid] + saved
    rows_all = gather_rows(payload)
    sums_second = scatter_rows(experts(1, rows_all, g_second)[0]).reshape(rows, WIDE)
    (grad_second,) = attn_backward(
        False, order, sums_second, cotangent, layer_in, saved, cosine, sine, w_all
    )

    passed_grad = lax.ppermute(grad_second, "section", [(1, 0)])
    g_third = jnp.where(first_section, passed_grad, cotangent)
    payload_third, (grad_in, grad_down) = experts(2, rows_all, gather_rows(g_third))
    sums_third = scatter_rows(payload_third)
    second_out = (resid.reshape(seqs, length, D) + sums_third[..., :D]).astype(bf16)
    section_out = jnp.where(first_section, first_out, second_out)
    sums = jnp.where(first_section, sums_third.reshape(rows, WIDE), sums_second)
    section_grad, big = attn_backward(
        True, order, sums, g_third, layer_in, saved, cosine, sine, w_all
    )

    if ringed:
        part = lambda k, b: big[k, b]
        own_groups = [[part(0, 0), part(0, 1)]]
        for k in (1, 2, 3):
            own_groups.append([part(8 - k, 0), part(k, 0), part(8 - k, 1), part(k, 1)])
        own_groups.append(
            [part(4, 0)[:32], part(4, 0)[32:], part(4, 1)[:32], part(4, 1)[32:]]
        )
        summed = ring.scatter(own_groups)
        g_qkv, g_out = summed[:, :QKV], summed[:, QKV : QKV + D]
        small = summed[:, QKV + D :]
        g_router, g_gain_attn, g_gain_moe = small[:, :EXPERTS], small[0, 64:], small[1, 64:]
    else:
        total = big.reshape(D, WCOLS)
        sum_up = lambda a: lax.psum_scatter(a, "fsdp", scatter_dimension=0, tiled=True)
        small = total[:, QKV + D :].astype(f32)
        g_qkv, g_out = sum_up(total[:, :QKV].astype(f32)), sum_up(total[:, QKV : QKV + D].astype(f32))
        g_router = sum_up(small[:, :EXPERTS])
        gains = small.reshape(16, 64, LANES)
        g_gain_attn = sum_up(gains[:, 0, 64:].reshape(D))
        g_gain_moe = sum_up(gains[:, 1, 64:].reshape(D))
    return (
        section_out[None],
        section_grad[None],
        g_qkv[None],
        g_out[None],
        g_router[None],
        g_gain_attn[None],
        g_gain_moe[None],
        grad_in[None],
        grad_down[None],
    )


def solution(mesh):
    return jax.shard_map(
        on_device,
        mesh=mesh,
        in_specs=(
            P(None, "fsdp", None),
            P(None, "fsdp", None),
            P("section", None, "fsdp", None),
            P(None, "fsdp"),
            P("section", "fsdp", None),
            P("section", "fsdp", None),
            P("section", "fsdp", None),
            P("section", "fsdp"),
            P("section", "fsdp"),
            P("section", "fsdp", None),
            P("section", "fsdp", None),
        ),
        out_specs=(
            P("section", None, "fsdp", None),
            P("section", None, "fsdp", None),
            P("section", "fsdp", None),
            P("section", "fsdp", None),
            P("section", "fsdp", None),
            P("section", "fsdp"),
            P("section", "fsdp"),
            P("section", "fsdp", None),
            P("section", "fsdp", None),
        ),
        check_vma=False,
    )
```

time: 1260 us -> 694 us (0.55)
  blocking collectives: 387 us -> 0 us
  local copies, waits for them, and re-layouts: 258 us -> 29.9 us
  Pallas kernels: 0 us -> 216 us
  matrix products: 178 us -> 1.52 us
  starting transfers between devices: 50.1 us -> 92.5 us
  other arithmetic: 60.8 us -> 24.9 us
    ppermute x4 -> x138, waiting for transfers between devices: 24 us -> 302 us  [the longest x32 141 us: minus(): return lax.ppermute(a, 'fsdp', self.behind)]
    all_to_all x5 -> x0, blocking collectives: 260 us -> none  [the longest x3 157 us: backward_tick(): lax.all_to_all(grad_slots, 'fsdp', split_axis=0, concat_axis=0, tiled=True)]
    pallas_call x0 -> x20, Pallas kernels: none -> 216 us  [the longest x15 149 us: expert_call(): pl.pallas_call(body, out_shape=outs, grid_spec=pltpu.PrefetchScalarGridSp...]
    all_to_all x7 -> x0, waiting for transfers between devices: 180 us -> none  [the longest x3 94.1 us: backward_tick(): lax.all_to_all(partial_in.astype(jnp.bfloat16), 'fsdp', split_axis=0, con...]
    dot_general x78 -> x1, matrix products: 173 us -> 1.52 us  [on_device(): jnp.einsum('ts,mse->mte', earlier, named.astype(bf16), preferred_element_...]
    gather x21 -> x1, local copies, waits for them, and re-layouts: 89.1 us -> 1.3 us  [__init__(): chips = jnp.asarray(PATH, jnp.int32)[(place + jnp.arange(8)) % 8]]
    ppermute x4 -> x138, starting transfers between devices: 11.3 us -> 92.4 us  [the longest x32 48.7 us: minus(): return lax.ppermute(a, 'fsdp', self.behind)]
    unnamed x2 -> x0, blocking collectives: 75.6 us -> none
  transfers between devices with their start and end apart: 16 -> 139, of which waited for: 13 -> 52; matrix products, arithmetic and copies ran while one was open for 16% -> 6% of each run, Pallas kernels for 0% -> 27%
where the time goes in v1:
time: 694 us; the launch traced here: 688 us
  waiting for transfers between devices  302 us (44%)
  Pallas kernels  216 us (31%)
  starting transfers between devices  92.5 us (13%)
  local copies, waits for them, and re-layouts  29.9 us (4%)
  other arithmetic  24.9 us (4%)
  between operations  21 us (3%)
    pallas_call x15, Pallas kernels, expert_call(): pl.pallas_call(body, out_shape=outs, grid_spec=pltpu.PrefetchScalarGridSp...  149 us
    ppermute x32, waiting for transfers between devices, minus(): return lax.ppermute(a, 'fsdp', self.behind)  141 us
    ppermute x32, waiting for transfers between devices, plus(): return lax.ppermute(a, 'fsdp', self.ahead)  136 us
    ppermute x32, starting transfers between devices, minus(): return lax.ppermute(a, 'fsdp', self.behind)  48.7 us
    pallas_call x2, Pallas kernels, attn_backward(): pl.pallas_call(functools.partial(attn_backward_kernel, with_grads), out_s...  32.7 us
    ppermute x32, starting transfers between devices, plus(): return lax.ppermute(a, 'fsdp', self.ahead)  23.8 us
    pallas_call x2, Pallas kernels, attn_forward(): pl.pallas_call(functools.partial(attn_forward_kernel, save), out_shape=ou...  19.1 us
    unnamed x194, local copies, waits for them, and re-layouts  16 us
  transfers between devices with their start and end apart: 139, of which 52 were waited for; matrix products, arithmetic and copies ran while one was open for 6% of the time, Pallas kernels for 27%

profile of v1, /device:TPU:0, one launch (start us, length us, event | category | flops | bytes accessed | tf_op | source)
XLA Modules:
  0.0 687.7 jit_solution(7046024765757897667)
XLA Ops:
  26.8 20.3 %collective-permute-done.3 = bf16[64,3200]{1,0:T(8,128)(2,1)S(1)} collective-permute-done((bf16[64,3200]{1,0:T(8,128)(2,1)S(1)}, bf16[64,3200]{1,0:T(8,128)(2,1)S(1)}, u32[]{:S(2)}, u32[]{:S(2)}) %collective-permute-start.3) | collective-permute-done | bytes 409632 | tf_op jit(solution)/shard_map/ppermute | solution.py:600
  50.8 15.3 %collective-permute-done.5 = bf16[64,3200]{1,0:T(8,128)(2,1)S(1)} collective-permute-done((bf16[64,3200]{1,0:T(8,128)(2,1)S(1)}, bf16[64,3200]{1,0:T(8,128)(2,1)S(1)}, u32[]{:S(2)}, u32[]{:S(2)}) %collective-permute-start.5) | collective-permute-done | bytes 409632 | tf_op jit(solution)/shard_map/ppermute | solution.py:600
  69.9 15.9 %collective-permute-done.11 = bf16[32,3200]{1,0:T(8,128)(2,1)S(1)} collective-permute-done((bf16[32,3200]{1,0:T(8,128)(2,1)S(1)}, bf16[32,3200]{1,0:T(8,128)(2,1)S(1)}, u32[]{:S(2)}, u32[]{:S(2)}) %collective-permute-start.11) | collective-permute-done | bytes 204832 | tf_op jit(solution)/shard_map/ppermute | solution.py:600
  93.9 9.3 %attn_forward.2 = (bf16[2,96,1152]{2,1,0:T(8,128)(2,1)}, f32[192,1024]{1,0:T(8,128)}) custom-call(s32[2,8]{1,0:T(2,128)} %stack.132.order, s32[2]{0:T(128)} %bitcast.207, bf16[2,96,1024]{2,1,0:T(8,128)(2,1)} %x_ref.1, f32[192,128]{1,0:T(8,128)} %bitcast.199, f32[96,128]{1,0:T(8,128)} %constant.90.clone.cos_ref, f32[96,128]{1,0:T(8,128)} %constant.91.clone.sin_ref, ...), custom_call_target="tpu_custom_call" | custom-call | flops 1336934400 | bytes 12000000 | tf_op jit(solution)/shard_map/attn_forward/pallas_call | solution.py:228
  105.3 10.4 %collective-permute-done.19.refs_0_ = bf16[2,96,1152]{2,1,0:T(8,128)(2,1)S(1)} collective-permute-done((bf16[2,96,1152]{2,1,0:T(8,128)(2,1)}, bf16[2,96,1152]{2,1,0:T(8,128)(2,1)S(1)}, u32[]{:S(2)}, u32[]{:S(2)}) %collective-permute-start.19) | collective-permute-done | bytes 442400 | tf_op jit(solution)/shard_map/ppermute | solution.py:597
  117.8 9.4 %collective-permute-done.24.refs_0_ = bf16[2,96,1152]{2,1,0:T(8,128)(2,1)S(1)} collective-permute-done((bf16[2,96,1152]{2,1,0:T(8,128)(2,1)S(1)}, bf16[2,96,1152]{2,1,0:T(8,128)(2,1)S(1)}, u32[]{:S(2)}, u32[]{:S(2)}) %collective-permute-start.24) | collective-permute-done | bytes 442400 | tf_op jit(solution)/shard_map/ppermute | solution.py:597
  129.1 8.4 %collective-permute-done.29.refs_0_ = bf16[2,96,1152]{2,1,0:T(8,128)(2,1)S(1)} collective-permute-done((bf16[2,96,1152]{2,1,0:T(8,128)(2,1)S(1)}, bf16[2,96,1152]{2,1,0:T(8,128)(2,1)S(1)}, u32[]{:S(2)}, u32[]{:S(2)}) %collective-permute-start.29) | collective-permute-done | bytes 442400 | tf_op jit(solution)/shard_map/ppermute | solution.py:597
  155.9 8.9 %experts_0.7 = (bf16[2,96,1024]{2,1,0:T(8,128)(2,1)}, bf16[2,96,1024]{2,1,0:T(8,128)(2,1)}, bf16[2,96,1024]{2,1,0:T(8,128)(2,1)}, bf16[2,96,1024]{2,1,0:T(8,128)(2,1)}) custom-call(s32[2]{0:T(128)} %pad_add_fusion.which, bf16[2,96,1152]{2,1,0:T(8,128)(2,1)} %copy-done.41, bf16[2,96,1152]{2,1,0:T(8,128)(2,1)} %copy-done.42, bf16[2,96,1152]{2,1,0:T(8,128)(2,1)} %copy-done.46, ...), custom_call_target="tpu_custom_call" | custom-call | flops 1610612736 | bytes 9538944 | tf_op jit(solution)/shard_map/experts_0/pallas_call | solution.py:515
  165.6 8.9 %experts_0.8 = (bf16[2,96,1024]{2,1,0:T(8,128)(2,1)}, bf16[2,96,1024]{2,1,0:T(8,128)(2,1)}, bf16[2,96,1024]{2,1,0:T(8,128)(2,1)}, bf16[2,96,1024]{2,1,0:T(8,128)(2,1)}) custom-call(s32[2]{0:T(128)} %pad_add_fusion.which, bf16[2,96,1152]{2,1,0:T(8,128)(2,1)} %copy-done.10, bf16[2,96,1152]{2,1,0:T(8,128)(2,1)} %copy-done.11, bf16[2,96,1152]{2,1,0:T(8,128)(2,1)} %copy-done.45, ...), custom_call_target="tpu_custom_call" | custom-call | flops 1610612736 | bytes 9538944 | tf_op jit(solution)/shard_map/experts_0/pallas_call | solution.py:515
  194.7 8.9 %experts_0.6 = (bf16[2,96,1024]{2,1,0:T(8,128)(2,1)}, bf16[2,96,1024]{2,1,0:T(8,128)(2,1)}, bf16[2,96,1024]{2,1,0:T(8,128)(2,1)}, bf16[2,96,1024]{2,1,0:T(8,128)(2,1)}) custom-call(s32[2]{0:T(128)} %pad_add_fusion.which, bf16[2,96,1152]{2,1,0:T(8,128)(2,1)} %copy-done.38, bf16[2,96,1152]{2,1,0:T(8,128)(2,1)} %copy-done.39, bf16[2,96,1152]{2,1,0:T(8,128)(2,1)} %copy-done.43, ...), custom_call_target="tpu_custom_call" | custom-call | flops 1610612736 | bytes 9538944 | tf_op jit(solution)/shard_map/experts_0/pallas_call | solution.py:515
  218.2 8.5 %collective-permute-done.50 = bf16[2,96,1024]{2,1,0:T(8,128)(2,1)S(1)} collective-permute-done((bf16[2,96,1024]{2,1,0:T(8,128)(2,1)S(1)}, bf16[2,96,1024]{2,1,0:T(8,128)(2,1)S(1)}, u32[]{:S(2)}, u32[]{:S(2)}) %collective-permute-start.50) | collective-permute-done | bytes 393248 | tf_op jit(solution)/shard_map/ppermute | solution.py:597
  240.7 9.8 %attn_forward.3 = (bf16[2,96,1152]{2,1,0:T(8,128)(2,1)}, f32[192,1024]{1,0:T(8,128)}, f32[192,128]{1,0:T(8,128)}, bf16[192,1024]{1,0:T(8,128)(2,1)}, bf16[192,10...) custom-call(s32[2,8]{1,0:T(2,128)} %stack.132.order, ...), custom_call_target="tpu_custom_call" | custom-call | flops 1336934400 | bytes 12000000 | tf_op jit(solution)/shard_map/attn_forward/pallas_call | solution.py:228
  252.6 8.5 %collective-permute-done.54.refs_0_ = bf16[2,96,1152]{2,1,0:T(8,128)(2,1)S(1)} collective-permute-done((bf16[2,96,1152]{2,1,0:T(8,128)(2,1)}, bf16[2,96,1152]{2,1,0:T(8,128)(2,1)S(1)}, u32[]{:S(2)}, u32[]{:S(2)}) %collective-permute-start.54) | collective-permute-done | bytes 442400 | tf_op jit(solution)/shard_map/ppermute | solution.py:597
  291.7 9.1 %experts_1.9 = (bf16[1,96,1152]{2,1,0:T(8,128)(2,1)}, bf16[1,96,1152]{2,1,0:T(8,128)(2,1)}, bf16[1,96,1152]{2,1,0:T(8,128)(2,1)}, bf16[1,96,1152]{2,1,0:T(8,128)(2,1)}) custom-call(s32[2]{0:T(128)} %pad_add_fusion.which, s32[4]{0:T(128)} %pad_add_fusion.5.index, bf16[1,96,1152]{2,1,0:T(8,128)(2,1)} %copy-done.12, bf16[1,96,1152]{2,1,0:T(8,128)(2,1)} %copy-done.13, ...), custom_call_target="tpu_custom_call" | custom-call | flops 1342177280 | bytes 7769472 | tf_op jit(solution)/shard_map/experts_1/pallas_call | solution.py:515
  301.6 10.8 %experts_1.8 = (bf16[2,96,1152]{2,1,0:T(8,128)(2,1)}, bf16[2,96,1152]{2,1,0:T(8,128)(2,1)}, bf16[2,96,1152]{2,1,0:T(8,128)(2,1)}, bf16[2,96,1152]{2,1,0:T(8,128)(2,1)}) custom-call(s32[2]{0:T(128)} %pad_add_fusion.which, s32[4]{0:T(128)} %pad_add_fusion.4.index, bf16[2,96,1152]{2,1,0:T(8,128)(2,1)} %copy-done.8, bf16[2,96,1152]{2,1,0:T(8,128)(2,1)} %copy-done.9, ...), custom_call_target="tpu_custom_call" | custom-call | flops 2684354560 | bytes 9538944 | tf_op jit(solution)/shard_map/experts_1/pallas_call | solution.py:515
  313.1 11.1 %experts_1.7 = (bf16[2,96,1152]{2,1,0:T(8,128)(2,1)}, bf16[2,96,1152]{2,1,0:T(8,128)(2,1)}, bf16[2,96,1152]{2,1,0:T(8,128)(2,1)}, bf16[2,96,1152]{2,1,0:T(8,128)(2,1)}) custom-call(s32[2]{0:T(128)} %pad_add_fusion.which, s32[4]{0:T(128)} %pad_add_fusion.3.index, bf16[2,96,1152]{2,1,0:T(8,128)(2,1)} %copy-done.17, bf16[2,96,1152]{2,1,0:T(8,128)(2,1)} %copy-done.18, ...), custom_call_target="tpu_custom_call" | custom-call | flops 2684354560 | bytes 9538944 | tf_op jit(solution)/shard_map/experts_1/pallas_call | solution.py:515
  325.7 10.9 %experts_1.6 = (bf16[2,96,1152]{2,1,0:T(8,128)(2,1)}, bf16[2,96,1152]{2,1,0:T(8,128)(2,1)}, bf16[2,96,1152]{2,1,0:T(8,128)(2,1)}, bf16[2,96,1152]{2,1,0:T(8,128)(2,1)}) custom-call(s32[2]{0:T(128)} %pad_add_fusion.which, s32[4]{0:T(128)} %pad_add_fusion.2.index, bf16[2,96,1152]{2,1,0:T(8,128)(2,1)} %copy-done.20, bf16[2,96,1152]{2,1,0:T(8,128)(2,1)} %copy-done.22, ...), custom_call_target="tpu_custom_call" | custom-call | flops 2684354560 | bytes 9538944 | tf_op jit(solution)/shard_map/experts_1/pallas_call | solution.py:515
  337.6 9.0 %experts_1.5 = (bf16[2,96,1152]{2,1,0:T(8,128)(2,1)}, bf16[2,96,1152]{2,1,0:T(8,128)(2,1)}) custom-call(s32[2]{0:T(128)} %pad_add_fusion.which, s32[2]{0:T(128)} %pad_add_fusion.1.index, bf16[2,96,1152]{2,1,0:T(8,128)(2,1)} %get-tuple-element.124.refs_0_.wide_ref, bf16[2,96,1152]{2,1,0:T(8,128)(2,1)} %copy-done.5, bf16[16,2,96,1024]{3,2,1,0:T(8,128)(2,1)} %bitcast.161, ...), custom_call_target="tpu_custom_call" | custom-call | flops 1342177280 | bytes 7769472 | tf_op jit(solution)/shard_map/experts_1/pallas_call | solution.py:515
  365.8 10.4 %collective-permute-done.83 = bf16[2,96,1152]{2,1,0:T(8,128)(2,1)S(1)} collective-permute-done((bf16[2,96,1152]{2,1,0:T(8,128)(2,1)S(1)}, bf16[2,96,1152]{2,1,0:T(8,128)(2,1)S(1)}, u32[]{:S(2)}, u32[]{:S(2)}) %collective-permute-start.83) | collective-permute-done | bytes 442400 | tf_op jit(solution)/shard_map/ppermute | solution.py:597
  378.5 8.7 %collective-permute-done.75 = bf16[2,96,1152]{2,1,0:T(8,128)(2,1)S(1)} collective-permute-done((bf16[2,96,1152]{2,1,0:T(8,128)(2,1)S(1)}, bf16[2,96,1152]{2,1,0:T(8,128)(2,1)S(1)}, u32[]{:S(2)}, u32[]{:S(2)}) %collective-permute-start.75) | collective-permute-done | bytes 442400 | tf_op jit(solution)/shard_map/ppermute | solution.py:600
  408.1 14.1 %attn_backward.2 = bf16[2,96,1024]{2,1,0:T(8,128)(2,1)} custom-call(s32[2,8]{1,0:T(2,128)} %stack.132.order, f32[192,1152]{1,0:T(8,128)} %bitcast.197, bf16[2,96,1024]{2,1,0:T(8,128)(2,1)} %g_ref.1, bf16[2,96,1024]{2,1,0:T(8,128)(2,1)} %broadcast_select_fusion.1.x_ref, bf16[2,96,1152]{2,1,0:T(8,128)(2,1)} %get-tuple-element.124.refs_0_.wide_ref, ...), custom_call_target="tpu_custom_call" | custom-call | flops 2673868800 | bytes 20000000 | tf_op jit(solution)/shard_map/attn_backward/pallas_call | solution.py:363
  423.6 8.6 %collective-permute-done.86 = bf16[2,96,1024]{2,1,0:T(8,128)(2,1)S(1)} collective-permute-done((bf16[2,96,1024]{2,1,0:T(8,128)(2,1)}, bf16[2,96,1024]{2,1,0:T(8,128)(2,1)S(1)}, u32[]{:S(2)}, u32[]{:S(2)}) %collective-permute-start.86) | collective-permute-done | bytes 393248 | tf_op jit(solution)/shard_map/ppermute | solution.py:761
  434.3 9.3 %collective-permute-done.89.refs_4_ = bf16[2,96,1024]{2,1,0:T(8,128)(2,1)S(1)} collective-permute-done((bf16[2,96,1024]{2,1,0:T(8,128)(2,1)S(1)}, bf16[2,96,1024]{2,1,0:T(8,128)(2,1)S(1)}, u32[]{:S(2)}, u32[]{:S(2)}) %collective-permute-start.89) | collective-permute-done | bytes 393248 | tf_op jit(solution)/shard_map/ppermute | solution.py:597
  461.4 9.5 %experts_2.5 = (bf16[2,96,1152]{2,1,0:T(8,128)(2,1)}, bf16[2,96,1152]{2,1,0:T(8,128)(2,1)}, bf16[2,128,1024]{2,1,0:T(8,128)(2,1)}, bf16[2,128,1024]{2,1,0:T(8,12...) custom-call(s32[2]{0:T(128)} %pad_add_fusion.which, ...), custom_call_target="tpu_custom_call" | custom-call | flops 1879048192 | bytes 7769472 | tf_op jit(solution)/shard_map/experts_2/pallas_call | solution.py:515
  473.8 12.3 %experts_2.6 = (bf16[2,96,1152]{2,1,0:T(8,128)(2,1)}, bf16[2,96,1152]{2,1,0:T(8,128)(2,1)}, bf16[2,96,1152]{2,1,0:T(8,128)(2,1)}, bf16[2,96,1152]{2,1,0:T(8,128)...) custom-call(s32[2]{0:T(128)} %pad_add_fusion.which, ...), custom_call_target="tpu_custom_call" | custom-call | flops 3758096384 | bytes 9538944 | tf_op jit(solution)/shard_map/experts_2/pallas_call | solution.py:515
  487.3 12.5 %experts_2.7 = (bf16[2,96,1152]{2,1,0:T(8,128)(2,1)}, bf16[2,96,1152]{2,1,0:T(8,128)(2,1)}, bf16[2,96,1152]{2,1,0:T(8,128)(2,1)}, bf16[2,96,1152]{2,1,0:T(8,128)...) custom-call(s32[2]{0:T(128)} %pad_add_fusion.which, ...), custom_call_target="tpu_custom_call" | custom-call | flops 3758096384 | bytes 9538944 | tf_op jit(solution)/shard_map/experts_2/pallas_call | solution.py:515
  500.7 9.6 %experts_2.9 = (bf16[1,96,1152]{2,1,0:T(8,128)(2,1)}, bf16[1,96,1152]{2,1,0:T(8,128)(2,1)}, bf16[1,96,1152]{2,1,0:T(8,128)(2,1)}, bf16[1,96,1152]{2,1,0:T(8,128)...) custom-call(s32[2]{0:T(128)} %pad_add_fusion.which, ...), custom_call_target="tpu_custom_call" | custom-call | flops 1879048192 | bytes 7769472 | tf_op jit(solution)/shard_map/experts_2/pallas_call | solution.py:515
  511.5 12.2 %experts_2.8 = (bf16[2,96,1152]{2,1,0:T(8,128)(2,1)}, bf16[2,96,1152]{2,1,0:T(8,128)(2,1)}, bf16[2,96,1152]{2,1,0:T(8,128)(2,1)}, bf16[2,96,1152]{2,1,0:T(8,128)...) custom-call(s32[2]{0:T(128)} %pad_add_fusion.which, ...), custom_call_target="tpu_custom_call" | custom-call | flops 3758096384 | bytes 9538944 | tf_op jit(solution)/shard_map/experts_2/pallas_call | solution.py:515
  545.6 10.0 %collective-permute-done.118 = bf16[2,96,1152]{2,1,0:T(8,128)(2,1)S(1)} collective-permute-done((bf16[2,96,1152]{2,1,0:T(8,128)(2,1)S(1)}, bf16[2,96,1152]{2,1,0:T(8,128)(2,1)S(1)}, u32[]{:S(2)}, u32[]{:S(2)}) %collective-permute-start.118) | collective-permute-done | bytes 442400 | tf_op jit(solution)/shard_map/ppermute | solution.py:597
  586.6 18.5 %attn_backward.3 = (bf16[2,96,1024]{2,1,0:T(8,128)(2,1)}, bf16[8,2,64,3200]{3,2,1,0:T(8,128)(2,1)}) custom-call(s32[2,8]{1,0:T(2,128)} %stack.132.order, f32[192,1152]{1,0:T(8,128)} %bitcast_select_fusion.sum_ref, bf16[2,96,1024]{2,1,0:T(8,128)(2,1)} %copy-done.3, bf16[2,96,1024]{2,1,0:T(8,128)(2,1)} %broadcast_select_fusion.1.x_ref, ...), custom_call_target="tpu_custom_call" | custom-call | flops 2673868800 | bytes 20000000 | tf_op jit(solution)/shard_map/attn_backward/pallas_call | solution.py:363
  640.3 8.6 %collective-permute-done.135 = bf16[64,3200]{1,0:T(8,128)(2,1)S(1)} collective-permute-done((bf16[64,3200]{1,0:T(8,128)(2,1)S(1)}, bf16[64,3200]{1,0:T(8,128)(2,1)S(1)}, u32[]{:S(2)}, u32[]{:S(2)}) %collective-permute-start.135) | collective-permute-done | bytes 409632 | tf_op jit(solution)/shard_map/ppermute | solution.py:597
  659.1 15.2 %weight_grads.1 = (f32[1024,2048]{1,0:T(8,128)}, f32[1024,1024]{1,0:T(8,128)}) custom-call(bf16[2,128,1024]{2,1,0:T(8,128)(2,1)} %get-tuple-element.170.refs_0_, bf16[2,128,1024]{2,1,0:T(8,128)(2,1)} %get-tuple-element.171.refs_1_, bf16[2,128,512]{2,1,0:T(8,128)(2,1)} %get-tuple-element.172.refs_2_, bf16[2,128,512]{2,1,0:T(8,128)(2,1)} %get-tuple-element.173.refs_3_, ...), custom_call_target="tpu_custom_call" | custom-call | flops 6442450944 | bytes 27000000 | tf_op jit(solution)/shard_map/weight_grads/pallas_call | solution.py:565
  (561 shorter events, 313.9 us)
Async XLA Ops:
  7.2 284.1 %all-gather.3.cloned.1.call-start = ((), (), s32[]{:S(2)}) async-start(), calls=%async_computation | async-start | bytes 6684672 | tf_op jit(solution)/shard_map/all_gather | solution.py:747
  23.2 26.1 %collective-permute-start.2 = (bf16[64,3200]{1,0:T(8,128)(2,1)S(1)}, bf16[64,3200]{1,0:T(8,128)(2,1)S(1)}, u32[]{:S(2)}, u32[]{:S(2)}) collective-permute-start(bf16[64,3200]{1,0:T(8,128)(2,1)S(1)} %collective-permute-done.1), channel_id=1, source_target_pairs={{0,1},{1,0},{2,3},{3,2},{4,5},{5,4},{6,7},{7,6},{8,9},{9,8},{10,11... | collective-permute-start | bytes 1228808 | tf_op jit(solution)/shard_map/ppermute | solution.py:603
  23.2 23.9 %collective-permute-start.3 = (bf16[64,3200]{1,0:T(8,128)(2,1)S(1)}, bf16[64,3200]{1,0:T(8,128)(2,1)S(1)}, u32[]{:S(2)}, u32[]{:S(2)}) collective-permute-start(bf16[64,3200]{1,0:T(8,128)(2,1)S(1)} %collective-permute-done.1), channel_id=1, source_target_pairs={{0,2},{1,3},{4,0},{5,1},{8,4},{9,5},{12,8},{13,9},{14,12},{15,13},... | collective-permute-start | bytes 1228808 | tf_op jit(solution)/shard_map/ppermute | solution.py:600
  24.8 22.4 %collective-permute-start.8 = (bf16[64,3200]{1,0:T(8,128)(2,1)S(1)}, bf16[64,3200]{1,0:T(8,128)(2,1)S(1)}, u32[]{:S(2)}, u32[]{:S(2)}) collective-permute-start(bf16[64,3200]{1,0:T(8,128)(2,1)S(1)} %collective-permute-done.7), channel_id=1, source_target_pairs={{0,4},{1,5},{4,8},{5,9},{8,12},{9,13},{12,14},{13,15},{14,10},{15,... | collective-permute-start | bytes 1228808 | tf_op jit(solution)/shard_map/ppermute | solution.py:597
  25.2 67.9 %collective-permute-start.16 = (bf16[64,3200]{1,0:T(8,128)(2,1)S(1)}, bf16[64,3200]{1,0:T(8,128)(2,1)S(1)}, u32[]{:S(2)}, u32[]{:S(2)}) collective-permute-start(bf16[64,3200]{1,0:T(8,128)(2,1)S(1)} %collective-permute-done.7), channel_id=1, source_target_pairs={{0,1},{1,0},{2,3},{3,2},{4,5},{5,4},{6,7},{7,6},{8,9},{9,8},{10,11... | collective-permute-start | bytes 1228808 | tf_op jit(solution)/shard_map/ppermute | solution.py:603
  49.3 42.3 %collective-permute-start.15 = (bf16[64,3200]{1,0:T(8,128)(2,1)S(1)}, bf16[64,3200]{1,0:T(8,128)(2,1)S(1)}, u32[]{:S(2)}, u32[]{:S(2)}) collective-permute-start(bf16[64,3200]{1,0:T(8,128)(2,1)S(1)} %collective-permute-done.8), channel_id=1, source_target_pairs={{0,1},{1,0},{2,3},{3,2},{4,5},{5,4},{6,7},{7,6},{8,9},{9,8},{10,11... | collective-permute-start | bytes 1228808 | tf_op jit(solution)/shard_map/ppermute | solution.py:603
  147.3 59.1 %collective-permute-start.17 = (bf16[2,96,1152]{2,1,0:T(8,128)(2,1)}, bf16[2,96,1152]{2,1,0:T(8,128)(2,1)S(1)}, u32[]{:S(2)}, u32[]{:S(2)}) collective-permute-start(bf16[2,96,1152]{2,1,0:T(8,128)(2,1)} %get-tuple-element.104.refs_0_), channel_id=1, source_target_pairs={{0,1},{1,0},{2,3},{3,2},{4,5},{5,4},{6,7},{7,6},{8,9},{9,8},{10,11... | collective-permute-start | bytes 1327112 | tf_op jit(solution)/shard_map/ppermute | solution.py:603
  155.1 37.8 %collective-permute-start.21 = (bf16[2,96,1152]{2,1,0:T(8,128)(2,1)S(1)}, bf16[2,96,1152]{2,1,0:T(8,128)(2,1)S(1)}, u32[]{:S(2)}, u32[]{:S(2)}) collective-permute-start(bf16[2,96,1152]{2,1,0:T(8,128)(2,1)S(1)} %collective-permute-done.19.refs_0_), channel_id=1, source_target_pairs={{0,1},{1,0},{2,3},{3,2},{4,5},{5,4},{6,7},{7,6},{8,9},{9,8},{10,11... | collective-permute-start | bytes 1327112 | tf_op jit(solution)/shard_map/ppermute | solution.py:603
  164.8 28.2 %collective-permute-start.22 = (bf16[2,96,1152]{2,1,0:T(8,128)(2,1)S(1)}, bf16[2,96,1152]{2,1,0:T(8,128)(2,1)S(1)}, u32[]{:S(2)}, u32[]{:S(2)}) collective-permute-start(bf16[2,96,1152]{2,1,0:T(8,128)(2,1)S(1)} %collective-permute-done.20.refs_1_), channel_id=1, source_target_pairs={{0,1},{1,0},{2,3},{3,2},{4,5},{5,4},{6,7},{7,6},{8,9},{9,8},{10,11... | collective-permute-start | bytes 1327112 | tf_op jit(solution)/shard_map/ppermute | solution.py:603
  176.9 26.7 %collective-permute-start.44 = (bf16[2,96,1024]{2,1,0:T(8,128)(2,1)S(1)}, bf16[2,96,1024]{2,1,0:T(8,128)(2,1)S(1)}, u32[]{:S(2)}, u32[]{:S(2)}) collective-permute-start(bf16[2,96,1024]{2,1,0:T(8,128)(2,1)S(1)} %copy-done.77), channel_id=1, source_target_pairs={{0,1},{1,0},{2,3},{3,2},{4,5},{5,4},{6,7},{7,6},{8,9},{9,8},{10,11... | collective-permute-start | bytes 1179656 | tf_op jit(solution)/shard_map/ppermute | solution.py:603
  289.8 22.7 %collective-permute-start.61 = (bf16[2,96,1152]{2,1,0:T(8,128)(2,1)S(1)}, bf16[2,96,1152]{2,1,0:T(8,128)(2,1)}, u32[]{:S(2)}, u32[]{:S(2)}) collective-permute-start(bf16[2,96,1152]{2,1,0:T(8,128)(2,1)S(1)} %collective-permute-done.59.refs_0_), channel_id=1, source_target_pairs={{0,1},{1,0},{2,3},{3,2},{4,5},{5,4},{6,7},{7,6},{8,9},{9,8},{10,11... | collective-permute-start | bytes 1327112 | tf_op jit(solution)/shard_map/ppermute | solution.py:603
  290.1 22.7 %collective-permute-start.62 = (bf16[2,96,1152]{2,1,0:T(8,128)(2,1)S(1)}, bf16[2,96,1152]{2,1,0:T(8,128)(2,1)}, u32[]{:S(2)}, u32[]{:S(2)}) collective-permute-start(bf16[2,96,1152]{2,1,0:T(8,128)(2,1)S(1)} %collective-permute-done.60.refs_1_), channel_id=1, source_target_pairs={{0,1},{1,0},{2,3},{3,2},{4,5},{5,4},{6,7},{7,6},{8,9},{9,8},{10,11... | collective-permute-start | bytes 1327112 | tf_op jit(solution)/shard_map/ppermute | solution.py:603
  291.0 45.8 %collective-permute-start.52 = (bf16[2,96,1152]{2,1,0:T(8,128)(2,1)}, bf16[2,96,1152]{2,1,0:T(8,128)(2,1)S(1)}, u32[]{:S(2)}, u32[]{:S(2)}) collective-permute-start(bf16[2,96,1152]{2,1,0:T(8,128)(2,1)} %get-tuple-element.124.refs_0_.wide_ref), channel_id=1, source_target_pairs={{0,1},{1,0},{2,3},{3,2},{4,5},{5,4},{6,7},{7,6},{8,9},{9,8},{10,11... | collective-permute-start | bytes 1327112 | tf_op jit(solution)/shard_map/ppermute | solution.py:603
  300.8 23.3 %collective-permute-start.56 = (bf16[2,96,1152]{2,1,0:T(8,128)(2,1)S(1)}, bf16[2,96,1152]{2,1,0:T(8,128)(2,1)S(1)}, u32[]{:S(2)}, u32[]{:S(2)}) collective-permute-start(bf16[2,96,1152]{2,1,0:T(8,128)(2,1)S(1)} %copy-done.21), channel_id=1, source_target_pairs={{0,1},{1,0},{2,3},{3,2},{4,5},{5,4},{6,7},{7,6},{8,9},{9,8},{10,11... | collective-permute-start | bytes 1327112 | tf_op jit(solution)/shard_map/ppermute | solution.py:603
  301.2 23.3 %collective-permute-start.57 = (bf16[2,96,1152]{2,1,0:T(8,128)(2,1)S(1)}, bf16[2,96,1152]{2,1,0:T(8,128)(2,1)S(1)}, u32[]{:S(2)}, u32[]{:S(2)}) collective-permute-start(bf16[2,96,1152]{2,1,0:T(8,128)(2,1)S(1)} %copy-done.23), channel_id=1, source_target_pairs={{0,1},{1,0},{2,3},{3,2},{4,5},{5,4},{6,7},{7,6},{8,9},{9,8},{10,11... | collective-permute-start | bytes 1327112 | tf_op jit(solution)/shard_map/ppermute | solution.py:603
  312.5 36.0 %collective-permute-start.80 = (bf16[2,96,1152]{2,1,0:T(8,128)(2,1)}, bf16[2,96,1152]{2,1,0:T(8,128)(2,1)S(1)}, u32[]{:S(2)}, u32[]{:S(2)}) collective-permute-start(bf16[2,96,1152]{2,1,0:T(8,128)(2,1)} %get-tuple-element.140), channel_id=1, source_target_pairs={{0,1},{1,0},{2,3},{3,2},{4,5},{5,4},{6,7},{7,6},{8,9},{9,8},{10,11... | collective-permute-start | bytes 1327112 | tf_op jit(solution)/shard_map/ppermute | solution.py:603
  312.8 33.8 %collective-permute-start.81 = (bf16[1,96,1152]{2,1,0:T(8,128)(2,1)S(1)}, bf16[1,96,1152]{2,1,0:T(8,128)(2,1)S(1)}, u32[]{:S(2)}, u32[]{:S(2)}) collective-permute-start(bf16[1,96,1152]{2,1,0:T(8,128)(2,1)S(1)} %copy-done.87), channel_id=1, source_target_pairs={{0,1},{1,0},{2,3},{3,2},{4,5},{5,4},{6,7},{7,6},{8,9},{9,8},{10,11... | collective-permute-start | bytes 663560 | tf_op jit(solution)/shard_map/ppermute | solution.py:603
  324.1 41.5 %collective-permute-start.79 = (bf16[2,96,1152]{2,1,0:T(8,128)(2,1)}, bf16[2,96,1152]{2,1,0:T(8,128)(2,1)S(1)}, u32[]{:S(2)}, u32[]{:S(2)}) collective-permute-start(bf16[2,96,1152]{2,1,0:T(8,128)(2,1)} %get-tuple-element.138), channel_id=1, source_target_pairs={{0,1},{1,0},{2,3},{3,2},{4,5},{5,4},{6,7},{7,6},{8,9},{9,8},{10,11... | collective-permute-start | bytes 1327112 | tf_op jit(solution)/shard_map/ppermute | solution.py:603
  336.5 52.5 %collective-permute-start.78 = (bf16[2,96,1152]{2,1,0:T(8,128)(2,1)}, bf16[2,96,1152]{2,1,0:T(8,128)(2,1)S(1)}, u32[]{:S(2)}, u32[]{:S(2)}) collective-permute-start(bf16[2,96,1152]{2,1,0:T(8,128)(2,1)} %get-tuple-element.136), channel_id=1, source_target_pairs={{0,1},{1,0},{2,3},{3,2},{4,5},{5,4},{6,7},{7,6},{8,9},{9,8},{10,11... | collective-permute-start | bytes 1327112 | tf_op jit(solution)/shard_map/ppermute | solution.py:603
  348.2 29.9 %collective-permute-start.63 = (bf16[2,96,1152]{2,1,0:T(8,128)(2,1)S(1)}, bf16[2,96,1152]{2,1,0:T(8,128)(2,1)S(1)}, u32[]{:S(2)}, u32[]{:S(2)}) collective-permute-start(bf16[2,96,1152]{2,1,0:T(8,128)(2,1)S(1)} %copy-done.72), channel_id=1, source_target_pairs={{0,1},{1,0},{2,3},{3,2},{4,5},{5,4},{6,7},{7,6},{8,9},{9,8},{10,11... | collective-permute-start | bytes 1327112 | tf_op jit(solution)/shard_map/ppermute | solution.py:603
  356.5 33.1 %collective-permute-start.58 = (bf16[2,96,1152]{2,1,0:T(8,128)(2,1)S(1)}, bf16[2,96,1152]{2,1,0:T(8,128)(2,1)S(1)}, u32[]{:S(2)}, u32[]{:S(2)}) collective-permute-start(bf16[2,96,1152]{2,1,0:T(8,128)(2,1)S(1)} %copy-done.71), channel_id=1, source_target_pairs={{0,1},{1,0},{2,3},{3,2},{4,5},{5,4},{6,7},{7,6},{8,9},{9,8},{10,11... | collective-permute-start | bytes 1327112 | tf_op jit(solution)/shard_map/ppermute | solution.py:603
  365.7 34.0 %collective-permute-start.53 = (bf16[2,96,1152]{2,1,0:T(8,128)(2,1)S(1)}, bf16[2,96,1152]{2,1,0:T(8,128)(2,1)S(1)}, u32[]{:S(2)}, u32[]{:S(2)}) collective-permute-start(bf16[2,96,1152]{2,1,0:T(8,128)(2,1)S(1)} %copy-done.70), channel_id=1, source_target_pairs={{0,1},{1,0},{2,3},{3,2},{4,5},{5,4},{6,7},{7,6},{8,9},{9,8},{10,11... | collective-permute-start | bytes 1327112 | tf_op jit(solution)/shard_map/ppermute | solution.py:603
  456.9 29.2 %collective-permute-start.96 = (bf16[2,96,1024]{2,1,0:T(8,128)(2,1)S(1)}, bf16[2,96,1024]{2,1,0:T(8,128)(2,1)S(1)}, u32[]{:S(2)}, u32[]{:S(2)}) collective-permute-start(bf16[2,96,1024]{2,1,0:T(8,128)(2,1)S(1)} %collective-permute-done.94.refs_4_), channel_id=1, source_target_pairs={{0,1},{1,0},{2,3},{3,2},{4,5},{5,4},{6,7},{7,6},{8,9},{9,8},{10,11... | collective-permute-start | bytes 1179656 | tf_op jit(solution)/shard_map/ppermute | solution.py:603
  461.4 24.8 %collective-permute-start.97 = (bf16[2,96,1024]{2,1,0:T(8,128)(2,1)S(1)}, bf16[2,96,1024]{2,1,0:T(8,128)(2,1)S(1)}, u32[]{:S(2)}, u32[]{:S(2)}) collective-permute-start(bf16[2,96,1024]{2,1,0:T(8,128)(2,1)S(1)} %collective-permute-done.95.refs_5_), channel_id=1, source_target_pairs={{0,1},{1,0},{2,3},{3,2},{4,5},{5,4},{6,7},{7,6},{8,9},{9,8},{10,11... | collective-permute-start | bytes 1179656 | tf_op jit(solution)/shard_map/ppermute | solution.py:603
  471.0 107.4 %collective-permute-start.88 = (bf16[2,96,1152]{2,1,0:T(8,128)(2,1)}, bf16[2,96,1152]{2,1,0:T(8,128)(2,1)S(1)}, u32[]{:S(2)}, u32[]{:S(2)}) collective-permute-start(bf16[2,96,1152]{2,1,0:T(8,128)(2,1)} %get-tuple-element.151), channel_id=1, source_target_pairs={{0,1},{1,0},{2,3},{3,2},{4,5},{5,4},{6,7},{7,6},{8,9},{9,8},{10,11... | collective-permute-start | bytes 1327112 | tf_op jit(solution)/shard_map/ppermute | solution.py:603
  486.1 24.2 %collective-permute-start.101 = (bf16[2,96,1024]{2,1,0:T(8,128)(2,1)S(1)}, bf16[2,96,1024]{2,1,0:T(8,128)(2,1)S(1)}, u32[]{:S(2)}, u32[]{:S(2)}) collective-permute-start(bf16[2,96,1024]{2,1,0:T(8,128)(2,1)S(1)} %collective-permute-done.99.refs_4_), channel_id=1, source_target_pairs={{0,1},{1,0},{2,3},{3,2},{4,5},{5,4},{6,7},{7,6},{8,9},{9,8},{10,11... | collective-permute-start | bytes 1179656 | tf_op jit(solution)/shard_map/ppermute | solution.py:603
  486.2 24.6 %collective-permute-start.102 = (bf16[2,96,1024]{2,1,0:T(8,128)(2,1)S(1)}, bf16[2,96,1024]{2,1,0:T(8,128)(2,1)S(1)}, u32[]{:S(2)}, u32[]{:S(2)}) collective-permute-start(bf16[2,96,1024]{2,1,0:T(8,128)(2,1)S(1)} %collective-permute-done.100.refs_5_), channel_id=1, source_target_pairs={{0,1},{1,0},{2,3},{3,2},{4,5},{5,4},{6,7},{7,6},{8,9},{9,8},{10,11... | collective-permute-start | bytes 1179656 | tf_op jit(solution)/shard_map/ppermute | solution.py:603
  499.8 68.3 %collective-permute-start.113 = (bf16[2,96,1152]{2,1,0:T(8,128)(2,1)S(1)}, bf16[2,96,1152]{2,1,0:T(8,128)(2,1)S(1)}, u32[]{:S(2)}, u32[]{:S(2)}) collective-permute-start(bf16[2,96,1152]{2,1,0:T(8,128)(2,1)S(1)} %copy-done.67), channel_id=1, source_target_pairs={{0,1},{1,0},{2,3},{3,2},{4,5},{5,4},{6,7},{7,6},{8,9},{9,8},{10,11... | collective-permute-start | bytes 1327112 | tf_op jit(solution)/shard_map/ppermute | solution.py:603
  500.0 68.8 %collective-permute-start.93 = (bf16[2,96,1152]{2,1,0:T(8,128)(2,1)S(1)}, bf16[2,96,1152]{2,1,0:T(8,128)(2,1)S(1)}, u32[]{:S(2)}, u32[]{:S(2)}) collective-permute-start(bf16[2,96,1152]{2,1,0:T(8,128)(2,1)S(1)} %copy-done.66), channel_id=1, source_target_pairs={{0,1},{1,0},{2,3},{3,2},{4,5},{5,4},{6,7},{7,6},{8,9},{9,8},{10,11... | collective-permute-start | bytes 1327112 | tf_op jit(solution)/shard_map/ppermute | solution.py:603
  510.4 35.2 %collective-permute-start.114 = (bf16[2,96,1152]{2,1,0:T(8,128)(2,1)S(1)}, bf16[2,96,1152]{2,1,0:T(8,128)(2,1)S(1)}, u32[]{:S(2)}, u32[]{:S(2)}) collective-permute-start(bf16[2,96,1152]{2,1,0:T(8,128)(2,1)S(1)} %copy-done.69), channel_id=1, source_target_pairs={{0,1},{1,0},{2,3},{3,2},{4,5},{5,4},{6,7},{7,6},{8,9},{9,8},{10,11... | collective-permute-start | bytes 1327112 | tf_op jit(solution)/shard_map/ppermute | solution.py:603
  649.4 26.7 %collective-permute-start.121 = (bf16[64,3200]{1,0:T(8,128)(2,1)}, bf16[64,3200]{1,0:T(8,128)(2,1)}, u32[]{:S(2)}, u32[]{:S(2)}) collective-permute-start(bf16[64,3200]{1,0:T(8,128)(2,1)} %get-tuple-element.233), channel_id=1, source_target_pairs={{0,1},{1,0},{2,3},{3,2},{4,5},{5,4},{6,7},{7,6},{8,9},{9,8},{10,11... | collective-permute-start | bytes 1228808 | tf_op jit(solution)/shard_map/ppermute | solution.py:603
  649.4 26.7 %collective-permute-start.129 = (bf16[64,3200]{1,0:T(8,128)(2,1)}, bf16[64,3200]{1,0:T(8,128)(2,1)}, u32[]{:S(2)}, u32[]{:S(2)}) collective-permute-start(bf16[64,3200]{1,0:T(8,128)(2,1)} %get-tuple-element.240), channel_id=1, source_target_pairs={{0,2},{1,3},{4,0},{5,1},{8,4},{9,5},{12,8},{13,9},{14,12},{15,13},... | collective-permute-start | bytes 1228808 | tf_op jit(solution)/shard_map/ppermute | solution.py:600
  (197 other events, 2770.4 us)
Sparse Core Ops, SparseCore 0:
  13.3 77.1 all-gather.2

commit v2 on v1

--- a/solution.py
+++ b/solution.py
@@ -24,7 +24,7 @@
 scale = HEAD_SIZE ** (-0.5)
 f32 = jnp.float32
 bf16 = jnp.bfloat16
-VMEM_LIMIT = 56 * 1024 * 1024
+VMEM_LIMIT = 30 * 1024 * 1024
 
 PATH = (0, 2, 4, 6, 7, 5, 3, 1)
 PLACE = tuple(PATH.index(c) for c in range(8))
@@ -88,18 +88,30 @@
     return jnp.where(low, other, chunk) if odd else jnp.where(low, chunk, other)
 
 
-def load_weights(order, w_hbm, w_vmem, sems):
-    copies = []
-    for k in range(8):
-        for b in range(2):
-            copies.append(
-                pltpu.make_async_copy(
-                    w_hbm.at[k, b], w_vmem.at[order[0, k] * 2 + (order[1, 0] ^ b)], sems.at[k * 2 + b]
-                )
+PARTS = ((0, QKV), (QKV, QKV + D), (QKV + D, WCOLS))
+
+
+def load_weights(order, w_hbm, w_vmem, sems, first):
+    copies = {}
+    for part in first:
+        columns = pl.ds(PARTS[part][0], PARTS[part][1] - PARTS[part][0])
+        copies[part] = [
+            pltpu.make_async_copy(
+                w_hbm.at[k, b, :, columns],
+                w_vmem.at[order[0, k] * 2 + (order[1, 0] ^ b), :, columns],
+                sems.at[part * 16 + k * 2 + b],
             )
-    for copy in copies:
-        copy.start()
-    return copies
+            for k in range(8)
+            for b in range(2)
+        ]
+        for copy in copies[part]:
+            copy.start()
+
+    def wait(part):
+        for copy in copies[part]:
+            copy.wait()
+
+    return wait
 
 
 def gains_of(w_vmem):
@@ -117,19 +129,21 @@
 def attn_forward_kernel(
     save, order, starts, x_ref, pos_ref, cos_ref, sin_ref, w_hbm, *rest
 ):
+    if not save:
+        cot_ref, rest = rest[0], rest[1:]
     if save:
         (out_ref, resid_ref, gate_ref, normed_ref, q_ref, k_ref, v_ref, probs_ref, mixed_ref) = rest[:9]
         w_vmem, sems = rest[9:]
     else:
         out_ref, resid_ref, w_vmem, sems, mixed_ref = rest
-    copies = load_weights(order, w_hbm, w_vmem, sems)
+    wait = load_weights(order, w_hbm, w_vmem, sems, (2, 0, 1))
     seqs, length = x_ref.shape[0], x_ref.shape[1]
     rows = seqs * length
-    for copy in copies:
-        copy.wait()
+    wait(2)
     gain_attn, gain_moe = gains_of(w_vmem)
     x = x_ref[...].reshape(rows, D).astype(f32)
     normed = (x * rms(x) * gain_attn).astype(bf16)
+    wait(0)
     w_qkv = w_vmem[:, :, :QKV].reshape(D, QKV)
     qkv = nn(normed, w_qkv)
     cosine, sine = cos_ref[...], sin_ref[...]
@@ -165,6 +179,7 @@
                 probs_ref[s * KEY_VALUE_HEADS + j] = probs
             mixed = join(nn(probs.astype(bf16), value))
             mixed_ref[top, j * LANES : (j + 1) * LANES] = mixed.astype(bf16)
+    wait(1)
     w_out = w_vmem[:, :, QKV : QKV + D].reshape(D, D)
     resid = x + nn(mixed_ref[...], w_out)
     normed_moe = (resid * rms(resid) * gain_moe).astype(bf16)
@@ -190,6 +205,12 @@
     out_ref[:, :, :D] = normed_moe.reshape(seqs, length, D)
     out_ref[:, :, D:] = columns.astype(bf16).reshape(seqs, length, LANES)
     resid_ref[...] = resid
+    if not save:
+
+        @pl.when(order[2, 0] != 0)
+        def _():
+            out_ref[:, :, :D] = cot_ref[...]
+
     if save:
         gate_ref[...] = gate
         normed_ref[...] = normed
@@ -203,16 +224,20 @@
     return pl.BlockSpec(memory_space=pltpu.SMEM)
 
 
-def anywhere():
-    return pl.BlockSpec(memory_space=pl.ANY)
-
-
-def attn_forward(save, order, starts, x, pos, cosine, sine, w_all):
+def hbm():
+    return pl.BlockSpec(memory_space=pltpu.HBM)
+
+
+def in_hbm(a):
+    return pltpu.with_memory_space_constraint(a, pltpu.HBM)
+
+
+def attn_forward(save, order, starts, x, pos, cosine, sine, w_all, cot=None):
     seqs, length = x.shape[0], x.shape[1]
     rows = seqs * length
     shape = jax.ShapeDtypeStruct
     outs = [shape((seqs, length, WIDE), bf16), shape((rows, D), f32)]
-    scratch = [pltpu.VMEM((16, 64, WCOLS), bf16), pltpu.SemaphoreType.DMA((16,))]
+    scratch = [pltpu.VMEM((16, 64, WCOLS), bf16), pltpu.SemaphoreType.DMA((48,))]
     if save:
         outs += [
             shape((rows, LANES), f32),
@@ -228,7 +253,7 @@
     return pl.pallas_call(
         functools.partial(attn_forward_kernel, save),
         out_shape=outs,
-        in_specs=[smem(), smem(), vmem(), vmem(), vmem(), vmem(), anywhere()],
+        in_specs=[smem(), smem(), vmem(), vmem(), vmem(), vmem(), hbm()] + [vmem()] * (not save),
         out_specs=[vmem()] * len(outs),
         scratch_shapes=scratch,
         compiler_params=pltpu.CompilerParams(vmem_limit_bytes=VMEM_LIMIT),
@@ -236,7 +261,7 @@
             flops=2 * rows * D * 3400, bytes_accessed=12_000_000, transcendentals=rows * 2048
         ),
         name="attn_forward",
-    )(order, starts, x, pos, cosine, sine, w_all)
+    )(order, starts, x, pos, cosine, sine, in_hbm(w_all), *(() if save else (cot,)))
 
 
 def attn_backward_kernel(
@@ -263,11 +288,10 @@
         grad_ref, big_ref, w_vmem, sems, back_ref, gains_ref = rest
     else:
         grad_ref, w_vmem, sems, back_ref = rest
-    copies = load_weights(order, w_hbm, w_vmem, sems)
+    wait = load_weights(order, w_hbm, w_vmem, sems, (2, 1, 0))
     seqs, length = x_ref.shape[0], x_ref.shape[1]
     rows = seqs * length
-    for copy in copies:
-        copy.wait()
+    wait(2)
     gain_attn, gain_moe = gains_of(w_vmem)
     gate = gate_ref[...]
     high_low = sum_ref[:, D:]
@@ -283,6 +307,7 @@
         resid, inv_moe, gain_moe, grad_normed_moe
     )
     grad_branch = grad_resid.astype(bf16)
+    wait(1)
     w_out = w_vmem[:, :, QKV : QKV + D].reshape(D, D)
     grad_mixed = nt(grad_branch, w_out)
     cosine, sine = cos_ref[...], sin_ref[...]
@@ -314,6 +339,7 @@
                 grad_key, cosine, sine, True
             ).astype(bf16)
             back_ref[top, D + 512 + c * LANES : D + 512 + (c + 1) * LANES] = grad_value.astype(bf16)
+    wait(0)
     w_qkv = w_vmem[:, :, :QKV].reshape(D, QKV)
     grad_rows = back_ref[...]
     grad_normed = nt(grad_rows, w_qkv)
@@ -354,7 +380,7 @@
     outs = [shape((seqs, length, D), bf16)]
     scratch = [
         pltpu.VMEM((16, 64, WCOLS), bf16),
-        pltpu.SemaphoreType.DMA((16,)),
+        pltpu.SemaphoreType.DMA((48,)),
         pltpu.VMEM((rows, QKV), bf16),
     ]
     if with_grads:
@@ -363,7 +389,7 @@
     return pl.pallas_call(
         functools.partial(attn_backward_kernel, with_grads),
         out_shape=outs,
-        in_specs=[smem()] + [vmem()] * 14 + [anywhere()],
+        in_specs=[smem()] + [vmem()] * 14 + [hbm()],
         out_specs=[vmem()] * len(outs),
         scratch_shapes=scratch,
         compiler_params=pltpu.CompilerParams(vmem_limit_bytes=VMEM_LIMIT),
@@ -371,7 +397,7 @@
             flops=4 * rows * D * 3400, bytes_accessed=20_000_000, transcendentals=0
         ),
         name="attn_backward",
-    )(order, sums, g, x, *saved, cosine, sine, w_all)
+    )(order, sums, g, x, *saved, cosine, sine, in_hbm(w_all))
 
 
 def expert_kernel(mode, parts, which, *refs):
@@ -381,13 +407,17 @@
     g_refs = take(parts) if mode else []
     w_in, w_down = take(2)
     out_refs = take(parts)
+    saved_refs = take(5) if mode == 2 else []
+    x_rows = take(1)[0]
+    g_rows = take(1)[0] if mode else None
     if mode == 2:
-        x_rows, g_rows, act_rows, gate_rows, up_rows = take(5)
-    elif mode == 1:
-        x_rows, g_rows = take(2)
-    else:
-        (x_rows,) = take(1)
+        act_rows, gate_rows, up_rows, sems = take(4)
     hot_ref, scale_ref, result_ref = take(3)
+
+    def send(n, j):
+        source = (x_rows, g_rows, act_rows, gate_rows, up_rows)[n]
+        return pltpu.make_async_copy(source.at[j], saved_refs[n].at[j], sems.at[n, j])
+
     per = x_rows.shape[0]
     hid = w_down.shape[0] // per
     first = which[0]
@@ -414,11 +444,15 @@
             gate = jnp.sum(jnp.where(own, block[:, D:], 0.0), axis=-1, keepdims=True)
             scale_ref[j, here] = jnp.broadcast_to(gate, (SLOTS, LANES))
         if mode:
-            taken = nn(hot, g_refs[i][s])
+            taken = nn(hot, g_refs[i][s, :, :D])
             for j in range(per):
                 g_rows[j, here] = taken[j * SLOTS : (j + 1) * SLOTS].astype(bf16)
     total = len(spots) * SLOTS
     lane = lanes_of((total, LANES))
+    if mode == 2:
+        for n in range(2):
+            for j in range(per):
+                send(n, j).start()
     for j in range(per):
         own_rows = slice(j * hid, (j + 1) * hid)
         rows = x_rows[j]
@@ -442,6 +476,8 @@
                 act_rows[j] = (act * gate).astype(bf16)
                 gate_rows[j] = grad_gate
                 up_rows[j] = grad_up
+                for n in range(2, 5):
+                    send(n, j).start()
             grad_in = nn(grad_gate, w_in[own_rows, :D]) + nn(grad_up, w_in[own_rows, D:])
             high = grad_gw.astype(bf16).astype(f32)
             extra = jnp.where(
@@ -464,6 +500,10 @@
         here = slice(n * SLOTS, (n + 1) * SLOTS)
         block = jnp.concatenate([result_ref[j, here] for j in range(per)], axis=0)
         out_refs[i][s] = tn(hot_ref[n], block).astype(bf16)
+    if mode == 2:
+        for n in range(5):
+            for j in range(per):
+                send(n, j).wait()
 
 
 def expert_call(mode, which, x_parts, g_parts, w_in, w_down, per):
@@ -475,53 +515,31 @@
     out_width = WIDE if mode else D
     shape = jax.ShapeDtypeStruct
     outs = [shape((x.shape[0], length, out_width), bf16) for x in x_parts]
-    rows = (per, total, D)
-    scratch = [
+    out_specs = [vmem()] * parts
+    wide, narrow = (per, total, D), (per, total, hid)
+    scratch = [pltpu.VMEM(wide, bf16)] * (2 if mode else 1)
+    if mode == 2:
+        saved = [wide, wide, narrow, narrow, narrow]
+        outs += [pltpu.HBM(a, bf16) for a in saved]
+        out_specs += [hbm()] * 5
+        scratch += [pltpu.VMEM(narrow, bf16)] * 3 + [pltpu.SemaphoreType.DMA((5, per))]
+    scratch += [
         pltpu.VMEM((seqs, per * SLOTS, length), bf16),
         pltpu.VMEM((per, total, LANES), f32),
         pltpu.VMEM((per, total, out_width), bf16),
     ]
-    if mode == 2:
-        outs += [shape(rows, bf16), shape(rows, bf16)] + [shape((per, total, hid), bf16)] * 3
-    else:
-        scratch = [pltpu.VMEM(rows, bf16)] * (2 if mode else 1) + scratch
-    units = (3, 5, 7)[mode]
-    whole = lambda a: pl.BlockSpec(a.shape, lambda i, *_: (0,) * len(a.shape))
-    prefetch = [which]
-    g_specs = []
-    g_args = []
-    if mode:
-        if isinstance(g_parts, tuple):
-            g_all, picks = g_parts
-            prefetch.append(jnp.stack([p[0] for p in picks]))
-            for n, (x, pick) in enumerate(zip(x_parts, picks)):
-                count = x.shape[0]
-                g_specs.append(
-                    pl.BlockSpec(
-                        (None, count, length, D),
-                        functools.partial(
-                            lambda n, m, i, which, index: (index[n], m, 0, 0), n, pick[1]
-                        ),
-                    )
-                )
-                g_args.append(g_all)
-        else:
-            g_specs = [whole(g) for g in g_parts]
-            g_args = list(g_parts)
-    body = functools.partial(expert_kernel, mode, parts)
-    if len(prefetch) == 2:
-        inner_body = body
-        body = lambda which, index, *refs: inner_body(which, *refs)
+    units = (3, 5, 5)[mode]
+    g_args = list(g_parts) if mode else []
+
+    def body(which, *refs):
+        expert_kernel(mode, parts, which, *refs)
+
     return pl.pallas_call(
         body,
         out_shape=outs,
-        grid_spec=pltpu.PrefetchScalarGridSpec(
-            num_scalar_prefetch=len(prefetch),
-            grid=(1,),
-            in_specs=[whole(x) for x in x_parts] + g_specs + [whole(w_in), whole(w_down)],
-            out_specs=[whole(o) for o in outs],
-            scratch_shapes=scratch,
-        ),
+        in_specs=[smem()] + [vmem()] * (parts + len(g_args) + 2),
+        out_specs=out_specs,
+        scratch_shapes=scratch,
         compiler_params=pltpu.CompilerParams(vmem_limit_bytes=VMEM_LIMIT),
         cost_estimate=pl.CostEstimate(
             flops=2 * units * per * total * D * hid,
@@ -529,47 +547,84 @@
             transcendentals=per * total * hid,
         ),
         name="experts_%d" % mode,
-    )(*prefetch, *x_parts, *g_args, w_in, w_down)
-
-
-def weight_grad_kernel(groups, *refs):
+    )(which, *x_parts, *g_args, w_in, w_down)
+
+
+def weight_grad_kernel(groups, tile, *refs):
     refs = list(refs)
-    sets = [[refs.pop(0) for _ in range(5)] for _ in range(groups)]
-    in_ref, down_ref = refs
-    for half in range(2):
-        total = None
-        for x_rows, g_rows, act, gate, up in sets:
-            term = tn((up if half else gate)[0], x_rows[0])
-            total = term if total is None else total + term
-        in_ref[:, half * D : (half + 1) * D] = total
-    total = None
-    for x_rows, g_rows, act, gate, up in sets:
-        term = tn(act[0], g_rows[0])
-        total = term if total is None else total + term
-    down_ref[...] = total
+    sets = [refs[5 * n : 5 * n + 5] for n in range(groups)]
+    in_ref, down_ref = refs[5 * groups : 5 * groups + 2]
+    rows = refs[5 * groups + 2 : 5 * groups + 7]
+    in_tile, down_tile, load_sems, store_sems = refs[5 * groups + 7 :]
+    per, hid = rows[2].shape[0], rows[2].shape[2]
+    loads = []
+    for j in range(per):
+        loads.append([])
+        for n in (3, 4, 0, 2, 1):
+            offset = 0
+            for g in range(groups):
+                count = sets[g][n].shape[1]
+                loads[j].append(
+                    pltpu.make_async_copy(
+                        sets[g][n].at[j],
+                        rows[n].at[j, pl.ds(offset, count)],
+                        load_sems.at[j, n * groups + g],
+                    )
+                )
+                offset += count
+        for load in loads[j]:
+            load.start()
+    stores = []
+    for j in range(per):
+        for load in loads[j]:
+            load.wait()
+        for h in range(hid // tile):
+            turn_of = len(stores)
+            slot = turn_of % 2
+            if turn_of >= 2:
+                for store in stores[turn_of - 2]:
+                    store.wait()
+            columns = slice(h * tile, (h + 1) * tile)
+            in_tile[slot, :, :D] = tn(rows[3][j, :, columns], rows[0][j])
+            in_tile[slot, :, D:] = tn(rows[4][j, :, columns], rows[0][j])
+            down_tile[slot] = tn(rows[2][j, :, columns], rows[1][j])
+            where = pl.ds(j * hid + h * tile, tile)
+            stores.append(
+                [
+                    pltpu.make_async_copy(in_tile.at[slot], in_ref.at[where], store_sems.at[slot, 0]),
+                    pltpu.make_async_copy(
+                        down_tile.at[slot], down_ref.at[where], store_sems.at[slot, 1]
+                    ),
+                ]
+            )
+            for store in stores[-1]:
+                store.start()
+    for pair in stores[-2:]:
+        for store in pair:
+            store.wait()
 
 
 def weight_grads(saved, hid, per):
     tile = min(hid, 256)
-    tiles = hid // tile
-    specs, args = [], []
-    for group in saved:
-        for n, a in enumerate(group):
-            if n < 2:
-                specs.append(pl.BlockSpec((1,) + a.shape[1:], lambda j, h: (j, 0, 0)))
-            else:
-                specs.append(pl.BlockSpec((1, a.shape[1], tile), lambda j, h: (j, 0, h)))
-            args.append(a)
-    shape = jax.ShapeDtypeStruct
+    groups = len(saved)
+    args = [in_hbm(a) for group in saved for a in group]
     count = sum(group[0].shape[1] for group in saved)
+    wide, narrow = pltpu.VMEM((per, count, D), bf16), pltpu.VMEM((per, count, hid), bf16)
     return pl.pallas_call(
-        functools.partial(weight_grad_kernel, len(saved)),
-        out_shape=[shape((per * hid, 2 * D), f32), shape((per * hid, D), f32)],
-        grid=(per, tiles),
-        in_specs=specs,
-        out_specs=[
-            pl.BlockSpec((tile, 2 * D), lambda j, h: (j * tiles + h, 0)),
-            pl.BlockSpec((tile, D), lambda j, h: (j * tiles + h, 0)),
+        functools.partial(weight_grad_kernel, groups, tile),
+        out_shape=[pltpu.HBM((per * hid, 2 * D), f32), pltpu.HBM((per * hid, D), f32)],
+        in_specs=[hbm()] * len(args),
+        out_specs=[hbm()] * 2,
+        scratch_shapes=[
+            wide,
+            wide,
+            narrow,
+            narrow,
+            narrow,
+            pltpu.VMEM((2, tile, 2 * D), f32),
+            pltpu.VMEM((2, tile, D), f32),
+            pltpu.SemaphoreType.DMA((per, 5 * groups)),
+            pltpu.SemaphoreType.DMA((2, 2)),
         ],
         compiler_params=pltpu.CompilerParams(vmem_limit_bytes=VMEM_LIMIT),
         cost_estimate=pl.CostEstimate(
@@ -602,42 +657,50 @@
     def swap(self, a):
         return lax.ppermute(a, "fsdp", self.core)
 
-    def gather(self, own):
+    def gather(self, own, work=None):
         half = own.shape[0] // 2
-        groups = [[own]]
-        before = after = own
-        for _ in range(3):
-            before, after = self.plus(before), self.minus(after)
-            groups.append([before, after])
-        groups.append([self.plus(before[:half]), self.minus(after[half:])])
-        return [group + [self.swap(a) for a in group] for group in groups]
-
-    def picks(self):
-        core = self.order[1, 0]
-        out = []
-        for k in range(5):
-            chips = [self.chips[0]] if k == 0 else [self.chips[8 - k], self.chips[k]]
-            out.append([(chip * 2 + (core ^ b), m if k == 4 else 0) for b in range(2) for m, chip in enumerate(chips)])
-        return out
-
-    def scatter(self, groups):
-        kept = []
-        for group in groups:
-            count = len(group) // 2
-            came = [self.swap(a) for a in group[count:]]
-            kept.append([a.astype(f32) + b.astype(f32) for a, b in zip(group[:count], came)])
-        up = self.minus(kept[4][0].astype(bf16))
-        down = self.plus(kept[4][1].astype(bf16))
-        for k in (3, 2, 1):
-            to_before, to_after = kept[k]
+        group, out, kept = [own], [], []
+        for r in range(5):
+            if r < 3:
+                coming = [self.plus(group[0]), self.minus(group[-1])]
+            elif r == 3:
+                coming = [self.plus(group[0][:half]), self.minus(group[1][half:])]
+            full = group + [self.swap(a) for a in group]
+            done = work(r, full) if work else full
+            if work and r:
+                kept.append(self.meet(out[-1]))
+            if r < 4:
+                if work:
+                    coming, done, kept = lax.optimization_barrier((coming, done, kept))
+                group = coming
+            out.append(done)
+        return (out, kept) if work else out
+
+    def meet(self, done):
+        payload = done[0]
+        count = len(payload) // 2
+        return list(zip(payload[:count], [self.swap(a) for a in payload[count:]]))
+
+    def scatter(self, kept, beside=None):
+        add = lambda terms: functools.reduce(jnp.add, [a.astype(f32) for a in terms])
+        out = [add(pair).astype(bf16) for pair in kept[4]]
+        for k in (3, 2, 1, 0):
+            up, down = lax.optimization_barrier((out[0], out[1]))
+            up, down = self.minus(up), self.plus(down)
+            if k == 2 and beside is not None:
+                up, down, beside = lax.optimization_barrier((up, down, beside))
+            if k == 0:
+                return add(list(kept[0][0]) + [up, down]), beside
             if k == 3:
                 half = up.shape[0]
-                to_before = jnp.concatenate([to_before[:half] + up, to_before[half:]])
-                to_after = jnp.concatenate([to_after[:half], to_after[half:] + down])
+                top = [a[:half] for a in kept[3][0]], [a[half:] for a in kept[3][0]]
+                low = [a[:half] for a in kept[3][1]], [a[half:] for a in kept[3][1]]
+                out = [
+                    jnp.concatenate([add(list(top[0]) + [up]), add(top[1])]).astype(bf16),
+                    jnp.concatenate([add(low[0]), add(list(low[1]) + [down])]).astype(bf16),
+                ]
             else:
-                to_before, to_after = to_before + up, to_after + down
-            up, down = self.minus(to_before.astype(bf16)), self.plus(to_after.astype(bf16))
-        return kept[0][0] + up.astype(f32) + down.astype(f32)
+                out = [add(list(pair) + [a]).astype(bf16) for pair, a in zip(kept[k], (up, down))]
 
 
 def on_device(
@@ -678,19 +741,19 @@
 
     if ringed:
         ring = Ring()
-        order = ring.order
+        order = jnp.concatenate([ring.order, jnp.broadcast_to(section, (1, 8)).astype(jnp.int32)])
         gains = jnp.concatenate([gain_attn, gain_moe])
         side = jnp.concatenate([gains, jnp.zeros((62, 64), bf16)])
         small = jnp.concatenate([w_router[0], jnp.zeros((64, 32), bf16), side], axis=1)
         groups = ring.gather(jnp.concatenate([w_qkv[0], w_out[0], small], axis=1))
-        near = [jnp.concatenate(groups[4][:2]), jnp.concatenate(groups[4][2:])]
         blocks = [[groups[0][0], groups[0][1]]]
         blocks += [[groups[k][1], groups[k][3]] for k in (1, 2, 3)]
         blocks += [[jnp.concatenate(groups[4][0:2]), jnp.concatenate(groups[4][2:4])]]
         blocks += [[groups[k][0], groups[k][2]] for k in (3, 2, 1)]
         w_all = jnp.stack([b for pair in blocks for b in pair]).reshape(8, 2, 64, WCOLS)
     else:
-        order = jnp.stack([jnp.arange(8), jnp.zeros((8,))]).astype(jnp.int32)
+        order = jnp.stack([jnp.arange(8), jnp.zeros((8,)), jnp.broadcast_to(section, (8,))])
+        order = order.astype(jnp.int32)
         gather = lambda a: lax.all_gather(a[0], "fsdp", axis=0, tiled=True)
         big = jnp.concatenate([gather(w_qkv), gather(w_out)], axis=1).reshape(16, 64, QKV + D)
         gains = jnp.stack([gather(gain_attn), gather(gain_moe)]).reshape(2, 16, 64)
@@ -702,66 +765,62 @@
         w_all = jnp.concatenate([big, small], axis=2).reshape(8, 2, 64, WCOLS)
 
     def gather_rows(own):
-        if ringed:
-            return ring.gather(own)
         every = lax.all_gather(own, "fsdp", axis=0, tiled=True)
         return every.reshape(-1, 8, length, own.shape[-1])
 
-    def scatter_rows(groups):
+    def phase(mode, own, g, x_groups=None):
         if ringed:
-            return ring.scatter(groups)
-        every = groups.reshape((devices * seqs,) + groups.shape[2:])
-        return lax.psum_scatter(every, "fsdp", scatter_dimension=0, tiled=True).astype(f32)
-
-    def experts(mode, x_groups, g_groups):
-        if ringed:
-            payload, kept = [], []
-            for n, group in enumerate(x_groups):
-                g = None
-                if mode:
-                    g = (g_groups[0], g_groups[1][n]) if isinstance(g_groups, tuple) else g_groups[n]
-                out = expert_call(mode, which, group, g, w_in, w_down, per)
-                payload.append(out[: len(group)])
-                kept.append(out[len(group) :])
-            return payload, (weight_grads(kept, hid, per) if mode == 2 else None)
+            seen, kept_rows = [], []
+
+            def work(r, group):
+                seen.append(group)
+                x, other = (group, None) if x_groups is None else (x_groups[r], group)
+                if mode == 1:
+                    other = g[r]
+                out = expert_call(mode, which, x, other, w_in, w_down, per)
+                return [out[: len(x)], out[len(x) :]]
+
+            out, kept = ring.gather(own, work)
+            kept.append(ring.meet(out[4]))
+            grads = weight_grads([o[1] for o in out], hid, per) if mode == 2 else None
+            sums, grads = ring.scatter(kept, grads)
+            return sums, seen, grads
+
+        every = gather_rows(own)
+        x_all, g_all = (every, g) if x_groups is None else (x_groups, every)
 
         def step(total, both):
-            out = expert_call(
-                mode, which, [both[0]], [both[1]] if mode else None, w_in, w_down, per
-            )
+            out = expert_call(mode, which, [both[0]], [both[1]] if mode else None, w_in, w_down, per)
             if mode == 2:
                 total = jax.tree.map(jnp.add, total, list(weight_grads([out[1:]], hid, per)))
             return total, out[0]
 
         zero = [jnp.zeros((per * hid, 2 * D), f32), jnp.zeros((per * hid, D), f32)]
         total, payload = lax.scan(
-            step, zero if mode == 2 else None, (x_groups, g_groups if mode else x_groups)
+            step, zero if mode == 2 else None, (x_all, g_all if mode else x_all)
         )
-        return payload, total
-
-    payload, resid = attn_forward(False, order, starts, tokens, pos, cosine, sine, w_all)
-    mixture = scatter_rows(experts(0, gather_rows(payload), None)[0])
+        flat = payload.reshape((devices * seqs,) + payload.shape[2:])
+        sums = lax.psum_scatter(flat, "fsdp", scatter_dimension=0, tiled=True).astype(f32)
+        return sums, x_all, total
+
+    payload, resid = attn_forward(
+        False, order, starts, tokens, pos, cosine, sine, w_all, cotangent
+    )
+    mixture, g_second, _ = phase(0, payload, None)
     first_out = (resid.reshape(seqs, length, D) + mixture).astype(bf16)
     passed = lax.ppermute(first_out, "section", [(0, 1)])
-    if ringed:
-        g_all = lax.all_gather(cotangent, "fsdp", axis=0)
-        g_second = (g_all, ring.picks())
-    else:
-        g_second = gather_rows(cotangent)
-
     layer_in = jnp.where(first_section, tokens, passed)
     payload, resid, *saved = attn_forward(True, order, starts, layer_in, pos, cosine, sine, w_all)
     saved = [payload, resid] + saved
-    rows_all = gather_rows(payload)
-    sums_second = scatter_rows(experts(1, rows_all, g_second)[0]).reshape(rows, WIDE)
+    sums_second, rows_all, _ = phase(1, payload, g_second)
+    sums_second = sums_second.reshape(rows, WIDE)
     (grad_second,) = attn_backward(
         False, order, sums_second, cotangent, layer_in, saved, cosine, sine, w_all
     )
 
     passed_grad = lax.ppermute(grad_second, "section", [(1, 0)])
     g_third = jnp.where(first_section, passed_grad, cotangent)
-    payload_third, (grad_in, grad_down) = experts(2, rows_all, gather_rows(g_third))
-    sums_third = scatter_rows(payload_third)
+    sums_third, _, (grad_in, grad_down) = phase(2, g_third, None, rows_all)
     second_out = (resid.reshape(seqs, length, D) + sums_third[..., :D]).astype(bf16)
     section_out = jnp.where(first_section, first_out, second_out)
     sums = jnp.where(first_section, sums_third.reshape(rows, WIDE), sums_second)
@@ -771,13 +830,13 @@
 
     if ringed:
         part = lambda k, b: big[k, b]
-        own_groups = [[part(0, 0), part(0, 1)]]
+        own_groups = [[[part(0, 0), part(0, 1)]]]
         for k in (1, 2, 3):
-            own_groups.append([part(8 - k, 0), part(k, 0), part(8 - k, 1), part(k, 1)])
+            own_groups.append([[part(8 - k, 0), part(k, 0), part(8 - k, 1), part(k, 1)]])
         own_groups.append(
-            [part(4, 0)[:32], part(4, 0)[32:], part(4, 1)[:32], part(4, 1)[32:]]
+            [[part(4, 0)[:32], part(4, 0)[32:], part(4, 1)[:32], part(4, 1)[32:]]]
         )
-        summed = ring.scatter(own_groups)
+        summed, _ = ring.scatter([ring.meet(group) for group in own_groups])
         g_qkv, g_out = summed[:, :QKV], summed[:, QKV : QKV + D]
         small = summed[:, QKV + D :]
         g_router, g_gain_attn, g_gain_moe = small[:, :EXPERTS], small[0, 64:], small[1, 64:]

time: 694 us -> 475 us (0.68)
  waiting for transfers between devices: 302 us -> 210 us
  Pallas kernels: 216 us -> 128 us
  between operations: 21 us -> 2.01 us
  other arithmetic: 24.9 us -> 12.8 us
    pallas_call x16, Pallas kernels: 164 us -> 91.2 us  [the longest x15 79.3 us: expert_call(): pl.pallas_call(body, out_shape=outs, in_specs=[smem()] + [vmem()] * (part...]
    ppermute x32, waiting for transfers between devices: 136 us -> 89 us  [plus(): return lax.ppermute(a, 'fsdp', self.ahead)]
    ppermute x32, waiting for transfers between devices: 141 us -> 99 us  [minus(): return lax.ppermute(a, 'fsdp', self.behind)]
    ppermute x32, starting transfers between devices: 48.7 us -> 34 us  [minus(): return lax.ppermute(a, 'fsdp', self.behind)]
    ppermute x32, starting transfers between devices: 23.8 us -> 34.8 us  [plus(): return lax.ppermute(a, 'fsdp', self.ahead)]
    pallas_call x2, Pallas kernels: 32.7 us -> 22.4 us  [attn_backward(): pl.pallas_call(functools.partial(attn_backward_kernel, with_grads), out_s...]
    unnamed x194 -> x96, local copies, waits for them, and re-layouts: 16 us -> 16 us
  transfers between devices with their start and end apart: 139 -> 138, of which waited for: 52 -> 69; matrix products, arithmetic and copies ran while one was open for 6% -> 5% of each run, Pallas kernels for 27% -> 17%
where the time goes in v2:
time: 475 us; the launch traced here: 468 us
  waiting for transfers between devices  210 us (44%)
  Pallas kernels  128 us (27%)
  starting transfers between devices  89.3 us (19%)
  local copies, waits for them, and re-layouts  24.8 us (5%)
  other arithmetic  12.8 us (3%)
    ppermute x32, waiting for transfers between devices, minus(): return lax.ppermute(a, 'fsdp', self.behind)  99 us
    ppermute x32, waiting for transfers between devices, plus(): return lax.ppermute(a, 'fsdp', self.ahead)  89 us
    pallas_call x15, Pallas kernels, expert_call(): pl.pallas_call(body, out_shape=outs, in_specs=[smem()] + [vmem()] * (part...  79.3 us
    ppermute x32, starting transfers between devices, plus(): return lax.ppermute(a, 'fsdp', self.ahead)  34.8 us
    ppermute x32, starting transfers between devices, minus(): return lax.ppermute(a, 'fsdp', self.behind)  34 us
    pallas_call x2, Pallas kernels, attn_backward(): pl.pallas_call(functools.partial(attn_backward_kernel, with_grads), out_s...  22.4 us
    unnamed x96, local copies, waits for them, and re-layouts  16 us
    ppermute x72, starting transfers between devices, swap(): return lax.ppermute(a, 'fsdp', self.core)  15.1 us
  transfers between devices with their start and end apart: 138, of which 69 were waited for; matrix products, arithmetic and copies ran while one was open for 5% of the time, Pallas kernels for 17%

profile of v2, /device:TPU:0, one launch (start us, length us, event | category | flops | bytes accessed | tf_op | source)
XLA Modules:
  0.0 468.0 jit_solution(7715381764042790614)
XLA Ops:
  20.2 8.3 %collective-permute-done.3 = bf16[64,3200]{1,0:T(8,128)(2,1)S(1)} collective-permute-done((bf16[64,3200]{1,0:T(8,128)(2,1)S(1)}, bf16[64,3200]{1,0:T(8,128)(2,1)S(1)}, u32[]{:S(2)}, u32[]{:S(2)}) %collective-permute-start.3) | collective-permute-done | bytes 409632 | tf_op jit(solution)/shard_map/ppermute | solution.py:655
  32.1 8.3 %collective-permute-done.5 = bf16[64,3200]{1,0:T(8,128)(2,1)S(1)} collective-permute-done((bf16[64,3200]{1,0:T(8,128)(2,1)S(1)}, bf16[64,3200]{1,0:T(8,128)(2,1)S(1)}, u32[]{:S(2)}, u32[]{:S(2)}) %collective-permute-start.5) | collective-permute-done | bytes 409632 | tf_op jit(solution)/shard_map/ppermute | solution.py:655
  57.3 7.2 %attn_forward.2 = (bf16[2,96,1152]{2,1,0:T(8,128)(2,1)S(1)}, f32[192,1024]{1,0:T(8,128)S(1)}) custom-call(s32[3,8]{1,0:T(4,128)S(1)} %add_add_fusion.order, s32[2]{0:T(128)S(1)} %bitcast.163, bf16[2,96,1024]{2,1,0:T(8,128)(2,1)S(1)} %copy-done.5, f32[192,128]{1,0:T(8,128)S(1)} %bitcast.160, f32[96,128]{1,0:T(8,128)S(1)} %copy-done.18, ...), custom_call_target="tpu_custom_call" | custom-call | flops 1336934400 | bytes 12000000 | tf_op jit(solution)/shard_map/attn_forward/pallas_call | solution.py:253
  81.0 5.5 %experts_0.6 = (bf16[2,96,1024]{2,1,0:T(8,128)(2,1)S(1)}, bf16[2,96,1024]{2,1,0:T(8,128)(2,1)S(1)}, bf16[2,96,1024]{2,1,0:T(8,128)(2,1)S(1)}, bf16[2,96,1024]{2,1,0:T(8,128)(2,1)S(1)}) custom-call(s32[2]{0:T(128)S(1)} %pad_add_fusion.which, bf16[2,96,1152]{2,1,0:T(8,128)(2,1)} %collective-permute-done.17.refs_0_.refs_4_, ...), custom_call_target="tpu_custom_call" | custom-call | flops 1610612736 | bytes 9538944 | tf_op jit(solution)/shard_map/experts_0/pallas_call | solution.py:537
  100.2 5.0 %collective-permute-done.25.refs_0_.refs_4_ = bf16[2,96,1152]{2,1,0:T(8,128)(2,1)S(1)} collective-permute-done((bf16[2,96,1152]{2,1,0:T(8,128)(2,1)S(1)}, bf16[2,96,1152]{2,1,0:T(8,128)(2,1)S(1)}, u32[]{:S(2)}, u32[]{:S(2)}) %collective-permute-start.25) | collective-permute-done | bytes 442400 | tf_op jit(solution)/shard_map/ppermute | solution.py:652
  134.8 8.7 %collective-permute-done.45 = bf16[2,96,1024]{2,1,0:T(8,128)(2,1)S(1)} collective-permute-done((bf16[2,96,1024]{2,1,0:T(8,128)(2,1)S(1)}, bf16[2,96,1024]{2,1,0:T(8,128)(2,1)S(1)}, u32[]{:S(2)}, u32[]{:S(2)}) %collective-permute-start.45) | collective-permute-done | bytes 393248 | tf_op jit(solution)/shard_map/ppermute | solution.py:655
  146.1 7.8 %collective-permute-done.47 = bf16[2,96,1024]{2,1,0:T(8,128)(2,1)S(1)} collective-permute-done((bf16[2,96,1024]{2,1,0:T(8,128)(2,1)S(1)}, bf16[2,96,1024]{2,1,0:T(8,128)(2,1)S(1)}, u32[]{:S(2)}, u32[]{:S(2)}) %collective-permute-start.47) | collective-permute-done | bytes 393248 | tf_op jit(solution)/shard_map/ppermute | solution.py:655
  156.4 6.9 %collective-permute-done.50 = bf16[2,96,1024]{2,1,0:T(8,128)(2,1)S(1)} collective-permute-done((bf16[2,96,1024]{2,1,0:T(8,128)(2,1)S(1)}, bf16[2,96,1024]{2,1,0:T(8,128)(2,1)S(1)}, u32[]{:S(2)}, u32[]{:S(2)}) %collective-permute-start.50) | collective-permute-done | bytes 393248 | tf_op jit(solution)/shard_map/ppermute | solution.py:652
  169.8 4.9 %collective-permute-done.51 = bf16[2,96,1024]{2,1,0:T(8,128)(2,1)} collective-permute-done((bf16[2,96,1024]{2,1,0:T(8,128)(2,1)}, bf16[2,96,1024]{2,1,0:T(8,128)(2,1)}, u32[]{:S(2)}, u32[]{:S(2)}) %collective-permute-start.51) | collective-permute-done | bytes 393248 | tf_op jit(solution)/shard_map/ppermute | solution.py:811
  176.6 7.2 %attn_forward.3 = (bf16[2,96,1152]{2,1,0:T(8,128)(2,1)S(1)}, f32[192,1024]{1,0:T(8,128)S(1)}, f32[192,128]{1,0:T(8,128)S(1)}, bf16[192,1024]{1,0:T(8,128)(2,1)S(...) custom-call(s32[3,8]{1,0:T(4,128)S(1)} %add_add_fusion.order, ...), custom_call_target="tpu_custom_call" | custom-call | flops 1336934400 | bytes 12000000 | tf_op jit(solution)/shard_map/attn_forward/pallas_call | solution.py:253
  190.5 5.9 %collective-permute-done.52.refs_0_ = bf16[2,96,1152]{2,1,0:T(8,128)(2,1)S(1)} collective-permute-done((bf16[2,96,1152]{2,1,0:T(8,128)(2,1)S(1)}, bf16[2,96,1152]{2,1,0:T(8,128)(2,1)S(1)}, u32[]{:S(2)}, u32[]{:S(2)}) %collective-permute-start.52) | collective-permute-done | bytes 442400 | tf_op jit(solution)/shard_map/ppermute | solution.py:652
  200.4 6.6 %experts_1.6 = (bf16[2,96,1152]{2,1,0:T(8,128)(2,1)S(1)}, bf16[2,96,1152]{2,1,0:T(8,128)(2,1)S(1)}, bf16[2,96,1152]{2,1,0:T(8,128)(2,1)S(1)}, bf16[2,96,1152]{2,1,0:T(8,128)(2,1)S(1)}) custom-call(s32[2]{0:T(128)S(1)} %pad_add_fusion.which, bf16[2,96,1152]{2,1,0:T(8,128)(2,1)S(1)} %collective-permute-done.52.refs_0_, ...), custom_call_target="tpu_custom_call" | custom-call | flops 2684354560 | bytes 9538944 | tf_op jit(solution)/shard_map/experts_1/pallas_call | solution.py:537
  214.5 6.1 %experts_1.7 = (bf16[2,96,1152]{2,1,0:T(8,128)(2,1)S(1)}, bf16[2,96,1152]{2,1,0:T(8,128)(2,1)S(1)}, bf16[2,96,1152]{2,1,0:T(8,128)(2,1)S(1)}, bf16[2,96,1152]{2,1,0:T(8,128)(2,1)S(1)}) custom-call(s32[2]{0:T(128)S(1)} %pad_add_fusion.which, bf16[2,96,1152]{2,1,0:T(8,128)(2,1)S(1)} %collective-permute-done.55.refs_0_, ...), custom_call_target="tpu_custom_call" | custom-call | flops 2684354560 | bytes 9538944 | tf_op jit(solution)/shard_map/experts_1/pallas_call | solution.py:537
  227.9 6.1 %experts_1.8 = (bf16[2,96,1152]{2,1,0:T(8,128)(2,1)S(1)}, bf16[2,96,1152]{2,1,0:T(8,128)(2,1)S(1)}, bf16[2,96,1152]{2,1,0:T(8,128)(2,1)S(1)}, bf16[2,96,1152]{2,1,0:T(8,128)(2,1)S(1)}) custom-call(s32[2]{0:T(128)S(1)} %pad_add_fusion.which, bf16[2,96,1152]{2,1,0:T(8,128)(2,1)S(1)} %collective-permute-done.60.refs_0_, ...), custom_call_target="tpu_custom_call" | custom-call | flops 2684354560 | bytes 9538944 | tf_op jit(solution)/shard_map/experts_1/pallas_call | solution.py:537
  245.2 5.5 %collective-permute-done.77 = bf16[1,96,1152]{2,1,0:T(8,128)(2,1)S(1)} collective-permute-done((bf16[1,96,1152]{2,1,0:T(8,128)(2,1)S(1)}, bf16[1,96,1152]{2,1,0:T(8,128)(2,1)S(1)}, u32[]{:S(2)}, u32[]{:S(2)}) %collective-permute-start.77) | collective-permute-done | bytes 221216 | tf_op jit(solution)/shard_map/ppermute | solution.py:655
  254.4 9.8 %collective-permute-done.80 = bf16[2,96,1152]{2,1,0:T(8,128)(2,1)S(1)} collective-permute-done((bf16[2,96,1152]{2,1,0:T(8,128)(2,1)S(1)}, bf16[2,96,1152]{2,1,0:T(8,128)(2,1)S(1)}, u32[]{:S(2)}, u32[]{:S(2)}) %collective-permute-start.80) | collective-permute-done | bytes 442400 | tf_op jit(solution)/shard_map/ppermute | solution.py:655
  267.1 8.6 %collective-permute-done.82 = bf16[2,96,1152]{2,1,0:T(8,128)(2,1)S(1)} collective-permute-done((bf16[2,96,1152]{2,1,0:T(8,128)(2,1)S(1)}, bf16[2,96,1152]{2,1,0:T(8,128)(2,1)S(1)}, u32[]{:S(2)}, u32[]{:S(2)}) %collective-permute-start.82) | collective-permute-done | bytes 442400 | tf_op jit(solution)/shard_map/ppermute | solution.py:655
  278.8 7.0 %collective-permute-done.85 = bf16[2,96,1152]{2,1,0:T(8,128)(2,1)S(1)} collective-permute-done((bf16[2,96,1152]{2,1,0:T(8,128)(2,1)S(1)}, bf16[2,96,1152]{2,1,0:T(8,128)(2,1)S(1)}, u32[]{:S(2)}, u32[]{:S(2)}) %collective-permute-start.85) | collective-permute-done | bytes 442400 | tf_op jit(solution)/shard_map/ppermute | solution.py:652
  287.3 10.0 %attn_backward.2 = bf16[2,96,1024]{2,1,0:T(8,128)(2,1)S(1)} custom-call(s32[3,8]{1,0:T(4,128)S(1)} %add_add_fusion.order, f32[192,1152]{1,0:T(8,128)S(1)} %bitcast.158, bf16[2,96,1024]{2,1,0:T(8,128)(2,1)S(1)} %copy-done.4, bf16[2,96,1024]{2,1,0:T(8,128)(2,1)S(1)} %broadcast_select_fusion.1.x_ref, ...), custom_call_target="tpu_custom_call" | custom-call | flops 2673868800 | bytes 20000000 | tf_op jit(solution)/shard_map/attn_backward/pallas_call | solution.py:389
  298.6 8.4 %collective-permute-done.86 = bf16[2,96,1024]{2,1,0:T(8,128)(2,1)S(1)} collective-permute-done((bf16[2,96,1024]{2,1,0:T(8,128)(2,1)S(1)}, bf16[2,96,1024]{2,1,0:T(8,128)(2,1)S(1)}, u32[]{:S(2)}, u32[]{:S(2)}) %collective-permute-start.86) | collective-permute-done | bytes 393248 | tf_op jit(solution)/shard_map/ppermute | solution.py:821
  309.2 5.0 %experts_2.5 = (bf16[2,96,1152]{2,1,0:T(8,128)(2,1)S(1)}, bf16[2,96,1152]{2,1,0:T(8,128)(2,1)S(1)}, bf16[2,128,1024]{2,1,0:T(8,128)(2,1)}, bf16[2,128,1024]{2,1,...) custom-call(s32[2]{0:T(128)S(1)} %pad_add_fusion.which, ...), custom_call_target="tpu_custom_call" | custom-call | flops 1342177280 | bytes 7769472 | tf_op jit(solution)/shard_map/experts_2/pallas_call | solution.py:537
  322.1 6.6 %experts_2.6 = (bf16[2,96,1152]{2,1,0:T(8,128)(2,1)S(1)}, bf16[2,96,1152]{2,1,0:T(8,128)(2,1)S(1)}, bf16[2,96,1152]{2,1,0:T(8,128)(2,1)S(1)}, bf16[2,96,1152]{2,...) custom-call(s32[2]{0:T(128)S(1)} %pad_add_fusion.which, ...), custom_call_target="tpu_custom_call" | custom-call | flops 2684354560 | bytes 9538944 | tf_op jit(solution)/shard_map/experts_2/pallas_call | solution.py:537
  335.3 6.6 %experts_2.7 = (bf16[2,96,1152]{2,1,0:T(8,128)(2,1)S(1)}, bf16[2,96,1152]{2,1,0:T(8,128)(2,1)S(1)}, bf16[2,96,1152]{2,1,0:T(8,128)(2,1)S(1)}, bf16[2,96,1152]{2,...) custom-call(s32[2]{0:T(128)S(1)} %pad_add_fusion.which, ...), custom_call_target="tpu_custom_call" | custom-call | flops 2684354560 | bytes 9538944 | tf_op jit(solution)/shard_map/experts_2/pallas_call | solution.py:537
  348.7 6.6 %experts_2.8 = (bf16[2,96,1152]{2,1,0:T(8,128)(2,1)S(1)}, bf16[2,96,1152]{2,1,0:T(8,128)(2,1)S(1)}, bf16[2,96,1152]{2,1,0:T(8,128)(2,1)S(1)}, bf16[2,96,1152]{2,...) custom-call(s32[2]{0:T(128)S(1)} %pad_add_fusion.which, ...), custom_call_target="tpu_custom_call" | custom-call | flops 2684354560 | bytes 9538944 | tf_op jit(solution)/shard_map/experts_2/pallas_call | solution.py:537
  357.1 5.0 %experts_2.9 = (bf16[1,96,1152]{2,1,0:T(8,128)(2,1)S(1)}, bf16[1,96,1152]{2,1,0:T(8,128)(2,1)S(1)}, bf16[1,96,1152]{2,1,0:T(8,128)(2,1)S(1)}, bf16[1,96,1152]{2,...) custom-call(s32[2]{0:T(128)S(1)} %pad_add_fusion.which, ...), custom_call_target="tpu_custom_call" | custom-call | flops 1342177280 | bytes 7769472 | tf_op jit(solution)/shard_map/experts_2/pallas_call | solution.py:537
  366.8 5.5 %collective-permute-done.112 = bf16[1,96,1152]{2,1,0:T(8,128)(2,1)S(1)} collective-permute-done((bf16[1,96,1152]{2,1,0:T(8,128)(2,1)S(1)}, bf16[1,96,1152]{2,1,0:T(8,128)(2,1)S(1)}, u32[]{:S(2)}, u32[]{:S(2)}) %collective-permute-start.112) | collective-permute-done | bytes 221216 | tf_op jit(solution)/shard_map/ppermute | solution.py:655
  376.0 11.8 %weight_grads.1 = (f32[1024,2048]{1,0:T(8,128)}, f32[1024,1024]{1,0:T(8,128)}) custom-call(bf16[2,128,1024]{2,1,0:T(8,128)(2,1)} %get-tuple-element.500.refs_0_, bf16[2,128,1024]{2,1,0:T(8,128)(2,1)} %get-tuple-element.501.refs_1_, bf16[2,128,512]{2,1,0:T(8,128)(2,1)} %get-tuple-element.502.refs_2_, bf16[2,128,512]{2,1,0:T(8,128)(2,1)} %get-tuple-element.503.refs_3_, ...), custom_call_target="tpu_custom_call" | custom-call | flops 6442450944 | bytes 27000000 | tf_op jit(solution)/shard_map/weight_grads/pallas_call | solution.py:613
  390.3 9.2 %collective-permute-done.117 = bf16[2,96,1152]{2,1,0:T(8,128)(2,1)S(1)} collective-permute-done((bf16[2,96,1152]{2,1,0:T(8,128)(2,1)S(1)}, bf16[2,96,1152]{2,1,0:T(8,128)(2,1)S(1)}, u32[]{:S(2)}, u32[]{:S(2)}) %collective-permute-start.117) | collective-permute-done | bytes 442400 | tf_op jit(solution)/shard_map/ppermute | solution.py:655
  402.5 7.8 %collective-permute-done.120 = bf16[2,96,1152]{2,1,0:T(8,128)(2,1)S(1)} collective-permute-done((bf16[2,96,1152]{2,1,0:T(8,128)(2,1)S(1)}, bf16[2,96,1152]{2,1,0:T(8,128)(2,1)S(1)}, u32[]{:S(2)}, u32[]{:S(2)}) %collective-permute-start.120) | collective-permute-done | bytes 442400 | tf_op jit(solution)/shard_map/ppermute | solution.py:652
  411.7 12.4 %attn_backward.3 = (bf16[2,96,1024]{2,1,0:T(8,128)(2,1)}, bf16[8,2,64,3200]{3,2,1,0:T(8,128)(2,1)S(1)}) custom-call(s32[3,8]{1,0:T(4,128)S(1)} %add_add_fusion.order, f32[192,1152]{1,0:T(8,128)S(1)} %bitcast_select_fusion.sum_ref, bf16[2,96,1024]{2,1,0:T(8,128)(2,1)S(1)} %broadcast_select_fusion.refs_2_.g_ref, ...), custom_call_target="tpu_custom_call" | custom-call | flops 2673868800 | bytes 20000000 | tf_op jit(solution)/shard_map/attn_backward/pallas_call | solution.py:389
  436.8 7.9 %collective-permute-done.132 = bf16[64,3200]{1,0:T(8,128)(2,1)S(1)} collective-permute-done((bf16[64,3200]{1,0:T(8,128)(2,1)S(1)}, bf16[64,3200]{1,0:T(8,128)(2,1)S(1)}, u32[]{:S(2)}, u32[]{:S(2)}) %collective-permute-start.132) | collective-permute-done | bytes 409632 | tf_op jit(solution)/shard_map/ppermute | solution.py:652
  447.8 7.2 %collective-permute-done.135 = bf16[64,3200]{1,0:T(8,128)(2,1)S(1)} collective-permute-done((bf16[64,3200]{1,0:T(8,128)(2,1)S(1)}, bf16[64,3200]{1,0:T(8,128)(2,1)S(1)}, u32[]{:S(2)}, u32[]{:S(2)}) %collective-permute-start.135) | collective-permute-done | bytes 409632 | tf_op jit(solution)/shard_map/ppermute | solution.py:652
  (437 shorter events, 230.8 us)
Async XLA Ops:
  3.4 15.3 %collective-permute-start = (bf16[64,3200]{1,0:T(8,128)(2,1)S(1)}, bf16[64,3200]{1,0:T(8,128)(2,1)S(1)}, u32[]{:S(2)}, u32[]{:S(2)}) collective-permute-start(bf16[64,3200]{1,0:T(8,128)(2,1)S(1)} %concatenate.49), channel_id=1, source_target_pairs={{0,1},{1,0},{2,3},{3,2},{4,5},{5,4},{6,7},{7,6},{8,9},{9,8},{10,11... | collective-permute-start | bytes 1228808 | tf_op jit(solution)/shard_map/ppermute | solution.py:658
  3.9 12.7 %collective-permute-start.1 = (bf16[64,3200]{1,0:T(8,128)(2,1)S(1)}, bf16[64,3200]{1,0:T(8,128)(2,1)S(1)}, u32[]{:S(2)}, u32[]{:S(2)}) collective-permute-start(bf16[64,3200]{1,0:T(8,128)(2,1)S(1)} %concatenate.49), channel_id=1, source_target_pairs={{0,2},{1,3},{4,0},{5,1},{8,4},{9,5},{12,8},{13,9},{14,12},{15,13},... | collective-permute-start | bytes 1228808 | tf_op jit(solution)/shard_map/ppermute | solution.py:655
  6.4 11.8 %collective-permute-start.7 = (bf16[64,3200]{1,0:T(8,128)(2,1)S(1)}, bf16[64,3200]{1,0:T(8,128)(2,1)}, u32[]{:S(2)}, u32[]{:S(2)}) collective-permute-start(bf16[64,3200]{1,0:T(8,128)(2,1)S(1)} %concatenate.49), channel_id=1, source_target_pairs={{0,4},{1,5},{4,8},{5,9},{8,12},{9,13},{12,14},{13,15},{14,10},{15,... | collective-permute-start | bytes 1228808 | tf_op jit(solution)/shard_map/ppermute | solution.py:652
  16.6 13.9 %collective-permute-start.2 = (bf16[64,3200]{1,0:T(8,128)(2,1)S(1)}, bf16[64,3200]{1,0:T(8,128)(2,1)S(1)}, u32[]{:S(2)}, u32[]{:S(2)}) collective-permute-start(bf16[64,3200]{1,0:T(8,128)(2,1)S(1)} %collective-permute-done.1), channel_id=1, source_target_pairs={{0,1},{1,0},{2,3},{3,2},{4,5},{5,4},{6,7},{7,6},{8,9},{9,8},{10,11... | collective-permute-start | bytes 1228808 | tf_op jit(solution)/shard_map/ppermute | solution.py:658
  16.6 11.9 %collective-permute-start.3 = (bf16[64,3200]{1,0:T(8,128)(2,1)S(1)}, bf16[64,3200]{1,0:T(8,128)(2,1)S(1)}, u32[]{:S(2)}, u32[]{:S(2)}) collective-permute-start(bf16[64,3200]{1,0:T(8,128)(2,1)S(1)} %collective-permute-done.1), channel_id=1, source_target_pairs={{0,2},{1,3},{4,0},{5,1},{8,4},{9,5},{12,8},{13,9},{14,12},{15,13},... | collective-permute-start | bytes 1228808 | tf_op jit(solution)/shard_map/ppermute | solution.py:655
  18.2 11.9 %collective-permute-start.8 = (bf16[64,3200]{1,0:T(8,128)(2,1)}, bf16[64,3200]{1,0:T(8,128)(2,1)S(1)}, u32[]{:S(2)}, u32[]{:S(2)}) collective-permute-start(bf16[64,3200]{1,0:T(8,128)(2,1)} %collective-permute-done.7), channel_id=1, source_target_pairs={{0,4},{1,5},{4,8},{5,9},{8,12},{9,13},{12,14},{13,15},{14,10},{15,... | collective-permute-start | bytes 1228808 | tf_op jit(solution)/shard_map/ppermute | solution.py:652
  18.6 37.9 %collective-permute-start.16 = (bf16[64,3200]{1,0:T(8,128)(2,1)}, bf16[64,3200]{1,0:T(8,128)(2,1)S(1)}, u32[]{:S(2)}, u32[]{:S(2)}) collective-permute-start(bf16[64,3200]{1,0:T(8,128)(2,1)} %collective-permute-done.7), channel_id=1, source_target_pairs={{0,1},{1,0},{2,3},{3,2},{4,5},{5,4},{6,7},{7,6},{8,9},{9,8},{10,11... | collective-permute-start | bytes 1228808 | tf_op jit(solution)/shard_map/ppermute | solution.py:658
  28.5 14.1 %collective-permute-start.4 = (bf16[64,3200]{1,0:T(8,128)(2,1)S(1)}, bf16[64,3200]{1,0:T(8,128)(2,1)S(1)}, u32[]{:S(2)}, u32[]{:S(2)}) collective-permute-start(bf16[64,3200]{1,0:T(8,128)(2,1)S(1)} %collective-permute-done.3), channel_id=1, source_target_pairs={{0,1},{1,0},{2,3},{3,2},{4,5},{5,4},{6,7},{7,6},{8,9},{9,8},{10,11... | collective-permute-start | bytes 1228808 | tf_op jit(solution)/shard_map/ppermute | solution.py:658
  28.5 11.9 %collective-permute-start.5 = (bf16[64,3200]{1,0:T(8,128)(2,1)S(1)}, bf16[64,3200]{1,0:T(8,128)(2,1)S(1)}, u32[]{:S(2)}, u32[]{:S(2)}) collective-permute-start(bf16[64,3200]{1,0:T(8,128)(2,1)S(1)} %collective-permute-done.3), channel_id=1, source_target_pairs={{0,2},{1,3},{4,0},{5,1},{8,4},{9,5},{12,8},{13,9},{14,12},{15,13},... | collective-permute-start | bytes 1228808 | tf_op jit(solution)/shard_map/ppermute | solution.py:655
  30.1 11.9 %collective-permute-start.9 = (bf16[64,3200]{1,0:T(8,128)(2,1)S(1)}, bf16[64,3200]{1,0:T(8,128)(2,1)S(1)}, u32[]{:S(2)}, u32[]{:S(2)}) collective-permute-start(bf16[64,3200]{1,0:T(8,128)(2,1)S(1)} %collective-permute-done.8), channel_id=1, source_target_pairs={{0,4},{1,5},{4,8},{5,9},{8,12},{9,13},{12,14},{13,15},{14,10},{15,... | collective-permute-start | bytes 1228808 | tf_op jit(solution)/shard_map/ppermute | solution.py:652
  30.5 23.4 %collective-permute-start.15 = (bf16[64,3200]{1,0:T(8,128)(2,1)S(1)}, bf16[64,3200]{1,0:T(8,128)(2,1)S(1)}, u32[]{:S(2)}, u32[]{:S(2)}) collective-permute-start(bf16[64,3200]{1,0:T(8,128)(2,1)S(1)} %collective-permute-done.8), channel_id=1, source_target_pairs={{0,1},{1,0},{2,3},{3,2},{4,5},{5,4},{6,7},{7,6},{8,9},{9,8},{10,11... | collective-permute-start | bytes 1228808 | tf_op jit(solution)/shard_map/ppermute | solution.py:658
  65.3 12.7 %collective-permute-start.17 = (bf16[2,96,1152]{2,1,0:T(8,128)(2,1)S(1)}, bf16[2,96,1152]{2,1,0:T(8,128)(2,1)}, u32[]{:S(2)}, u32[]{:S(2)}) collective-permute-start(bf16[2,96,1152]{2,1,0:T(8,128)(2,1)S(1)} %get-tuple-element.280.refs_0_.refs_2_), channel_id=1, source_target_pairs={{0,4},{1,5},{4,8},{5,9},{8,12},{9,13},{12,14},{13,15},{14,10},{15,... | collective-permute-start | bytes 1327112 | tf_op jit(solution)/shard_map/ppermute | solution.py:652
  66.1 12.1 %collective-permute-start.18 = (bf16[2,96,1152]{2,1,0:T(8,128)(2,1)S(1)}, bf16[2,96,1152]{2,1,0:T(8,128)(2,1)}, u32[]{:S(2)}, u32[]{:S(2)}) collective-permute-start(bf16[2,96,1152]{2,1,0:T(8,128)(2,1)S(1)} %get-tuple-element.280.refs_0_.refs_2_), channel_id=1, source_target_pairs={{0,2},{1,3},{4,0},{5,1},{8,4},{9,5},{12,8},{13,9},{14,12},{15,13},... | collective-permute-start | bytes 1327112 | tf_op jit(solution)/shard_map/ppermute | solution.py:655
  78.8 12.3 %collective-permute-start.20 = (bf16[2,96,1152]{2,1,0:T(8,128)(2,1)}, bf16[2,96,1152]{2,1,0:T(8,128)(2,1)S(1)}, u32[]{:S(2)}, u32[]{:S(2)}) collective-permute-start(bf16[2,96,1152]{2,1,0:T(8,128)(2,1)} %collective-permute-done.17.refs_0_.refs_4_), channel_id=1, source_target_pairs={{0,4},{1,5},{4,8},{5,9},{8,12},{9,13},{12,14},{13,15},{14,10},{15,... | collective-permute-start | bytes 1327112 | tf_op jit(solution)/shard_map/ppermute | solution.py:652
  80.4 12.2 %collective-permute-start.21 = (bf16[2,96,1152]{2,1,0:T(8,128)(2,1)}, bf16[2,96,1152]{2,1,0:T(8,128)(2,1)S(1)}, u32[]{:S(2)}, u32[]{:S(2)}) collective-permute-start(bf16[2,96,1152]{2,1,0:T(8,128)(2,1)} %collective-permute-done.18.refs_1_.refs_5_), channel_id=1, source_target_pairs={{0,2},{1,3},{4,0},{5,1},{8,4},{9,5},{12,8},{13,9},{14,12},{15,13},... | collective-permute-start | bytes 1327112 | tf_op jit(solution)/shard_map/ppermute | solution.py:655
  93.1 12.1 %collective-permute-start.25 = (bf16[2,96,1152]{2,1,0:T(8,128)(2,1)S(1)}, bf16[2,96,1152]{2,1,0:T(8,128)(2,1)S(1)}, u32[]{:S(2)}, u32[]{:S(2)}) collective-permute-start(bf16[2,96,1152]{2,1,0:T(8,128)(2,1)S(1)} %collective-permute-done.20.refs_0_.refs_4_), channel_id=1, source_target_pairs={{0,4},{1,5},{4,8},{5,9},{8,12},{9,13},{12,14},{13,15},{14,10},{15,... | collective-permute-start | bytes 1327112 | tf_op jit(solution)/shard_map/ppermute | solution.py:652
  94.7 11.9 %collective-permute-start.26 = (bf16[2,96,1152]{2,1,0:T(8,128)(2,1)S(1)}, bf16[2,96,1152]{2,1,0:T(8,128)(2,1)S(1)}, u32[]{:S(2)}, u32[]{:S(2)}) collective-permute-start(bf16[2,96,1152]{2,1,0:T(8,128)(2,1)S(1)} %collective-permute-done.21.refs_1_.refs_5_), channel_id=1, source_target_pairs={{0,2},{1,3},{4,0},{5,1},{8,4},{9,5},{12,8},{13,9},{14,12},{15,13},... | collective-permute-start | bytes 1327112 | tf_op jit(solution)/shard_map/ppermute | solution.py:655
  183.8 12.6 %collective-permute-start.52 = (bf16[2,96,1152]{2,1,0:T(8,128)(2,1)S(1)}, bf16[2,96,1152]{2,1,0:T(8,128)(2,1)S(1)}, u32[]{:S(2)}, u32[]{:S(2)}) collective-permute-start(bf16[2,96,1152]{2,1,0:T(8,128)(2,1)S(1)} %get-tuple-element.348.refs_0_.wide_ref), channel_id=1, source_target_pairs={{0,4},{1,5},{4,8},{5,9},{8,12},{9,13},{12,14},{13,15},{14,10},{15,... | collective-permute-start | bytes 1327112 | tf_op jit(solution)/shard_map/ppermute | solution.py:652
  185.4 12.2 %collective-permute-start.53 = (bf16[2,96,1152]{2,1,0:T(8,128)(2,1)S(1)}, bf16[2,96,1152]{2,1,0:T(8,128)(2,1)S(1)}, u32[]{:S(2)}, u32[]{:S(2)}) collective-permute-start(bf16[2,96,1152]{2,1,0:T(8,128)(2,1)S(1)} %get-tuple-element.348.refs_0_.wide_ref), channel_id=1, source_target_pairs={{0,2},{1,3},{4,0},{5,1},{8,4},{9,5},{12,8},{13,9},{14,12},{15,13},... | collective-permute-start | bytes 1327112 | tf_op jit(solution)/shard_map/ppermute | solution.py:655
  198.2 12.1 %collective-permute-start.55 = (bf16[2,96,1152]{2,1,0:T(8,128)(2,1)S(1)}, bf16[2,96,1152]{2,1,0:T(8,128)(2,1)S(1)}, u32[]{:S(2)}, u32[]{:S(2)}) collective-permute-start(bf16[2,96,1152]{2,1,0:T(8,128)(2,1)S(1)} %collective-permute-done.52.refs_0_), channel_id=1, source_target_pairs={{0,4},{1,5},{4,8},{5,9},{8,12},{9,13},{12,14},{13,15},{14,10},{15,... | collective-permute-start | bytes 1327112 | tf_op jit(solution)/shard_map/ppermute | solution.py:652
  199.4 11.9 %collective-permute-start.56 = (bf16[2,96,1152]{2,1,0:T(8,128)(2,1)S(1)}, bf16[2,96,1152]{2,1,0:T(8,128)(2,1)S(1)}, u32[]{:S(2)}, u32[]{:S(2)}) collective-permute-start(bf16[2,96,1152]{2,1,0:T(8,128)(2,1)S(1)} %collective-permute-done.53.refs_1_), channel_id=1, source_target_pairs={{0,2},{1,3},{4,0},{5,1},{8,4},{9,5},{12,8},{13,9},{14,12},{15,13},... | collective-permute-start | bytes 1327112 | tf_op jit(solution)/shard_map/ppermute | solution.py:655
  211.9 12.1 %collective-permute-start.60 = (bf16[2,96,1152]{2,1,0:T(8,128)(2,1)S(1)}, bf16[2,96,1152]{2,1,0:T(8,128)(2,1)S(1)}, u32[]{:S(2)}, u32[]{:S(2)}) collective-permute-start(bf16[2,96,1152]{2,1,0:T(8,128)(2,1)S(1)} %collective-permute-done.55.refs_0_), channel_id=1, source_target_pairs={{0,4},{1,5},{4,8},{5,9},{8,12},{9,13},{12,14},{13,15},{14,10},{15,... | collective-permute-start | bytes 1327112 | tf_op jit(solution)/shard_map/ppermute | solution.py:652
  212.8 11.8 %collective-permute-start.61 = (bf16[2,96,1152]{2,1,0:T(8,128)(2,1)S(1)}, bf16[2,96,1152]{2,1,0:T(8,128)(2,1)S(1)}, u32[]{:S(2)}, u32[]{:S(2)}) collective-permute-start(bf16[2,96,1152]{2,1,0:T(8,128)(2,1)S(1)} %collective-permute-done.56.refs_1_), channel_id=1, source_target_pairs={{0,2},{1,3},{4,0},{5,1},{8,4},{9,5},{12,8},{13,9},{14,12},{15,13},... | collective-permute-start | bytes 1327112 | tf_op jit(solution)/shard_map/ppermute | solution.py:655
  252.3 11.9 %collective-permute-start.80 = (bf16[2,96,1152]{2,1,0:T(8,128)(2,1)S(1)}, bf16[2,96,1152]{2,1,0:T(8,128)(2,1)S(1)}, u32[]{:S(2)}, u32[]{:S(2)}) collective-permute-start(bf16[2,96,1152]{2,1,0:T(8,128)(2,1)S(1)} %pad_maximum_fusion), channel_id=1, source_target_pairs={{0,2},{1,3},{4,0},{5,1},{8,4},{9,5},{12,8},{13,9},{14,12},{15,13},... | collective-permute-start | bytes 1327112 | tf_op jit(solution)/shard_map/ppermute | solution.py:655
  320.0 12.3 %collective-permute-start.94 = (bf16[2,96,1152]{2,1,0:T(8,128)(2,1)S(1)}, bf16[2,96,1152]{2,1,0:T(8,128)(2,1)S(1)}, u32[]{:S(2)}, u32[]{:S(2)}) collective-permute-start(bf16[2,96,1152]{2,1,0:T(8,128)(2,1)S(1)} %get-tuple-element.441), channel_id=1, source_target_pairs={{0,1},{1,0},{2,3},{3,2},{4,5},{5,4},{6,7},{7,6},{8,9},{9,8},{10,11... | collective-permute-start | bytes 1327112 | tf_op jit(solution)/shard_map/ppermute | solution.py:658
  320.0 11.5 %collective-permute-start.90 = (bf16[2,96,1024]{2,1,0:T(8,128)(2,1)S(1)}, bf16[2,96,1024]{2,1,0:T(8,128)(2,1)S(1)}, u32[]{:S(2)}, u32[]{:S(2)}) collective-permute-start(bf16[2,96,1024]{2,1,0:T(8,128)(2,1)S(1)} %collective-permute-done.87.refs_4_), channel_id=1, source_target_pairs={{0,4},{1,5},{4,8},{5,9},{8,12},{9,13},{12,14},{13,15},{14,10},{15,... | collective-permute-start | bytes 1179656 | tf_op jit(solution)/shard_map/ppermute | solution.py:652
  332.7 12.4 %collective-permute-start.99 = (bf16[2,96,1152]{2,1,0:T(8,128)(2,1)S(1)}, bf16[2,96,1152]{2,1,0:T(8,128)(2,1)S(1)}, u32[]{:S(2)}, u32[]{:S(2)}) collective-permute-start(bf16[2,96,1152]{2,1,0:T(8,128)(2,1)S(1)} %get-tuple-element.456), channel_id=1, source_target_pairs={{0,1},{1,0},{2,3},{3,2},{4,5},{5,4},{6,7},{7,6},{8,9},{9,8},{10,11... | collective-permute-start | bytes 1327112 | tf_op jit(solution)/shard_map/ppermute | solution.py:658
  332.8 12.4 %collective-permute-start.100 = (bf16[2,96,1152]{2,1,0:T(8,128)(2,1)S(1)}, bf16[2,96,1152]{2,1,0:T(8,128)(2,1)S(1)}, u32[]{:S(2)}, u32[]{:S(2)}) collective-permute-start(bf16[2,96,1152]{2,1,0:T(8,128)(2,1)S(1)} %get-tuple-element.458), channel_id=1, source_target_pairs={{0,1},{1,0},{2,3},{3,2},{4,5},{5,4},{6,7},{7,6},{8,9},{9,8},{10,11... | collective-permute-start | bytes 1327112 | tf_op jit(solution)/shard_map/ppermute | solution.py:658
  373.9 13.9 %collective-permute-start.115 = (bf16[2,96,1152]{2,1,0:T(8,128)(2,1)S(1)}, bf16[2,96,1152]{2,1,0:T(8,128)(2,1)S(1)}, u32[]{:S(2)}, u32[]{:S(2)}) collective-permute-start(bf16[2,96,1152]{2,1,0:T(8,128)(2,1)S(1)} %pad_maximum_fusion.2), channel_id=1, source_target_pairs={{0,2},{1,3},{4,0},{5,1},{8,4},{9,5},{12,8},{13,9},{14,12},{15,13},... | collective-permute-start | bytes 1327112 | tf_op jit(solution)/shard_map/ppermute | solution.py:655
  374.9 12.9 %collective-permute-start.116 = (bf16[2,96,1152]{2,1,0:T(8,128)(2,1)S(1)}, bf16[2,96,1152]{2,1,0:T(8,128)(2,1)S(1)}, u32[]{:S(2)}, u32[]{:S(2)}) collective-permute-start(bf16[2,96,1152]{2,1,0:T(8,128)(2,1)S(1)} %pad_maximum_fusion.3), channel_id=1, source_target_pairs={{0,4},{1,5},{4,8},{5,9},{8,12},{9,13},{12,14},{13,15},{14,10},{15,... | collective-permute-start | bytes 1327112 | tf_op jit(solution)/shard_map/ppermute | solution.py:652
  436.3 11.5 %collective-permute-start.134 = (bf16[64,3200]{1,0:T(8,128)(2,1)S(1)}, bf16[64,3200]{1,0:T(8,128)(2,1)S(1)}, u32[]{:S(2)}, u32[]{:S(2)}) collective-permute-start(bf16[64,3200]{1,0:T(8,128)(2,1)S(1)} %get-tuple-element.581), channel_id=1, source_target_pairs={{0,1},{1,0},{2,3},{3,2},{4,5},{5,4},{6,7},{7,6},{8,9},{9,8},{10,11... | collective-permute-start | bytes 1228808 | tf_op jit(solution)/shard_map/ppermute | solution.py:658
  447.8 11.9 %collective-permute-start.121 = (bf16[64,3200]{1,0:T(8,128)(2,1)S(1)}, bf16[64,3200]{1,0:T(8,128)(2,1)S(1)}, u32[]{:S(2)}, u32[]{:S(2)}) collective-permute-start(bf16[64,3200]{1,0:T(8,128)(2,1)S(1)} %get-tuple-element.580), channel_id=1, source_target_pairs={{0,1},{1,0},{2,3},{3,2},{4,5},{5,4},{6,7},{7,6},{8,9},{9,8},{10,11... | collective-permute-start | bytes 1228808 | tf_op jit(solution)/shard_map/ppermute | solution.py:658
  (147 other events, 1539.2 us)

commit v3 on v2

v3 whole, which is shorter than its diff:
```python
import functools

import jax
import jax.numpy as jnp
import numpy as np
from jax import lax
from jax.experimental import pallas as pl
from jax.experimental.pallas import tpu as pltpu
from jax.sharding import PartitionSpec as P

D = 1024
QUERY_HEADS = 16
KEY_VALUE_HEADS = 8
HEAD_SIZE = 64
EXPERTS = 32
TOP = 8
PIC = 64
SLOTS = 32
LANES = 128
QKV = 2048
TILE = 16
TILES = D // LANES
WCOLS = QKV + D + LANES
epsilon = 1e-05
scale = HEAD_SIZE ** (-0.5)
f32 = jnp.float32
bf16 = jnp.bfloat16
VMEM_LIMIT = 30 * 1024 * 1024

PATH = (0, 2, 4, 6, 7, 5, 3, 1)
PLACE = tuple(PATH.index(c) for c in range(8))


def dot(a, b, ca, cb):
    return lax.dot_general(a, b, (((ca,), (cb,)), ((), ())), preferred_element_type=f32)


def nn(a, b):
    return dot(a, b, 1, 0)


def nt(a, b):
    return dot(a, b, 1, 1)


def tn(a, b):
    return dot(a, b, 0, 0)


def lanes_of(shape):
    return lax.broadcasted_iota(jnp.int32, shape, len(shape) - 1)


def rms(values):
    return lax.rsqrt(jnp.mean(values * values, axis=-1, keepdims=True) + epsilon)


def norm_back(values, inv, gain, grad):
    scaled = grad * gain
    inner = jnp.mean(scaled * values, axis=-1, keepdims=True)
    return inv * scaled - values * (inv * inv * inv * inner)


def turn(chunk, cosine, sine, back):
    first = (lanes_of(chunk.shape) & 63) < 32
    ahead = pltpu.roll(chunk, 96, 1)
    behind = pltpu.roll(chunk, 32, 1)
    if back:
        swapped = jnp.where(first, ahead, -behind)
    else:
        swapped = jnp.where(first, -ahead, behind)
    return chunk * cosine + swapped * sine


def halves(chunk):
    low = lanes_of(chunk.shape) < 64
    return jnp.concatenate([jnp.where(low, chunk, 0.0), jnp.where(low, 0.0, chunk)], axis=0)


def join(stacked):
    rows = stacked.shape[0] // 2
    low = lanes_of((rows, LANES)) < 64
    return jnp.where(low, stacked[:rows], stacked[rows:])


def doubled(chunk, odd):
    low = lanes_of(chunk.shape) < 64
    other = pltpu.roll(chunk, 64, 1)
    return jnp.where(low, other, chunk) if odd else jnp.where(low, chunk, other)


PARTS = ((0, QKV), (QKV, QKV + D), (QKV + D, WCOLS))


def wide(length):
    return length * TILES + length // 2


def plain(tiles):
    count = tiles.shape[0] // (TILE * TILES)
    tiles = tiles.reshape(count, TILES, TILE, LANES)
    columns = [tiles[:, c].reshape(count * TILE, LANES) for c in range(TILES)]
    return jnp.concatenate(columns, axis=1)


def store_tiles(ref, s, rows):
    for r in range(rows.shape[0] // TILE):
        for c in range(TILES):
            place = (r * TILES + c) * TILE
            block = rows[r * TILE : (r + 1) * TILE, c * LANES : (c + 1) * LANES]
            ref[s, place : place + TILE] = block.astype(ref.dtype)


def fold(columns):
    half = columns.shape[0] // 2
    low = lanes_of((half, LANES)) < 64
    return jnp.where(low, columns[:half], pltpu.roll(columns[half:], 64, 1))


def unfold(folded):
    return jnp.concatenate([folded, pltpu.roll(folded, 64, 1)], axis=0)


def load_weights(order, blocks, w_vmem, sems, turn_of):
    copies = {}
    for part in turn_of:
        columns = pl.ds(PARTS[part][0], PARTS[part][1] - PARTS[part][0])
        copies[part] = []
        for k in range(8):
            for b in range(2):
                target = w_vmem.at[order[0, k] * 2 + (order[1, 0] ^ b), :, columns]
                if k != 4:
                    pairs = [(blocks[(k if k < 4 else k + 1) * 2 + b], target)]
                else:
                    pairs = [(blocks[8 + 2 * b + h], target.at[pl.ds(32 * h, 32)]) for h in range(2)]
                for block, target in pairs:
                    sem = sems.at[part * 18 + len(copies[part])]
                    copies[part].append(pltpu.make_async_copy(block.at[:, columns], target, sem))
        for copy in copies[part]:
            copy.start()

    def wait(part):
        for copy in copies[part]:
            copy.wait()

    return wait


def gains_of(w_vmem):
    pieces = ([], [])
    for c in range(8):
        even = w_vmem[2 * c, 0:16, QKV + D :].astype(f32)
        odd = w_vmem[2 * c + 1, 0:16, QKV + D :].astype(f32)
        even = pltpu.roll(even, 64, 1)
        both = jnp.where(lanes_of(even.shape) < 64, even, odd)
        for i in range(2):
            pieces[i].append(both[i : i + 1])
    return jnp.concatenate(pieces[0], axis=1), jnp.concatenate(pieces[1], axis=1)


def attn_forward_kernel(save, order, starts, table_hbm, pos_hbm, *refs):
    x_hbms, blocks, refs = refs[:2], refs[2:20], refs[20:]
    out_ref, resid_ref, refs = refs[0], refs[1], refs[2:]
    if save:
        x_ref, gate_ref, normed_ref, q_ref, k_ref, v_ref, probs_ref, mixed_ref = refs[:8]
        passed_ref, refs = refs[8], refs[9:]
    else:
        x_ref, cot_ref, mixed_ref = refs[:3]
        refs = refs[3:]
    w_vmem, table_ref, pos_ref, sems, side_sems = refs
    second = order[2, 0] != 0
    if save:
        loads = [
            pltpu.make_async_copy(x_hbms[0], x_ref, side_sems.at[0]),
            pltpu.make_async_copy(x_hbms[1], passed_ref, side_sems.at[3]),
        ]
        loads[0].start()
        loads[1].start()

    else:
        loads = [
            pltpu.make_async_copy(x_hbms[0], x_ref, side_sems.at[0]),
            pltpu.make_async_copy(x_hbms[1], cot_ref, side_sems.at[3]),
        ]
        loads[0].start()
        loads[1].start()
    load_table = pltpu.make_async_copy(table_hbm, table_ref, side_sems.at[1])
    load_table.start()
    wait = load_weights(order, blocks, w_vmem, sems, (2, 0, 1))
    load_pos = pltpu.make_async_copy(pos_hbm, pos_ref, side_sems.at[2])
    load_pos.start()
    seqs, length = x_ref.shape[0], x_ref.shape[1]
    rows = seqs * length
    loads[0].wait()
    if save:
        loads[1].wait()

        @pl.when(second)
        def _():
            for s in range(seqs):
                x_ref[s] = plain(passed_ref[s])

    wait(2)
    gain_attn, gain_moe = gains_of(w_vmem)
    x = x_ref[...].reshape(rows, D).astype(f32)
    normed = (x * rms(x) * gain_attn).astype(bf16)
    row_pos = lax.broadcasted_iota(jnp.int32, (length, length), 0)
    col_pos = lax.broadcasted_iota(jnp.int32, (length, length), 1)
    load_table.wait()
    cosine, sine = table_ref[:, :LANES], table_ref[:, LANES:]
    wait(0)
    w_qkv = w_vmem[:, :, :QKV].reshape(D, QKV)
    qkv = nn(normed, w_qkv)
    heads = range(KEY_VALUE_HEADS)
    for s in range(seqs):
        top = slice(s * length, (s + 1) * length)
        start = starts[s]
        both = (
            (row_pos >= start) & (row_pos < start + PIC) & (col_pos >= start) & (col_pos < start + PIC)
        )
        bias = jnp.where((col_pos <= row_pos) | both, 0.0, -1e30)
        bias = jnp.concatenate([bias, bias], axis=0)
        keys, values = [], []
        for c in range(4):
            key = turn(qkv[top, D + c * LANES : D + (c + 1) * LANES], cosine, sine, False)
            value = qkv[top, D + 512 + c * LANES : D + 512 + (c + 1) * LANES]
            if save:
                k_ref[top, c * LANES : (c + 1) * LANES] = key.astype(bf16)
                v_ref[top, c * LANES : (c + 1) * LANES] = value.astype(bf16)
            for odd in (False, True):
                keys.append(doubled(key, odd).astype(bf16))
                values.append(doubled(value, odd).astype(bf16))
        for j in heads:
            query = turn(qkv[top, j * LANES : (j + 1) * LANES], cosine, sine, False)
            if save:
                q_ref[top, j * LANES : (j + 1) * LANES] = query.astype(bf16)
            scores = nt(halves(query).astype(bf16), keys[j]) * scale + bias
            exponent = jnp.exp(scores - jnp.max(scores, axis=-1, keepdims=True))
            probs = exponent * (1.0 / jnp.sum(exponent, axis=-1, keepdims=True))
            if save:
                probs_ref[s * KEY_VALUE_HEADS + j] = probs
            mixed = join(nn(probs.astype(bf16), values[j]))
            mixed_ref[top, j * LANES : (j + 1) * LANES] = mixed.astype(bf16)
    wait(1)
    w_out = w_vmem[:, :, QKV : QKV + D].reshape(D, D)
    resid = x + nn(mixed_ref[...], w_out)
    normed_moe = (resid * rms(resid) * gain_moe).astype(bf16)
    w_small = w_vmem[:, :, QKV + D :].reshape(D, LANES)
    logits = nn(normed_moe, w_small)
    load_pos.wait()
    pos = pos_ref[...]
    routed = pos < 64.0
    logits = jnp.where(routed, logits, -1e30)
    exponent = jnp.where(routed, jnp.exp(logits - jnp.max(logits, axis=-1, keepdims=True)), 0.0)
    gate = exponent * (1.0 / jnp.sum(exponent, axis=-1, keepdims=True))
    lane = lanes_of(gate.shape)
    columns = jnp.where(lane < 32, gate, pltpu.roll(pos, 32, 1))
    for s in range(seqs):
        top = slice(s * length, (s + 1) * length)
        store_tiles(out_ref, s, normed_moe[top])
        out_ref[s, length * TILES :] = fold(columns[top]).astype(bf16)
    if save:
        resid_ref[...] = resid
        gate_ref[...] = gate
        normed_ref[...] = normed
    else:
        for s in range(seqs):
            store_tiles(resid_ref, s, resid[s * length : (s + 1) * length])
        loads[1].wait()

        @pl.when(second)
        def _():
            for s in range(seqs):
                store_tiles(out_ref, s, cot_ref[s])


def vmem():
    return pl.BlockSpec(memory_space=pltpu.VMEM)


def smem():
    return pl.BlockSpec(memory_space=pltpu.SMEM)


def hbm():
    return pl.BlockSpec(memory_space=pltpu.HBM)


def in_hbm(a):
    return pltpu.with_memory_space_constraint(a, pltpu.HBM)


def attn_forward(save, order, starts, table, pos, x, other, w_all):
    seqs, length = x.shape[0], x.shape[1]
    rows = seqs * length
    shape = jax.ShapeDtypeStruct
    tiles = (seqs, length * TILES, LANES)
    outs = [shape((seqs, wide(length), LANES), bf16), shape((rows, D) if save else tiles, f32)]
    probs = (seqs * KEY_VALUE_HEADS, 2 * length, length)
    scratch = []
    if save:
        outs += [
            shape((seqs, length, D), bf16),
            shape((rows, LANES), f32),
            shape((rows, D), bf16),
            shape((rows, D), bf16),
            shape((rows, 512), bf16),
            shape((rows, 512), bf16),
            shape(probs, f32),
            shape((rows, D), bf16),
        ]
        scratch = [pltpu.VMEM(tiles, bf16)]
    else:
        scratch = [pltpu.VMEM((seqs, length, D), bf16)] * 2
        scratch.append(pltpu.VMEM((rows, D), bf16))
    scratch += [
        pltpu.VMEM((16, 64, WCOLS), bf16),
        pltpu.VMEM((length, 2 * LANES), f32),
        pltpu.VMEM((rows, LANES), f32),
        pltpu.SemaphoreType.DMA((54,)),
        pltpu.SemaphoreType.DMA((4,)),
    ]
    return pl.pallas_call(
        functools.partial(attn_forward_kernel, save),
        out_shape=outs,
        in_specs=[smem(), smem()] + [hbm()] * 22,
        out_specs=[vmem()] * len(outs),
        scratch_shapes=scratch,
        compiler_params=pltpu.CompilerParams(vmem_limit_bytes=VMEM_LIMIT),
        cost_estimate=pl.CostEstimate(
            flops=2 * rows * D * 3400, bytes_accessed=12_000_000, transcendentals=rows * 2048
        ),
        name="attn_forward",
    )(order, starts, *map(in_hbm, [table, pos, x, other] + w_all))


def attn_backward_kernel(
    with_grads,
    order,
    sum_ref,
    g_ref,
    x_ref,
    wide_ref,
    resid_ref,
    gate_ref,
    normed_ref,
    q_ref,
    k_ref,
    v_ref,
    probs_ref,
    mixed_ref,
    table_ref,
    *rest,
):
    blocks, rest = rest[:18], rest[18:]
    if with_grads:
        grad_ref, big_refs, rest = rest[0], rest[1:11], rest[11:]
        w_vmem, sems, back_ref, gains_ref = rest
    else:
        grad_ref, w_vmem, sems, back_ref = rest
    wait = load_weights(order, blocks, w_vmem, sems, (2, 1, 0))
    seqs, length = x_ref.shape[0], x_ref.shape[1]
    rows = seqs * length
    wait(2)
    gain_attn, gain_moe = gains_of(w_vmem)
    gate = gate_ref[...]
    tiles = length * TILES
    high_low = jnp.concatenate([unfold(sum_ref[s, tiles:]) for s in range(seqs)], axis=0)
    grad_gate = high_low + pltpu.roll(high_low, 96, 1)
    inner = jnp.sum(gate * grad_gate, axis=-1, keepdims=True)
    grad_logits = jnp.where(lanes_of(gate.shape) < 32, gate * (grad_gate - inner), 0.0)
    grad_logits = grad_logits.astype(bf16)
    w_small = w_vmem[:, :, QKV + D :].reshape(D, LANES)
    summed = jnp.concatenate([plain(sum_ref[s, :tiles]) for s in range(seqs)], axis=0)
    grad_normed_moe = summed + nt(grad_logits, w_small)
    resid = resid_ref[...]
    inv_moe = rms(resid)
    if with_grads:
        g = jnp.concatenate([plain(g_ref[s]) for s in range(seqs)], axis=0)
    else:
        g = g_ref[...].reshape(rows, D)
    grad_resid = g.astype(f32) + norm_back(resid, inv_moe, gain_moe, grad_normed_moe)
    grad_branch = grad_resid.astype(bf16)
    wait(1)
    w_out = w_vmem[:, :, QKV : QKV + D].reshape(D, D)
    grad_mixed = nt(grad_branch, w_out)
    cosine, sine = table_ref[:, :LANES], table_ref[:, LANES:]
    low = lanes_of((length, LANES)) < 64
    for s in range(seqs):
        top = slice(s * length, (s + 1) * length)
        key_parts, value_parts = [], []
        for j in range(KEY_VALUE_HEADS):
            here = slice(j * LANES, (j + 1) * LANES)
            pair = slice((j // 2) * LANES, (j // 2 + 1) * LANES)
            query = halves(q_ref[top, here].astype(f32)).astype(bf16)
            key = doubled(k_ref[top, pair].astype(f32), j % 2 == 1).astype(bf16)
            value = doubled(v_ref[top, pair].astype(f32), j % 2 == 1).astype(bf16)
            grad_heads = halves(grad_mixed[top, here]).astype(bf16)
            probs = probs_ref[s * KEY_VALUE_HEADS + j]
            grad_probs = nt(grad_heads, value)
            grad_value = tn(probs.astype(bf16), grad_heads)
            grad_scores = probs * (grad_probs - jnp.sum(probs * grad_probs, axis=-1, keepdims=True))
            grad_scores = grad_scores.astype(bf16)
            grad_query = join(nn(grad_scores, key)) * scale
            grad_key = tn(grad_scores, query) * scale
            back_ref[top, here] = turn(grad_query, cosine, sine, True).astype(bf16)
            key_parts.append(grad_key + pltpu.roll(grad_key, 64, 1))
            value_parts.append(grad_value + pltpu.roll(grad_value, 64, 1))
        for c in range(4):
            grad_key = jnp.where(low, key_parts[2 * c], key_parts[2 * c + 1])
            grad_value = jnp.where(low, value_parts[2 * c], value_parts[2 * c + 1])
            back_ref[top, D + c * LANES : D + (c + 1) * LANES] = turn(
                grad_key, cosine, sine, True
            ).astype(bf16)
            back_ref[top, D + 512 + c * LANES : D + 512 + (c + 1) * LANES] = grad_value.astype(bf16)
    wait(0)
    w_qkv = w_vmem[:, :, :QKV].reshape(D, QKV)
    grad_rows = back_ref[...]
    grad_normed = nt(grad_rows, w_qkv)
    x = x_ref[...].reshape(rows, D).astype(f32)
    inv_attn = rms(x)
    grad_in = grad_resid + norm_back(x, inv_attn, gain_attn, grad_normed)
    if with_grads:
        grad_ref[...] = grad_in.astype(bf16).reshape(seqs, length, D)
    else:
        for s in range(seqs):
            store_tiles(grad_ref, s, grad_in[s * length : (s + 1) * length])

        @pl.when(order[2, 0] == 0)
        def _():
            for s in range(seqs):
                store_tiles(grad_ref, s, g_ref[s])

    if with_grads:
        gains_ref[0:1] = jnp.sum(grad_normed * x * inv_attn, axis=0, keepdims=True)
        gains_ref[1:2] = jnp.sum(grad_normed_moe * resid * inv_moe, axis=0, keepdims=True)
        row = lax.broadcasted_iota(jnp.int32, (LANES, LANES), 0)
        lane = lanes_of((LANES, LANES))
        for k in range(8):
            columns = pl.ds(pl.multiple_of(order[0, k] * LANES, LANES), LANES)
            part_qkv = tn(normed_ref[:, columns], grad_rows)
            part_out = tn(mixed_ref[:, columns], grad_branch)
            places = [(r * TILES + order[0, k]) * TILE for r in range(length // TILE)]
            moe_rows = jnp.concatenate(
                [
                    wide_ref[s, pl.ds(pl.multiple_of(place, TILE), TILE)]
                    for s in range(seqs)
                    for place in places
                ],
                axis=0,
            )
            part_small = tn(moe_rows, grad_logits)
            for i in range(2):
                piece = gains_ref[i : i + 1, columns]
                turned = pltpu.roll(piece, 64, 1)
                part_small = part_small + jnp.where((row == i) & (lane >= 64), turned, 0.0)
                part_small = part_small + jnp.where((row == 64 + i) & (lane >= 64), piece, 0.0)
            n = min(k, 8 - k)
            place = slice(64, 128) if 0 < k < 4 else slice(0, 64)
            for part, columns in (
                (part_qkv, slice(0, QKV)),
                (part_out, slice(QKV, QKV + D)),
                (part_small, slice(QKV + D, WCOLS)),
            ):
                first_core = order[1, 0] == 0
                upper, lower = part[:64], part[64:]
                mine = jnp.where(first_core, upper, lower)
                big_refs[n][place, columns] = mine.astype(bf16)
                other = jnp.where(first_core, lower, upper)
                big_refs[5 + n][place, columns] = other.astype(bf16)


def attn_backward(with_grads, order, sums, g, saved, table, w_all):
    payload, resid, x, gate, normed, q, k, v, probs, mixed = saved
    seqs, length = x.shape[0], x.shape[1]
    rows = seqs * length
    shape = jax.ShapeDtypeStruct
    outs = [shape((seqs, length, D) if with_grads else (seqs, length * TILES, LANES), bf16)]
    scratch = [
        pltpu.VMEM((16, 64, WCOLS), bf16),
        pltpu.SemaphoreType.DMA((54,)),
        pltpu.VMEM((rows, QKV), bf16),
    ]
    if with_grads:
        outs += [shape((n, WCOLS), bf16) for n in (64, 128, 128, 128, 64)] * 2
        scratch.append(pltpu.VMEM((8, D), f32))
    return pl.pallas_call(
        functools.partial(attn_backward_kernel, with_grads),
        out_shape=outs,
        in_specs=[smem()] + [vmem()] * 13 + [hbm()] * 18,
        out_specs=[vmem()] * len(outs),
        scratch_shapes=scratch,
        compiler_params=pltpu.CompilerParams(vmem_limit_bytes=VMEM_LIMIT),
        cost_estimate=pl.CostEstimate(
            flops=4 * rows * D * 3400, bytes_accessed=20_000_000, transcendentals=0
        ),
        name="attn_backward",
    )(
        order, sums, g, x, payload, resid, gate, normed, q, k, v, probs, mixed, table, *map(in_hbm, w_all)
    )


def expert_kernel(mode, parts, which, *refs):
    refs = list(refs)
    take = lambda count: [refs.pop(0) for _ in range(count)]
    x_refs = take(parts)
    g_refs = take(parts) if mode else []
    w_in, w_down = take(2)
    out_refs = take(parts)
    saved_refs = take(5) if mode == 2 else []
    x_rows = take(1)[0]
    g_rows = take(1)[0] if mode else None
    if mode == 2:
        act_rows, gate_rows, up_rows, sems = take(4)
    hot_ref, scale_ref, result_ref = take(3)

    def send(n, j):
        source = (x_rows, g_rows, act_rows, gate_rows, up_rows)[n]
        return pltpu.make_async_copy(source.at[j], saved_refs[n].at[j], sems.at[n, j])

    per = x_rows.shape[0]
    hid = w_down.shape[0] // per
    first = which[0]
    spots = [(i, s) for i in range(parts) for s in range(x_refs[i].shape[0])]
    tiles = x_refs[0].shape[1] // 17 * 16
    length = tiles // TILES
    row8 = lax.broadcasted_iota(jnp.int32, (8, LANES), 0)
    lane8 = lanes_of((8, LANES))
    pick = jnp.where((lane8 == 32 + first + row8) & (row8 < per), 1.0, 0.0).astype(bf16)
    slot = lax.broadcasted_iota(jnp.int32, (SLOTS, length), 0).astype(f32)
    lane = lanes_of((SLOTS, LANES))
    for n, (i, s) in enumerate(spots):
        columns = unfold(x_refs[i][s, tiles:].astype(f32)).astype(bf16)
        places = nt(pick, columns)
        hot = jnp.concatenate(
            [jnp.where(places[j : j + 1] == slot, 1.0, 0.0) for j in range(per)], axis=0
        ).astype(bf16)
        hot_ref[n] = hot
        taken = nn(hot, jnp.concatenate([plain(x_refs[i][s, :tiles]), columns], axis=1))
        here = slice(n * SLOTS, (n + 1) * SLOTS)
        for j in range(per):
            block = taken[j * SLOTS : (j + 1) * SLOTS]
            x_rows[j, here] = block[:, :D].astype(bf16)
            gate = jnp.sum(jnp.where(lane == first + j, block[:, D:], 0.0), axis=-1, keepdims=True)
            scale_ref[j, here] = jnp.broadcast_to(gate, (SLOTS, LANES))
        if mode:
            taken = nn(hot, plain(g_refs[i][s, :tiles]))
            for j in range(per):
                g_rows[j, here] = taken[j * SLOTS : (j + 1) * SLOTS].astype(bf16)
    total = len(spots) * SLOTS
    lane = lanes_of((total, LANES))
    if mode == 2:
        for n in range(2):
            for j in range(per):
                send(n, j).start()
    for j in range(per):
        own_rows = slice(j * hid, (j + 1) * hid)
        rows = x_rows[j]
        gate_val = nt(rows, w_in[own_rows, :D])
        up_val = nt(rows, w_in[own_rows, D:])
        sig = jax.nn.sigmoid(gate_val)
        silu = gate_val * sig
        act = silu * up_val
        gate = scale_ref[j][:, 0:1]

        def forward():
            result_ref[j, :, :D] = (nn(act.astype(bf16), w_down[own_rows]) * gate).astype(bf16)

        def backward():
            inner = nt(g_rows[j], w_down[own_rows])
            grad_gw = jnp.sum(act.astype(bf16).astype(f32) * inner, axis=-1, keepdims=True)
            inner = inner * gate
            grad_gate = (inner * up_val * sig * (1.0 + gate_val * (1.0 - sig))).astype(bf16)
            grad_up = (inner * silu).astype(bf16)
            if mode == 2:
                act_rows[j] = (act * gate).astype(bf16)
                gate_rows[j] = grad_gate
                up_rows[j] = grad_up
                for n in range(2, 5):
                    send(n, j).start()
            grad_in = nn(grad_gate, w_in[own_rows, :D]) + nn(grad_up, w_in[own_rows, D:])
            high = grad_gw.astype(bf16).astype(f32)
            extra = jnp.where(
                lane == first + j, high, jnp.where(lane == 32 + first + j, grad_gw - high, 0.0)
            )
            result_ref[j, :, :D] = grad_in.astype(bf16)
            result_ref[j, :, D:] = extra.astype(bf16)

        if mode == 0:
            forward()
        else:
            backward()
            if mode == 2:

                @pl.when(which[1] != 0)
                def _():
                    forward()

    for n, (i, s) in enumerate(spots):
        here = slice(n * SLOTS, (n + 1) * SLOTS)
        block = jnp.concatenate([result_ref[j, here] for j in range(per)], axis=0)
        block = tn(hot_ref[n], block)
        store_tiles(out_refs[i], s, block[:, :D])
        if mode:
            out_refs[i][s, tiles:] = fold(block[:, D:]).astype(bf16)
    if mode == 2:
        for n in range(5):
            for j in range(per):
                send(n, j).wait()


def expert_call(mode, which, x_parts, g_parts, w_in, w_down, per):
    parts = len(x_parts)
    seqs = sum(x.shape[0] for x in x_parts)
    whole = x_parts[0].shape[1]
    length = whole // 17 * 16 // TILES
    hid = w_down.shape[0] // per
    total = seqs * SLOTS
    out_width = D + LANES if mode else D
    out_rows = whole if mode else length * TILES
    shape = jax.ShapeDtypeStruct
    outs = [shape((x.shape[0], out_rows, LANES), bf16) for x in x_parts]
    out_specs = [vmem()] * parts
    wide, narrow = (per, total, D), (per, total, hid)
    scratch = [pltpu.VMEM(wide, bf16)] * (2 if mode else 1)
    if mode == 2:
        saved = [wide, wide, narrow, narrow, narrow]
        outs += [pltpu.HBM(a, bf16) for a in saved]
        out_specs += [hbm()] * 5
        scratch += [pltpu.VMEM(narrow, bf16)] * 3 + [pltpu.SemaphoreType.DMA((5, per))]
    scratch += [
        pltpu.VMEM((seqs, per * SLOTS, length), bf16),
        pltpu.VMEM((per, total, LANES), f32),
        pltpu.VMEM((per, total, out_width), bf16),
    ]
    units = (3, 5, 5)[mode]
    g_args = list(g_parts) if mode else []

    def body(which, *refs):
        expert_kernel(mode, parts, which, *refs)

    return pl.pallas_call(
        body,
        out_shape=outs,
        in_specs=[smem()] + [vmem()] * (parts + len(g_args) + 2),
        out_specs=out_specs,
        scratch_shapes=scratch,
        compiler_params=pltpu.CompilerParams(vmem_limit_bytes=VMEM_LIMIT),
        cost_estimate=pl.CostEstimate(
            flops=2 * units * per * total * D * hid,
            bytes_accessed=6_000_000 + 4 * seqs * length * D,
            transcendentals=per * total * hid,
        ),
        name="experts_%d" % mode,
    )(which, *x_parts, *g_args, w_in, w_down)


def weight_grad_kernel(groups, tile, j, *refs):
    refs = list(refs)
    sets = [refs[5 * n : 5 * n + 5] for n in range(groups)]
    refs = refs[5 * groups + (2 if j else 0) :]
    in_ref, down_ref, rows = refs[0], refs[1], refs[2:7]
    in_tile, down_tile, load_sems, store_sems = refs[7:]
    hid = rows[2].shape[1]
    loads = []
    for n in (3, 0, 4, 2, 1):
        offset = 0
        for g in range(groups):
            count = sets[g][n].shape[1]
            loads.append(
                pltpu.make_async_copy(
                    sets[g][n].at[j],
                    rows[n].at[pl.ds(offset, count)],
                    load_sems.at[n * groups + g],
                )
            )
            offset += count
    for load in loads:
        load.start()
    tiles = hid // tile
    stores = []

    def store(source, target, sem):
        stores.append(pltpu.make_async_copy(source, target, sem))
        stores[-1].start()

    waited = 0
    for h in range(tiles):
        columns = slice(h * tile, (h + 1) * tile)
        where = pl.ds(j * hid + h * tile, tile)
        for n, upto, target in ((3, 2, 0), (4, 3, 1), (2, 5, 2)):
            for load in loads[waited : upto * groups]:
                load.wait()
            waited = max(waited, upto * groups)
            if target < 2:
                part = pl.ds(target * D, D)
                in_tile[h, :, part] = tn(rows[n][:, columns], rows[0][...])
                store(in_tile.at[h, :, part], in_ref.at[where, part], store_sems.at[h, target])
            else:
                down_tile[h] = tn(rows[n][:, columns], rows[1][...])
                store(down_tile.at[h], down_ref.at[where], store_sems.at[h, 2])
    for copy in stores:
        copy.wait()


def weight_grads(saved, hid, per, j, earlier=()):
    tile = min(hid, 256)
    groups = len(saved)
    args = [in_hbm(a) for group in saved for a in group]
    count = sum(group[0].shape[1] for group in saved)
    wide, narrow = pltpu.VMEM((count, D), bf16), pltpu.VMEM((count, hid), bf16)
    earlier = [in_hbm(a) for a in earlier]
    return pl.pallas_call(
        functools.partial(weight_grad_kernel, groups, tile, j),
        out_shape=[pltpu.HBM((per * hid, 2 * D), f32), pltpu.HBM((per * hid, D), f32)],
        in_specs=[hbm()] * (len(args) + len(earlier)),
        out_specs=[hbm()] * 2,
        scratch_shapes=[
            wide,
            wide,
            narrow,
            narrow,
            narrow,
            pltpu.VMEM((hid // tile, tile, 2 * D), f32),
            pltpu.VMEM((hid // tile, tile, D), f32),
            pltpu.SemaphoreType.DMA((5 * groups,)),
            pltpu.SemaphoreType.DMA((hid // tile, 3)),
        ],
        input_output_aliases={len(args) + n: n for n in range(len(earlier))},
        compiler_params=pltpu.CompilerParams(vmem_limit_bytes=VMEM_LIMIT),
        cost_estimate=pl.CostEstimate(
            flops=6 * count * D * hid, bytes_accessed=14_000_000, transcendentals=0
        ),
        name="weight_grads_%d" % j,
    )(*args, *earlier)


def last_sum_kernel(*refs):
    terms, (qkv_ref, out_ref, router_ref, attn_ref, moe_ref) = refs[:-5], refs[-5:]
    columns = lambda low, high: total([ref[:, low:high] for ref in terms])
    qkv_ref[...] = columns(0, QKV)
    out_ref[...] = columns(QKV, QKV + D)
    small = columns(QKV + D, WCOLS)
    router_ref[...] = small[:, :EXPERTS]
    attn_ref[...] = small[0:1, 64:]
    moe_ref[...] = small[1:2, 64:]


def last_sum(terms):
    rows = terms[0].shape[0]
    shape = lambda *dims: jax.ShapeDtypeStruct(dims, f32)
    return pl.pallas_call(
        last_sum_kernel,
        out_shape=[shape(rows, QKV), shape(rows, D), shape(rows, EXPERTS), shape(1, 64), shape(1, 64)],
        in_specs=[vmem()] * len(terms),
        out_specs=[vmem()] * 5,
        compiler_params=pltpu.CompilerParams(vmem_limit_bytes=VMEM_LIMIT),
        cost_estimate=pl.CostEstimate(
            flops=rows * WCOLS * 4, bytes_accessed=rows * WCOLS * 12, transcendentals=0
        ),
        name="last_sum",
    )(*terms)


class Ring:
    def __init__(self):
        self.ahead, self.behind, self.core = [], [], [(i, i ^ 1) for i in range(16)]
        for p, chip in enumerate(PATH):
            for b in range(2):
                here = chip * 2 + b
                self.ahead.append((here, PATH[(p + 1) % 8] * 2 + b))
                self.behind.append((here, PATH[(p - 1) % 8] * 2 + b))
        index = lax.axis_index("fsdp")
        place = jnp.asarray(PLACE, jnp.int32)[index // 2]
        chips = jnp.asarray(PATH, jnp.int32)[(place + jnp.arange(8)) % 8]
        self.chips = chips
        self.order = jnp.stack([chips, jnp.broadcast_to(index % 2, (8,))]).astype(jnp.int32)

    def plus(self, a):
        return lax.ppermute(a, "fsdp", self.ahead)

    def minus(self, a):
        return lax.ppermute(a, "fsdp", self.behind)

    def swap(self, a):
        return lax.ppermute(a, "fsdp", self.core)

    def gather(self, own, work):
        half = own.shape[0] // 2
        group, terms, more, done = [own], [], [], None
        for r in range(5):
            if r < 3:
                coming = [self.plus(group[0]), self.minus(group[-1])]
            elif r == 3:
                coming = [self.plus(group[0][:half]), self.minus(group[1][half:])]
            if r:
                terms.append(self.meet(done, len(old)))
                more.append(done[2 * len(old) :])
            old = group
            done = work(r, group + [self.swap(a) for a in group])
            if r < 4:
                coming, done, terms = lax.optimization_barrier((coming, done, terms))
                group = coming
        terms.append(self.meet(done, 2))
        more.append(done[4:])
        return terms, more

    def meet(self, payload, count):
        return [(payload[n], self.swap(payload[count + n])) for n in range(count)]

    def gather_whole(self, own, beside):
        half = own.shape[0] // 2
        behind, ahead = [own], [own]
        for r in range(3):
            new = self.plus(behind[-1]), self.minus(ahead[-1])
            if r == 1:
                new, beside = lax.optimization_barrier((new, beside))
            else:
                new = lax.optimization_barrier(new)
            behind.append(new[0])
            ahead.append(new[1])
        far = [self.plus(behind[3][:half]), self.minus(ahead[3][half:])]
        both = lambda a: [a, self.swap(a)]
        out = [both(a) for a in ahead]
        out += [far + [self.swap(a) for a in far]]
        out += [both(a) for a in behind[:0:-1]]
        return sum(out, []), beside

    def scatter(self, terms, work=()):
        work, beside = list(work), ()
        out = [total(values).astype(bf16) for values in terms[4]]
        half = out[0].shape[0]
        for k in (3, 2, 1, 0):
            up, down = lax.optimization_barrier((out[0], out[1]))
            up, down = self.minus(up), self.plus(down)
            if len(work) > 0 and k < 3:
                up, down, beside = lax.optimization_barrier((up, down, work.pop(0)(beside)))
            if k == 0:
                return list(terms[0][0]) + [up, down], beside
            behind, ahead = terms[k]
            if k == 3:
                upper = lambda values: [a[:half] for a in values]
                lower = lambda values: [a[half:] for a in values]
                out = [
                    jnp.concatenate([total(upper(behind) + [up]), total(lower(behind))]),
                    jnp.concatenate([total(upper(ahead)), total(lower(ahead) + [down])]),
                ]
            else:
                out = [total(list(behind) + [up]), total(list(ahead) + [down])]
            out = [a.astype(bf16) for a in out]


def total(values):
    return functools.reduce(jnp.add, [a.astype(f32) for a in values])


def on_device(
    tokens,
    cotangent,
    routes,
    picture_start,
    w_qkv,
    w_out,
    w_router,
    gain_attn,
    gain_moe,
    w_gate_up,
    w_down,
):
    section = lax.axis_index("section")
    first_section = section == 0
    index = lax.axis_index("fsdp")
    devices = lax.axis_size("fsdp")
    seqs, length = tokens.shape[0], tokens.shape[1]
    rows = seqs * length
    w_in, w_down = w_gate_up[0], w_down[0]
    per = max(1, EXPERTS // devices)
    hid = w_down.shape[0] // per
    first_expert = index * EXPERTS // devices
    which = jnp.stack([first_expert, section]).astype(jnp.int32)
    ringed = devices == 16

    angles = np.arange(length)[:, None] * 10000.0 ** (-2.0 * (np.arange(LANES) % 32) / HEAD_SIZE)
    table = jnp.asarray(np.concatenate([np.cos(angles), np.sin(angles)], axis=1), f32)
    starts = picture_start[:, 0]

    named = jnp.any(routes[0][..., None] == jnp.arange(LANES, dtype=jnp.int32), axis=2)
    earlier = jnp.asarray(np.tril(np.ones((length, length)), -1), bf16)
    place = jnp.einsum("ts,mse->mte", earlier, named.astype(bf16), preferred_element_type=f32)
    pos = jnp.where(named, place, 255.0).reshape(rows, LANES)

    if ringed:
        ring = Ring()
        order = jnp.concatenate([ring.order, jnp.broadcast_to(section, (1, 8)).astype(jnp.int32)])
        gains = jnp.concatenate([gain_attn, gain_moe])
        side = jnp.concatenate([gains, jnp.zeros((62, 64), bf16)])
        small = jnp.concatenate([w_out[0], w_router[0], jnp.zeros((64, 32), bf16), side], axis=1)
        whole = jnp.concatenate([w_qkv[0], small], axis=1)
        w_all, (pos, order, starts) = ring.gather_whole(whole, (pos, order, starts))
    else:
        order = jnp.stack([jnp.arange(8), jnp.zeros((8,)), jnp.broadcast_to(section, (8,))])
        order = order.astype(jnp.int32)
        gather = lambda a: lax.all_gather(a[0], "fsdp", axis=0, tiled=True)
        big = jnp.concatenate([gather(w_qkv), gather(w_out)], axis=1).reshape(16, 64, QKV + D)
        gains = jnp.stack([gather(gain_attn), gather(gain_moe)]).reshape(2, 16, 64)
        side = jnp.concatenate(
            [jnp.moveaxis(gains, 0, 1), jnp.zeros((16, 62, 64), bf16)], axis=1
        )
        router = gather(w_router).reshape(16, 64, EXPERTS)
        small = jnp.concatenate([router, jnp.zeros((16, 64, 32), bf16), side], axis=2)
        w_all = jnp.concatenate([big, small], axis=2)
        far = [w_all[i, h : h + 32] for i in (8, 9) for h in (0, 32)]
        w_all = [w_all[i] for i in range(8)] + far + [w_all[i] for i in range(10, 16)]

    def gather_rows(own):
        every = lax.all_gather(own, "fsdp", axis=0, tiled=True)
        return every.reshape((-1, 8) + own.shape[1:])

    def phase(mode, own, g, x_groups=None):
        if ringed:
            seen = []

            def work(r, group):
                seen.append(group)
                x, beside = (group, g and g[r]) if x_groups is None else (x_groups[r], group)
                return expert_call(mode, which, x, beside, w_in, w_down, per)

            terms, saved = ring.gather(own, work)
            last = [functools.partial(weight_grads, saved, hid, per, j) for j in range(per)]
            sums, grads = ring.scatter(terms, last if mode == 2 else ())
            return total(sums), seen, grads

        every = gather_rows(own)
        x_all, g_all = (every, g) if x_groups is None else (x_groups, every)

        def step(grads, both):
            out = expert_call(mode, which, [both[0]], [both[1]] if mode else None, w_in, w_down, per)
            if mode == 2:
                grads = jax.tree.map(jnp.add, grads, list(weight_grads([out[1:]], hid, per, 0)))
            return grads, out[0]

        zero = [jnp.zeros((per * hid, 2 * D), f32), jnp.zeros((per * hid, D), f32)]
        grads, payload = lax.scan(
            step, zero if mode == 2 else None, (x_all, g_all if mode else x_all)
        )
        flat = payload.reshape((devices * seqs,) + payload.shape[2:])
        sums = lax.psum_scatter(flat, "fsdp", scatter_dimension=0, tiled=True).astype(f32)
        return sums, x_all, grads

    payload, resid = attn_forward(False, order, starts, table, pos, tokens, cotangent, w_all)
    mixture, g_second, _ = phase(0, payload, None)
    first_out = (resid + mixture).astype(bf16)
    passed = lax.ppermute(first_out, "section", [(0, 1), (1, 0)])
    payload, resid, *saved = attn_forward(True, order, starts, table, pos, tokens, passed, w_all)
    saved = [payload, resid] + saved
    sums_second, rows_all, _ = phase(1, payload, g_second)
    (grad_second,) = attn_backward(False, order, sums_second, cotangent, saved, table, w_all)

    g_third = lax.ppermute(grad_second, "section", [(0, 1), (1, 0)])
    sums_third, _, (grad_in, grad_down) = phase(2, g_third, None, rows_all)
    tiles = length * TILES

    def rows_of(array):
        array = array.reshape(seqs, length // TILE, TILES, TILE, LANES)
        return jnp.swapaxes(array, 2, 3).reshape(seqs, length, D)

    second_out = (resid.reshape(seqs, length, D) + rows_of(sums_third[:, :tiles])).astype(bf16)
    section_out = jnp.where(first_section, rows_of(first_out), second_out)
    sums = jnp.where(first_section, sums_third, sums_second)
    section_grad, *big = attn_backward(True, order, sums, g_third, saved, table, w_all)

    if ringed:
        pairs = [(a, ring.swap(b)) for a, b in zip(big[:5], big[5:])]
        part = lambda pair, low, high: [a[low:high] for a in pair]
        terms = [[pairs[0]]]
        terms += [[part(pair, 0, 64), part(pair, 64, 128)] for pair in pairs[1:4]]
        terms += [[part(pairs[4], 0, 32), part(pairs[4], 32, 64)]]
        summed, _ = ring.scatter(terms)
        g_qkv, g_out, g_router, g_gain_attn, g_gain_moe = last_sum(summed)
        g_gain_attn, g_gain_moe = g_gain_attn[0], g_gain_moe[0]
    else:
        chips = [(big[0], big[5])] + [(big[k][64:], big[5 + k][64:]) for k in (1, 2, 3)]
        chips += [(big[4], big[9])] + [(big[k][:64], big[5 + k][:64]) for k in (3, 2, 1)]
        whole = jnp.concatenate([a for chip in chips for a in chip]).astype(f32)
        sum_up = lambda a: lax.psum_scatter(a, "fsdp", scatter_dimension=0, tiled=True)
        small = whole[:, QKV + D :]
        g_qkv, g_out = sum_up(whole[:, :QKV]), sum_up(whole[:, QKV : QKV + D])
        g_router = sum_up(small[:, :EXPERTS])
        gains = small.reshape(16, 64, LANES)
        g_gain_attn = sum_up(gains[:, 0, 64:].reshape(D))
        g_gain_moe = sum_up(gains[:, 1, 64:].reshape(D))
    return (
        section_out[None],
        section_grad[None],
        g_qkv[None],
        g_out[None],
        g_router[None],
        g_gain_attn[None],
        g_gain_moe[None],
        grad_in[None],
        grad_down[None],
    )


def solution(mesh):
    return jax.shard_map(
        on_device,
        mesh=mesh,
        in_specs=(
            P(None, "fsdp", None),
            P(None, "fsdp", None),
            P("section", None, "fsdp", None),
            P(None, "fsdp"),
            P("section", "fsdp", None),
            P("section", "fsdp", None),
            P("section", "fsdp", None),
            P("section", "fsdp"),
            P("section", "fsdp"),
            P("section", "fsdp", None),
            P("section", "fsdp", None),
        ),
        out_specs=(
            P("section", None, "fsdp", None),
            P("section", None, "fsdp", None),
            P("section", "fsdp", None),
            P("section", "fsdp", None),
            P("section", "fsdp", None),
            P("section", "fsdp"),
            P("section", "fsdp"),
            P("section", "fsdp", None),
            P("section", "fsdp", None),
        ),
        check_vma=False,
    )
```

time: 475 us -> 464 us (0.977)
  waiting for transfers between devices: 210 us -> 199 us
  local copies, waits for them, and re-layouts: 24.8 us -> 18.6 us
  Pallas kernels: 128 us -> 134 us
    ppermute x32, waiting for transfers between devices: 99 us -> 69.7 us  [minus(): return lax.ppermute(a, 'fsdp', self.behind)]
    ppermute x32, waiting for transfers between devices: 89 us -> 105 us  [plus(): return lax.ppermute(a, 'fsdp', self.ahead)]
    unnamed x96 -> x100, local copies, waits for them, and re-layouts: 16 us -> 9.28 us
    pallas_call x1 -> x3, Pallas kernels: 11.8 us -> 15.1 us  [the longest x2 13.9 us: weight_grads(): pl.pallas_call(functools.partial(weight_grad_kernel, groups, tile, j), ou...]
    ppermute x72 -> x68, waiting for transfers between devices: 9.17 us -> 11.3 us  [swap(): return lax.ppermute(a, 'fsdp', self.core)]
    ppermute x72 -> x68, starting transfers between devices: 15.1 us -> 13.5 us  [swap(): return lax.ppermute(a, 'fsdp', self.core)]
  transfers between devices with their start and end apart: 138 -> 134, of which waited for: 69 -> 78; matrix products, arithmetic and copies ran while one was open for 5% -> 4% of each run, Pallas kernels for 17% -> 18%
where the time goes in v3:
time: 464 us; the launch traced here: 454 us
  waiting for transfers between devices  199 us (43%)
  Pallas kernels  134 us (29%)
  starting transfers between devices  85.4 us (18%)
  local copies, waits for them, and re-layouts  18.6 us (4%)
  other arithmetic  13.7 us (3%)
    ppermute x32, waiting for transfers between devices, plus(): return lax.ppermute(a, 'fsdp', self.ahead)  105 us
    pallas_call x15, Pallas kernels, expert_call(): pl.pallas_call(body, out_shape=outs, in_specs=[smem()] + [vmem()] * (part...  80.1 us
    ppermute x32, waiting for transfers between devices, minus(): return lax.ppermute(a, 'fsdp', self.behind)  69.7 us
    ppermute x32, starting transfers between devices, minus(): return lax.ppermute(a, 'fsdp', self.behind)  34.6 us
    ppermute x32, starting transfers between devices, plus(): return lax.ppermute(a, 'fsdp', self.ahead)  33.9 us
    pallas_call x2, Pallas kernels, attn_backward(): pl.pallas_call(functools.partial(attn_backward_kernel, with_grads), out_s...  22.7 us
    pallas_call x2, Pallas kernels, attn_forward(): pl.pallas_call(functools.partial(attn_forward_kernel, save), out_shape=ou...  16.5 us
    pallas_call x2, Pallas kernels, weight_grads(): pl.pallas_call(functools.partial(weight_grad_kernel, groups, tile, j), ou...  13.9 us
  transfers between devices with their start and end apart: 134, of which 78 were waited for; matrix products, arithmetic and copies ran while one was open for 4% of the time, Pallas kernels for 18%

profile of v3, /device:TPU:0, one launch (start us, length us, event | category | flops | bytes accessed | tf_op | source)
XLA Modules:
  0.0 454.5 jit_solution(4345159619854095299)
XLA Ops:
  9.8 6.0 %collective-permute-done.refs_18_.rest_16_ = bf16[64,3200]{1,0:T(8,128)(2,1)S(1)} collective-permute-done((bf16[64,3200]{1,0:T(8,128)(2,1)S(1)}, bf16[64,3200]{1,0:T(8,128)(2,1)S(1)}, u32[]{:S(2)}, u32[]{:S(2)}) %collective-permute-start) | collective-permute-done | bytes 409632 | tf_op jit(solution)/shard_map/ppermute | solution.py:780
  22.2 5.3 %collective-permute-done.2.refs_16_.rest_14_ = bf16[64,3200]{1,0:T(8,128)(2,1)} collective-permute-done((bf16[64,3200]{1,0:T(8,128)(2,1)S(1)}, bf16[64,3200]{1,0:T(8,128)(2,1)}, u32[]{:S(2)}, u32[]{:S(2)}) %collective-permute-start.2) | collective-permute-done | bytes 409632 | tf_op jit(solution)/shard_map/ppermute | solution.py:780
  31.6 6.5 %collective-permute-done.7.refs_14_.rest_12_ = bf16[64,3200]{1,0:T(8,128)(2,1)S(1)} collective-permute-done((bf16[64,3200]{1,0:T(8,128)(2,1)}, bf16[64,3200]{1,0:T(8,128)(2,1)S(1)}, u32[]{:S(2)}, u32[]{:S(2)}) %collective-permute-start.7) | collective-permute-done | bytes 409632 | tf_op jit(solution)/shard_map/ppermute | solution.py:780
  51.9 8.1 %attn_forward.2 = (bf16[2,816,128]{2,1,0:T(8,128)(2,1)S(1)}, f32[2,768,128]{2,1,0:T(8,128)S(1)}) custom-call(s32[3,8]{1,0:T(4,128)S(1)} %add_add_fusion.order, s32[2]{0:T(128)S(1)} %bitcast.72, f32[96,256]{1,0:T(8,128)} %constant.78.clone.table_hbm.table_ref, f32[192,128]{1,0:T(8,128)} %bitcast.78, bf16[2,96,1024]{2,1,0:T(8,128)(2,1)} %refs_0_.3, ...), custom_call_target="tpu_custom_call" | custom-call | flops 1336934400 | bytes 12000000 | tf_op jit(solution)/shard_map/attn_forward/pallas_call | solution.py:323
  126.6 8.7 %collective-permute-done.45 = bf16[2,768,128]{2,1,0:T(8,128)(2,1)S(1)} collective-permute-done((bf16[2,768,128]{2,1,0:T(8,128)(2,1)S(1)}, bf16[2,768,128]{2,1,0:T(8,128)(2,1)S(1)}, u32[]{:S(2)}, u32[]{:S(2)}) %collective-permute-start.45) | collective-permute-done | bytes 393248 | tf_op jit(solution)/shard_map/ppermute | solution.py:783
  138.6 7.5 %collective-permute-done.47 = bf16[2,768,128]{2,1,0:T(8,128)(2,1)S(1)} collective-permute-done((bf16[2,768,128]{2,1,0:T(8,128)(2,1)S(1)}, bf16[2,768,128]{2,1,0:T(8,128)(2,1)S(1)}, u32[]{:S(2)}, u32[]{:S(2)}) %collective-permute-start.47) | collective-permute-done | bytes 393248 | tf_op jit(solution)/shard_map/ppermute | solution.py:783
  149.4 6.3 %collective-permute-done.50 = bf16[2,768,128]{2,1,0:T(8,128)(2,1)S(1)} collective-permute-done((bf16[2,768,128]{2,1,0:T(8,128)(2,1)S(1)}, bf16[2,768,128]{2,1,0:T(8,128)(2,1)S(1)}, u32[]{:S(2)}, u32[]{:S(2)}) %collective-permute-start.50) | collective-permute-done | bytes 393248 | tf_op jit(solution)/shard_map/ppermute | solution.py:780
  158.1 6.2 %collective-permute-done.51.refs_1_ = bf16[2,768,128]{2,1,0:T(8,128)(2,1)S(1)} collective-permute-done((bf16[2,768,128]{2,1,0:T(8,128)(2,1)S(1)}, bf16[2,768,128]{2,1,0:T(8,128)(2,1)S(1)}, u32[]{:S(2)}, u32[]{:S(2)}) %collective-permute-start.51) | collective-permute-done | bytes 393248 | tf_op jit(solution)/shard_map/ppermute | solution.py:953
  165.0 8.5 %attn_forward.3 = (bf16[2,816,128]{2,1,0:T(8,128)(2,1)S(1)}, f32[192,1024]{1,0:T(8,128)S(1)}, bf16[2,96,1024]{2,1,0:T(8,128)(2,1)S(1)}, f32[192,128]{1,0:T(8,128...) custom-call(s32[3,8]{1,0:T(4,128)S(1)} %add_add_fusion.order, ...), custom_call_target="tpu_custom_call" | custom-call | flops 1336934400 | bytes 12000000 | tf_op jit(solution)/shard_map/attn_forward/pallas_call | solution.py:323
  180.4 5.3 %collective-permute-done.52.refs_0_ = bf16[2,816,128]{2,1,0:T(8,128)(2,1)S(1)} collective-permute-done((bf16[2,816,128]{2,1,0:T(8,128)(2,1)S(1)}, bf16[2,816,128]{2,1,0:T(8,128)(2,1)S(1)}, u32[]{:S(2)}, u32[]{:S(2)}) %collective-permute-start.52) | collective-permute-done | bytes 417824 | tf_op jit(solution)/shard_map/ppermute | solution.py:780
  189.1 6.6 %experts_1.6 = (bf16[2,816,128]{2,1,0:T(8,128)(2,1)S(1)}, bf16[2,816,128]{2,1,0:T(8,128)(2,1)S(1)}, bf16[2,816,128]{2,1,0:T(8,128)(2,1)S(1)}, bf16[2,816,128]{2,1,0:T(8,128)(2,1)S(1)}) custom-call(s32[2]{0:T(128)S(1)} %pad_add_fusion.which, bf16[2,816,128]{2,1,0:T(8,128)(2,1)S(1)} %collective-permute-done.52.refs_0_, ...), custom_call_target="tpu_custom_call" | custom-call | flops 2684354560 | bytes 9145728 | tf_op jit(solution)/shard_map/experts_1/pallas_call | solution.py:642
  201.9 6.2 %experts_1.7 = (bf16[2,816,128]{2,1,0:T(8,128)(2,1)S(1)}, bf16[2,816,128]{2,1,0:T(8,128)(2,1)S(1)}, bf16[2,816,128]{2,1,0:T(8,128)(2,1)S(1)}, bf16[2,816,128]{2,1,0:T(8,128)(2,1)S(1)}) custom-call(s32[2]{0:T(128)S(1)} %pad_add_fusion.which, bf16[2,816,128]{2,1,0:T(8,128)(2,1)S(1)} %collective-permute-done.55.refs_0_, ...), custom_call_target="tpu_custom_call" | custom-call | flops 2684354560 | bytes 9145728 | tf_op jit(solution)/shard_map/experts_1/pallas_call | solution.py:642
  215.2 6.2 %experts_1.8 = (bf16[2,816,128]{2,1,0:T(8,128)(2,1)S(1)}, bf16[2,816,128]{2,1,0:T(8,128)(2,1)S(1)}, bf16[2,816,128]{2,1,0:T(8,128)(2,1)S(1)}, bf16[2,816,128]{2,1,0:T(8,128)(2,1)S(1)}) custom-call(s32[2]{0:T(128)S(1)} %pad_add_fusion.which, bf16[2,816,128]{2,1,0:T(8,128)(2,1)S(1)} %collective-permute-done.60.refs_0_, ...), custom_call_target="tpu_custom_call" | custom-call | flops 2684354560 | bytes 9145728 | tf_op jit(solution)/shard_map/experts_1/pallas_call | solution.py:642
  232.5 5.3 %collective-permute-done.77 = bf16[1,816,128]{2,1,0:T(8,128)(2,1)S(1)} collective-permute-done((bf16[1,816,128]{2,1,0:T(8,128)(2,1)S(1)}, bf16[1,816,128]{2,1,0:T(8,128)(2,1)S(1)}, u32[]{:S(2)}, u32[]{:S(2)}) %collective-permute-start.77) | collective-permute-done | bytes 208928 | tf_op jit(solution)/shard_map/ppermute | solution.py:783
  241.2 9.2 %collective-permute-done.80 = bf16[2,816,128]{2,1,0:T(8,128)(2,1)S(1)} collective-permute-done((bf16[2,816,128]{2,1,0:T(8,128)(2,1)S(1)}, bf16[2,816,128]{2,1,0:T(8,128)(2,1)S(1)}, u32[]{:S(2)}, u32[]{:S(2)}) %collective-permute-start.80) | collective-permute-done | bytes 417824 | tf_op jit(solution)/shard_map/ppermute | solution.py:783
  253.8 8.0 %collective-permute-done.82 = bf16[2,816,128]{2,1,0:T(8,128)(2,1)S(1)} collective-permute-done((bf16[2,816,128]{2,1,0:T(8,128)(2,1)S(1)}, bf16[2,816,128]{2,1,0:T(8,128)(2,1)S(1)}, u32[]{:S(2)}, u32[]{:S(2)}) %collective-permute-start.82) | collective-permute-done | bytes 417824 | tf_op jit(solution)/shard_map/ppermute | solution.py:783
  265.3 6.7 %collective-permute-done.85 = bf16[2,816,128]{2,1,0:T(8,128)(2,1)S(1)} collective-permute-done((bf16[2,816,128]{2,1,0:T(8,128)(2,1)S(1)}, bf16[2,816,128]{2,1,0:T(8,128)(2,1)S(1)}, u32[]{:S(2)}, u32[]{:S(2)}) %collective-permute-start.85) | collective-permute-done | bytes 417824 | tf_op jit(solution)/shard_map/ppermute | solution.py:780
  272.9 10.2 %attn_backward.2 = bf16[2,768,128]{2,1,0:T(8,128)(2,1)S(1)} custom-call(s32[3,8]{1,0:T(4,128)S(1)} %add_add_fusion.order, f32[2,816,128]{2,1,0:T(8,128)S(1)} %convert_add_fusion.1.sum_ref, bf16[2,96,1024]{2,1,0:T(8,128)(2,1)S(1)} %copy-done.8, bf16[2,96,1024]{2,1,0:T(8,128)(2,1)S(1)} %get-tuple-element.454.x_ref, ...), custom_call_target="tpu_custom_call" | custom-call | flops 2673868800 | bytes 20000000 | tf_op jit(solution)/shard_map/attn_backward/pallas_call | solution.py:487
  284.7 6.2 %collective-permute-done.86.refs_2_.g_ref = bf16[2,768,128]{2,1,0:T(8,128)(2,1)S(1)} collective-permute-done((bf16[2,768,128]{2,1,0:T(8,128)(2,1)S(1)}, bf16[2,768,128]{2,1,0:T(8,128)(2,1)S(1)}, u32[]{:S(2)}, u32[]{:S(2)}) %collective-permute-start.86) | collective-permute-done | bytes 393248 | tf_op jit(solution)/shard_map/ppermute | solution.py:959
  292.9 5.1 %experts_2.5 = (bf16[2,816,128]{2,1,0:T(8,128)(2,1)S(1)}, bf16[2,816,128]{2,1,0:T(8,128)(2,1)S(1)}, bf16[2,128,1024]{2,1,0:T(8,128)(2,1)}, bf16[2,128,1024]{2,1,...) custom-call(s32[2]{0:T(128)S(1)} %pad_add_fusion.which, ...), custom_call_target="tpu_custom_call" | custom-call | flops 1342177280 | bytes 7572864 | tf_op jit(solution)/shard_map/experts_2/pallas_call | solution.py:642
  306.0 6.7 %experts_2.6 = (bf16[2,816,128]{2,1,0:T(8,128)(2,1)S(1)}, bf16[2,816,128]{2,1,0:T(8,128)(2,1)S(1)}, bf16[2,816,128]{2,1,0:T(8,128)(2,1)S(1)}, bf16[2,816,128]{2,...) custom-call(s32[2]{0:T(128)S(1)} %pad_add_fusion.which, ...), custom_call_target="tpu_custom_call" | custom-call | flops 2684354560 | bytes 9145728 | tf_op jit(solution)/shard_map/experts_2/pallas_call | solution.py:642
  319.5 6.7 %experts_2.7 = (bf16[2,816,128]{2,1,0:T(8,128)(2,1)S(1)}, bf16[2,816,128]{2,1,0:T(8,128)(2,1)S(1)}, bf16[2,816,128]{2,1,0:T(8,128)(2,1)S(1)}, bf16[2,816,128]{2,...) custom-call(s32[2]{0:T(128)S(1)} %pad_add_fusion.which, ...), custom_call_target="tpu_custom_call" | custom-call | flops 2684354560 | bytes 9145728 | tf_op jit(solution)/shard_map/experts_2/pallas_call | solution.py:642
  332.8 6.7 %experts_2.8 = (bf16[2,816,128]{2,1,0:T(8,128)(2,1)S(1)}, bf16[2,816,128]{2,1,0:T(8,128)(2,1)S(1)}, bf16[2,816,128]{2,1,0:T(8,128)(2,1)S(1)}, bf16[2,816,128]{2,...) custom-call(s32[2]{0:T(128)S(1)} %pad_add_fusion.which, ...), custom_call_target="tpu_custom_call" | custom-call | flops 2684354560 | bytes 9145728 | tf_op jit(solution)/shard_map/experts_2/pallas_call | solution.py:642
  341.3 5.1 %experts_2.9 = (bf16[1,816,128]{2,1,0:T(8,128)(2,1)S(1)}, bf16[1,816,128]{2,1,0:T(8,128)(2,1)S(1)}, bf16[1,816,128]{2,1,0:T(8,128)(2,1)S(1)}, bf16[1,816,128]{2,...) custom-call(s32[2]{0:T(128)S(1)} %pad_add_fusion.which, ...), custom_call_target="tpu_custom_call" | custom-call | flops 1342177280 | bytes 7572864 | tf_op jit(solution)/shard_map/experts_2/pallas_call | solution.py:642
  351.0 5.3 %collective-permute-done.112 = bf16[1,816,128]{2,1,0:T(8,128)(2,1)S(1)} collective-permute-done((bf16[1,816,128]{2,1,0:T(8,128)(2,1)S(1)}, bf16[1,816,128]{2,1,0:T(8,128)(2,1)S(1)}, u32[]{:S(2)}, u32[]{:S(2)}) %collective-permute-start.112) | collective-permute-done | bytes 208928 | tf_op jit(solution)/shard_map/ppermute | solution.py:783
  359.9 7.0 %weight_grads_0.1 = (f32[1024,2048]{1,0:T(8,128)}, f32[1024,1024]{1,0:T(8,128)}) custom-call(bf16[2,128,1024]{2,1,0:T(8,128)(2,1)} %get-tuple-element.540.refs_0_, bf16[2,128,1024]{2,1,0:T(8,128)(2,1)} %get-tuple-element.541.refs_1_, bf16[2,128,512]{2,1,0:T(8,128)(2,1)} %get-tuple-element.542.refs_2_, bf16[2,128,512]{2,1,0:T(8,128)(2,1)} %get-tuple-element.543.refs_3_, ...), custom_call_target="tpu_custom_call" | custom-call | flops 3221225472 | bytes 14000000 | tf_op jit(solution)/shard_map/weight_grads_0/pallas_call | solution.py:713
  372.2 7.0 %weight_grads_1.1 = (f32[1024,2048]{1,0:T(8,128)}, f32[1024,1024]{1,0:T(8,128)}) custom-call(bf16[2,128,1024]{2,1,0:T(8,128)(2,1)} %get-tuple-element.540.refs_0_, bf16[2,128,1024]{2,1,0:T(8,128)(2,1)} %get-tuple-element.541.refs_1_, bf16[2,128,512]{2,1,0:T(8,128)(2,1)} %get-tuple-element.542.refs_2_, ...), custom_call_target="tpu_custom_call", output_to_operand_aliasing={{0}: (25, {}), {1}: (26, {})} | custom-call | flops 3221225472 | bytes 14000000 | tf_op jit(solution)/shard_map/weight_grads_1/pallas_call | solution.py:713
  385.4 6.9 %collective-permute-done.120 = bf16[2,816,128]{2,1,0:T(8,128)(2,1)} collective-permute-done((bf16[2,816,128]{2,1,0:T(8,128)(2,1)}, bf16[2,816,128]{2,1,0:T(8,128)(2,1)}, u32[]{:S(2)}, u32[]{:S(2)}) %collective-permute-start.120) | collective-permute-done | bytes 417824 | tf_op jit(solution)/shard_map/ppermute | solution.py:780
  397.4 12.6 %attn_backward.3 = (bf16[2,96,1024]{2,1,0:T(8,128)(2,1)}, bf16[64,3200]{1,0:T(8,128)(2,1)S(1)}, bf16[128,3200]{1,0:T(8,128)(2,1)S(1)}, bf16[128,3200]{1,0:T(8,12...) custom-call(s32[3,8]{1,0:T(4,128)S(1)} %add_add_fusion.order, ...), custom_call_target="tpu_custom_call" | custom-call | flops 2673868800 | bytes 20000000 | tf_op jit(solution)/shard_map/attn_backward/pallas_call | solution.py:487
  414.0 5.1 %collective-permute-done.127 = bf16[32,3200]{1,0:T(8,128)(2,1)S(1)} collective-permute-done((bf16[32,3200]{1,0:T(8,128)(2,1)S(1)}, bf16[32,3200]{1,0:T(8,128)(2,1)S(1)}, u32[]{:S(2)}, u32[]{:S(2)}) %collective-permute-start.127) | collective-permute-done | bytes 204832 | tf_op jit(solution)/shard_map/ppermute | solution.py:780
  422.3 8.3 %collective-permute-done.129 = bf16[64,3200]{1,0:T(8,128)(2,1)S(1)} collective-permute-done((bf16[64,3200]{1,0:T(8,128)(2,1)S(1)}, bf16[64,3200]{1,0:T(8,128)(2,1)S(1)}, u32[]{:S(2)}, u32[]{:S(2)}) %collective-permute-start.129) | collective-permute-done | bytes 409632 | tf_op jit(solution)/shard_map/ppermute | solution.py:780
  433.9 7.1 %collective-permute-done.131 = bf16[64,3200]{1,0:T(8,128)(2,1)S(1)} collective-permute-done((bf16[64,3200]{1,0:T(8,128)(2,1)S(1)}, bf16[64,3200]{1,0:T(8,128)(2,1)S(1)}, u32[]{:S(2)}, u32[]{:S(2)}) %collective-permute-start.131) | collective-permute-done | bytes 409632 | tf_op jit(solution)/shard_map/ppermute | solution.py:780
  (426 shorter events, 229.8 us)
Async XLA Ops:
  3.4 12.5 %collective-permute-start = (bf16[64,3200]{1,0:T(8,128)(2,1)S(1)}, bf16[64,3200]{1,0:T(8,128)(2,1)S(1)}, u32[]{:S(2)}, u32[]{:S(2)}) collective-permute-start(bf16[64,3200]{1,0:T(8,128)(2,1)S(1)} %concatenate.42.refs_2_.rest_0_), channel_id=1, source_target_pairs={{0,4},{1,5},{4,8},{5,9},{8,12},{9,13},{12,14},{13,15},{14,10},{15,... | collective-permute-start | bytes 1228808 | tf_op jit(solution)/shard_map/ppermute | solution.py:780
  6.4 11.0 %collective-permute-start.1 = (bf16[64,3200]{1,0:T(8,128)(2,1)S(1)}, bf16[64,3200]{1,0:T(8,128)(2,1)}, u32[]{:S(2)}, u32[]{:S(2)}) collective-permute-start(bf16[64,3200]{1,0:T(8,128)(2,1)S(1)} %concatenate.42.refs_2_.rest_0_), channel_id=1, source_target_pairs={{0,2},{1,3},{4,0},{5,1},{8,4},{9,5},{12,8},{13,9},{14,12},{15,13},... | collective-permute-start | bytes 1228808 | tf_op jit(solution)/shard_map/ppermute | solution.py:783
  61.0 11.9 %collective-permute-start.17 = (bf16[2,816,128]{2,1,0:T(8,128)(2,1)S(1)}, bf16[2,816,128]{2,1,0:T(8,128)(2,1)S(1)}, u32[]{:S(2)}, u32[]{:S(2)}) collective-permute-start(bf16[2,816,128]{2,1,0:T(8,128)(2,1)S(1)} %get-tuple-element.319.refs_0_.refs_2_), channel_id=1, source_target_pairs={{0,4},{1,5},{4,8},{5,9},{8,12},{9,13},{12,14},{13,15},{14,10},{15,... | collective-permute-start | bytes 1253384 | tf_op jit(solution)/shard_map/ppermute | solution.py:780
  61.8 11.7 %collective-permute-start.18 = (bf16[2,816,128]{2,1,0:T(8,128)(2,1)S(1)}, bf16[2,816,128]{2,1,0:T(8,128)(2,1)}, u32[]{:S(2)}, u32[]{:S(2)}) collective-permute-start(bf16[2,816,128]{2,1,0:T(8,128)(2,1)S(1)} %get-tuple-element.319.refs_0_.refs_2_), channel_id=1, source_target_pairs={{0,2},{1,3},{4,0},{5,1},{8,4},{9,5},{12,8},{13,9},{14,12},{15,13},... | collective-permute-start | bytes 1253384 | tf_op jit(solution)/shard_map/ppermute | solution.py:783
  74.0 11.6 %collective-permute-start.20 = (bf16[2,816,128]{2,1,0:T(8,128)(2,1)S(1)}, bf16[2,816,128]{2,1,0:T(8,128)(2,1)S(1)}, u32[]{:S(2)}, u32[]{:S(2)}) collective-permute-start(bf16[2,816,128]{2,1,0:T(8,128)(2,1)S(1)} %collective-permute-done.17.refs_0_.refs_4_), channel_id=1, source_target_pairs={{0,4},{1,5},{4,8},{5,9},{8,12},{9,13},{12,14},{13,15},{14,10},{15,... | collective-permute-start | bytes 1253384 | tf_op jit(solution)/shard_map/ppermute | solution.py:780
  74.7 11.5 %collective-permute-start.21 = (bf16[2,816,128]{2,1,0:T(8,128)(2,1)}, bf16[2,816,128]{2,1,0:T(8,128)(2,1)S(1)}, u32[]{:S(2)}, u32[]{:S(2)}) collective-permute-start(bf16[2,816,128]{2,1,0:T(8,128)(2,1)} %collective-permute-done.18.refs_1_.refs_5_), channel_id=1, source_target_pairs={{0,2},{1,3},{4,0},{5,1},{8,4},{9,5},{12,8},{13,9},{14,12},{15,13},... | collective-permute-start | bytes 1253384 | tf_op jit(solution)/shard_map/ppermute | solution.py:783
  86.7 11.6 %collective-permute-start.25 = (bf16[2,816,128]{2,1,0:T(8,128)(2,1)S(1)}, bf16[2,816,128]{2,1,0:T(8,128)(2,1)S(1)}, u32[]{:S(2)}, u32[]{:S(2)}) collective-permute-start(bf16[2,816,128]{2,1,0:T(8,128)(2,1)S(1)} %collective-permute-done.20.refs_0_.refs_4_), channel_id=1, source_target_pairs={{0,4},{1,5},{4,8},{5,9},{8,12},{9,13},{12,14},{13,15},{14,10},{15,... | collective-permute-start | bytes 1253384 | tf_op jit(solution)/shard_map/ppermute | solution.py:780
  87.3 11.4 %collective-permute-start.26 = (bf16[2,816,128]{2,1,0:T(8,128)(2,1)S(1)}, bf16[2,816,128]{2,1,0:T(8,128)(2,1)S(1)}, u32[]{:S(2)}, u32[]{:S(2)}) collective-permute-start(bf16[2,816,128]{2,1,0:T(8,128)(2,1)S(1)} %collective-permute-done.21.refs_1_.refs_5_), channel_id=1, source_target_pairs={{0,2},{1,3},{4,0},{5,1},{8,4},{9,5},{12,8},{13,9},{14,12},{15,13},... | collective-permute-start | bytes 1253384 | tf_op jit(solution)/shard_map/ppermute | solution.py:783
  124.5 10.8 %collective-permute-start.45 = (bf16[2,768,128]{2,1,0:T(8,128)(2,1)S(1)}, bf16[2,768,128]{2,1,0:T(8,128)(2,1)S(1)}, u32[]{:S(2)}, u32[]{:S(2)}) collective-permute-start(bf16[2,768,128]{2,1,0:T(8,128)(2,1)S(1)} %get-tuple-element.376), channel_id=1, source_target_pairs={{0,2},{1,3},{4,0},{5,1},{8,4},{9,5},{12,8},{13,9},{14,12},{15,13},... | collective-permute-start | bytes 1179656 | tf_op jit(solution)/shard_map/ppermute | solution.py:783
  173.7 12.0 %collective-permute-start.52 = (bf16[2,816,128]{2,1,0:T(8,128)(2,1)S(1)}, bf16[2,816,128]{2,1,0:T(8,128)(2,1)S(1)}, u32[]{:S(2)}, u32[]{:S(2)}) collective-permute-start(bf16[2,816,128]{2,1,0:T(8,128)(2,1)S(1)} %get-tuple-element.387.refs_0_.wide_ref), channel_id=1, source_target_pairs={{0,4},{1,5},{4,8},{5,9},{8,12},{9,13},{12,14},{13,15},{14,10},{15,... | collective-permute-start | bytes 1253384 | tf_op jit(solution)/shard_map/ppermute | solution.py:780
  174.4 11.7 %collective-permute-start.53 = (bf16[2,816,128]{2,1,0:T(8,128)(2,1)S(1)}, bf16[2,816,128]{2,1,0:T(8,128)(2,1)S(1)}, u32[]{:S(2)}, u32[]{:S(2)}) collective-permute-start(bf16[2,816,128]{2,1,0:T(8,128)(2,1)S(1)} %get-tuple-element.387.refs_0_.wide_ref), channel_id=1, source_target_pairs={{0,2},{1,3},{4,0},{5,1},{8,4},{9,5},{12,8},{13,9},{14,12},{15,13},... | collective-permute-start | bytes 1253384 | tf_op jit(solution)/shard_map/ppermute | solution.py:783
  186.7 11.6 %collective-permute-start.55 = (bf16[2,816,128]{2,1,0:T(8,128)(2,1)S(1)}, bf16[2,816,128]{2,1,0:T(8,128)(2,1)S(1)}, u32[]{:S(2)}, u32[]{:S(2)}) collective-permute-start(bf16[2,816,128]{2,1,0:T(8,128)(2,1)S(1)} %collective-permute-done.52.refs_0_), channel_id=1, source_target_pairs={{0,4},{1,5},{4,8},{5,9},{8,12},{9,13},{12,14},{13,15},{14,10},{15,... | collective-permute-start | bytes 1253384 | tf_op jit(solution)/shard_map/ppermute | solution.py:780
  187.2 11.7 %collective-permute-start.56 = (bf16[2,816,128]{2,1,0:T(8,128)(2,1)S(1)}, bf16[2,816,128]{2,1,0:T(8,128)(2,1)S(1)}, u32[]{:S(2)}, u32[]{:S(2)}) collective-permute-start(bf16[2,816,128]{2,1,0:T(8,128)(2,1)S(1)} %collective-permute-done.53.refs_1_), channel_id=1, source_target_pairs={{0,2},{1,3},{4,0},{5,1},{8,4},{9,5},{12,8},{13,9},{14,12},{15,13},... | collective-permute-start | bytes 1253384 | tf_op jit(solution)/shard_map/ppermute | solution.py:783
  199.4 11.6 %collective-permute-start.60 = (bf16[2,816,128]{2,1,0:T(8,128)(2,1)S(1)}, bf16[2,816,128]{2,1,0:T(8,128)(2,1)S(1)}, u32[]{:S(2)}, u32[]{:S(2)}) collective-permute-start(bf16[2,816,128]{2,1,0:T(8,128)(2,1)S(1)} %collective-permute-done.55.refs_0_), channel_id=1, source_target_pairs={{0,4},{1,5},{4,8},{5,9},{8,12},{9,13},{12,14},{13,15},{14,10},{15,... | collective-permute-start | bytes 1253384 | tf_op jit(solution)/shard_map/ppermute | solution.py:780
  200.7 11.3 %collective-permute-start.61 = (bf16[2,816,128]{2,1,0:T(8,128)(2,1)S(1)}, bf16[2,816,128]{2,1,0:T(8,128)(2,1)S(1)}, u32[]{:S(2)}, u32[]{:S(2)}) collective-permute-start(bf16[2,816,128]{2,1,0:T(8,128)(2,1)S(1)} %collective-permute-done.56.refs_1_), channel_id=1, source_target_pairs={{0,2},{1,3},{4,0},{5,1},{8,4},{9,5},{12,8},{13,9},{14,12},{15,13},... | collective-permute-start | bytes 1253384 | tf_op jit(solution)/shard_map/ppermute | solution.py:783
  201.4 10.5 %collective-permute-start.64 = (bf16[2,816,128]{2,1,0:T(8,128)(2,1)S(1)}, bf16[2,816,128]{2,1,0:T(8,128)(2,1)S(1)}, u32[]{:S(2)}, u32[]{:S(2)}) collective-permute-start(bf16[2,816,128]{2,1,0:T(8,128)(2,1)S(1)} %get-tuple-element.407), channel_id=1, source_target_pairs={{0,1},{1,0},{2,3},{3,2},{4,5},{5,4},{6,7},{7,6},{8,9},{9,8},{10,11... | collective-permute-start | bytes 1253384 | tf_op jit(solution)/shard_map/ppermute | solution.py:786
  201.4 10.5 %collective-permute-start.65 = (bf16[2,816,128]{2,1,0:T(8,128)(2,1)S(1)}, bf16[2,816,128]{2,1,0:T(8,128)(2,1)S(1)}, u32[]{:S(2)}, u32[]{:S(2)}) collective-permute-start(bf16[2,816,128]{2,1,0:T(8,128)(2,1)S(1)} %get-tuple-element.409), channel_id=1, source_target_pairs={{0,1},{1,0},{2,3},{3,2},{4,5},{5,4},{6,7},{7,6},{8,9},{9,8},{10,11... | collective-permute-start | bytes 1253384 | tf_op jit(solution)/shard_map/ppermute | solution.py:786
  239.1 11.3 %collective-permute-start.80 = (bf16[2,816,128]{2,1,0:T(8,128)(2,1)S(1)}, bf16[2,816,128]{2,1,0:T(8,128)(2,1)S(1)}, u32[]{:S(2)}, u32[]{:S(2)}) collective-permute-start(bf16[2,816,128]{2,1,0:T(8,128)(2,1)S(1)} %pad_maximum_fusion), channel_id=1, source_target_pairs={{0,2},{1,3},{4,0},{5,1},{8,4},{9,5},{12,8},{13,9},{14,12},{15,13},... | collective-permute-start | bytes 1253384 | tf_op jit(solution)/shard_map/ppermute | solution.py:783
  240.5 11.0 %collective-permute-start.81 = (bf16[2,816,128]{2,1,0:T(8,128)(2,1)S(1)}, bf16[2,816,128]{2,1,0:T(8,128)(2,1)S(1)}, u32[]{:S(2)}, u32[]{:S(2)}) collective-permute-start(bf16[2,816,128]{2,1,0:T(8,128)(2,1)S(1)} %pad_maximum_fusion.1), channel_id=1, source_target_pairs={{0,4},{1,5},{4,8},{5,9},{8,12},{9,13},{12,14},{13,15},{14,10},{15,... | collective-permute-start | bytes 1253384 | tf_op jit(solution)/shard_map/ppermute | solution.py:780
  290.9 11.5 %collective-permute-start.87 = (bf16[2,768,128]{2,1,0:T(8,128)(2,1)S(1)}, bf16[2,768,128]{2,1,0:T(8,128)(2,1)S(1)}, u32[]{:S(2)}, u32[]{:S(2)}) collective-permute-start(bf16[2,768,128]{2,1,0:T(8,128)(2,1)S(1)} %collective-permute-done.86.refs_2_.g_ref), channel_id=1, source_target_pairs={{0,4},{1,5},{4,8},{5,9},{8,12},{9,13},{12,14},{13,15},{14,10},{15,... | collective-permute-start | bytes 1179656 | tf_op jit(solution)/shard_map/ppermute | solution.py:780
  291.8 11.2 %collective-permute-start.88 = (bf16[2,768,128]{2,1,0:T(8,128)(2,1)S(1)}, bf16[2,768,128]{2,1,0:T(8,128)(2,1)S(1)}, u32[]{:S(2)}, u32[]{:S(2)}) collective-permute-start(bf16[2,768,128]{2,1,0:T(8,128)(2,1)S(1)} %collective-permute-done.86.refs_2_.g_ref), channel_id=1, source_target_pairs={{0,2},{1,3},{4,0},{5,1},{8,4},{9,5},{12,8},{13,9},{14,12},{15,13},... | collective-permute-start | bytes 1179656 | tf_op jit(solution)/shard_map/ppermute | solution.py:783
  303.6 12.9 %collective-permute-start.94 = (bf16[2,816,128]{2,1,0:T(8,128)(2,1)S(1)}, bf16[2,816,128]{2,1,0:T(8,128)(2,1)S(1)}, u32[]{:S(2)}, u32[]{:S(2)}) collective-permute-start(bf16[2,816,128]{2,1,0:T(8,128)(2,1)S(1)} %get-tuple-element.481), channel_id=1, source_target_pairs={{0,1},{1,0},{2,3},{3,2},{4,5},{5,4},{6,7},{7,6},{8,9},{9,8},{10,11... | collective-permute-start | bytes 1253384 | tf_op jit(solution)/shard_map/ppermute | solution.py:786
  303.6 11.5 %collective-permute-start.90 = (bf16[2,768,128]{2,1,0:T(8,128)(2,1)S(1)}, bf16[2,768,128]{2,1,0:T(8,128)(2,1)S(1)}, u32[]{:S(2)}, u32[]{:S(2)}) collective-permute-start(bf16[2,768,128]{2,1,0:T(8,128)(2,1)S(1)} %collective-permute-done.87.refs_4_), channel_id=1, source_target_pairs={{0,4},{1,5},{4,8},{5,9},{8,12},{9,13},{12,14},{13,15},{14,10},{15,... | collective-permute-start | bytes 1179656 | tf_op jit(solution)/shard_map/ppermute | solution.py:780
  304.8 11.6 %collective-permute-start.91 = (bf16[2,768,128]{2,1,0:T(8,128)(2,1)S(1)}, bf16[2,768,128]{2,1,0:T(8,128)(2,1)S(1)}, u32[]{:S(2)}, u32[]{:S(2)}) collective-permute-start(bf16[2,768,128]{2,1,0:T(8,128)(2,1)S(1)} %collective-permute-done.88.refs_5_), channel_id=1, source_target_pairs={{0,2},{1,3},{4,0},{5,1},{8,4},{9,5},{12,8},{13,9},{14,12},{15,13},... | collective-permute-start | bytes 1179656 | tf_op jit(solution)/shard_map/ppermute | solution.py:783
  317.0 12.5 %collective-permute-start.99 = (bf16[2,816,128]{2,1,0:T(8,128)(2,1)S(1)}, bf16[2,816,128]{2,1,0:T(8,128)(2,1)S(1)}, u32[]{:S(2)}, u32[]{:S(2)}) collective-permute-start(bf16[2,816,128]{2,1,0:T(8,128)(2,1)S(1)} %get-tuple-element.496), channel_id=1, source_target_pairs={{0,1},{1,0},{2,3},{3,2},{4,5},{5,4},{6,7},{7,6},{8,9},{9,8},{10,11... | collective-permute-start | bytes 1253384 | tf_op jit(solution)/shard_map/ppermute | solution.py:786
  317.1 12.4 %collective-permute-start.100 = (bf16[2,816,128]{2,1,0:T(8,128)(2,1)S(1)}, bf16[2,816,128]{2,1,0:T(8,128)(2,1)S(1)}, u32[]{:S(2)}, u32[]{:S(2)}) collective-permute-start(bf16[2,816,128]{2,1,0:T(8,128)(2,1)S(1)} %get-tuple-element.498), channel_id=1, source_target_pairs={{0,1},{1,0},{2,3},{3,2},{4,5},{5,4},{6,7},{7,6},{8,9},{9,8},{10,11... | collective-permute-start | bytes 1253384 | tf_op jit(solution)/shard_map/ppermute | solution.py:786
  317.5 11.1 %collective-permute-start.95 = (bf16[2,768,128]{2,1,0:T(8,128)(2,1)S(1)}, bf16[2,768,128]{2,1,0:T(8,128)(2,1)S(1)}, u32[]{:S(2)}, u32[]{:S(2)}) collective-permute-start(bf16[2,768,128]{2,1,0:T(8,128)(2,1)S(1)} %collective-permute-done.90.refs_4_), channel_id=1, source_target_pairs={{0,4},{1,5},{4,8},{5,9},{8,12},{9,13},{12,14},{13,15},{14,10},{15,... | collective-permute-start | bytes 1179656 | tf_op jit(solution)/shard_map/ppermute | solution.py:780
  318.7 10.8 %collective-permute-start.96 = (bf16[2,768,128]{2,1,0:T(8,128)(2,1)S(1)}, bf16[2,768,128]{2,1,0:T(8,128)(2,1)S(1)}, u32[]{:S(2)}, u32[]{:S(2)}) collective-permute-start(bf16[2,768,128]{2,1,0:T(8,128)(2,1)S(1)} %collective-permute-done.91.refs_5_), channel_id=1, source_target_pairs={{0,2},{1,3},{4,0},{5,1},{8,4},{9,5},{12,8},{13,9},{14,12},{15,13},... | collective-permute-start | bytes 1179656 | tf_op jit(solution)/shard_map/ppermute | solution.py:783
  357.6 11.3 %collective-permute-start.115 = (bf16[2,816,128]{2,1,0:T(8,128)(2,1)S(1)}, bf16[2,816,128]{2,1,0:T(8,128)(2,1)S(1)}, u32[]{:S(2)}, u32[]{:S(2)}) collective-permute-start(bf16[2,816,128]{2,1,0:T(8,128)(2,1)S(1)} %pad_maximum_fusion.2), channel_id=1, source_target_pairs={{0,2},{1,3},{4,0},{5,1},{8,4},{9,5},{12,8},{13,9},{14,12},{15,13},... | collective-permute-start | bytes 1253384 | tf_op jit(solution)/shard_map/ppermute | solution.py:783
  358.6 11.2 %collective-permute-start.116 = (bf16[2,816,128]{2,1,0:T(8,128)(2,1)S(1)}, bf16[2,816,128]{2,1,0:T(8,128)(2,1)S(1)}, u32[]{:S(2)}, u32[]{:S(2)}) collective-permute-start(bf16[2,816,128]{2,1,0:T(8,128)(2,1)S(1)} %pad_maximum_fusion.3), channel_id=1, source_target_pairs={{0,4},{1,5},{4,8},{5,9},{8,12},{9,13},{12,14},{13,15},{14,10},{15,... | collective-permute-start | bytes 1253384 | tf_op jit(solution)/shard_map/ppermute | solution.py:780
  422.3 11.6 %collective-permute-start.122 = (bf16[128,3200]{1,0:T(8,128)(2,1)S(1)}, bf16[128,3200]{1,0:T(8,128)(2,1)S(1)}, u32[]{:S(2)}, u32[]{:S(2)}) collective-permute-start(bf16[128,3200]{1,0:T(8,128)(2,1)S(1)} %get-tuple-element.587), channel_id=1, source_target_pairs={{0,1},{1,0},{2,3},{3,2},{4,5},{5,4},{6,7},{7,6},{8,9},{9,8},{10,11... | collective-permute-start | bytes 2457608 | tf_op jit(solution)/shard_map/ppermute | solution.py:786
  433.9 17.8 %collective-permute-start.121 = (bf16[64,3200]{1,0:T(8,128)(2,1)}, bf16[64,3200]{1,0:T(8,128)(2,1)S(1)}, u32[]{:S(2)}, u32[]{:S(2)}) collective-permute-start(bf16[64,3200]{1,0:T(8,128)(2,1)} %get-tuple-element.585), channel_id=1, source_target_pairs={{0,1},{1,0},{2,3},{3,2},{4,5},{5,4},{6,7},{7,6},{8,9},{9,8},{10,11... | collective-permute-start | bytes 1228808 | tf_op jit(solution)/shard_map/ppermute | solution.py:786
  (151 other events, 1966.8 us)

commit v4 on v3

--- a/solution.py
+++ b/solution.py
@@ -25,7 +25,7 @@
 scale = HEAD_SIZE ** (-0.5)
 f32 = jnp.float32
 bf16 = jnp.bfloat16
-VMEM_LIMIT = 30 * 1024 * 1024
+VMEM_LIMIT = 20 * 1024 * 1024
 
 PATH = (0, 2, 4, 6, 7, 5, 3, 1)
 PLACE = tuple(PATH.index(c) for c in range(8))
@@ -158,8 +158,12 @@
     return jnp.concatenate(pieces[0], axis=1), jnp.concatenate(pieces[1], axis=1)
 
 
-def attn_forward_kernel(save, order, starts, table_hbm, pos_hbm, *refs):
-    x_hbms, blocks, refs = refs[:2], refs[2:20], refs[20:]
+def attn_forward_kernel(save, order, table_hbm, pos_hbm, *refs):
+    x_hbms, refs = refs[:2], refs[2:]
+    if save:
+        w_vmem, refs = refs[0], refs[1:]
+    else:
+        blocks, w_hbm, refs = refs[:18], refs[20], refs[18:20] + refs[21:]
     out_ref, resid_ref, refs = refs[0], refs[1], refs[2:]
     if save:
         x_ref, gate_ref, normed_ref, q_ref, k_ref, v_ref, probs_ref, mixed_ref = refs[:8]
@@ -167,7 +171,10 @@
     else:
         x_ref, cot_ref, mixed_ref = refs[:3]
         refs = refs[3:]
-    w_vmem, table_ref, pos_ref, sems, side_sems = refs
+    if save:
+        table_ref, pos_ref, side_sems = refs
+    else:
+        table_ref, pos_ref, side_sems, sems, w_vmem, resid_vmem = refs
     second = order[2, 0] != 0
     if save:
         loads = [
@@ -186,7 +193,17 @@
         loads[1].start()
     load_table = pltpu.make_async_copy(table_hbm, table_ref, side_sems.at[1])
     load_table.start()
-    wait = load_weights(order, blocks, w_vmem, sems, (2, 0, 1))
+    wait = keep = lambda part: None
+    if not save:
+        kept = []
+
+        def keep(part):
+            columns = pl.ds(PARTS[part][0], PARTS[part][1] - PARTS[part][0])
+            source, target = w_vmem.at[:, :, columns], w_hbm.at[:, :, columns]
+            kept.append(pltpu.make_async_copy(source, target, side_sems.at[4 + part]))
+            kept[-1].start()
+
+        wait = load_weights(order, blocks, w_vmem, sems, (2, 0, 1))
     load_pos = pltpu.make_async_copy(pos_hbm, pos_ref, side_sems.at[2])
     load_pos.start()
     seqs, length = x_ref.shape[0], x_ref.shape[1]
@@ -201,6 +218,7 @@
                 x_ref[s] = plain(passed_ref[s])
 
     wait(2)
+    keep(2)
     gain_attn, gain_moe = gains_of(w_vmem)
     x = x_ref[...].reshape(rows, D).astype(f32)
     normed = (x * rms(x) * gain_attn).astype(bf16)
@@ -209,12 +227,15 @@
     load_table.wait()
     cosine, sine = table_ref[:, :LANES], table_ref[:, LANES:]
     wait(0)
+    keep(0)
     w_qkv = w_vmem[:, :, :QKV].reshape(D, QKV)
     qkv = nn(normed, w_qkv)
+    wait(1)
+    keep(1)
     heads = range(KEY_VALUE_HEADS)
     for s in range(seqs):
         top = slice(s * length, (s + 1) * length)
-        start = starts[s]
+        start = order[3, s]
         both = (
             (row_pos >= start) & (row_pos < start + PIC) & (col_pos >= start) & (col_pos < start + PIC)
         )
@@ -241,9 +262,13 @@
                 probs_ref[s * KEY_VALUE_HEADS + j] = probs
             mixed = join(nn(probs.astype(bf16), values[j]))
             mixed_ref[top, j * LANES : (j + 1) * LANES] = mixed.astype(bf16)
-    wait(1)
     w_out = w_vmem[:, :, QKV : QKV + D].reshape(D, D)
     resid = x + nn(mixed_ref[...], w_out)
+    if not save:
+        for s in range(seqs):
+            store_tiles(resid_vmem, s, resid[s * length : (s + 1) * length])
+        kept.append(pltpu.make_async_copy(resid_vmem, resid_ref, side_sems.at[7]))
+        kept[-1].start()
     normed_moe = (resid * rms(resid) * gain_moe).astype(bf16)
     w_small = w_vmem[:, :, QKV + D :].reshape(D, LANES)
     logits = nn(normed_moe, w_small)
@@ -264,8 +289,6 @@
         gate_ref[...] = gate
         normed_ref[...] = normed
     else:
-        for s in range(seqs):
-            store_tiles(resid_ref, s, resid[s * length : (s + 1) * length])
         loads[1].wait()
 
         @pl.when(second)
@@ -273,6 +296,9 @@
             for s in range(seqs):
                 store_tiles(out_ref, s, cot_ref[s])
 
+        for copy in kept:
+            copy.wait()
+
 
 def vmem():
     return pl.BlockSpec(memory_space=pltpu.VMEM)
@@ -282,6 +308,10 @@
     return pl.BlockSpec(memory_space=pltpu.SMEM)
 
 
+def in_vmem(a):
+    return pltpu.with_memory_space_constraint(a, pltpu.VMEM)
+
+
 def hbm():
     return pl.BlockSpec(memory_space=pltpu.HBM)
 
@@ -290,12 +320,13 @@
     return pltpu.with_memory_space_constraint(a, pltpu.HBM)
 
 
-def attn_forward(save, order, starts, table, pos, x, other, w_all):
+def attn_forward(save, order, table, pos, x, other, w_all):
     seqs, length = x.shape[0], x.shape[1]
     rows = seqs * length
     shape = jax.ShapeDtypeStruct
     tiles = (seqs, length * TILES, LANES)
-    outs = [shape((seqs, wide(length), LANES), bf16), shape((rows, D) if save else tiles, f32)]
+    outs = [shape((seqs, wide(length), LANES), bf16)]
+    outs.append(shape((rows, D), f32) if save else pltpu.HBM(tiles, f32))
     probs = (seqs * KEY_VALUE_HEADS, 2 * length, length)
     scratch = []
     if save:
@@ -310,28 +341,35 @@
             shape((rows, D), bf16),
         ]
         scratch = [pltpu.VMEM(tiles, bf16)]
+        w_specs, w_args = [vmem()], [in_vmem(w_all)]
     else:
+        outs.append(pltpu.HBM((16, 64, WCOLS), bf16))
+        w_specs, w_args = [pl.BlockSpec(memory_space=pl.ANY)] * 18, w_all
         scratch = [pltpu.VMEM((seqs, length, D), bf16)] * 2
         scratch.append(pltpu.VMEM((rows, D), bf16))
     scratch += [
-        pltpu.VMEM((16, 64, WCOLS), bf16),
         pltpu.VMEM((length, 2 * LANES), f32),
         pltpu.VMEM((rows, LANES), f32),
-        pltpu.SemaphoreType.DMA((54,)),
-        pltpu.SemaphoreType.DMA((4,)),
+        pltpu.SemaphoreType.DMA((8,)),
     ]
+    if not save:
+        scratch += [
+            pltpu.SemaphoreType.DMA((54,)),
+            pltpu.VMEM((16, 64, WCOLS), bf16),
+            pltpu.VMEM(tiles, f32),
+        ]
     return pl.pallas_call(
         functools.partial(attn_forward_kernel, save),
         out_shape=outs,
-        in_specs=[smem(), smem()] + [hbm()] * 22,
-        out_specs=[vmem()] * len(outs),
+        in_specs=[smem()] + [hbm()] * 4 + w_specs,
+        out_specs=[vmem()] * len(outs) if save else [vmem(), hbm(), hbm()],
         scratch_shapes=scratch,
         compiler_params=pltpu.CompilerParams(vmem_limit_bytes=VMEM_LIMIT),
         cost_estimate=pl.CostEstimate(
             flops=2 * rows * D * 3400, bytes_accessed=12_000_000, transcendentals=rows * 2048
         ),
         name="attn_forward",
-    )(order, starts, *map(in_hbm, [table, pos, x, other] + w_all))
+    )(order, *map(in_hbm, [table, pos, x, other]), *w_args)
 
 
 def attn_backward_kernel(
@@ -352,16 +390,28 @@
     table_ref,
     *rest,
 ):
-    blocks, rest = rest[:18], rest[18:]
+    w_vmem, rest = rest[0], rest[1:]
+    loads = [None] * 3
     if with_grads:
         grad_ref, big_refs, rest = rest[0], rest[1:11], rest[11:]
-        w_vmem, sems, back_ref, gains_ref = rest
+        back_ref, gains_ref, w_scratch, k_scratch, v_scratch, sems = rest
+        for part in (2, 1, 0):
+            columns = pl.ds(PARTS[part][0], PARTS[part][1] - PARTS[part][0])
+            loads[part] = pltpu.make_async_copy(
+                w_vmem.at[:, :, columns], w_scratch.at[:, :, columns], sems.at[part]
+            )
+            loads[part].start()
+        w_vmem = w_scratch
+        k_load = pltpu.make_async_copy(k_ref, k_scratch, sems.at[3])
+        v_load = pltpu.make_async_copy(v_ref, v_scratch, sems.at[4])
+        k_load.start()
+        v_load.start()
+        k_ref, v_ref = k_scratch, v_scratch
+        loads[2].wait()
     else:
-        grad_ref, w_vmem, sems, back_ref = rest
-    wait = load_weights(order, blocks, w_vmem, sems, (2, 1, 0))
+        grad_ref, back_ref = rest
     seqs, length = x_ref.shape[0], x_ref.shape[1]
     rows = seqs * length
-    wait(2)
     gain_attn, gain_moe = gains_of(w_vmem)
     gate = gate_ref[...]
     tiles = length * TILES
@@ -381,9 +431,13 @@
         g = g_ref[...].reshape(rows, D)
     grad_resid = g.astype(f32) + norm_back(resid, inv_moe, gain_moe, grad_normed_moe)
     grad_branch = grad_resid.astype(bf16)
-    wait(1)
+    if with_grads:
+        loads[1].wait()
     w_out = w_vmem[:, :, QKV : QKV + D].reshape(D, D)
     grad_mixed = nt(grad_branch, w_out)
+    if with_grads:
+        k_load.wait()
+        v_load.wait()
     cosine, sine = table_ref[:, :LANES], table_ref[:, LANES:]
     low = lanes_of((length, LANES)) < 64
     for s in range(seqs):
@@ -413,7 +467,8 @@
                 grad_key, cosine, sine, True
             ).astype(bf16)
             back_ref[top, D + 512 + c * LANES : D + 512 + (c + 1) * LANES] = grad_value.astype(bf16)
-    wait(0)
+    if with_grads:
+        loads[0].wait()
     w_qkv = w_vmem[:, :, :QKV].reshape(D, QKV)
     grad_rows = back_ref[...]
     grad_normed = nt(grad_rows, w_qkv)
@@ -472,22 +527,25 @@
 
 def attn_backward(with_grads, order, sums, g, saved, table, w_all):
     payload, resid, x, gate, normed, q, k, v, probs, mixed = saved
+    late = hbm if with_grads else vmem
     seqs, length = x.shape[0], x.shape[1]
     rows = seqs * length
     shape = jax.ShapeDtypeStruct
     outs = [shape((seqs, length, D) if with_grads else (seqs, length * TILES, LANES), bf16)]
-    scratch = [
-        pltpu.VMEM((16, 64, WCOLS), bf16),
-        pltpu.SemaphoreType.DMA((54,)),
-        pltpu.VMEM((rows, QKV), bf16),
-    ]
+    scratch = [pltpu.VMEM((rows, QKV), bf16)]
     if with_grads:
         outs += [shape((n, WCOLS), bf16) for n in (64, 128, 128, 128, 64)] * 2
-        scratch.append(pltpu.VMEM((8, D), f32))
+        scratch += [
+            pltpu.VMEM((8, D), f32),
+            pltpu.VMEM((16, 64, WCOLS), bf16),
+            pltpu.VMEM((rows, 512), bf16),
+            pltpu.VMEM((rows, 512), bf16),
+            pltpu.SemaphoreType.DMA((5,)),
+        ]
     return pl.pallas_call(
         functools.partial(attn_backward_kernel, with_grads),
         out_shape=outs,
-        in_specs=[smem()] + [vmem()] * 13 + [hbm()] * 18,
+        in_specs=[smem()] + [vmem()] * 8 + [late()] * 2 + [vmem()] * 3 + [late()],
         out_specs=[vmem()] * len(outs),
         scratch_shapes=scratch,
         compiler_params=pltpu.CompilerParams(vmem_limit_bytes=VMEM_LIMIT),
@@ -496,7 +554,10 @@
         ),
         name="attn_backward",
     )(
-        order, sums, g, x, payload, resid, gate, normed, q, k, v, probs, mixed, table, *map(in_hbm, w_all)
+        order,
+        *(sums, g, x, payload, resid, gate, normed, q),
+        *((in_hbm(k), in_hbm(v)) if with_grads else (k, v)),
+        *(probs, mixed, table, (in_hbm if with_grads else in_vmem)(w_all)),
     )
 
 
@@ -735,31 +796,68 @@
     )(*args, *earlier)
 
 
-def last_sum_kernel(*refs):
-    terms, (qkv_ref, out_ref, router_ref, attn_ref, moe_ref) = refs[:-5], refs[-5:]
-    columns = lambda low, high: total([ref[:, low:high] for ref in terms])
-    qkv_ref[...] = columns(0, QKV)
-    out_ref[...] = columns(QKV, QKV + D)
-    small = columns(QKV + D, WCOLS)
-    router_ref[...] = small[:, :EXPERTS]
-    attn_ref[...] = small[0:1, 64:]
-    moe_ref[...] = small[1:2, 64:]
-
-
-def last_sum(terms):
-    rows = terms[0].shape[0]
+def last_sum_kernel(plans, *refs):
+    refs, (qkv_ref, out_ref, router_ref, attn_ref, moe_ref) = refs[:-5], refs[-5:]
+    for n, plan in enumerate(plans):
+        columns = lambda first, last: total([refs[m][low:high, first:last] for m, low, high in plan])
+        rows = plan[0][2] - plan[0][1]
+        place = slice(n * rows, (n + 1) * rows)
+        qkv_ref[place] = columns(0, QKV)
+        out_ref[place] = columns(QKV, QKV + D)
+        small = columns(QKV + D, WCOLS)
+        router_ref[place] = small[:, :EXPERTS]
+        if n == 0:
+            attn_ref[...] = small[0:1, 64:]
+            moe_ref[...] = small[1:2, 64:]
+
+
+def last_sum(halves):
+    args, plans = [], []
+    for terms in halves:
+        plans.append([(len(args) + n, low, high) for n, (a, low, high) in enumerate(terms)])
+        args += [a for a, low, high in terms]
+    rows = sum(terms[0][2] - terms[0][1] for terms in halves)
     shape = lambda *dims: jax.ShapeDtypeStruct(dims, f32)
     return pl.pallas_call(
-        last_sum_kernel,
+        functools.partial(last_sum_kernel, plans),
         out_shape=[shape(rows, QKV), shape(rows, D), shape(rows, EXPERTS), shape(1, 64), shape(1, 64)],
-        in_specs=[vmem()] * len(terms),
+        in_specs=[vmem()] * len(args),
         out_specs=[vmem()] * 5,
         compiler_params=pltpu.CompilerParams(vmem_limit_bytes=VMEM_LIMIT),
         cost_estimate=pl.CostEstimate(
             flops=rows * WCOLS * 4, bytes_accessed=rows * WCOLS * 12, transcendentals=0
         ),
         name="last_sum",
-    )(*terms)
+    )(*args)
+
+
+def add_kernel(plans, *refs):
+    outs = refs[len(refs) - len(plans) :]
+    for out_ref, plan in zip(outs, plans):
+        out_ref[...] = total([refs[n][low:high] for n, low, high in plan]).astype(out_ref.dtype)
+
+
+def add_call(sums, dtype=bf16, stated=16_000_000):
+    args, plans, shapes = [], [], []
+    for terms in sums:
+        plan = []
+        for array, low, high in terms:
+            found = [n for n, a in enumerate(args) if a is array]
+            plan.append((found[0] if found else len(args), low, high))
+            if not found:
+                args.append(array)
+        plans.append(plan)
+        array, low, high = terms[0]
+        shapes.append(jax.ShapeDtypeStruct((high - low,) + array.shape[1:], dtype))
+    return pl.pallas_call(
+        functools.partial(add_kernel, plans),
+        out_shape=shapes,
+        in_specs=[vmem()] * len(args),
+        out_specs=[vmem()] * len(shapes),
+        compiler_params=pltpu.CompilerParams(vmem_limit_bytes=VMEM_LIMIT),
+        cost_estimate=pl.CostEstimate(flops=0, bytes_accessed=stated, transcendentals=0),
+        name="add",
+    )(*args)
 
 
 class Ring:
@@ -825,6 +923,32 @@
         out += [far + [self.swap(a) for a in far]]
         out += [both(a) for a in behind[:0:-1]]
         return sum(out, []), beside
+
+    def scatter_halves(self, terms):
+        half = terms[4][0][0].shape[0]
+        came = [[[], []], [[], []]]
+        last = ()
+        for r in range(4):
+            for c in range(2):
+                low, high = c * half, (c + 1) * half
+                whole = lambda values: [(a, 0, half) for a in values]
+                part = lambda values: [(a, low, high) for a in values]
+                came[c], last = lax.optimization_barrier((came[c], last))
+                if r == 0:
+                    last = add_call([whole(terms[4][c])])
+                else:
+                    behind, ahead = terms[4 - r]
+                    last = add_call(
+                        [part(behind) + whole(came[c][0]), part(ahead) + whole(came[c][1])]
+                    )
+                if r:
+                    came[c] = [[self.minus(last[0])], [self.plus(last[1])]]
+                else:
+                    came[c] = [[], [self.plus(last[0])]] if c else [[self.minus(last[0])], []]
+        return [
+            [(a, c * half, (c + 1) * half) for a in terms[0][0]] + [(a, 0, half) for a in sum(came[c], [])]
+            for c in range(2)
+        ]
 
     def scatter(self, terms, work=()):
         work, beside = list(work), ()
@@ -882,7 +1006,7 @@
 
     angles = np.arange(length)[:, None] * 10000.0 ** (-2.0 * (np.arange(LANES) % 32) / HEAD_SIZE)
     table = jnp.asarray(np.concatenate([np.cos(angles), np.sin(angles)], axis=1), f32)
-    starts = picture_start[:, 0]
+    starts = jnp.pad(picture_start[:, 0], (0, 6))[None]
 
     named = jnp.any(routes[0][..., None] == jnp.arange(LANES, dtype=jnp.int32), axis=2)
     earlier = jnp.asarray(np.tril(np.ones((length, length)), -1), bf16)
@@ -891,15 +1015,14 @@
 
     if ringed:
         ring = Ring()
-        order = jnp.concatenate([ring.order, jnp.broadcast_to(section, (1, 8)).astype(jnp.int32)])
+        order = jnp.concatenate([ring.order, jnp.broadcast_to(section, (1, 8)).astype(jnp.int32), starts])
         gains = jnp.concatenate([gain_attn, gain_moe])
         side = jnp.concatenate([gains, jnp.zeros((62, 64), bf16)])
-        small = jnp.concatenate([w_out[0], w_router[0], jnp.zeros((64, 32), bf16), side], axis=1)
-        whole = jnp.concatenate([w_qkv[0], small], axis=1)
-        w_all, (pos, order, starts) = ring.gather_whole(whole, (pos, order, starts))
+        whole = jnp.concatenate([w_qkv[0], w_out[0], w_router[0], jnp.zeros((64, 32), bf16), side], axis=1)
+        w_all, (pos, order) = ring.gather_whole(whole, (pos, order))
     else:
         order = jnp.stack([jnp.arange(8), jnp.zeros((8,)), jnp.broadcast_to(section, (8,))])
-        order = order.astype(jnp.int32)
+        order = jnp.concatenate([order.astype(jnp.int32), starts])
         gather = lambda a: lax.all_gather(a[0], "fsdp", axis=0, tiled=True)
         big = jnp.concatenate([gather(w_qkv), gather(w_out)], axis=1).reshape(16, 64, QKV + D)
         gains = jnp.stack([gather(gain_attn), gather(gain_moe)]).reshape(2, 16, 64)
@@ -927,8 +1050,12 @@
 
             terms, saved = ring.gather(own, work)
             last = [functools.partial(weight_grads, saved, hid, per, j) for j in range(per)]
-            sums, grads = ring.scatter(terms, last if mode == 2 else ())
-            return total(sums), seen, grads
+            if mode == 2:
+                sums, grads = ring.scatter(terms, last)
+                return total(sums), seen, grads
+            sums = ring.scatter_halves(terms)
+            sums = [total([a[low:high] for a, low, high in half]) for half in sums]
+            return jnp.concatenate(sums), seen, ()
 
         every = gather_rows(own)
         x_all, g_all = (every, g) if x_groups is None else (x_groups, every)
@@ -947,11 +1074,11 @@
         sums = lax.psum_scatter(flat, "fsdp", scatter_dimension=0, tiled=True).astype(f32)
         return sums, x_all, grads
 
-    payload, resid = attn_forward(False, order, starts, table, pos, tokens, cotangent, w_all)
+    payload, resid, w_all = attn_forward(False, order, table, pos, tokens, cotangent, w_all)
     mixture, g_second, _ = phase(0, payload, None)
     first_out = (resid + mixture).astype(bf16)
     passed = lax.ppermute(first_out, "section", [(0, 1), (1, 0)])
-    payload, resid, *saved = attn_forward(True, order, starts, table, pos, tokens, passed, w_all)
+    payload, resid, *saved = attn_forward(True, order, table, pos, tokens, passed, w_all)
     saved = [payload, resid] + saved
     sums_second, rows_all, _ = phase(1, payload, g_second)
     (grad_second,) = attn_backward(False, order, sums_second, cotangent, saved, table, w_all)
@@ -970,13 +1097,16 @@
     section_grad, *big = attn_backward(True, order, sums, g_third, saved, table, w_all)
 
     if ringed:
-        pairs = [(a, ring.swap(b)) for a, b in zip(big[:5], big[5:])]
+        pairs, came = [None] * 5, ()
+        for n in (4, 3, 2, 1, 0):
+            going, came = lax.optimization_barrier((big[5 + n], came))
+            came = ring.swap(going)
+            pairs[n] = (big[n], came)
         part = lambda pair, low, high: [a[low:high] for a in pair]
         terms = [[pairs[0]]]
         terms += [[part(pair, 0, 64), part(pair, 64, 128)] for pair in pairs[1:4]]
         terms += [[part(pairs[4], 0, 32), part(pairs[4], 32, 64)]]
-        summed, _ = ring.scatter(terms)
-        g_qkv, g_out, g_router, g_gain_attn, g_gain_moe = last_sum(summed)
+        g_qkv, g_out, g_router, g_gain_attn, g_gain_moe = last_sum(ring.scatter_halves(terms))
         g_gain_attn, g_gain_moe = g_gain_attn[0], g_gain_moe[0]
     else:
         chips = [(big[0], big[5])] + [(big[k][64:], big[5 + k][64:]) for k in (1, 2, 3)]

time: 464 us -> 446 us (0.961)
  waiting for transfers between devices: 199 us -> 164 us
  starting transfers between devices: 85.4 us -> 104 us
  other arithmetic: 13.7 us -> 7.32 us
    ppermute x32 -> x41, waiting for transfers between devices: 105 us -> 77.8 us  [plus(): return lax.ppermute(a, 'fsdp', self.ahead)]
    ppermute x32 -> x41, starting transfers between devices: 33.9 us -> 48.4 us  [plus(): return lax.ppermute(a, 'fsdp', self.ahead)]
    ppermute x32 -> x41, waiting for transfers between devices: 69.7 us -> 63.1 us  [minus(): return lax.ppermute(a, 'fsdp', self.behind)]
    pallas_call x1 -> x25, Pallas kernels: 1.18 us -> 7.35 us  [the longest x24 6.29 us: add_call(): pl.pallas_call(functools.partial(add_kernel, plans), out_shape=shapes, in...]
    ppermute x32 -> x41, starting transfers between devices: 34.6 us -> 39 us  [minus(): return lax.ppermute(a, 'fsdp', self.behind)]
  transfers between devices with their start and end apart: 134 -> 152, of which waited for: 78 -> 88; matrix products, arithmetic and copies ran while one was open for 4% -> 4% of each run, Pallas kernels for 18% -> 20%
where the time goes in v4:
time: 446 us; the launch traced here: 437 us
  waiting for transfers between devices  164 us (37%)
  Pallas kernels  138 us (31%)
  starting transfers between devices  104 us (23%)
  local copies, waits for them, and re-layouts  19.8 us (4%)
  other arithmetic  7.32 us (2%)
    pallas_call x15, Pallas kernels, expert_call(): pl.pallas_call(body, out_shape=outs, in_specs=[smem()] + [vmem()] * (part...  80.3 us
    ppermute x41, waiting for transfers between devices, plus(): return lax.ppermute(a, 'fsdp', self.ahead)  77.8 us
    ppermute x41, waiting for transfers between devices, minus(): return lax.ppermute(a, 'fsdp', self.behind)  63.1 us
    ppermute x41, starting transfers between devices, plus(): return lax.ppermute(a, 'fsdp', self.ahead)  48.4 us
    ppermute x41, starting transfers between devices, minus(): return lax.ppermute(a, 'fsdp', self.behind)  39 us
    pallas_call x2, Pallas kernels, attn_backward(): pl.pallas_call(functools.partial(attn_backward_kernel, with_grads), out_s...  21.4 us
    pallas_call x2, Pallas kernels, attn_forward(): pl.pallas_call(functools.partial(attn_forward_kernel, save), out_shape=ou...  15 us
    pallas_call x2, Pallas kernels, weight_grads(): pl.pallas_call(functools.partial(weight_grad_kernel, groups, tile, j), ou...  13.9 us
  transfers between devices with their start and end apart: 152, of which 88 were waited for; matrix products, arithmetic and copies ran while one was open for 4% of the time, Pallas kernels for 20%

profile of v4, /device:TPU:0, one launch (start us, length us, event | category | flops | bytes accessed | tf_op | source)
XLA Modules:
  0.0 437.3 jit_solution(13764607443636166888)
XLA Ops:
  10.5 5.4 %collective-permute-done.refs_18_ = bf16[64,3200]{1,0:T(8,128)(2,1)S(1)} collective-permute-done((bf16[64,3200]{1,0:T(8,128)(2,1)S(1)}, bf16[64,3200]{1,0:T(8,128)(2,1)S(1)}, u32[]{:S(2)}, u32[]{:S(2)}) %collective-permute-start) | collective-permute-done | bytes 409632 | tf_op jit(solution)/shard_map/ppermute | solution.py:878
  22.1 5.3 %collective-permute-done.2.refs_16_ = bf16[64,3200]{1,0:T(8,128)(2,1)} collective-permute-done((bf16[64,3200]{1,0:T(8,128)(2,1)S(1)}, bf16[64,3200]{1,0:T(8,128)(2,1)}, u32[]{:S(2)}, u32[]{:S(2)}) %collective-permute-start.2) | collective-permute-done | bytes 409632 | tf_op jit(solution)/shard_map/ppermute | solution.py:878
  31.3 6.5 %collective-permute-done.7.refs_14_ = bf16[64,3200]{1,0:T(8,128)(2,1)S(1)} collective-permute-done((bf16[64,3200]{1,0:T(8,128)(2,1)}, bf16[64,3200]{1,0:T(8,128)(2,1)S(1)}, u32[]{:S(2)}, u32[]{:S(2)}) %collective-permute-start.7) | collective-permute-done | bytes 409632 | tf_op jit(solution)/shard_map/ppermute | solution.py:878
  41.8 5.0 %collective-permute-done.10.refs_10_ = bf16[32,3200]{1,0:T(8,128)(2,1)S(1)} collective-permute-done((bf16[32,3200]{1,0:T(8,128)(2,1)S(1)}, bf16[32,3200]{1,0:T(8,128)(2,1)S(1)}, u32[]{:S(2)}, u32[]{:S(2)}) %collective-permute-start.10) | collective-permute-done | bytes 204832 | tf_op jit(solution)/shard_map/ppermute | solution.py:878
  50.5 8.6 %attn_forward.2 = (bf16[2,816,128]{2,1,0:T(8,128)(2,1)S(1)}, f32[2,768,128]{2,1,0:T(8,128)}, bf16[16,64,3200]{2,1,0:T(8,128)(2,1)}) custom-call(s32[4,8]{1,0:T(4,128)S(1)} %pad_add_fusion.order, f32[96,256]{1,0:T(8,128)} %constant.78.clone.table_hbm.table_ref, f32[192,128]{1,0:T(8,128)} %bitcast.80, bf16[2,96,1024]{2,1,0:T(8,128)(2,1)} %refs_0_.3, ...), custom_call_target="tpu_custom_call" | custom-call | flops 1336934400 | bytes 12000000 | tf_op jit(solution)/shard_map/attn_forward/pallas_call | solution.py:361
  74.5 5.1 %experts_0.6 = (bf16[2,768,128]{2,1,0:T(8,128)(2,1)S(1)}, bf16[2,768,128]{2,1,0:T(8,128)(2,1)S(1)}, bf16[2,768,128]{2,1,0:T(8,128)(2,1)S(1)}, bf16[2,768,128]{2,1,0:T(8,128)(2,1)S(1)}) custom-call(s32[2]{0:T(128)S(1)} %pad_add_fusion.1.which, bf16[2,816,128]{2,1,0:T(8,128)(2,1)S(1)} %collective-permute-done.17.refs_0_.refs_4_, ...), custom_call_target="tpu_custom_call" | custom-call | flops 1610612736 | bytes 9145728 | tf_op jit(solution)/shard_map/experts_0/pallas_call | solution.py:703
  87.8 4.6 %experts_0.7 = (bf16[2,768,128]{2,1,0:T(8,128)(2,1)S(1)}, bf16[2,768,128]{2,1,0:T(8,128)(2,1)S(1)}, bf16[2,768,128]{2,1,0:T(8,128)(2,1)S(1)}, bf16[2,768,128]{2,1,0:T(8,128)(2,1)S(1)}) custom-call(s32[2]{0:T(128)S(1)} %pad_add_fusion.1.which, bf16[2,816,128]{2,1,0:T(8,128)(2,1)S(1)} %collective-permute-done.20.refs_0_.refs_4_, ...), custom_call_target="tpu_custom_call" | custom-call | flops 1610612736 | bytes 9145728 | tf_op jit(solution)/shard_map/experts_0/pallas_call | solution.py:703
  92.4 4.4 collective-permute-done.25.refs_0_.refs_4_
  100.3 4.6 %experts_0.8 = (bf16[2,768,128]{2,1,0:T(8,128)(2,1)S(1)}, bf16[2,768,128]{2,1,0:T(8,128)(2,1)S(1)}, bf16[2,768,128]{2,1,0:T(8,128)(2,1)S(1)}, bf16[2,768,128]{2,1,0:T(8,128)(2,1)S(1)}) custom-call(s32[2]{0:T(128)S(1)} %pad_add_fusion.1.which, bf16[2,816,128]{2,1,0:T(8,128)(2,1)S(1)} %collective-permute-done.25.refs_0_.refs_4_, ...), custom_call_target="tpu_custom_call" | custom-call | flops 1610612736 | bytes 9145728 | tf_op jit(solution)/shard_map/experts_0/pallas_call | solution.py:703
  115.5 4.5 %collective-permute-done.41.refs_2_ = bf16[1,768,128]{2,1,0:T(8,128)(2,1)S(1)} collective-permute-done((bf16[1,768,128]{2,1,0:T(8,128)(2,1)S(1)}, bf16[1,768,128]{2,1,0:T(8,128)(2,1)S(1)}, u32[]{:S(2)}, u32[]{:S(2)}) %collective-permute-start.41) | collective-permute-done | bytes 196640 | tf_op jit(solution)/shard_map/ppermute | solution.py:881
  151.6 6.3 %collective-permute-done.57.refs_1_ = bf16[2,768,128]{2,1,0:T(8,128)(2,1)S(1)} collective-permute-done((bf16[2,768,128]{2,1,0:T(8,128)(2,1)S(1)}, bf16[2,768,128]{2,1,0:T(8,128)(2,1)S(1)}, u32[]{:S(2)}, u32[]{:S(2)}) %collective-permute-start.57) | collective-permute-done | bytes 393248 | tf_op jit(solution)/shard_map/ppermute | solution.py:1080
  158.6 6.4 %attn_forward.3 = (bf16[2,816,128]{2,1,0:T(8,128)(2,1)S(1)}, f32[192,1024]{1,0:T(8,128)S(1)}, bf16[2,96,1024]{2,1,0:T(8,128)(2,1)S(1)}, f32[192,128]{1,0:T(8,128...) custom-call(s32[4,8]{1,0:T(4,128)S(1)} %pad_add_fusion.order, ...), custom_call_target="tpu_custom_call" | custom-call | flops 1336934400 | bytes 12000000 | tf_op jit(solution)/shard_map/attn_forward/pallas_call | solution.py:361
  167.2 4.7 %experts_1.5 = (bf16[2,816,128]{2,1,0:T(8,128)(2,1)S(1)}, bf16[2,816,128]{2,1,0:T(8,128)(2,1)S(1)}) custom-call(s32[2]{0:T(128)S(1)} %pad_add_fusion.1.which, bf16[2,816,128]{2,1,0:T(8,128)(2,1)S(1)} %get-tuple-element.447.refs_0_.wide_ref, bf16[2,816,128]{2,1,0:T(8,128)(2,1)S(1)} %collective-permute-done.60.refs_1_, bf16[2,816,128]{2,1,0:T(8,128)(2,1)S(1)} %copy-done.6, ...), custom_call_target="tpu_custom_call" | custom-call | flops 1342177280 | bytes 7572864 | tf_op jit(solution)/shard_map/experts_1/pallas_call | solution.py:703
  171.9 5.3 %collective-permute-done.58.refs_0_ = bf16[2,816,128]{2,1,0:T(8,128)(2,1)S(1)} collective-permute-done((bf16[2,816,128]{2,1,0:T(8,128)(2,1)S(1)}, bf16[2,816,128]{2,1,0:T(8,128)(2,1)S(1)}, u32[]{:S(2)}, u32[]{:S(2)}) %collective-permute-start.58) | collective-permute-done | bytes 417824 | tf_op jit(solution)/shard_map/ppermute | solution.py:878
  180.2 6.7 %experts_1.6 = (bf16[2,816,128]{2,1,0:T(8,128)(2,1)S(1)}, bf16[2,816,128]{2,1,0:T(8,128)(2,1)S(1)}, bf16[2,816,128]{2,1,0:T(8,128)(2,1)S(1)}, bf16[2,816,128]{2,1,0:T(8,128)(2,1)S(1)}) custom-call(s32[2]{0:T(128)S(1)} %pad_add_fusion.1.which, bf16[2,816,128]{2,1,0:T(8,128)(2,1)S(1)} %collective-permute-done.58.refs_0_, ...), custom_call_target="tpu_custom_call" | custom-call | flops 2684354560 | bytes 9145728 | tf_op jit(solution)/shard_map/experts_1/pallas_call | solution.py:703
  193.1 6.2 %experts_1.7 = (bf16[2,816,128]{2,1,0:T(8,128)(2,1)S(1)}, bf16[2,816,128]{2,1,0:T(8,128)(2,1)S(1)}, bf16[2,816,128]{2,1,0:T(8,128)(2,1)S(1)}, bf16[2,816,128]{2,1,0:T(8,128)(2,1)S(1)}) custom-call(s32[2]{0:T(128)S(1)} %pad_add_fusion.1.which, bf16[2,816,128]{2,1,0:T(8,128)(2,1)S(1)} %collective-permute-done.61.refs_0_, ...), custom_call_target="tpu_custom_call" | custom-call | flops 2684354560 | bytes 9145728 | tf_op jit(solution)/shard_map/experts_1/pallas_call | solution.py:703
  206.7 6.2 %experts_1.8 = (bf16[2,816,128]{2,1,0:T(8,128)(2,1)S(1)}, bf16[2,816,128]{2,1,0:T(8,128)(2,1)S(1)}, bf16[2,816,128]{2,1,0:T(8,128)(2,1)S(1)}, bf16[2,816,128]{2,1,0:T(8,128)(2,1)S(1)}) custom-call(s32[2]{0:T(128)S(1)} %pad_add_fusion.1.which, bf16[2,816,128]{2,1,0:T(8,128)(2,1)S(1)} %collective-permute-done.66.refs_0_, ...), custom_call_target="tpu_custom_call" | custom-call | flops 2684354560 | bytes 9145728 | tf_op jit(solution)/shard_map/experts_1/pallas_call | solution.py:703
  215.0 4.7 %experts_1.9 = (bf16[1,816,128]{2,1,0:T(8,128)(2,1)S(1)}, bf16[1,816,128]{2,1,0:T(8,128)(2,1)S(1)}, bf16[1,816,128]{2,1,0:T(8,128)(2,1)S(1)}, bf16[1,816,128]{2,1,0:T(8,128)(2,1)S(1)}) custom-call(s32[2]{0:T(128)S(1)} %pad_add_fusion.1.which, bf16[1,816,128]{2,1,0:T(8,128)(2,1)S(1)} %collective-permute-done.72.refs_0_, ...), custom_call_target="tpu_custom_call" | custom-call | flops 1342177280 | bytes 7572864 | tf_op jit(solution)/shard_map/experts_1/pallas_call | solution.py:703
  224.3 4.3 collective-permute-done.82.refs_2_
  259.1 8.4 %attn_backward.2 = bf16[2,768,128]{2,1,0:T(8,128)(2,1)S(1)} custom-call(s32[4,8]{1,0:T(4,128)S(1)} %pad_add_fusion.order, f32[2,816,128]{2,1,0:T(8,128)S(1)} %pad_maximum_fusion.sum_ref, bf16[2,96,1024]{2,1,0:T(8,128)(2,1)S(1)} %copy-done.12, bf16[2,96,1024]{2,1,0:T(8,128)(2,1)S(1)} %get-tuple-element.528.x_ref, ...), custom_call_target="tpu_custom_call" | custom-call | flops 2673868800 | bytes 20000000 | tf_op jit(solution)/shard_map/attn_backward/pallas_call | solution.py:545
  269.1 6.8 %collective-permute-done.98.refs_2_.g_ref = bf16[2,768,128]{2,1,0:T(8,128)(2,1)S(1)} collective-permute-done((bf16[2,768,128]{2,1,0:T(8,128)(2,1)S(1)}, bf16[2,768,128]{2,1,0:T(8,128)(2,1)S(1)}, u32[]{:S(2)}, u32[]{:S(2)}) %collective-permute-start.98) | collective-permute-done | bytes 393248 | tf_op jit(solution)/shard_map/ppermute | solution.py:1086
  277.9 5.1 %experts_2.5 = (bf16[2,816,128]{2,1,0:T(8,128)(2,1)S(1)}, bf16[2,816,128]{2,1,0:T(8,128)(2,1)S(1)}, bf16[2,128,1024]{2,1,0:T(8,128)(2,1)}, bf16[2,128,1024]{2,1,...) custom-call(s32[2]{0:T(128)S(1)} %pad_add_fusion.1.which, ...), custom_call_target="tpu_custom_call" | custom-call | flops 1342177280 | bytes 7572864 | tf_op jit(solution)/shard_map/experts_2/pallas_call | solution.py:703
  283.0 4.4 collective-permute-done.99.refs_4_
  291.4 6.7 %experts_2.6 = (bf16[2,816,128]{2,1,0:T(8,128)(2,1)S(1)}, bf16[2,816,128]{2,1,0:T(8,128)(2,1)S(1)}, bf16[2,816,128]{2,1,0:T(8,128)(2,1)S(1)}, bf16[2,816,128]{2,...) custom-call(s32[2]{0:T(128)S(1)} %pad_add_fusion.1.which, ...), custom_call_target="tpu_custom_call" | custom-call | flops 2684354560 | bytes 9145728 | tf_op jit(solution)/shard_map/experts_2/pallas_call | solution.py:703
  305.1 6.7 %experts_2.7 = (bf16[2,816,128]{2,1,0:T(8,128)(2,1)S(1)}, bf16[2,816,128]{2,1,0:T(8,128)(2,1)S(1)}, bf16[2,816,128]{2,1,0:T(8,128)(2,1)S(1)}, bf16[2,816,128]{2,...) custom-call(s32[2]{0:T(128)S(1)} %pad_add_fusion.1.which, ...), custom_call_target="tpu_custom_call" | custom-call | flops 2684354560 | bytes 9145728 | tf_op jit(solution)/shard_map/experts_2/pallas_call | solution.py:703
  318.8 6.7 %experts_2.8 = (bf16[2,816,128]{2,1,0:T(8,128)(2,1)S(1)}, bf16[2,816,128]{2,1,0:T(8,128)(2,1)S(1)}, bf16[2,816,128]{2,1,0:T(8,128)(2,1)S(1)}, bf16[2,816,128]{2,...) custom-call(s32[2]{0:T(128)S(1)} %pad_add_fusion.1.which, ...), custom_call_target="tpu_custom_call" | custom-call | flops 2684354560 | bytes 9145728 | tf_op jit(solution)/shard_map/experts_2/pallas_call | solution.py:703
  327.4 5.1 %experts_2.9 = (bf16[1,816,128]{2,1,0:T(8,128)(2,1)S(1)}, bf16[1,816,128]{2,1,0:T(8,128)(2,1)S(1)}, bf16[1,816,128]{2,1,0:T(8,128)(2,1)S(1)}, bf16[1,816,128]{2,...) custom-call(s32[2]{0:T(128)S(1)} %pad_add_fusion.1.which, ...), custom_call_target="tpu_custom_call" | custom-call | flops 1342177280 | bytes 7572864 | tf_op jit(solution)/shard_map/experts_2/pallas_call | solution.py:703
  337.1 5.3 %collective-permute-done.124 = bf16[1,816,128]{2,1,0:T(8,128)(2,1)S(1)} collective-permute-done((bf16[1,816,128]{2,1,0:T(8,128)(2,1)S(1)}, bf16[1,816,128]{2,1,0:T(8,128)(2,1)S(1)}, u32[]{:S(2)}, u32[]{:S(2)}) %collective-permute-start.124) | collective-permute-done | bytes 208928 | tf_op jit(solution)/shard_map/ppermute | solution.py:881
  345.6 7.0 %weight_grads_0.1 = (f32[1024,2048]{1,0:T(8,128)}, f32[1024,1024]{1,0:T(8,128)}) custom-call(bf16[2,128,1024]{2,1,0:T(8,128)(2,1)} %get-tuple-element.614.refs_0_, bf16[2,128,1024]{2,1,0:T(8,128)(2,1)} %get-tuple-element.615.refs_1_, bf16[2,128,512]{2,1,0:T(8,128)(2,1)} %get-tuple-element.616.refs_2_, bf16[2,128,512]{2,1,0:T(8,128)(2,1)} %get-tuple-element.617.refs_3_, ...), custom_call_target="tpu_custom_call" | custom-call | flops 3221225472 | bytes 14000000 | tf_op jit(solution)/shard_map/weight_grads_0/pallas_call | solution.py:774
  357.5 6.9 %weight_grads_1.1 = (f32[1024,2048]{1,0:T(8,128)}, f32[1024,1024]{1,0:T(8,128)}) custom-call(bf16[2,128,1024]{2,1,0:T(8,128)(2,1)} %get-tuple-element.614.refs_0_, bf16[2,128,1024]{2,1,0:T(8,128)(2,1)} %get-tuple-element.615.refs_1_, bf16[2,128,512]{2,1,0:T(8,128)(2,1)} %get-tuple-element.616.refs_2_, ...), custom_call_target="tpu_custom_call", output_to_operand_aliasing={{0}: (25, {}), {1}: (26, {})} | custom-call | flops 3221225472 | bytes 14000000 | tf_op jit(solution)/shard_map/weight_grads_1/pallas_call | solution.py:774
  379.6 13.0 %attn_backward.3 = (bf16[2,96,1024]{2,1,0:T(8,128)(2,1)}, bf16[64,3200]{1,0:T(8,128)(2,1)S(1)}, bf16[128,3200]{1,0:T(8,128)(2,1)S(1)}, bf16[128,3200]{1,0:T(8,12...) custom-call(s32[4,8]{1,0:T(4,128)S(1)} %pad_add_fusion.order, ...), custom_call_target="tpu_custom_call" | custom-call | flops 2673868800 | bytes 20000000 | tf_op jit(solution)/shard_map/attn_backward/pallas_call | solution.py:545
  396.9 5.1 %collective-permute-done.138.refs_2_ = bf16[32,3200]{1,0:T(8,128)(2,1)S(1)} collective-permute-done((bf16[32,3200]{1,0:T(8,128)(2,1)S(1)}, bf16[32,3200]{1,0:T(8,128)(2,1)S(1)}, u32[]{:S(2)}, u32[]{:S(2)}) %collective-permute-start.138) | collective-permute-done | bytes 204832 | tf_op jit(solution)/shard_map/ppermute | solution.py:881
  (456 shorter events, 243.5 us)
Async XLA Ops:
  3.4 12.5 %collective-permute-start = (bf16[64,3200]{1,0:T(8,128)(2,1)S(1)}, bf16[64,3200]{1,0:T(8,128)(2,1)S(1)}, u32[]{:S(2)}, u32[]{:S(2)}) collective-permute-start(bf16[64,3200]{1,0:T(8,128)(2,1)S(1)} %concatenate.24.refs_2_), channel_id=1, source_target_pairs={{0,4},{1,5},{4,8},{5,9},{8,12},{9,13},{12,14},{13,15},{14,10},{15,... | collective-permute-start | bytes 1228808 | tf_op jit(solution)/shard_map/ppermute | solution.py:878
  6.4 10.9 %collective-permute-start.1 = (bf16[64,3200]{1,0:T(8,128)(2,1)S(1)}, bf16[64,3200]{1,0:T(8,128)(2,1)S(1)}, u32[]{:S(2)}, u32[]{:S(2)}) collective-permute-start(bf16[64,3200]{1,0:T(8,128)(2,1)S(1)} %concatenate.24.refs_2_), channel_id=1, source_target_pairs={{0,2},{1,3},{4,0},{5,1},{8,4},{9,5},{12,8},{13,9},{14,12},{15,13},... | collective-permute-start | bytes 1228808 | tf_op jit(solution)/shard_map/ppermute | solution.py:881
  59.3 11.9 %collective-permute-start.17 = (bf16[2,816,128]{2,1,0:T(8,128)(2,1)S(1)}, bf16[2,816,128]{2,1,0:T(8,128)(2,1)S(1)}, u32[]{:S(2)}, u32[]{:S(2)}) collective-permute-start(bf16[2,816,128]{2,1,0:T(8,128)(2,1)S(1)} %get-tuple-element.364.refs_0_.refs_2_), channel_id=1, source_target_pairs={{0,4},{1,5},{4,8},{5,9},{8,12},{9,13},{12,14},{13,15},{14,10},{15,... | collective-permute-start | bytes 1253384 | tf_op jit(solution)/shard_map/ppermute | solution.py:878
  60.1 11.7 %collective-permute-start.18 = (bf16[2,816,128]{2,1,0:T(8,128)(2,1)S(1)}, bf16[2,816,128]{2,1,0:T(8,128)(2,1)}, u32[]{:S(2)}, u32[]{:S(2)}) collective-permute-start(bf16[2,816,128]{2,1,0:T(8,128)(2,1)S(1)} %get-tuple-element.364.refs_0_.refs_2_), channel_id=1, source_target_pairs={{0,2},{1,3},{4,0},{5,1},{8,4},{9,5},{12,8},{13,9},{14,12},{15,13},... | collective-permute-start | bytes 1253384 | tf_op jit(solution)/shard_map/ppermute | solution.py:881
  72.3 11.6 %collective-permute-start.20 = (bf16[2,816,128]{2,1,0:T(8,128)(2,1)S(1)}, bf16[2,816,128]{2,1,0:T(8,128)(2,1)S(1)}, u32[]{:S(2)}, u32[]{:S(2)}) collective-permute-start(bf16[2,816,128]{2,1,0:T(8,128)(2,1)S(1)} %collective-permute-done.17.refs_0_.refs_4_), channel_id=1, source_target_pairs={{0,4},{1,5},{4,8},{5,9},{8,12},{9,13},{12,14},{13,15},{14,10},{15,... | collective-permute-start | bytes 1253384 | tf_op jit(solution)/shard_map/ppermute | solution.py:878
  73.0 11.7 %collective-permute-start.21 = (bf16[2,816,128]{2,1,0:T(8,128)(2,1)}, bf16[2,816,128]{2,1,0:T(8,128)(2,1)S(1)}, u32[]{:S(2)}, u32[]{:S(2)}) collective-permute-start(bf16[2,816,128]{2,1,0:T(8,128)(2,1)} %collective-permute-done.18.refs_1_.refs_5_), channel_id=1, source_target_pairs={{0,2},{1,3},{4,0},{5,1},{8,4},{9,5},{12,8},{13,9},{14,12},{15,13},... | collective-permute-start | bytes 1253384 | tf_op jit(solution)/shard_map/ppermute | solution.py:881
  85.2 11.6 %collective-permute-start.25 = (bf16[2,816,128]{2,1,0:T(8,128)(2,1)S(1)}, bf16[2,816,128]{2,1,0:T(8,128)(2,1)S(1)}, u32[]{:S(2)}, u32[]{:S(2)}) collective-permute-start(bf16[2,816,128]{2,1,0:T(8,128)(2,1)S(1)} %collective-permute-done.20.refs_0_.refs_4_), channel_id=1, source_target_pairs={{0,4},{1,5},{4,8},{5,9},{8,12},{9,13},{12,14},{13,15},{14,10},{15,... | collective-permute-start | bytes 1253384 | tf_op jit(solution)/shard_map/ppermute | solution.py:878
  85.8 11.3 %collective-permute-start.26 = (bf16[2,816,128]{2,1,0:T(8,128)(2,1)S(1)}, bf16[2,816,128]{2,1,0:T(8,128)(2,1)S(1)}, u32[]{:S(2)}, u32[]{:S(2)}) collective-permute-start(bf16[2,816,128]{2,1,0:T(8,128)(2,1)S(1)} %collective-permute-done.21.refs_1_.refs_5_), channel_id=1, source_target_pairs={{0,2},{1,3},{4,0},{5,1},{8,4},{9,5},{12,8},{13,9},{14,12},{15,13},... | collective-permute-start | bytes 1253384 | tf_op jit(solution)/shard_map/ppermute | solution.py:881
  165.2 12.0 %collective-permute-start.58 = (bf16[2,816,128]{2,1,0:T(8,128)(2,1)S(1)}, bf16[2,816,128]{2,1,0:T(8,128)(2,1)S(1)}, u32[]{:S(2)}, u32[]{:S(2)}) collective-permute-start(bf16[2,816,128]{2,1,0:T(8,128)(2,1)S(1)} %get-tuple-element.447.refs_0_.wide_ref), channel_id=1, source_target_pairs={{0,4},{1,5},{4,8},{5,9},{8,12},{9,13},{12,14},{13,15},{14,10},{15,... | collective-permute-start | bytes 1253384 | tf_op jit(solution)/shard_map/ppermute | solution.py:878
  165.8 11.7 %collective-permute-start.59 = (bf16[2,816,128]{2,1,0:T(8,128)(2,1)S(1)}, bf16[2,816,128]{2,1,0:T(8,128)(2,1)S(1)}, u32[]{:S(2)}, u32[]{:S(2)}) collective-permute-start(bf16[2,816,128]{2,1,0:T(8,128)(2,1)S(1)} %get-tuple-element.447.refs_0_.wide_ref), channel_id=1, source_target_pairs={{0,2},{1,3},{4,0},{5,1},{8,4},{9,5},{12,8},{13,9},{14,12},{15,13},... | collective-permute-start | bytes 1253384 | tf_op jit(solution)/shard_map/ppermute | solution.py:881
  178.0 11.6 %collective-permute-start.61 = (bf16[2,816,128]{2,1,0:T(8,128)(2,1)S(1)}, bf16[2,816,128]{2,1,0:T(8,128)(2,1)S(1)}, u32[]{:S(2)}, u32[]{:S(2)}) collective-permute-start(bf16[2,816,128]{2,1,0:T(8,128)(2,1)S(1)} %collective-permute-done.58.refs_0_), channel_id=1, source_target_pairs={{0,4},{1,5},{4,8},{5,9},{8,12},{9,13},{12,14},{13,15},{14,10},{15,... | collective-permute-start | bytes 1253384 | tf_op jit(solution)/shard_map/ppermute | solution.py:878
  178.6 11.4 %collective-permute-start.62 = (bf16[2,816,128]{2,1,0:T(8,128)(2,1)S(1)}, bf16[2,816,128]{2,1,0:T(8,128)(2,1)S(1)}, u32[]{:S(2)}, u32[]{:S(2)}) collective-permute-start(bf16[2,816,128]{2,1,0:T(8,128)(2,1)S(1)} %collective-permute-done.59.refs_1_), channel_id=1, source_target_pairs={{0,2},{1,3},{4,0},{5,1},{8,4},{9,5},{12,8},{13,9},{14,12},{15,13},... | collective-permute-start | bytes 1253384 | tf_op jit(solution)/shard_map/ppermute | solution.py:881
  190.5 11.6 %collective-permute-start.66 = (bf16[2,816,128]{2,1,0:T(8,128)(2,1)S(1)}, bf16[2,816,128]{2,1,0:T(8,128)(2,1)S(1)}, u32[]{:S(2)}, u32[]{:S(2)}) collective-permute-start(bf16[2,816,128]{2,1,0:T(8,128)(2,1)S(1)} %collective-permute-done.61.refs_0_), channel_id=1, source_target_pairs={{0,4},{1,5},{4,8},{5,9},{8,12},{9,13},{12,14},{13,15},{14,10},{15,... | collective-permute-start | bytes 1253384 | tf_op jit(solution)/shard_map/ppermute | solution.py:878
  192.1 11.3 %collective-permute-start.67 = (bf16[2,816,128]{2,1,0:T(8,128)(2,1)S(1)}, bf16[2,816,128]{2,1,0:T(8,128)(2,1)S(1)}, u32[]{:S(2)}, u32[]{:S(2)}) collective-permute-start(bf16[2,816,128]{2,1,0:T(8,128)(2,1)S(1)} %collective-permute-done.62.refs_1_), channel_id=1, source_target_pairs={{0,2},{1,3},{4,0},{5,1},{8,4},{9,5},{12,8},{13,9},{14,12},{15,13},... | collective-permute-start | bytes 1253384 | tf_op jit(solution)/shard_map/ppermute | solution.py:881
  192.5 10.8 %collective-permute-start.70 = (bf16[2,816,128]{2,1,0:T(8,128)(2,1)S(1)}, bf16[2,816,128]{2,1,0:T(8,128)(2,1)S(1)}, u32[]{:S(2)}, u32[]{:S(2)}) collective-permute-start(bf16[2,816,128]{2,1,0:T(8,128)(2,1)S(1)} %get-tuple-element.467), channel_id=1, source_target_pairs={{0,1},{1,0},{2,3},{3,2},{4,5},{5,4},{6,7},{7,6},{8,9},{9,8},{10,11... | collective-permute-start | bytes 1253384 | tf_op jit(solution)/shard_map/ppermute | solution.py:884
  192.5 10.8 %collective-permute-start.71 = (bf16[2,816,128]{2,1,0:T(8,128)(2,1)S(1)}, bf16[2,816,128]{2,1,0:T(8,128)(2,1)S(1)}, u32[]{:S(2)}, u32[]{:S(2)}) collective-permute-start(bf16[2,816,128]{2,1,0:T(8,128)(2,1)S(1)} %get-tuple-element.469), channel_id=1, source_target_pairs={{0,1},{1,0},{2,3},{3,2},{4,5},{5,4},{6,7},{7,6},{8,9},{9,8},{10,11... | collective-permute-start | bytes 1253384 | tf_op jit(solution)/shard_map/ppermute | solution.py:884
  231.0 10.4 %collective-permute-start.90 = (bf16[1,816,128]{2,1,0:T(8,128)(2,1)S(1)}, bf16[1,816,128]{2,1,0:T(8,128)(2,1)S(1)}, u32[]{:S(2)}, u32[]{:S(2)}) collective-permute-start(bf16[1,816,128]{2,1,0:T(8,128)(2,1)S(1)} %get-tuple-element.506), channel_id=1, source_target_pairs={{0,2},{1,3},{4,0},{5,1},{8,4},{9,5},{12,8},{13,9},{14,12},{15,13},... | collective-permute-start | bytes 626696 | tf_op jit(solution)/shard_map/ppermute | solution.py:881
  231.3 10.4 %collective-permute-start.91 = (bf16[1,816,128]{2,1,0:T(8,128)(2,1)S(1)}, bf16[1,816,128]{2,1,0:T(8,128)(2,1)S(1)}, u32[]{:S(2)}, u32[]{:S(2)}) collective-permute-start(bf16[1,816,128]{2,1,0:T(8,128)(2,1)S(1)} %get-tuple-element.507), channel_id=1, source_target_pairs={{0,4},{1,5},{4,8},{5,9},{8,12},{9,13},{12,14},{13,15},{14,10},{15,... | collective-permute-start | bytes 626696 | tf_op jit(solution)/shard_map/ppermute | solution.py:878
  275.9 11.5 %collective-permute-start.99 = (bf16[2,768,128]{2,1,0:T(8,128)(2,1)S(1)}, bf16[2,768,128]{2,1,0:T(8,128)(2,1)S(1)}, u32[]{:S(2)}, u32[]{:S(2)}) collective-permute-start(bf16[2,768,128]{2,1,0:T(8,128)(2,1)S(1)} %collective-permute-done.98.refs_2_.g_ref), channel_id=1, source_target_pairs={{0,4},{1,5},{4,8},{5,9},{8,12},{9,13},{12,14},{13,15},{14,10},{15,... | collective-permute-start | bytes 1179656 | tf_op jit(solution)/shard_map/ppermute | solution.py:878
  277.5 11.2 %collective-permute-start.100 = (bf16[2,768,128]{2,1,0:T(8,128)(2,1)S(1)}, bf16[2,768,128]{2,1,0:T(8,128)(2,1)S(1)}, u32[]{:S(2)}, u32[]{:S(2)}) collective-permute-start(bf16[2,768,128]{2,1,0:T(8,128)(2,1)S(1)} %collective-permute-done.98.refs_2_.g_ref), channel_id=1, source_target_pairs={{0,2},{1,3},{4,0},{5,1},{8,4},{9,5},{12,8},{13,9},{14,12},{15,13},... | collective-permute-start | bytes 1179656 | tf_op jit(solution)/shard_map/ppermute | solution.py:881
  289.2 12.8 %collective-permute-start.106 = (bf16[2,816,128]{2,1,0:T(8,128)(2,1)S(1)}, bf16[2,816,128]{2,1,0:T(8,128)(2,1)S(1)}, u32[]{:S(2)}, u32[]{:S(2)}) collective-permute-start(bf16[2,816,128]{2,1,0:T(8,128)(2,1)S(1)} %get-tuple-element.555), channel_id=1, source_target_pairs={{0,1},{1,0},{2,3},{3,2},{4,5},{5,4},{6,7},{7,6},{8,9},{9,8},{10,11... | collective-permute-start | bytes 1253384 | tf_op jit(solution)/shard_map/ppermute | solution.py:884
  289.2 11.5 %collective-permute-start.102 = (bf16[2,768,128]{2,1,0:T(8,128)(2,1)S(1)}, bf16[2,768,128]{2,1,0:T(8,128)(2,1)S(1)}, u32[]{:S(2)}, u32[]{:S(2)}) collective-permute-start(bf16[2,768,128]{2,1,0:T(8,128)(2,1)S(1)} %collective-permute-done.99.refs_4_), channel_id=1, source_target_pairs={{0,4},{1,5},{4,8},{5,9},{8,12},{9,13},{12,14},{13,15},{14,10},{15,... | collective-permute-start | bytes 1179656 | tf_op jit(solution)/shard_map/ppermute | solution.py:878
  290.6 11.4 %collective-permute-start.103 = (bf16[2,768,128]{2,1,0:T(8,128)(2,1)S(1)}, bf16[2,768,128]{2,1,0:T(8,128)(2,1)S(1)}, u32[]{:S(2)}, u32[]{:S(2)}) collective-permute-start(bf16[2,768,128]{2,1,0:T(8,128)(2,1)S(1)} %collective-permute-done.100.refs_5_), channel_id=1, source_target_pairs={{0,2},{1,3},{4,0},{5,1},{8,4},{9,5},{12,8},{13,9},{14,12},{15,13},... | collective-permute-start | bytes 1179656 | tf_op jit(solution)/shard_map/ppermute | solution.py:881
  302.6 12.7 %collective-permute-start.111 = (bf16[2,816,128]{2,1,0:T(8,128)(2,1)S(1)}, bf16[2,816,128]{2,1,0:T(8,128)(2,1)S(1)}, u32[]{:S(2)}, u32[]{:S(2)}) collective-permute-start(bf16[2,816,128]{2,1,0:T(8,128)(2,1)S(1)} %get-tuple-element.570), channel_id=1, source_target_pairs={{0,1},{1,0},{2,3},{3,2},{4,5},{5,4},{6,7},{7,6},{8,9},{9,8},{10,11... | collective-permute-start | bytes 1253384 | tf_op jit(solution)/shard_map/ppermute | solution.py:884
  302.6 12.7 %collective-permute-start.112 = (bf16[2,816,128]{2,1,0:T(8,128)(2,1)S(1)}, bf16[2,816,128]{2,1,0:T(8,128)(2,1)S(1)}, u32[]{:S(2)}, u32[]{:S(2)}) collective-permute-start(bf16[2,816,128]{2,1,0:T(8,128)(2,1)S(1)} %get-tuple-element.572), channel_id=1, source_target_pairs={{0,1},{1,0},{2,3},{3,2},{4,5},{5,4},{6,7},{7,6},{8,9},{9,8},{10,11... | collective-permute-start | bytes 1253384 | tf_op jit(solution)/shard_map/ppermute | solution.py:884
  303.1 11.1 %collective-permute-start.107 = (bf16[2,768,128]{2,1,0:T(8,128)(2,1)S(1)}, bf16[2,768,128]{2,1,0:T(8,128)(2,1)S(1)}, u32[]{:S(2)}, u32[]{:S(2)}) collective-permute-start(bf16[2,768,128]{2,1,0:T(8,128)(2,1)S(1)} %collective-permute-done.102.refs_4_), channel_id=1, source_target_pairs={{0,4},{1,5},{4,8},{5,9},{8,12},{9,13},{12,14},{13,15},{14,10},{15,... | collective-permute-start | bytes 1179656 | tf_op jit(solution)/shard_map/ppermute | solution.py:878
  304.5 10.8 %collective-permute-start.108 = (bf16[2,768,128]{2,1,0:T(8,128)(2,1)S(1)}, bf16[2,768,128]{2,1,0:T(8,128)(2,1)S(1)}, u32[]{:S(2)}, u32[]{:S(2)}) collective-permute-start(bf16[2,768,128]{2,1,0:T(8,128)(2,1)S(1)} %collective-permute-done.103.refs_5_), channel_id=1, source_target_pairs={{0,2},{1,3},{4,0},{5,1},{8,4},{9,5},{12,8},{13,9},{14,12},{15,13},... | collective-permute-start | bytes 1179656 | tf_op jit(solution)/shard_map/ppermute | solution.py:881
  343.5 11.3 %collective-permute-start.127 = (bf16[2,816,128]{2,1,0:T(8,128)(2,1)S(1)}, bf16[2,816,128]{2,1,0:T(8,128)(2,1)S(1)}, u32[]{:S(2)}, u32[]{:S(2)}) collective-permute-start(bf16[2,816,128]{2,1,0:T(8,128)(2,1)S(1)} %pad_maximum_fusion.1), channel_id=1, source_target_pairs={{0,2},{1,3},{4,0},{5,1},{8,4},{9,5},{12,8},{13,9},{14,12},{15,13},... | collective-permute-start | bytes 1253384 | tf_op jit(solution)/shard_map/ppermute | solution.py:881
  344.1 11.0 %collective-permute-start.128 = (bf16[2,816,128]{2,1,0:T(8,128)(2,1)S(1)}, bf16[2,816,128]{2,1,0:T(8,128)(2,1)S(1)}, u32[]{:S(2)}, u32[]{:S(2)}) collective-permute-start(bf16[2,816,128]{2,1,0:T(8,128)(2,1)S(1)} %pad_maximum_fusion.2), channel_id=1, source_target_pairs={{0,4},{1,5},{4,8},{5,9},{8,12},{9,13},{12,14},{13,15},{14,10},{15,... | collective-permute-start | bytes 1253384 | tf_op jit(solution)/shard_map/ppermute | solution.py:878
  405.3 12.1 %collective-permute-start.144 = (bf16[32,3200]{1,0:T(8,128)(2,1)}, bf16[32,3200]{1,0:T(8,128)(2,1)}, u32[]{:S(2)}, u32[]{:S(2)}) collective-permute-start(bf16[32,3200]{1,0:T(8,128)(2,1)} %get-tuple-element.676), channel_id=1, source_target_pairs={{0,2},{1,3},{4,0},{5,1},{8,4},{9,5},{12,8},{13,9},{14,12},{15,13},... | collective-permute-start | bytes 614408 | tf_op jit(solution)/shard_map/ppermute | solution.py:881
  406.0 11.4 %collective-permute-start.145 = (bf16[32,3200]{1,0:T(8,128)(2,1)}, bf16[32,3200]{1,0:T(8,128)(2,1)}, u32[]{:S(2)}, u32[]{:S(2)}) collective-permute-start(bf16[32,3200]{1,0:T(8,128)(2,1)} %get-tuple-element.677), channel_id=1, source_target_pairs={{0,4},{1,5},{4,8},{5,9},{8,12},{9,13},{12,14},{13,15},{14,10},{15,... | collective-permute-start | bytes 614408 | tf_op jit(solution)/shard_map/ppermute | solution.py:878
  420.7 14.7 %collective-permute-start.137 = (bf16[64,3200]{1,0:T(8,128)(2,1)}, bf16[64,3200]{1,0:T(8,128)(2,1)S(1)}, u32[]{:S(2)}, u32[]{:S(2)}) collective-permute-start(bf16[64,3200]{1,0:T(8,128)(2,1)} %copy-done.30), channel_id=1, source_target_pairs={{0,1},{1,0},{2,3},{3,2},{4,5},{5,4},{6,7},{7,6},{8,9},{9,8},{10,11... | collective-permute-start | bytes 1228808 | tf_op jit(solution)/shard_map/ppermute | solution.py:884
  (161 other events, 1894.7 us)

commit v5 on v4

--- a/solution.py
+++ b/solution.py
@@ -393,7 +393,8 @@
     w_vmem, rest = rest[0], rest[1:]
     loads = [None] * 3
     if with_grads:
-        grad_ref, big_refs, rest = rest[0], rest[1:11], rest[11:]
+        second_ref, first_ref, grad_ref, section_ref, rest = rest[0], rest[1], rest[2], rest[3], rest[4:]
+        big_refs, rest = rest[:10], rest[10:]
         back_ref, gains_ref, w_scratch, k_scratch, v_scratch, sems = rest
         for part in (2, 1, 0):
             columns = pl.ds(PARTS[part][0], PARTS[part][1] - PARTS[part][0])
@@ -415,13 +416,17 @@
     gain_attn, gain_moe = gains_of(w_vmem)
     gate = gate_ref[...]
     tiles = length * TILES
-    high_low = jnp.concatenate([unfold(sum_ref[s, tiles:]) for s in range(seqs)], axis=0)
+    sums = [sum_ref[s] for s in range(seqs)]
+    if with_grads:
+        lower = order[2, 0] == 0
+        sums = [jnp.where(lower, a, second_ref[s]) for s, a in enumerate(sums)]
+    high_low = jnp.concatenate([unfold(a[tiles:]) for a in sums], axis=0)
     grad_gate = high_low + pltpu.roll(high_low, 96, 1)
     inner = jnp.sum(gate * grad_gate, axis=-1, keepdims=True)
     grad_logits = jnp.where(lanes_of(gate.shape) < 32, gate * (grad_gate - inner), 0.0)
     grad_logits = grad_logits.astype(bf16)
     w_small = w_vmem[:, :, QKV + D :].reshape(D, LANES)
-    summed = jnp.concatenate([plain(sum_ref[s, :tiles]) for s in range(seqs)], axis=0)
+    summed = jnp.concatenate([plain(a[:tiles]) for a in sums], axis=0)
     grad_normed_moe = summed + nt(grad_logits, w_small)
     resid = resid_ref[...]
     inv_moe = rms(resid)
@@ -477,6 +482,18 @@
     grad_in = grad_resid + norm_back(x, inv_attn, gain_attn, grad_normed)
     if with_grads:
         grad_ref[...] = grad_in.astype(bf16).reshape(seqs, length, D)
+
+        @pl.when(lower)
+        def _():
+            for s in range(seqs):
+                section_ref[s] = plain(first_ref[s])
+
+        @pl.when(jnp.logical_not(lower))
+        def _():
+            for s in range(seqs):
+                top = slice(s * length, (s + 1) * length)
+                section_ref[s] = (resid_ref[top] + plain(sum_ref[s, :tiles])).astype(bf16)
+
     else:
         for s in range(seqs):
             store_tiles(grad_ref, s, grad_in[s * length : (s + 1) * length])
@@ -525,7 +542,7 @@
                 big_refs[5 + n][place, columns] = other.astype(bf16)
 
 
-def attn_backward(with_grads, order, sums, g, saved, table, w_all):
+def attn_backward(with_grads, order, sums, g, saved, table, w_all, others=()):
     payload, resid, x, gate, normed, q, k, v, probs, mixed = saved
     late = hbm if with_grads else vmem
     seqs, length = x.shape[0], x.shape[1]
@@ -534,6 +551,7 @@
     outs = [shape((seqs, length, D) if with_grads else (seqs, length * TILES, LANES), bf16)]
     scratch = [pltpu.VMEM((rows, QKV), bf16)]
     if with_grads:
+        outs.append(shape((seqs, length, D), bf16))
         outs += [shape((n, WCOLS), bf16) for n in (64, 128, 128, 128, 64)] * 2
         scratch += [
             pltpu.VMEM((8, D), f32),
@@ -545,7 +563,7 @@
     return pl.pallas_call(
         functools.partial(attn_backward_kernel, with_grads),
         out_shape=outs,
-        in_specs=[smem()] + [vmem()] * 8 + [late()] * 2 + [vmem()] * 3 + [late()],
+        in_specs=[smem()] + [vmem()] * 8 + [late()] * 2 + [vmem()] * 3 + [late()] + [vmem()] * len(others),
         out_specs=[vmem()] * len(outs),
         scratch_shapes=scratch,
         compiler_params=pltpu.CompilerParams(vmem_limit_bytes=VMEM_LIMIT),
@@ -558,6 +576,7 @@
         *(sums, g, x, payload, resid, gate, normed, q),
         *((in_hbm(k), in_hbm(v)) if with_grads else (k, v)),
         *(probs, mixed, table, (in_hbm if with_grads else in_vmem)(w_all)),
+        *others,
     )
 
 
@@ -924,7 +943,7 @@
         out += [both(a) for a in behind[:0:-1]]
         return sum(out, []), beside
 
-    def scatter_halves(self, terms):
+    def scatter_halves(self, terms, beside=(), work=None):
         half = terms[4][0][0].shape[0]
         came = [[[], []], [[], []]]
         last = ()
@@ -933,7 +952,13 @@
                 low, high = c * half, (c + 1) * half
                 whole = lambda values: [(a, 0, half) for a in values]
                 part = lambda values: [(a, low, high) for a in values]
-                came[c], last = lax.optimization_barrier((came[c], last))
+                if r == 1 and c == 0:
+                    if work:
+                        beside, last = lax.optimization_barrier((beside, last))
+                        beside = work(beside)
+                    came[c], last, beside = lax.optimization_barrier((came[c], last, beside))
+                else:
+                    came[c], last = lax.optimization_barrier((came[c], last))
                 if r == 0:
                     last = add_call([whole(terms[4][c])])
                 else:
@@ -948,30 +973,7 @@
         return [
             [(a, c * half, (c + 1) * half) for a in terms[0][0]] + [(a, 0, half) for a in sum(came[c], [])]
             for c in range(2)
-        ]
-
-    def scatter(self, terms, work=()):
-        work, beside = list(work), ()
-        out = [total(values).astype(bf16) for values in terms[4]]
-        half = out[0].shape[0]
-        for k in (3, 2, 1, 0):
-            up, down = lax.optimization_barrier((out[0], out[1]))
-            up, down = self.minus(up), self.plus(down)
-            if len(work) > 0 and k < 3:
-                up, down, beside = lax.optimization_barrier((up, down, work.pop(0)(beside)))
-            if k == 0:
-                return list(terms[0][0]) + [up, down], beside
-            behind, ahead = terms[k]
-            if k == 3:
-                upper = lambda values: [a[:half] for a in values]
-                lower = lambda values: [a[half:] for a in values]
-                out = [
-                    jnp.concatenate([total(upper(behind) + [up]), total(lower(behind))]),
-                    jnp.concatenate([total(upper(ahead)), total(lower(ahead) + [down])]),
-                ]
-            else:
-                out = [total(list(behind) + [up]), total(list(ahead) + [down])]
-            out = [a.astype(bf16) for a in out]
+        ], beside
 
 
 def total(values):
@@ -1049,13 +1051,14 @@
                 return expert_call(mode, which, x, beside, w_in, w_down, per)
 
             terms, saved = ring.gather(own, work)
-            last = [functools.partial(weight_grads, saved, hid, per, j) for j in range(per)]
+            grads = ()
             if mode == 2:
-                sums, grads = ring.scatter(terms, last)
-                return total(sums), seen, grads
-            sums = ring.scatter_halves(terms)
+                grads = weight_grads(saved, hid, per, 0)
+            sums, grads = ring.scatter_halves(terms, grads)
+            if mode == 2:
+                grads = (saved, grads)
             sums = [total([a[low:high] for a, low, high in half]) for half in sums]
-            return jnp.concatenate(sums), seen, ()
+            return jnp.concatenate(sums), seen, grads
 
         every = gather_rows(own)
         x_all, g_all = (every, g) if x_groups is None else (x_groups, every)
@@ -1084,17 +1087,10 @@
     (grad_second,) = attn_backward(False, order, sums_second, cotangent, saved, table, w_all)
 
     g_third = lax.ppermute(grad_second, "section", [(0, 1), (1, 0)])
-    sums_third, _, (grad_in, grad_down) = phase(2, g_third, None, rows_all)
-    tiles = length * TILES
-
-    def rows_of(array):
-        array = array.reshape(seqs, length // TILE, TILES, TILE, LANES)
-        return jnp.swapaxes(array, 2, 3).reshape(seqs, length, D)
-
-    second_out = (resid.reshape(seqs, length, D) + rows_of(sums_third[:, :tiles])).astype(bf16)
-    section_out = jnp.where(first_section, rows_of(first_out), second_out)
-    sums = jnp.where(first_section, sums_third, sums_second)
-    section_grad, *big = attn_backward(True, order, sums, g_third, saved, table, w_all)
+    sums_third, _, grads = phase(2, g_third, None, rows_all)
+    section_grad, section_out, *big = attn_backward(
+        True, order, sums_third, g_third, saved, table, w_all, (sums_second, first_out)
+    )
 
     if ringed:
         pairs, came = [None] * 5, ()
@@ -1106,7 +1102,15 @@
         terms = [[pairs[0]]]
         terms += [[part(pair, 0, 64), part(pair, 64, 128)] for pair in pairs[1:4]]
         terms += [[part(pairs[4], 0, 32), part(pairs[4], 32, 64)]]
-        g_qkv, g_out, g_router, g_gain_attn, g_gain_moe = last_sum(ring.scatter_halves(terms))
+
+        def other_experts(given):
+            saved_rows, done = given
+            for j in range(1, per):
+                done = weight_grads(saved_rows, hid, per, j, done)
+            return done
+
+        halves_of, grads = ring.scatter_halves(terms, grads, other_experts)
+        g_qkv, g_out, g_router, g_gain_attn, g_gain_moe = last_sum(halves_of)
         g_gain_attn, g_gain_moe = g_gain_attn[0], g_gain_moe[0]
     else:
         chips = [(big[0], big[5])] + [(big[k][64:], big[5 + k][64:]) for k in (1, 2, 3)]
@@ -1119,6 +1123,7 @@
         gains = small.reshape(16, 64, LANES)
         g_gain_attn = sum_up(gains[:, 0, 64:].reshape(D))
         g_gain_moe = sum_up(gains[:, 1, 64:].reshape(D))
+    grad_in, grad_down = grads
     return (
         section_out[None],
         section_grad[None],

time: 446 us -> 443 us (level)
  local copies, waits for them, and re-layouts: 19.8 us -> 11.3 us
  starting transfers between devices: 104 us -> 112 us
  waiting for transfers between devices: 164 us -> 169 us
  other arithmetic: 7.32 us -> 2.7 us
    ppermute x41 -> x44, waiting for transfers between devices: 63.1 us -> 88.9 us  [minus(): return lax.ppermute(a, 'fsdp', self.behind)]
    ppermute x41 -> x44, starting transfers between devices: 39 us -> 58.7 us  [minus(): return lax.ppermute(a, 'fsdp', self.behind)]
    ppermute x41 -> x44, waiting for transfers between devices: 77.8 us -> 58.9 us  [plus(): return lax.ppermute(a, 'fsdp', self.ahead)]
    ppermute x41 -> x44, starting transfers between devices: 48.4 us -> 36.4 us  [plus(): return lax.ppermute(a, 'fsdp', self.ahead)]
  transfers between devices with their start and end apart: 152 -> 158, of which waited for: 88 -> 94; matrix products, arithmetic and copies ran while one was open for 4% -> 2% of each run, Pallas kernels for 20% -> 19%
where the time goes in v5:
time: 443 us; the launch traced here: 435 us
  waiting for transfers between devices  169 us (38%)
  Pallas kernels  136 us (31%)
  starting transfers between devices  112 us (25%)
  local copies, waits for them, and re-layouts  11.3 us (3%)
    ppermute x44, waiting for transfers between devices, minus(): return lax.ppermute(a, 'fsdp', self.behind)  88.9 us
    pallas_call x15, Pallas kernels, expert_call(): pl.pallas_call(body, out_shape=outs, in_specs=[smem()] + [vmem()] * (part...  80.3 us
    ppermute x44, waiting for transfers between devices, plus(): return lax.ppermute(a, 'fsdp', self.ahead)  58.9 us
    ppermute x44, starting transfers between devices, minus(): return lax.ppermute(a, 'fsdp', self.behind)  58.7 us
    ppermute x44, starting transfers between devices, plus(): return lax.ppermute(a, 'fsdp', self.ahead)  36.4 us
    pallas_call x2, Pallas kernels, attn_backward(): pl.pallas_call(functools.partial(attn_backward_kernel, with_grads), out_s...  21.8 us
    pallas_call x2, Pallas kernels, attn_forward(): pl.pallas_call(functools.partial(attn_forward_kernel, save), out_shape=ou...  15 us
    ppermute x68, starting transfers between devices, swap(): return lax.ppermute(a, 'fsdp', self.core)  14 us
  transfers between devices with their start and end apart: 158, of which 94 were waited for; matrix products, arithmetic and copies ran while one was open for 2% of the time, Pallas kernels for 19%

profile of v5, /device:TPU:0, one launch (start us, length us, event | category | flops | bytes accessed | tf_op | source)
XLA Modules:
  0.0 434.9 jit_solution(1612241060115987143)
XLA Ops:
  10.5 5.4 %collective-permute-done.1.refs_4_ = bf16[64,3200]{1,0:T(8,128)(2,1)S(1)} collective-permute-done((bf16[64,3200]{1,0:T(8,128)(2,1)S(1)}, bf16[64,3200]{1,0:T(8,128)(2,1)S(1)}, u32[]{:S(2)}, u32[]{:S(2)}) %collective-permute-start.1) | collective-permute-done | bytes 409632 | tf_op jit(solution)/shard_map/ppermute | solution.py:900
  22.0 5.4 %collective-permute-done.2.refs_16_ = bf16[64,3200]{1,0:T(8,128)(2,1)} collective-permute-done((bf16[64,3200]{1,0:T(8,128)(2,1)S(1)}, bf16[64,3200]{1,0:T(8,128)(2,1)}, u32[]{:S(2)}, u32[]{:S(2)}) %collective-permute-start.2) | collective-permute-done | bytes 409632 | tf_op jit(solution)/shard_map/ppermute | solution.py:897
  30.4 6.8 %collective-permute-done.8.refs_8_ = bf16[64,3200]{1,0:T(8,128)(2,1)S(1)} collective-permute-done((bf16[64,3200]{1,0:T(8,128)(2,1)}, bf16[64,3200]{1,0:T(8,128)(2,1)S(1)}, u32[]{:S(2)}, u32[]{:S(2)}) %collective-permute-start.8) | collective-permute-done | bytes 409632 | tf_op jit(solution)/shard_map/ppermute | solution.py:900
  40.7 4.9 %collective-permute-done.10.refs_10_ = bf16[32,3200]{1,0:T(8,128)(2,1)S(1)} collective-permute-done((bf16[32,3200]{1,0:T(8,128)(2,1)S(1)}, bf16[32,3200]{1,0:T(8,128)(2,1)S(1)}, u32[]{:S(2)}, u32[]{:S(2)}) %collective-permute-start.10) | collective-permute-done | bytes 204832 | tf_op jit(solution)/shard_map/ppermute | solution.py:897
  48.7 8.6 %attn_forward.2 = (bf16[2,816,128]{2,1,0:T(8,128)(2,1)S(1)}, f32[2,768,128]{2,1,0:T(8,128)}, bf16[16,64,3200]{2,1,0:T(8,128)(2,1)}) custom-call(s32[4,8]{1,0:T(4,128)S(1)} %pad_add_fusion.order, f32[96,256]{1,0:T(8,128)} %constant.78.clone.table_hbm.table_ref, f32[192,128]{1,0:T(8,128)} %bitcast.67, bf16[2,96,1024]{2,1,0:T(8,128)(2,1)} %refs_0_.3, ...), custom_call_target="tpu_custom_call" | custom-call | flops 1336934400 | bytes 12000000 | tf_op jit(solution)/shard_map/attn_forward/pallas_call | solution.py:361
  65.5 4.0 collective-permute-done.18.refs_1_.refs_5_
  73.2 5.1 %experts_0.6 = (bf16[2,768,128]{2,1,0:T(8,128)(2,1)S(1)}, bf16[2,768,128]{2,1,0:T(8,128)(2,1)S(1)}, bf16[2,768,128]{2,1,0:T(8,128)(2,1)S(1)}, bf16[2,768,128]{2,1,0:T(8,128)(2,1)S(1)}) custom-call(s32[2]{0:T(128)S(1)} %pad_add_fusion.1.which, bf16[2,816,128]{2,1,0:T(8,128)(2,1)} %collective-permute-done.17.refs_0_.refs_4_, ...), custom_call_target="tpu_custom_call" | custom-call | flops 1610612736 | bytes 9145728 | tf_op jit(solution)/shard_map/experts_0/pallas_call | solution.py:722
  78.3 4.5 %collective-permute-done.20.refs_0_.refs_4_ = bf16[2,816,128]{2,1,0:T(8,128)(2,1)S(1)} collective-permute-done((bf16[2,816,128]{2,1,0:T(8,128)(2,1)}, bf16[2,816,128]{2,1,0:T(8,128)(2,1)S(1)}, u32[]{:S(2)}, u32[]{:S(2)}) %collective-permute-start.20) | collective-permute-done | bytes 417824 | tf_op jit(solution)/shard_map/ppermute | solution.py:897
  86.3 4.6 %experts_0.7 = (bf16[2,768,128]{2,1,0:T(8,128)(2,1)S(1)}, bf16[2,768,128]{2,1,0:T(8,128)(2,1)S(1)}, bf16[2,768,128]{2,1,0:T(8,128)(2,1)S(1)}, bf16[2,768,128]{2,1,0:T(8,128)(2,1)S(1)}) custom-call(s32[2]{0:T(128)S(1)} %pad_add_fusion.1.which, bf16[2,816,128]{2,1,0:T(8,128)(2,1)S(1)} %collective-permute-done.20.refs_0_.refs_4_, ...), custom_call_target="tpu_custom_call" | custom-call | flops 1610612736 | bytes 9145728 | tf_op jit(solution)/shard_map/experts_0/pallas_call | solution.py:722
  91.0 4.4 %collective-permute-done.25.refs_0_.refs_4_ = bf16[2,816,128]{2,1,0:T(8,128)(2,1)S(1)} collective-permute-done((bf16[2,816,128]{2,1,0:T(8,128)(2,1)S(1)}, bf16[2,816,128]{2,1,0:T(8,128)(2,1)S(1)}, u32[]{:S(2)}, u32[]{:S(2)}) %collective-permute-start.25) | collective-permute-done | bytes 417824 | tf_op jit(solution)/shard_map/ppermute | solution.py:897
  99.7 4.6 %experts_0.8 = (bf16[2,768,128]{2,1,0:T(8,128)(2,1)S(1)}, bf16[2,768,128]{2,1,0:T(8,128)(2,1)S(1)}, bf16[2,768,128]{2,1,0:T(8,128)(2,1)S(1)}, bf16[2,768,128]{2,1,0:T(8,128)(2,1)S(1)}) custom-call(s32[2]{0:T(128)S(1)} %pad_add_fusion.1.which, bf16[2,816,128]{2,1,0:T(8,128)(2,1)S(1)} %collective-permute-done.25.refs_0_.refs_4_, ...), custom_call_target="tpu_custom_call" | custom-call | flops 1610612736 | bytes 9145728 | tf_op jit(solution)/shard_map/experts_0/pallas_call | solution.py:722
  151.2 6.3 %collective-permute-done.57.refs_1_ = bf16[2,768,128]{2,1,0:T(8,128)(2,1)S(1)} collective-permute-done((bf16[2,768,128]{2,1,0:T(8,128)(2,1)S(1)}, bf16[2,768,128]{2,1,0:T(8,128)(2,1)S(1)}, u32[]{:S(2)}, u32[]{:S(2)}) %collective-permute-start.57) | collective-permute-done | bytes 393248 | tf_op jit(solution)/shard_map/ppermute | solution.py:1083
  158.2 6.4 %attn_forward.3 = (bf16[2,816,128]{2,1,0:T(8,128)(2,1)S(1)}, f32[192,1024]{1,0:T(8,128)S(1)}, bf16[2,96,1024]{2,1,0:T(8,128)(2,1)S(1)}, f32[192,128]{1,0:T(8,128...) custom-call(s32[4,8]{1,0:T(4,128)S(1)} %pad_add_fusion.order, ...), custom_call_target="tpu_custom_call" | custom-call | flops 1336934400 | bytes 12000000 | tf_op jit(solution)/shard_map/attn_forward/pallas_call | solution.py:361
  166.8 4.7 %experts_1.5 = (bf16[2,816,128]{2,1,0:T(8,128)(2,1)S(1)}, bf16[2,816,128]{2,1,0:T(8,128)(2,1)S(1)}) custom-call(s32[2]{0:T(128)S(1)} %pad_add_fusion.1.which, bf16[2,816,128]{2,1,0:T(8,128)(2,1)S(1)} %get-tuple-element.484.refs_0_.wide_ref, bf16[2,816,128]{2,1,0:T(8,128)(2,1)S(1)} %collective-permute-done.60.refs_1_, ...), custom_call_target="tpu_custom_call" | custom-call | flops 1342177280 | bytes 7572864 | tf_op jit(solution)/shard_map/experts_1/pallas_call | solution.py:722
  171.5 5.3 %collective-permute-done.59.refs_1_ = bf16[2,816,128]{2,1,0:T(8,128)(2,1)S(1)} collective-permute-done((bf16[2,816,128]{2,1,0:T(8,128)(2,1)S(1)}, bf16[2,816,128]{2,1,0:T(8,128)(2,1)S(1)}, u32[]{:S(2)}, u32[]{:S(2)}) %collective-permute-start.59) | collective-permute-done | bytes 417824 | tf_op jit(solution)/shard_map/ppermute | solution.py:900
  180.7 6.7 %experts_1.6 = (bf16[2,816,128]{2,1,0:T(8,128)(2,1)S(1)}, bf16[2,816,128]{2,1,0:T(8,128)(2,1)S(1)}, bf16[2,816,128]{2,1,0:T(8,128)(2,1)S(1)}, bf16[2,816,128]{2,1,0:T(8,128)(2,1)S(1)}) custom-call(s32[2]{0:T(128)S(1)} %pad_add_fusion.1.which, bf16[2,816,128]{2,1,0:T(8,128)(2,1)S(1)} %collective-permute-done.58.refs_0_, ...), custom_call_target="tpu_custom_call" | custom-call | flops 2684354560 | bytes 9145728 | tf_op jit(solution)/shard_map/experts_1/pallas_call | solution.py:722
  194.3 6.2 %experts_1.7 = (bf16[2,816,128]{2,1,0:T(8,128)(2,1)S(1)}, bf16[2,816,128]{2,1,0:T(8,128)(2,1)S(1)}, bf16[2,816,128]{2,1,0:T(8,128)(2,1)S(1)}, bf16[2,816,128]{2,1,0:T(8,128)(2,1)S(1)}) custom-call(s32[2]{0:T(128)S(1)} %pad_add_fusion.1.which, bf16[2,816,128]{2,1,0:T(8,128)(2,1)S(1)} %collective-permute-done.61.refs_0_, ...), custom_call_target="tpu_custom_call" | custom-call | flops 2684354560 | bytes 9145728 | tf_op jit(solution)/shard_map/experts_1/pallas_call | solution.py:722
  207.9 6.2 %experts_1.8 = (bf16[2,816,128]{2,1,0:T(8,128)(2,1)S(1)}, bf16[2,816,128]{2,1,0:T(8,128)(2,1)S(1)}, bf16[2,816,128]{2,1,0:T(8,128)(2,1)S(1)}, bf16[2,816,128]{2,1,0:T(8,128)(2,1)S(1)}) custom-call(s32[2]{0:T(128)S(1)} %pad_add_fusion.1.which, bf16[2,816,128]{2,1,0:T(8,128)(2,1)S(1)} %collective-permute-done.66.refs_0_, ...), custom_call_target="tpu_custom_call" | custom-call | flops 2684354560 | bytes 9145728 | tf_op jit(solution)/shard_map/experts_1/pallas_call | solution.py:722
  216.0 4.7 %experts_1.9 = (bf16[1,816,128]{2,1,0:T(8,128)(2,1)S(1)}, bf16[1,816,128]{2,1,0:T(8,128)(2,1)S(1)}, bf16[1,816,128]{2,1,0:T(8,128)(2,1)S(1)}, bf16[1,816,128]{2,1,0:T(8,128)(2,1)S(1)}) custom-call(s32[2]{0:T(128)S(1)} %pad_add_fusion.1.which, bf16[1,816,128]{2,1,0:T(8,128)(2,1)S(1)} %collective-permute-done.72.refs_0_, ...), custom_call_target="tpu_custom_call" | custom-call | flops 1342177280 | bytes 7572864 | tf_op jit(solution)/shard_map/experts_1/pallas_call | solution.py:722
  224.8 4.7 %collective-permute-done.82.refs_2_ = bf16[1,816,128]{2,1,0:T(8,128)(2,1)S(1)} collective-permute-done((bf16[1,816,128]{2,1,0:T(8,128)(2,1)S(1)}, bf16[1,816,128]{2,1,0:T(8,128)(2,1)S(1)}, u32[]{:S(2)}, u32[]{:S(2)}) %collective-permute-start.82) | collective-permute-done | bytes 208928 | tf_op jit(solution)/shard_map/ppermute | solution.py:900
  234.0 3.9 collective-permute-done.85.refs_2_
  261.4 8.4 %attn_backward.2 = bf16[2,768,128]{2,1,0:T(8,128)(2,1)S(1)} custom-call(s32[4,8]{1,0:T(4,128)S(1)} %pad_add_fusion.order, f32[2,816,128]{2,1,0:T(8,128)S(1)} %pad_maximum_fusion.sum_ref.rest_1_, bf16[2,96,1024]{2,1,0:T(8,128)(2,1)S(1)} %copy-done.4, bf16[2,96,1024]{2,1,0:T(8,128)(2,1)S(1)} %get-tuple-element.565.x_ref, ...), custom_call_target="tpu_custom_call" | custom-call | flops 2673868800 | bytes 20000000 | tf_op jit(solution)/shard_map/attn_backward/pallas_call | solution.py:563
  271.2 6.3 %collective-permute-done.98.refs_2_.g_ref = bf16[2,768,128]{2,1,0:T(8,128)(2,1)S(1)} collective-permute-done((bf16[2,768,128]{2,1,0:T(8,128)(2,1)S(1)}, bf16[2,768,128]{2,1,0:T(8,128)(2,1)S(1)}, u32[]{:S(2)}, u32[]{:S(2)}) %collective-permute-start.98) | collective-permute-done | bytes 393248 | tf_op jit(solution)/shard_map/ppermute | solution.py:1089
  279.6 5.1 %experts_2.5 = (bf16[2,816,128]{2,1,0:T(8,128)(2,1)S(1)}, bf16[2,816,128]{2,1,0:T(8,128)(2,1)S(1)}, bf16[2,128,1024]{2,1,0:T(8,128)(2,1)}, bf16[2,128,1024]{2,1,...) custom-call(s32[2]{0:T(128)S(1)} %pad_add_fusion.1.which, ...), custom_call_target="tpu_custom_call" | custom-call | flops 1342177280 | bytes 7572864 | tf_op jit(solution)/shard_map/experts_2/pallas_call | solution.py:722
  284.7 4.4 %collective-permute-done.100.refs_5_ = bf16[2,768,128]{2,1,0:T(8,128)(2,1)S(1)} collective-permute-done((bf16[2,768,128]{2,1,0:T(8,128)(2,1)S(1)}, bf16[2,768,128]{2,1,0:T(8,128)(2,1)S(1)}, u32[]{:S(2)}, u32[]{:S(2)}) %collective-permute-start.100) | collective-permute-done | bytes 393248 | tf_op jit(solution)/shard_map/ppermute | solution.py:900
  293.4 6.7 %experts_2.6 = (bf16[2,816,128]{2,1,0:T(8,128)(2,1)S(1)}, bf16[2,816,128]{2,1,0:T(8,128)(2,1)S(1)}, bf16[2,816,128]{2,1,0:T(8,128)(2,1)S(1)}, bf16[2,816,128]{2,...) custom-call(s32[2]{0:T(128)S(1)} %pad_add_fusion.1.which, ...), custom_call_target="tpu_custom_call" | custom-call | flops 2684354560 | bytes 9145728 | tf_op jit(solution)/shard_map/experts_2/pallas_call | solution.py:722
  306.4 6.7 %experts_2.7 = (bf16[2,816,128]{2,1,0:T(8,128)(2,1)S(1)}, bf16[2,816,128]{2,1,0:T(8,128)(2,1)S(1)}, bf16[2,816,128]{2,1,0:T(8,128)(2,1)S(1)}, bf16[2,816,128]{2,...) custom-call(s32[2]{0:T(128)S(1)} %pad_add_fusion.1.which, ...), custom_call_target="tpu_custom_call" | custom-call | flops 2684354560 | bytes 9145728 | tf_op jit(solution)/shard_map/experts_2/pallas_call | solution.py:722
  319.2 6.7 %experts_2.8 = (bf16[2,816,128]{2,1,0:T(8,128)(2,1)S(1)}, bf16[2,816,128]{2,1,0:T(8,128)(2,1)S(1)}, bf16[2,816,128]{2,1,0:T(8,128)(2,1)S(1)}, bf16[2,816,128]{2,...) custom-call(s32[2]{0:T(128)S(1)} %pad_add_fusion.1.which, ...), custom_call_target="tpu_custom_call" | custom-call | flops 2684354560 | bytes 9145728 | tf_op jit(solution)/shard_map/experts_2/pallas_call | solution.py:722
  327.8 5.1 %experts_2.9 = (bf16[1,816,128]{2,1,0:T(8,128)(2,1)S(1)}, bf16[1,816,128]{2,1,0:T(8,128)(2,1)S(1)}, bf16[1,816,128]{2,1,0:T(8,128)(2,1)S(1)}, bf16[1,816,128]{2,...) custom-call(s32[2]{0:T(128)S(1)} %pad_add_fusion.1.which, ...), custom_call_target="tpu_custom_call" | custom-call | flops 1342177280 | bytes 7572864 | tf_op jit(solution)/shard_map/experts_2/pallas_call | solution.py:722
  336.9 7.0 %weight_grads_0.1 = (f32[1024,2048]{1,0:T(8,128)}, f32[1024,1024]{1,0:T(8,128)}) custom-call(bf16[2,128,1024]{2,1,0:T(8,128)(2,1)} %get-tuple-element.719.refs_0_, bf16[2,128,1024]{2,1,0:T(8,128)(2,1)} %get-tuple-element.720.refs_1_, bf16[2,128,512]{2,1,0:T(8,128)(2,1)} %get-tuple-element.721.refs_2_, bf16[2,128,512]{2,1,0:T(8,128)(2,1)} %get-tuple-element.722.refs_3_, ...), custom_call_target="tpu_custom_call" | custom-call | flops 3221225472 | bytes 14000000 | tf_op jit(solution)/shard_map/weight_grads_0/pallas_call | solution.py:793
  376.8 13.4 %attn_backward.3 = (bf16[2,96,1024]{2,1,0:T(8,128)(2,1)}, bf16[2,96,1024]{2,1,0:T(8,128)(2,1)}, bf16[64,3200]{1,0:T(8,128)(2,1)S(1)}, bf16[128,3200]{1,0:T(8,128...) custom-call(s32[4,8]{1,0:T(4,128)S(1)} %pad_add_fusion.order, ...), custom_call_target="tpu_custom_call" | custom-call | flops 2673868800 | bytes 20000000 | tf_op jit(solution)/shard_map/attn_backward/pallas_call | solution.py:563
  394.4 7.0 %weight_grads_1.1 = (f32[1024,2048]{1,0:T(8,128)}, f32[1024,1024]{1,0:T(8,128)}) custom-call(bf16[2,128,1024]{2,1,0:T(8,128)(2,1)} %get-tuple-element.719.refs_0_, bf16[2,128,1024]{2,1,0:T(8,128)(2,1)} %get-tuple-element.720.refs_1_, bf16[2,128,512]{2,1,0:T(8,128)(2,1)} %get-tuple-element.721.refs_2_, ...), custom_call_target="tpu_custom_call", output_to_operand_aliasing={{0}: (25, {}), {1}: (26, {})} | custom-call | flops 3221225472 | bytes 14000000 | tf_op jit(solution)/shard_map/weight_grads_1/pallas_call | solution.py:793
  (406 shorter events, 243.0 us)
Async XLA Ops:
  3.4 12.5 %collective-permute-start.1 = (bf16[64,3200]{1,0:T(8,128)(2,1)S(1)}, bf16[64,3200]{1,0:T(8,128)(2,1)S(1)}, u32[]{:S(2)}, u32[]{:S(2)}) collective-permute-start(bf16[64,3200]{1,0:T(8,128)(2,1)S(1)} %concatenate.19.refs_2_), channel_id=1, source_target_pairs={{0,2},{1,3},{4,0},{5,1},{8,4},{9,5},{12,8},{13,9},{14,12},{15,13},... | collective-permute-start | bytes 1228808 | tf_op jit(solution)/shard_map/ppermute | solution.py:900
  6.3 10.9 %collective-permute-start = (bf16[64,3200]{1,0:T(8,128)(2,1)S(1)}, bf16[64,3200]{1,0:T(8,128)(2,1)S(1)}, u32[]{:S(2)}, u32[]{:S(2)}) collective-permute-start(bf16[64,3200]{1,0:T(8,128)(2,1)S(1)} %concatenate.19.refs_2_), channel_id=1, source_target_pairs={{0,4},{1,5},{4,8},{5,9},{8,12},{9,13},{12,14},{13,15},{14,10},{15,... | collective-permute-start | bytes 1228808 | tf_op jit(solution)/shard_map/ppermute | solution.py:897
  17.7 10.2 %collective-permute-start.3 = (bf16[64,3200]{1,0:T(8,128)(2,1)S(1)}, bf16[64,3200]{1,0:T(8,128)(2,1)}, u32[]{:S(2)}, u32[]{:S(2)}) collective-permute-start(bf16[64,3200]{1,0:T(8,128)(2,1)S(1)} %collective-permute-done.1.refs_4_), channel_id=1, source_target_pairs={{0,2},{1,3},{4,0},{5,1},{8,4},{9,5},{12,8},{13,9},{14,12},{15,13},... | collective-permute-start | bytes 1228808 | tf_op jit(solution)/shard_map/ppermute | solution.py:900
  57.6 11.9 %collective-permute-start.18 = (bf16[2,816,128]{2,1,0:T(8,128)(2,1)S(1)}, bf16[2,816,128]{2,1,0:T(8,128)(2,1)S(1)}, u32[]{:S(2)}, u32[]{:S(2)}) collective-permute-start(bf16[2,816,128]{2,1,0:T(8,128)(2,1)S(1)} %get-tuple-element.402.refs_0_.refs_2_), channel_id=1, source_target_pairs={{0,2},{1,3},{4,0},{5,1},{8,4},{9,5},{12,8},{13,9},{14,12},{15,13},... | collective-permute-start | bytes 1253384 | tf_op jit(solution)/shard_map/ppermute | solution.py:900
  58.9 11.7 %collective-permute-start.17 = (bf16[2,816,128]{2,1,0:T(8,128)(2,1)S(1)}, bf16[2,816,128]{2,1,0:T(8,128)(2,1)}, u32[]{:S(2)}, u32[]{:S(2)}) collective-permute-start(bf16[2,816,128]{2,1,0:T(8,128)(2,1)S(1)} %get-tuple-element.402.refs_0_.refs_2_), channel_id=1, source_target_pairs={{0,4},{1,5},{4,8},{5,9},{8,12},{9,13},{12,14},{13,15},{14,10},{15,... | collective-permute-start | bytes 1253384 | tf_op jit(solution)/shard_map/ppermute | solution.py:897
  71.0 11.8 %collective-permute-start.20 = (bf16[2,816,128]{2,1,0:T(8,128)(2,1)}, bf16[2,816,128]{2,1,0:T(8,128)(2,1)S(1)}, u32[]{:S(2)}, u32[]{:S(2)}) collective-permute-start(bf16[2,816,128]{2,1,0:T(8,128)(2,1)} %collective-permute-done.17.refs_0_.refs_4_), channel_id=1, source_target_pairs={{0,4},{1,5},{4,8},{5,9},{8,12},{9,13},{12,14},{13,15},{14,10},{15,... | collective-permute-start | bytes 1253384 | tf_op jit(solution)/shard_map/ppermute | solution.py:897
  71.9 11.4 %collective-permute-start.21 = (bf16[2,816,128]{2,1,0:T(8,128)(2,1)S(1)}, bf16[2,816,128]{2,1,0:T(8,128)(2,1)S(1)}, u32[]{:S(2)}, u32[]{:S(2)}) collective-permute-start(bf16[2,816,128]{2,1,0:T(8,128)(2,1)S(1)} %collective-permute-done.18.refs_1_.refs_5_), channel_id=1, source_target_pairs={{0,2},{1,3},{4,0},{5,1},{8,4},{9,5},{12,8},{13,9},{14,12},{15,13},... | collective-permute-start | bytes 1253384 | tf_op jit(solution)/shard_map/ppermute | solution.py:900
  83.8 11.6 %collective-permute-start.25 = (bf16[2,816,128]{2,1,0:T(8,128)(2,1)S(1)}, bf16[2,816,128]{2,1,0:T(8,128)(2,1)S(1)}, u32[]{:S(2)}, u32[]{:S(2)}) collective-permute-start(bf16[2,816,128]{2,1,0:T(8,128)(2,1)S(1)} %collective-permute-done.20.refs_0_.refs_4_), channel_id=1, source_target_pairs={{0,4},{1,5},{4,8},{5,9},{8,12},{9,13},{12,14},{13,15},{14,10},{15,... | collective-permute-start | bytes 1253384 | tf_op jit(solution)/shard_map/ppermute | solution.py:897
  85.1 11.3 %collective-permute-start.26 = (bf16[2,816,128]{2,1,0:T(8,128)(2,1)S(1)}, bf16[2,816,128]{2,1,0:T(8,128)(2,1)S(1)}, u32[]{:S(2)}, u32[]{:S(2)}) collective-permute-start(bf16[2,816,128]{2,1,0:T(8,128)(2,1)S(1)} %collective-permute-done.21.refs_1_.refs_5_), channel_id=1, source_target_pairs={{0,2},{1,3},{4,0},{5,1},{8,4},{9,5},{12,8},{13,9},{14,12},{15,13},... | collective-permute-start | bytes 1253384 | tf_op jit(solution)/shard_map/ppermute | solution.py:900
  164.7 12.0 %collective-permute-start.59 = (bf16[2,816,128]{2,1,0:T(8,128)(2,1)S(1)}, bf16[2,816,128]{2,1,0:T(8,128)(2,1)S(1)}, u32[]{:S(2)}, u32[]{:S(2)}) collective-permute-start(bf16[2,816,128]{2,1,0:T(8,128)(2,1)S(1)} %get-tuple-element.484.refs_0_.wide_ref), channel_id=1, source_target_pairs={{0,2},{1,3},{4,0},{5,1},{8,4},{9,5},{12,8},{13,9},{14,12},{15,13},... | collective-permute-start | bytes 1253384 | tf_op jit(solution)/shard_map/ppermute | solution.py:900
  166.1 11.7 %collective-permute-start.58 = (bf16[2,816,128]{2,1,0:T(8,128)(2,1)S(1)}, bf16[2,816,128]{2,1,0:T(8,128)(2,1)S(1)}, u32[]{:S(2)}, u32[]{:S(2)}) collective-permute-start(bf16[2,816,128]{2,1,0:T(8,128)(2,1)S(1)} %get-tuple-element.484.refs_0_.wide_ref), channel_id=1, source_target_pairs={{0,4},{1,5},{4,8},{5,9},{8,12},{9,13},{12,14},{13,15},{14,10},{15,... | collective-permute-start | bytes 1253384 | tf_op jit(solution)/shard_map/ppermute | solution.py:897
  178.3 12.1 %collective-permute-start.61 = (bf16[2,816,128]{2,1,0:T(8,128)(2,1)S(1)}, bf16[2,816,128]{2,1,0:T(8,128)(2,1)S(1)}, u32[]{:S(2)}, u32[]{:S(2)}) collective-permute-start(bf16[2,816,128]{2,1,0:T(8,128)(2,1)S(1)} %collective-permute-done.58.refs_0_), channel_id=1, source_target_pairs={{0,4},{1,5},{4,8},{5,9},{8,12},{9,13},{12,14},{13,15},{14,10},{15,... | collective-permute-start | bytes 1253384 | tf_op jit(solution)/shard_map/ppermute | solution.py:897
  179.0 12.2 %collective-permute-start.62 = (bf16[2,816,128]{2,1,0:T(8,128)(2,1)S(1)}, bf16[2,816,128]{2,1,0:T(8,128)(2,1)S(1)}, u32[]{:S(2)}, u32[]{:S(2)}) collective-permute-start(bf16[2,816,128]{2,1,0:T(8,128)(2,1)S(1)} %collective-permute-done.59.refs_1_), channel_id=1, source_target_pairs={{0,2},{1,3},{4,0},{5,1},{8,4},{9,5},{12,8},{13,9},{14,12},{15,13},... | collective-permute-start | bytes 1253384 | tf_op jit(solution)/shard_map/ppermute | solution.py:900
  191.7 11.6 %collective-permute-start.66 = (bf16[2,816,128]{2,1,0:T(8,128)(2,1)S(1)}, bf16[2,816,128]{2,1,0:T(8,128)(2,1)S(1)}, u32[]{:S(2)}, u32[]{:S(2)}) collective-permute-start(bf16[2,816,128]{2,1,0:T(8,128)(2,1)S(1)} %collective-permute-done.61.refs_0_), channel_id=1, source_target_pairs={{0,4},{1,5},{4,8},{5,9},{8,12},{9,13},{12,14},{13,15},{14,10},{15,... | collective-permute-start | bytes 1253384 | tf_op jit(solution)/shard_map/ppermute | solution.py:897
  192.9 11.7 %collective-permute-start.67 = (bf16[2,816,128]{2,1,0:T(8,128)(2,1)S(1)}, bf16[2,816,128]{2,1,0:T(8,128)(2,1)S(1)}, u32[]{:S(2)}, u32[]{:S(2)}) collective-permute-start(bf16[2,816,128]{2,1,0:T(8,128)(2,1)S(1)} %collective-permute-done.62.refs_1_), channel_id=1, source_target_pairs={{0,2},{1,3},{4,0},{5,1},{8,4},{9,5},{12,8},{13,9},{14,12},{15,13},... | collective-permute-start | bytes 1253384 | tf_op jit(solution)/shard_map/ppermute | solution.py:900
  231.9 10.4 %collective-permute-start.90 = (bf16[1,816,128]{2,1,0:T(8,128)(2,1)S(1)}, bf16[1,816,128]{2,1,0:T(8,128)(2,1)S(1)}, u32[]{:S(2)}, u32[]{:S(2)}) collective-permute-start(bf16[1,816,128]{2,1,0:T(8,128)(2,1)S(1)} %get-tuple-element.543), channel_id=1, source_target_pairs={{0,2},{1,3},{4,0},{5,1},{8,4},{9,5},{12,8},{13,9},{14,12},{15,13},... | collective-permute-start | bytes 626696 | tf_op jit(solution)/shard_map/ppermute | solution.py:900
  233.3 10.4 %collective-permute-start.91 = (bf16[1,816,128]{2,1,0:T(8,128)(2,1)S(1)}, bf16[1,816,128]{2,1,0:T(8,128)(2,1)S(1)}, u32[]{:S(2)}, u32[]{:S(2)}) collective-permute-start(bf16[1,816,128]{2,1,0:T(8,128)(2,1)S(1)} %get-tuple-element.544), channel_id=1, source_target_pairs={{0,4},{1,5},{4,8},{5,9},{8,12},{9,13},{12,14},{13,15},{14,10},{15,... | collective-permute-start | bytes 626696 | tf_op jit(solution)/shard_map/ppermute | solution.py:897
  277.6 11.5 %collective-permute-start.100 = (bf16[2,768,128]{2,1,0:T(8,128)(2,1)S(1)}, bf16[2,768,128]{2,1,0:T(8,128)(2,1)S(1)}, u32[]{:S(2)}, u32[]{:S(2)}) collective-permute-start(bf16[2,768,128]{2,1,0:T(8,128)(2,1)S(1)} %collective-permute-done.98.refs_2_.g_ref), channel_id=1, source_target_pairs={{0,2},{1,3},{4,0},{5,1},{8,4},{9,5},{12,8},{13,9},{14,12},{15,13},... | collective-permute-start | bytes 1179656 | tf_op jit(solution)/shard_map/ppermute | solution.py:900
  279.3 11.2 %collective-permute-start.99 = (bf16[2,768,128]{2,1,0:T(8,128)(2,1)S(1)}, bf16[2,768,128]{2,1,0:T(8,128)(2,1)S(1)}, u32[]{:S(2)}, u32[]{:S(2)}) collective-permute-start(bf16[2,768,128]{2,1,0:T(8,128)(2,1)S(1)} %collective-permute-done.98.refs_2_.g_ref), channel_id=1, source_target_pairs={{0,4},{1,5},{4,8},{5,9},{8,12},{9,13},{12,14},{13,15},{14,10},{15,... | collective-permute-start | bytes 1179656 | tf_op jit(solution)/shard_map/ppermute | solution.py:897
  291.0 12.0 %collective-permute-start.106 = (bf16[2,816,128]{2,1,0:T(8,128)(2,1)S(1)}, bf16[2,816,128]{2,1,0:T(8,128)(2,1)S(1)}, u32[]{:S(2)}, u32[]{:S(2)}) collective-permute-start(bf16[2,816,128]{2,1,0:T(8,128)(2,1)S(1)} %get-tuple-element.593), channel_id=1, source_target_pairs={{0,1},{1,0},{2,3},{3,2},{4,5},{5,4},{6,7},{7,6},{8,9},{9,8},{10,11... | collective-permute-start | bytes 1253384 | tf_op jit(solution)/shard_map/ppermute | solution.py:903
  291.0 11.5 %collective-permute-start.102 = (bf16[2,768,128]{2,1,0:T(8,128)(2,1)S(1)}, bf16[2,768,128]{2,1,0:T(8,128)(2,1)S(1)}, u32[]{:S(2)}, u32[]{:S(2)}) collective-permute-start(bf16[2,768,128]{2,1,0:T(8,128)(2,1)S(1)} %collective-permute-done.99.refs_4_), channel_id=1, source_target_pairs={{0,4},{1,5},{4,8},{5,9},{8,12},{9,13},{12,14},{13,15},{14,10},{15,... | collective-permute-start | bytes 1179656 | tf_op jit(solution)/shard_map/ppermute | solution.py:897
  291.4 11.6 %collective-permute-start.103 = (bf16[2,768,128]{2,1,0:T(8,128)(2,1)S(1)}, bf16[2,768,128]{2,1,0:T(8,128)(2,1)S(1)}, u32[]{:S(2)}, u32[]{:S(2)}) collective-permute-start(bf16[2,768,128]{2,1,0:T(8,128)(2,1)S(1)} %collective-permute-done.100.refs_5_), channel_id=1, source_target_pairs={{0,2},{1,3},{4,0},{5,1},{8,4},{9,5},{12,8},{13,9},{14,12},{15,13},... | collective-permute-start | bytes 1179656 | tf_op jit(solution)/shard_map/ppermute | solution.py:900
  303.5 12.4 %collective-permute-start.111 = (bf16[2,816,128]{2,1,0:T(8,128)(2,1)S(1)}, bf16[2,816,128]{2,1,0:T(8,128)(2,1)S(1)}, u32[]{:S(2)}, u32[]{:S(2)}) collective-permute-start(bf16[2,816,128]{2,1,0:T(8,128)(2,1)S(1)} %get-tuple-element.608), channel_id=1, source_target_pairs={{0,1},{1,0},{2,3},{3,2},{4,5},{5,4},{6,7},{7,6},{8,9},{9,8},{10,11... | collective-permute-start | bytes 1253384 | tf_op jit(solution)/shard_map/ppermute | solution.py:903
  303.5 12.4 %collective-permute-start.112 = (bf16[2,816,128]{2,1,0:T(8,128)(2,1)S(1)}, bf16[2,816,128]{2,1,0:T(8,128)(2,1)S(1)}, u32[]{:S(2)}, u32[]{:S(2)}) collective-permute-start(bf16[2,816,128]{2,1,0:T(8,128)(2,1)S(1)} %get-tuple-element.610), channel_id=1, source_target_pairs={{0,1},{1,0},{2,3},{3,2},{4,5},{5,4},{6,7},{7,6},{8,9},{9,8},{10,11... | collective-permute-start | bytes 1253384 | tf_op jit(solution)/shard_map/ppermute | solution.py:903
  304.0 11.0 %collective-permute-start.107 = (bf16[2,768,128]{2,1,0:T(8,128)(2,1)S(1)}, bf16[2,768,128]{2,1,0:T(8,128)(2,1)S(1)}, u32[]{:S(2)}, u32[]{:S(2)}) collective-permute-start(bf16[2,768,128]{2,1,0:T(8,128)(2,1)S(1)} %collective-permute-done.102.refs_4_), channel_id=1, source_target_pairs={{0,4},{1,5},{4,8},{5,9},{8,12},{9,13},{12,14},{13,15},{14,10},{15,... | collective-permute-start | bytes 1179656 | tf_op jit(solution)/shard_map/ppermute | solution.py:897
  304.7 11.2 %collective-permute-start.108 = (bf16[2,768,128]{2,1,0:T(8,128)(2,1)S(1)}, bf16[2,768,128]{2,1,0:T(8,128)(2,1)S(1)}, u32[]{:S(2)}, u32[]{:S(2)}) collective-permute-start(bf16[2,768,128]{2,1,0:T(8,128)(2,1)S(1)} %collective-permute-done.103.refs_5_), channel_id=1, source_target_pairs={{0,2},{1,3},{4,0},{5,1},{8,4},{9,5},{12,8},{13,9},{14,12},{15,13},... | collective-permute-start | bytes 1179656 | tf_op jit(solution)/shard_map/ppermute | solution.py:900
  333.4 10.4 %collective-permute-start.119 = (bf16[2,816,128]{2,1,0:T(8,128)(2,1)S(1)}, bf16[2,816,128]{2,1,0:T(8,128)(2,1)S(1)}, u32[]{:S(2)}, u32[]{:S(2)}) collective-permute-start(bf16[2,816,128]{2,1,0:T(8,128)(2,1)S(1)} %get-tuple-element.639), channel_id=1, source_target_pairs={{0,1},{1,0},{2,3},{3,2},{4,5},{5,4},{6,7},{7,6},{8,9},{9,8},{10,11... | collective-permute-start | bytes 1253384 | tf_op jit(solution)/shard_map/ppermute | solution.py:903
  333.7 10.2 %collective-permute-start.125 = (bf16[2,816,128]{2,1,0:T(8,128)(2,1)S(1)}, bf16[2,816,128]{2,1,0:T(8,128)(2,1)S(1)}, u32[]{:S(2)}, u32[]{:S(2)}) collective-permute-start(bf16[2,816,128]{2,1,0:T(8,128)(2,1)S(1)} %get-tuple-element.675), channel_id=1, source_target_pairs={{0,1},{1,0},{2,3},{3,2},{4,5},{5,4},{6,7},{7,6},{8,9},{9,8},{10,11... | collective-permute-start | bytes 1253384 | tf_op jit(solution)/shard_map/ppermute | solution.py:903
  346.2 10.4 %collective-permute-start.131 = (bf16[1,816,128]{2,1,0:T(8,128)(2,1)S(1)}, bf16[1,816,128]{2,1,0:T(8,128)(2,1)S(1)}, u32[]{:S(2)}, u32[]{:S(2)}) collective-permute-start(bf16[1,816,128]{2,1,0:T(8,128)(2,1)S(1)} %get-tuple-element.679), channel_id=1, source_target_pairs={{0,2},{1,3},{4,0},{5,1},{8,4},{9,5},{12,8},{13,9},{14,12},{15,13},... | collective-permute-start | bytes 626696 | tf_op jit(solution)/shard_map/ppermute | solution.py:900
  348.0 10.4 %collective-permute-start.132 = (bf16[1,816,128]{2,1,0:T(8,128)(2,1)S(1)}, bf16[1,816,128]{2,1,0:T(8,128)(2,1)S(1)}, u32[]{:S(2)}, u32[]{:S(2)}) collective-permute-start(bf16[1,816,128]{2,1,0:T(8,128)(2,1)S(1)} %get-tuple-element.680), channel_id=1, source_target_pairs={{0,4},{1,5},{4,8},{5,9},{8,12},{9,13},{12,14},{13,15},{14,10},{15,... | collective-permute-start | bytes 626696 | tf_op jit(solution)/shard_map/ppermute | solution.py:897
  392.2 11.5 %collective-permute-start.147 = (bf16[32,3200]{1,0:T(8,128)(2,1)S(1)}, bf16[32,3200]{1,0:T(8,128)(2,1)S(1)}, u32[]{:S(2)}, u32[]{:S(2)}) collective-permute-start(bf16[32,3200]{1,0:T(8,128)(2,1)S(1)} %add.225), channel_id=1, source_target_pairs={{0,4},{1,5},{4,8},{5,9},{8,12},{9,13},{12,14},{13,15},{14,10},{15,... | collective-permute-start | bytes 614408 | tf_op jit(solution)/shard_map/ppermute | solution.py:897
  418.5 14.2 %collective-permute-start.143 = (bf16[64,3200]{1,0:T(8,128)(2,1)S(1)}, bf16[64,3200]{1,0:T(8,128)(2,1)S(1)}, u32[]{:S(2)}, u32[]{:S(2)}) collective-permute-start(bf16[64,3200]{1,0:T(8,128)(2,1)S(1)} %get-tuple-element.712), channel_id=1, source_target_pairs={{0,1},{1,0},{2,3},{3,2},{4,5},{5,4},{6,7},{7,6},{8,9},{9,8},{10,11... | collective-permute-start | bytes 1228808 | tf_op jit(solution)/shard_map/ppermute | solution.py:903
  (139 other events, 1167.2 us)

commit v6 on v5

--- a/solution.py
+++ b/solution.py
@@ -395,7 +395,7 @@
     if with_grads:
         second_ref, first_ref, grad_ref, section_ref, rest = rest[0], rest[1], rest[2], rest[3], rest[4:]
         big_refs, rest = rest[:10], rest[10:]
-        back_ref, gains_ref, w_scratch, k_scratch, v_scratch, sems = rest
+        back_ref, gains_ref, w_scratch, sems = rest
         for part in (2, 1, 0):
             columns = pl.ds(PARTS[part][0], PARTS[part][1] - PARTS[part][0])
             loads[part] = pltpu.make_async_copy(
@@ -403,11 +403,6 @@
             )
             loads[part].start()
         w_vmem = w_scratch
-        k_load = pltpu.make_async_copy(k_ref, k_scratch, sems.at[3])
-        v_load = pltpu.make_async_copy(v_ref, v_scratch, sems.at[4])
-        k_load.start()
-        v_load.start()
-        k_ref, v_ref = k_scratch, v_scratch
         loads[2].wait()
     else:
         grad_ref, back_ref = rest
@@ -440,9 +435,6 @@
         loads[1].wait()
     w_out = w_vmem[:, :, QKV : QKV + D].reshape(D, D)
     grad_mixed = nt(grad_branch, w_out)
-    if with_grads:
-        k_load.wait()
-        v_load.wait()
     cosine, sine = table_ref[:, :LANES], table_ref[:, LANES:]
     low = lanes_of((length, LANES)) < 64
     for s in range(seqs):
@@ -556,14 +548,12 @@
         scratch += [
             pltpu.VMEM((8, D), f32),
             pltpu.VMEM((16, 64, WCOLS), bf16),
-            pltpu.VMEM((rows, 512), bf16),
-            pltpu.VMEM((rows, 512), bf16),
-            pltpu.SemaphoreType.DMA((5,)),
+            pltpu.SemaphoreType.DMA((3,)),
         ]
     return pl.pallas_call(
         functools.partial(attn_backward_kernel, with_grads),
         out_shape=outs,
-        in_specs=[smem()] + [vmem()] * 8 + [late()] * 2 + [vmem()] * 3 + [late()] + [vmem()] * len(others),
+        in_specs=[smem()] + [vmem()] * 8 + [vmem()] * 5 + [late()] + [vmem()] * len(others),
         out_specs=[vmem()] * len(outs),
         scratch_shapes=scratch,
         compiler_params=pltpu.CompilerParams(vmem_limit_bytes=VMEM_LIMIT),
@@ -574,7 +564,7 @@
     )(
         order,
         *(sums, g, x, payload, resid, gate, normed, q),
-        *((in_hbm(k), in_hbm(v)) if with_grads else (k, v)),
+        *(k, v),
         *(probs, mixed, table, (in_hbm if with_grads else in_vmem)(w_all)),
         *others,
     )

time: 443 us -> 442 us (level)
  transfers between devices with their start and end apart: 158 -> 158, of which waited for: 94 -> 93; matrix products, arithmetic and copies ran while one was open for 2% -> 2% of each run, Pallas kernels for 19% -> 19%
where the time goes in v6:
time: 442 us; the launch traced here: 434 us
  waiting for transfers between devices  169 us (38%)
  Pallas kernels  135 us (31%)
  starting transfers between devices  112 us (25%)
  local copies, waits for them, and re-layouts  11.3 us (3%)
    ppermute x44, waiting for transfers between devices, minus(): return lax.ppermute(a, 'fsdp', self.behind)  89 us
    pallas_call x15, Pallas kernels, expert_call(): pl.pallas_call(body, out_shape=outs, in_specs=[smem()] + [vmem()] * (part...  80.3 us
    ppermute x44, starting transfers between devices, minus(): return lax.ppermute(a, 'fsdp', self.behind)  59.1 us
    ppermute x44, waiting for transfers between devices, plus(): return lax.ppermute(a, 'fsdp', self.ahead)  58.8 us
    ppermute x44, starting transfers between devices, plus(): return lax.ppermute(a, 'fsdp', self.ahead)  36 us
    pallas_call x2, Pallas kernels, attn_backward(): pl.pallas_call(functools.partial(attn_backward_kernel, with_grads), out_s...  21.2 us
    pallas_call x2, Pallas kernels, attn_forward(): pl.pallas_call(functools.partial(attn_forward_kernel, save), out_shape=ou...  15 us
    ppermute x68, starting transfers between devices, swap(): return lax.ppermute(a, 'fsdp', self.core)  14 us
  transfers between devices with their start and end apart: 158, of which 93 were waited for; matrix products, arithmetic and copies ran while one was open for 2% of the time, Pallas kernels for 19%

profile of v6, /device:TPU:0, one launch (start us, length us, event | category | flops | bytes accessed | tf_op | source)
XLA Modules:
  0.0 434.4 jit_solution(4401493761529069166)
XLA Ops:
  10.5 5.4 %collective-permute-done.1.refs_4_ = bf16[64,3200]{1,0:T(8,128)(2,1)S(1)} collective-permute-done((bf16[64,3200]{1,0:T(8,128)(2,1)S(1)}, bf16[64,3200]{1,0:T(8,128)(2,1)S(1)}, u32[]{:S(2)}, u32[]{:S(2)}) %collective-permute-start.1) | collective-permute-done | bytes 409632 | tf_op jit(solution)/shard_map/ppermute | solution.py:890
  22.0 5.4 %collective-permute-done.2.refs_16_ = bf16[64,3200]{1,0:T(8,128)(2,1)} collective-permute-done((bf16[64,3200]{1,0:T(8,128)(2,1)S(1)}, bf16[64,3200]{1,0:T(8,128)(2,1)}, u32[]{:S(2)}, u32[]{:S(2)}) %collective-permute-start.2) | collective-permute-done | bytes 409632 | tf_op jit(solution)/shard_map/ppermute | solution.py:887
  30.4 6.8 %collective-permute-done.8.refs_8_ = bf16[64,3200]{1,0:T(8,128)(2,1)S(1)} collective-permute-done((bf16[64,3200]{1,0:T(8,128)(2,1)}, bf16[64,3200]{1,0:T(8,128)(2,1)S(1)}, u32[]{:S(2)}, u32[]{:S(2)}) %collective-permute-start.8) | collective-permute-done | bytes 409632 | tf_op jit(solution)/shard_map/ppermute | solution.py:890
  40.7 4.9 %collective-permute-done.10.refs_10_ = bf16[32,3200]{1,0:T(8,128)(2,1)S(1)} collective-permute-done((bf16[32,3200]{1,0:T(8,128)(2,1)S(1)}, bf16[32,3200]{1,0:T(8,128)(2,1)S(1)}, u32[]{:S(2)}, u32[]{:S(2)}) %collective-permute-start.10) | collective-permute-done | bytes 204832 | tf_op jit(solution)/shard_map/ppermute | solution.py:887
  48.7 8.6 %attn_forward.2 = (bf16[2,816,128]{2,1,0:T(8,128)(2,1)S(1)}, f32[2,768,128]{2,1,0:T(8,128)}, bf16[16,64,3200]{2,1,0:T(8,128)(2,1)}) custom-call(s32[4,8]{1,0:T(4,128)S(1)} %pad_add_fusion.order, f32[96,256]{1,0:T(8,128)} %constant.78.clone.table_hbm.table_ref, f32[192,128]{1,0:T(8,128)} %bitcast.67, bf16[2,96,1024]{2,1,0:T(8,128)(2,1)} %refs_0_.3, ...), custom_call_target="tpu_custom_call" | custom-call | flops 1336934400 | bytes 12000000 | tf_op jit(solution)/shard_map/attn_forward/pallas_call | solution.py:361
  65.5 4.0 collective-permute-done.18.refs_1_.refs_5_
  73.2 5.1 %experts_0.6 = (bf16[2,768,128]{2,1,0:T(8,128)(2,1)S(1)}, bf16[2,768,128]{2,1,0:T(8,128)(2,1)S(1)}, bf16[2,768,128]{2,1,0:T(8,128)(2,1)S(1)}, bf16[2,768,128]{2,1,0:T(8,128)(2,1)S(1)}) custom-call(s32[2]{0:T(128)S(1)} %pad_add_fusion.1.which, bf16[2,816,128]{2,1,0:T(8,128)(2,1)} %collective-permute-done.17.refs_0_.refs_4_, ...), custom_call_target="tpu_custom_call" | custom-call | flops 1610612736 | bytes 9145728 | tf_op jit(solution)/shard_map/experts_0/pallas_call | solution.py:712
  78.3 4.5 %collective-permute-done.20.refs_0_.refs_4_ = bf16[2,816,128]{2,1,0:T(8,128)(2,1)S(1)} collective-permute-done((bf16[2,816,128]{2,1,0:T(8,128)(2,1)}, bf16[2,816,128]{2,1,0:T(8,128)(2,1)S(1)}, u32[]{:S(2)}, u32[]{:S(2)}) %collective-permute-start.20) | collective-permute-done | bytes 417824 | tf_op jit(solution)/shard_map/ppermute | solution.py:887
  86.3 4.6 %experts_0.7 = (bf16[2,768,128]{2,1,0:T(8,128)(2,1)S(1)}, bf16[2,768,128]{2,1,0:T(8,128)(2,1)S(1)}, bf16[2,768,128]{2,1,0:T(8,128)(2,1)S(1)}, bf16[2,768,128]{2,1,0:T(8,128)(2,1)S(1)}) custom-call(s32[2]{0:T(128)S(1)} %pad_add_fusion.1.which, bf16[2,816,128]{2,1,0:T(8,128)(2,1)S(1)} %collective-permute-done.20.refs_0_.refs_4_, ...), custom_call_target="tpu_custom_call" | custom-call | flops 1610612736 | bytes 9145728 | tf_op jit(solution)/shard_map/experts_0/pallas_call | solution.py:712
  91.0 4.4 %collective-permute-done.25.refs_0_.refs_4_ = bf16[2,816,128]{2,1,0:T(8,128)(2,1)S(1)} collective-permute-done((bf16[2,816,128]{2,1,0:T(8,128)(2,1)S(1)}, bf16[2,816,128]{2,1,0:T(8,128)(2,1)S(1)}, u32[]{:S(2)}, u32[]{:S(2)}) %collective-permute-start.25) | collective-permute-done | bytes 417824 | tf_op jit(solution)/shard_map/ppermute | solution.py:887
  99.7 4.6 %experts_0.8 = (bf16[2,768,128]{2,1,0:T(8,128)(2,1)S(1)}, bf16[2,768,128]{2,1,0:T(8,128)(2,1)S(1)}, bf16[2,768,128]{2,1,0:T(8,128)(2,1)S(1)}, bf16[2,768,128]{2,1,0:T(8,128)(2,1)S(1)}) custom-call(s32[2]{0:T(128)S(1)} %pad_add_fusion.1.which, bf16[2,816,128]{2,1,0:T(8,128)(2,1)S(1)} %collective-permute-done.25.refs_0_.refs_4_, ...), custom_call_target="tpu_custom_call" | custom-call | flops 1610612736 | bytes 9145728 | tf_op jit(solution)/shard_map/experts_0/pallas_call | solution.py:712
  151.2 6.3 %collective-permute-done.57.refs_1_ = bf16[2,768,128]{2,1,0:T(8,128)(2,1)S(1)} collective-permute-done((bf16[2,768,128]{2,1,0:T(8,128)(2,1)S(1)}, bf16[2,768,128]{2,1,0:T(8,128)(2,1)S(1)}, u32[]{:S(2)}, u32[]{:S(2)}) %collective-permute-start.57) | collective-permute-done | bytes 393248 | tf_op jit(solution)/shard_map/ppermute | solution.py:1073
  158.2 6.4 %attn_forward.3 = (bf16[2,816,128]{2,1,0:T(8,128)(2,1)S(1)}, f32[192,1024]{1,0:T(8,128)S(1)}, bf16[2,96,1024]{2,1,0:T(8,128)(2,1)S(1)}, f32[192,128]{1,0:T(8,128...) custom-call(s32[4,8]{1,0:T(4,128)S(1)} %pad_add_fusion.order, ...), custom_call_target="tpu_custom_call" | custom-call | flops 1336934400 | bytes 12000000 | tf_op jit(solution)/shard_map/attn_forward/pallas_call | solution.py:361
  166.8 4.7 %experts_1.5 = (bf16[2,816,128]{2,1,0:T(8,128)(2,1)S(1)}, bf16[2,816,128]{2,1,0:T(8,128)(2,1)S(1)}) custom-call(s32[2]{0:T(128)S(1)} %pad_add_fusion.1.which, bf16[2,816,128]{2,1,0:T(8,128)(2,1)S(1)} %get-tuple-element.484.refs_0_.wide_ref, bf16[2,816,128]{2,1,0:T(8,128)(2,1)S(1)} %collective-permute-done.60.refs_1_, ...), custom_call_target="tpu_custom_call" | custom-call | flops 1342177280 | bytes 7572864 | tf_op jit(solution)/shard_map/experts_1/pallas_call | solution.py:712
  171.5 5.3 %collective-permute-done.59.refs_1_ = bf16[2,816,128]{2,1,0:T(8,128)(2,1)S(1)} collective-permute-done((bf16[2,816,128]{2,1,0:T(8,128)(2,1)S(1)}, bf16[2,816,128]{2,1,0:T(8,128)(2,1)S(1)}, u32[]{:S(2)}, u32[]{:S(2)}) %collective-permute-start.59) | collective-permute-done | bytes 417824 | tf_op jit(solution)/shard_map/ppermute | solution.py:890
  180.8 6.7 %experts_1.6 = (bf16[2,816,128]{2,1,0:T(8,128)(2,1)S(1)}, bf16[2,816,128]{2,1,0:T(8,128)(2,1)S(1)}, bf16[2,816,128]{2,1,0:T(8,128)(2,1)S(1)}, bf16[2,816,128]{2,1,0:T(8,128)(2,1)S(1)}) custom-call(s32[2]{0:T(128)S(1)} %pad_add_fusion.1.which, bf16[2,816,128]{2,1,0:T(8,128)(2,1)S(1)} %collective-permute-done.58.refs_0_, ...), custom_call_target="tpu_custom_call" | custom-call | flops 2684354560 | bytes 9145728 | tf_op jit(solution)/shard_map/experts_1/pallas_call | solution.py:712
  194.3 6.2 %experts_1.7 = (bf16[2,816,128]{2,1,0:T(8,128)(2,1)S(1)}, bf16[2,816,128]{2,1,0:T(8,128)(2,1)S(1)}, bf16[2,816,128]{2,1,0:T(8,128)(2,1)S(1)}, bf16[2,816,128]{2,1,0:T(8,128)(2,1)S(1)}) custom-call(s32[2]{0:T(128)S(1)} %pad_add_fusion.1.which, bf16[2,816,128]{2,1,0:T(8,128)(2,1)S(1)} %collective-permute-done.61.refs_0_, ...), custom_call_target="tpu_custom_call" | custom-call | flops 2684354560 | bytes 9145728 | tf_op jit(solution)/shard_map/experts_1/pallas_call | solution.py:712
  207.9 6.2 %experts_1.8 = (bf16[2,816,128]{2,1,0:T(8,128)(2,1)S(1)}, bf16[2,816,128]{2,1,0:T(8,128)(2,1)S(1)}, bf16[2,816,128]{2,1,0:T(8,128)(2,1)S(1)}, bf16[2,816,128]{2,1,0:T(8,128)(2,1)S(1)}) custom-call(s32[2]{0:T(128)S(1)} %pad_add_fusion.1.which, bf16[2,816,128]{2,1,0:T(8,128)(2,1)S(1)} %collective-permute-done.66.refs_0_, ...), custom_call_target="tpu_custom_call" | custom-call | flops 2684354560 | bytes 9145728 | tf_op jit(solution)/shard_map/experts_1/pallas_call | solution.py:712
  216.0 4.7 %experts_1.9 = (bf16[1,816,128]{2,1,0:T(8,128)(2,1)S(1)}, bf16[1,816,128]{2,1,0:T(8,128)(2,1)S(1)}, bf16[1,816,128]{2,1,0:T(8,128)(2,1)S(1)}, bf16[1,816,128]{2,1,0:T(8,128)(2,1)S(1)}) custom-call(s32[2]{0:T(128)S(1)} %pad_add_fusion.1.which, bf16[1,816,128]{2,1,0:T(8,128)(2,1)S(1)} %collective-permute-done.72.refs_0_, ...), custom_call_target="tpu_custom_call" | custom-call | flops 1342177280 | bytes 7572864 | tf_op jit(solution)/shard_map/experts_1/pallas_call | solution.py:712
  224.8 4.7 %collective-permute-done.82.refs_2_ = bf16[1,816,128]{2,1,0:T(8,128)(2,1)S(1)} collective-permute-done((bf16[1,816,128]{2,1,0:T(8,128)(2,1)S(1)}, bf16[1,816,128]{2,1,0:T(8,128)(2,1)S(1)}, u32[]{:S(2)}, u32[]{:S(2)}) %collective-permute-start.82) | collective-permute-done | bytes 208928 | tf_op jit(solution)/shard_map/ppermute | solution.py:890
  234.0 3.9 collective-permute-done.85.refs_2_
  261.4 8.3 %attn_backward.2 = bf16[2,768,128]{2,1,0:T(8,128)(2,1)S(1)} custom-call(s32[4,8]{1,0:T(4,128)S(1)} %pad_add_fusion.order, f32[2,816,128]{2,1,0:T(8,128)S(1)} %pad_maximum_fusion.sum_ref.rest_1_, bf16[2,96,1024]{2,1,0:T(8,128)(2,1)S(1)} %copy-done.4, bf16[2,96,1024]{2,1,0:T(8,128)(2,1)S(1)} %get-tuple-element.565.x_ref, ...), custom_call_target="tpu_custom_call" | custom-call | flops 2673868800 | bytes 20000000 | tf_op jit(solution)/shard_map/attn_backward/pallas_call | solution.py:553
  271.2 6.4 %collective-permute-done.98.refs_2_.g_ref = bf16[2,768,128]{2,1,0:T(8,128)(2,1)S(1)} collective-permute-done((bf16[2,768,128]{2,1,0:T(8,128)(2,1)S(1)}, bf16[2,768,128]{2,1,0:T(8,128)(2,1)S(1)}, u32[]{:S(2)}, u32[]{:S(2)}) %collective-permute-start.98) | collective-permute-done | bytes 393248 | tf_op jit(solution)/shard_map/ppermute | solution.py:1079
  279.6 5.1 %experts_2.5 = (bf16[2,816,128]{2,1,0:T(8,128)(2,1)S(1)}, bf16[2,816,128]{2,1,0:T(8,128)(2,1)S(1)}, bf16[2,128,1024]{2,1,0:T(8,128)(2,1)}, bf16[2,128,1024]{2,1,...) custom-call(s32[2]{0:T(128)S(1)} %pad_add_fusion.1.which, ...), custom_call_target="tpu_custom_call" | custom-call | flops 1342177280 | bytes 7572864 | tf_op jit(solution)/shard_map/experts_2/pallas_call | solution.py:712
  284.7 4.4 %collective-permute-done.100.refs_5_ = bf16[2,768,128]{2,1,0:T(8,128)(2,1)S(1)} collective-permute-done((bf16[2,768,128]{2,1,0:T(8,128)(2,1)S(1)}, bf16[2,768,128]{2,1,0:T(8,128)(2,1)S(1)}, u32[]{:S(2)}, u32[]{:S(2)}) %collective-permute-start.100) | collective-permute-done | bytes 393248 | tf_op jit(solution)/shard_map/ppermute | solution.py:890
  293.5 6.7 %experts_2.6 = (bf16[2,816,128]{2,1,0:T(8,128)(2,1)S(1)}, bf16[2,816,128]{2,1,0:T(8,128)(2,1)S(1)}, bf16[2,816,128]{2,1,0:T(8,128)(2,1)S(1)}, bf16[2,816,128]{2,...) custom-call(s32[2]{0:T(128)S(1)} %pad_add_fusion.1.which, ...), custom_call_target="tpu_custom_call" | custom-call | flops 2684354560 | bytes 9145728 | tf_op jit(solution)/shard_map/experts_2/pallas_call | solution.py:712
  306.5 6.7 %experts_2.7 = (bf16[2,816,128]{2,1,0:T(8,128)(2,1)S(1)}, bf16[2,816,128]{2,1,0:T(8,128)(2,1)S(1)}, bf16[2,816,128]{2,1,0:T(8,128)(2,1)S(1)}, bf16[2,816,128]{2,...) custom-call(s32[2]{0:T(128)S(1)} %pad_add_fusion.1.which, ...), custom_call_target="tpu_custom_call" | custom-call | flops 2684354560 | bytes 9145728 | tf_op jit(solution)/shard_map/experts_2/pallas_call | solution.py:712
  319.2 6.7 %experts_2.8 = (bf16[2,816,128]{2,1,0:T(8,128)(2,1)S(1)}, bf16[2,816,128]{2,1,0:T(8,128)(2,1)S(1)}, bf16[2,816,128]{2,1,0:T(8,128)(2,1)S(1)}, bf16[2,816,128]{2,...) custom-call(s32[2]{0:T(128)S(1)} %pad_add_fusion.1.which, ...), custom_call_target="tpu_custom_call" | custom-call | flops 2684354560 | bytes 9145728 | tf_op jit(solution)/shard_map/experts_2/pallas_call | solution.py:712
  327.8 5.1 %experts_2.9 = (bf16[1,816,128]{2,1,0:T(8,128)(2,1)S(1)}, bf16[1,816,128]{2,1,0:T(8,128)(2,1)S(1)}, bf16[1,816,128]{2,1,0:T(8,128)(2,1)S(1)}, bf16[1,816,128]{2,...) custom-call(s32[2]{0:T(128)S(1)} %pad_add_fusion.1.which, ...), custom_call_target="tpu_custom_call" | custom-call | flops 1342177280 | bytes 7572864 | tf_op jit(solution)/shard_map/experts_2/pallas_call | solution.py:712
  336.9 7.0 %weight_grads_0.1 = (f32[1024,2048]{1,0:T(8,128)}, f32[1024,1024]{1,0:T(8,128)}) custom-call(bf16[2,128,1024]{2,1,0:T(8,128)(2,1)} %get-tuple-element.719.refs_0_, bf16[2,128,1024]{2,1,0:T(8,128)(2,1)} %get-tuple-element.720.refs_1_, bf16[2,128,512]{2,1,0:T(8,128)(2,1)} %get-tuple-element.721.refs_2_, bf16[2,128,512]{2,1,0:T(8,128)(2,1)} %get-tuple-element.722.refs_3_, ...), custom_call_target="tpu_custom_call" | custom-call | flops 3221225472 | bytes 14000000 | tf_op jit(solution)/shard_map/weight_grads_0/pallas_call | solution.py:783
  376.8 12.9 %attn_backward.3 = (bf16[2,96,1024]{2,1,0:T(8,128)(2,1)}, bf16[2,96,1024]{2,1,0:T(8,128)(2,1)}, bf16[64,3200]{1,0:T(8,128)(2,1)S(1)}, bf16[128,3200]{1,0:T(8,128...) custom-call(s32[4,8]{1,0:T(4,128)S(1)} %pad_add_fusion.order, ...), custom_call_target="tpu_custom_call" | custom-call | flops 2673868800 | bytes 20000000 | tf_op jit(solution)/shard_map/attn_backward/pallas_call | solution.py:553
  393.9 7.0 %weight_grads_1.1 = (f32[1024,2048]{1,0:T(8,128)}, f32[1024,1024]{1,0:T(8,128)}) custom-call(bf16[2,128,1024]{2,1,0:T(8,128)(2,1)} %get-tuple-element.719.refs_0_, bf16[2,128,1024]{2,1,0:T(8,128)(2,1)} %get-tuple-element.720.refs_1_, bf16[2,128,512]{2,1,0:T(8,128)(2,1)} %get-tuple-element.721.refs_2_, ...), custom_call_target="tpu_custom_call", output_to_operand_aliasing={{0}: (25, {}), {1}: (26, {})} | custom-call | flops 3221225472 | bytes 14000000 | tf_op jit(solution)/shard_map/weight_grads_1/pallas_call | solution.py:783
  (402 shorter events, 243.1 us)
Async XLA Ops:
  3.4 12.5 %collective-permute-start.1 = (bf16[64,3200]{1,0:T(8,128)(2,1)S(1)}, bf16[64,3200]{1,0:T(8,128)(2,1)S(1)}, u32[]{:S(2)}, u32[]{:S(2)}) collective-permute-start(bf16[64,3200]{1,0:T(8,128)(2,1)S(1)} %concatenate.19.refs_2_), channel_id=1, source_target_pairs={{0,2},{1,3},{4,0},{5,1},{8,4},{9,5},{12,8},{13,9},{14,12},{15,13},... | collective-permute-start | bytes 1228808 | tf_op jit(solution)/shard_map/ppermute | solution.py:890
  6.3 10.9 %collective-permute-start = (bf16[64,3200]{1,0:T(8,128)(2,1)S(1)}, bf16[64,3200]{1,0:T(8,128)(2,1)S(1)}, u32[]{:S(2)}, u32[]{:S(2)}) collective-permute-start(bf16[64,3200]{1,0:T(8,128)(2,1)S(1)} %concatenate.19.refs_2_), channel_id=1, source_target_pairs={{0,4},{1,5},{4,8},{5,9},{8,12},{9,13},{12,14},{13,15},{14,10},{15,... | collective-permute-start | bytes 1228808 | tf_op jit(solution)/shard_map/ppermute | solution.py:887
  17.7 10.2 %collective-permute-start.3 = (bf16[64,3200]{1,0:T(8,128)(2,1)S(1)}, bf16[64,3200]{1,0:T(8,128)(2,1)}, u32[]{:S(2)}, u32[]{:S(2)}) collective-permute-start(bf16[64,3200]{1,0:T(8,128)(2,1)S(1)} %collective-permute-done.1.refs_4_), channel_id=1, source_target_pairs={{0,2},{1,3},{4,0},{5,1},{8,4},{9,5},{12,8},{13,9},{14,12},{15,13},... | collective-permute-start | bytes 1228808 | tf_op jit(solution)/shard_map/ppermute | solution.py:890
  57.6 11.9 %collective-permute-start.18 = (bf16[2,816,128]{2,1,0:T(8,128)(2,1)S(1)}, bf16[2,816,128]{2,1,0:T(8,128)(2,1)S(1)}, u32[]{:S(2)}, u32[]{:S(2)}) collective-permute-start(bf16[2,816,128]{2,1,0:T(8,128)(2,1)S(1)} %get-tuple-element.402.refs_0_.refs_2_), channel_id=1, source_target_pairs={{0,2},{1,3},{4,0},{5,1},{8,4},{9,5},{12,8},{13,9},{14,12},{15,13},... | collective-permute-start | bytes 1253384 | tf_op jit(solution)/shard_map/ppermute | solution.py:890
  58.9 11.7 %collective-permute-start.17 = (bf16[2,816,128]{2,1,0:T(8,128)(2,1)S(1)}, bf16[2,816,128]{2,1,0:T(8,128)(2,1)}, u32[]{:S(2)}, u32[]{:S(2)}) collective-permute-start(bf16[2,816,128]{2,1,0:T(8,128)(2,1)S(1)} %get-tuple-element.402.refs_0_.refs_2_), channel_id=1, source_target_pairs={{0,4},{1,5},{4,8},{5,9},{8,12},{9,13},{12,14},{13,15},{14,10},{15,... | collective-permute-start | bytes 1253384 | tf_op jit(solution)/shard_map/ppermute | solution.py:887
  71.0 11.8 %collective-permute-start.20 = (bf16[2,816,128]{2,1,0:T(8,128)(2,1)}, bf16[2,816,128]{2,1,0:T(8,128)(2,1)S(1)}, u32[]{:S(2)}, u32[]{:S(2)}) collective-permute-start(bf16[2,816,128]{2,1,0:T(8,128)(2,1)} %collective-permute-done.17.refs_0_.refs_4_), channel_id=1, source_target_pairs={{0,4},{1,5},{4,8},{5,9},{8,12},{9,13},{12,14},{13,15},{14,10},{15,... | collective-permute-start | bytes 1253384 | tf_op jit(solution)/shard_map/ppermute | solution.py:887
  71.9 11.4 %collective-permute-start.21 = (bf16[2,816,128]{2,1,0:T(8,128)(2,1)S(1)}, bf16[2,816,128]{2,1,0:T(8,128)(2,1)S(1)}, u32[]{:S(2)}, u32[]{:S(2)}) collective-permute-start(bf16[2,816,128]{2,1,0:T(8,128)(2,1)S(1)} %collective-permute-done.18.refs_1_.refs_5_), channel_id=1, source_target_pairs={{0,2},{1,3},{4,0},{5,1},{8,4},{9,5},{12,8},{13,9},{14,12},{15,13},... | collective-permute-start | bytes 1253384 | tf_op jit(solution)/shard_map/ppermute | solution.py:890
  83.8 11.6 %collective-permute-start.25 = (bf16[2,816,128]{2,1,0:T(8,128)(2,1)S(1)}, bf16[2,816,128]{2,1,0:T(8,128)(2,1)S(1)}, u32[]{:S(2)}, u32[]{:S(2)}) collective-permute-start(bf16[2,816,128]{2,1,0:T(8,128)(2,1)S(1)} %collective-permute-done.20.refs_0_.refs_4_), channel_id=1, source_target_pairs={{0,4},{1,5},{4,8},{5,9},{8,12},{9,13},{12,14},{13,15},{14,10},{15,... | collective-permute-start | bytes 1253384 | tf_op jit(solution)/shard_map/ppermute | solution.py:887
  85.1 11.3 %collective-permute-start.26 = (bf16[2,816,128]{2,1,0:T(8,128)(2,1)S(1)}, bf16[2,816,128]{2,1,0:T(8,128)(2,1)S(1)}, u32[]{:S(2)}, u32[]{:S(2)}) collective-permute-start(bf16[2,816,128]{2,1,0:T(8,128)(2,1)S(1)} %collective-permute-done.21.refs_1_.refs_5_), channel_id=1, source_target_pairs={{0,2},{1,3},{4,0},{5,1},{8,4},{9,5},{12,8},{13,9},{14,12},{15,13},... | collective-permute-start | bytes 1253384 | tf_op jit(solution)/shard_map/ppermute | solution.py:890
  164.7 12.0 %collective-permute-start.59 = (bf16[2,816,128]{2,1,0:T(8,128)(2,1)S(1)}, bf16[2,816,128]{2,1,0:T(8,128)(2,1)S(1)}, u32[]{:S(2)}, u32[]{:S(2)}) collective-permute-start(bf16[2,816,128]{2,1,0:T(8,128)(2,1)S(1)} %get-tuple-element.484.refs_0_.wide_ref), channel_id=1, source_target_pairs={{0,2},{1,3},{4,0},{5,1},{8,4},{9,5},{12,8},{13,9},{14,12},{15,13},... | collective-permute-start | bytes 1253384 | tf_op jit(solution)/shard_map/ppermute | solution.py:890
  166.1 11.7 %collective-permute-start.58 = (bf16[2,816,128]{2,1,0:T(8,128)(2,1)S(1)}, bf16[2,816,128]{2,1,0:T(8,128)(2,1)S(1)}, u32[]{:S(2)}, u32[]{:S(2)}) collective-permute-start(bf16[2,816,128]{2,1,0:T(8,128)(2,1)S(1)} %get-tuple-element.484.refs_0_.wide_ref), channel_id=1, source_target_pairs={{0,4},{1,5},{4,8},{5,9},{8,12},{9,13},{12,14},{13,15},{14,10},{15,... | collective-permute-start | bytes 1253384 | tf_op jit(solution)/shard_map/ppermute | solution.py:887
  178.3 12.1 %collective-permute-start.61 = (bf16[2,816,128]{2,1,0:T(8,128)(2,1)S(1)}, bf16[2,816,128]{2,1,0:T(8,128)(2,1)S(1)}, u32[]{:S(2)}, u32[]{:S(2)}) collective-permute-start(bf16[2,816,128]{2,1,0:T(8,128)(2,1)S(1)} %collective-permute-done.58.refs_0_), channel_id=1, source_target_pairs={{0,4},{1,5},{4,8},{5,9},{8,12},{9,13},{12,14},{13,15},{14,10},{15,... | collective-permute-start | bytes 1253384 | tf_op jit(solution)/shard_map/ppermute | solution.py:887
  179.0 12.2 %collective-permute-start.62 = (bf16[2,816,128]{2,1,0:T(8,128)(2,1)S(1)}, bf16[2,816,128]{2,1,0:T(8,128)(2,1)S(1)}, u32[]{:S(2)}, u32[]{:S(2)}) collective-permute-start(bf16[2,816,128]{2,1,0:T(8,128)(2,1)S(1)} %collective-permute-done.59.refs_1_), channel_id=1, source_target_pairs={{0,2},{1,3},{4,0},{5,1},{8,4},{9,5},{12,8},{13,9},{14,12},{15,13},... | collective-permute-start | bytes 1253384 | tf_op jit(solution)/shard_map/ppermute | solution.py:890
  191.7 11.6 %collective-permute-start.66 = (bf16[2,816,128]{2,1,0:T(8,128)(2,1)S(1)}, bf16[2,816,128]{2,1,0:T(8,128)(2,1)S(1)}, u32[]{:S(2)}, u32[]{:S(2)}) collective-permute-start(bf16[2,816,128]{2,1,0:T(8,128)(2,1)S(1)} %collective-permute-done.61.refs_0_), channel_id=1, source_target_pairs={{0,4},{1,5},{4,8},{5,9},{8,12},{9,13},{12,14},{13,15},{14,10},{15,... | collective-permute-start | bytes 1253384 | tf_op jit(solution)/shard_map/ppermute | solution.py:887
  192.9 11.7 %collective-permute-start.67 = (bf16[2,816,128]{2,1,0:T(8,128)(2,1)S(1)}, bf16[2,816,128]{2,1,0:T(8,128)(2,1)S(1)}, u32[]{:S(2)}, u32[]{:S(2)}) collective-permute-start(bf16[2,816,128]{2,1,0:T(8,128)(2,1)S(1)} %collective-permute-done.62.refs_1_), channel_id=1, source_target_pairs={{0,2},{1,3},{4,0},{5,1},{8,4},{9,5},{12,8},{13,9},{14,12},{15,13},... | collective-permute-start | bytes 1253384 | tf_op jit(solution)/shard_map/ppermute | solution.py:890
  231.9 10.4 %collective-permute-start.90 = (bf16[1,816,128]{2,1,0:T(8,128)(2,1)S(1)}, bf16[1,816,128]{2,1,0:T(8,128)(2,1)S(1)}, u32[]{:S(2)}, u32[]{:S(2)}) collective-permute-start(bf16[1,816,128]{2,1,0:T(8,128)(2,1)S(1)} %get-tuple-element.543), channel_id=1, source_target_pairs={{0,2},{1,3},{4,0},{5,1},{8,4},{9,5},{12,8},{13,9},{14,12},{15,13},... | collective-permute-start | bytes 626696 | tf_op jit(solution)/shard_map/ppermute | solution.py:890
  233.3 10.4 %collective-permute-start.91 = (bf16[1,816,128]{2,1,0:T(8,128)(2,1)S(1)}, bf16[1,816,128]{2,1,0:T(8,128)(2,1)S(1)}, u32[]{:S(2)}, u32[]{:S(2)}) collective-permute-start(bf16[1,816,128]{2,1,0:T(8,128)(2,1)S(1)} %get-tuple-element.544), channel_id=1, source_target_pairs={{0,4},{1,5},{4,8},{5,9},{8,12},{9,13},{12,14},{13,15},{14,10},{15,... | collective-permute-start | bytes 626696 | tf_op jit(solution)/shard_map/ppermute | solution.py:887
  277.6 11.5 %collective-permute-start.100 = (bf16[2,768,128]{2,1,0:T(8,128)(2,1)S(1)}, bf16[2,768,128]{2,1,0:T(8,128)(2,1)S(1)}, u32[]{:S(2)}, u32[]{:S(2)}) collective-permute-start(bf16[2,768,128]{2,1,0:T(8,128)(2,1)S(1)} %collective-permute-done.98.refs_2_.g_ref), channel_id=1, source_target_pairs={{0,2},{1,3},{4,0},{5,1},{8,4},{9,5},{12,8},{13,9},{14,12},{15,13},... | collective-permute-start | bytes 1179656 | tf_op jit(solution)/shard_map/ppermute | solution.py:890
  279.3 11.2 %collective-permute-start.99 = (bf16[2,768,128]{2,1,0:T(8,128)(2,1)S(1)}, bf16[2,768,128]{2,1,0:T(8,128)(2,1)S(1)}, u32[]{:S(2)}, u32[]{:S(2)}) collective-permute-start(bf16[2,768,128]{2,1,0:T(8,128)(2,1)S(1)} %collective-permute-done.98.refs_2_.g_ref), channel_id=1, source_target_pairs={{0,4},{1,5},{4,8},{5,9},{8,12},{9,13},{12,14},{13,15},{14,10},{15,... | collective-permute-start | bytes 1179656 | tf_op jit(solution)/shard_map/ppermute | solution.py:887
  291.1 11.9 %collective-permute-start.106 = (bf16[2,816,128]{2,1,0:T(8,128)(2,1)S(1)}, bf16[2,816,128]{2,1,0:T(8,128)(2,1)S(1)}, u32[]{:S(2)}, u32[]{:S(2)}) collective-permute-start(bf16[2,816,128]{2,1,0:T(8,128)(2,1)S(1)} %get-tuple-element.593), channel_id=1, source_target_pairs={{0,1},{1,0},{2,3},{3,2},{4,5},{5,4},{6,7},{7,6},{8,9},{9,8},{10,11... | collective-permute-start | bytes 1253384 | tf_op jit(solution)/shard_map/ppermute | solution.py:893
  291.1 11.5 %collective-permute-start.102 = (bf16[2,768,128]{2,1,0:T(8,128)(2,1)S(1)}, bf16[2,768,128]{2,1,0:T(8,128)(2,1)S(1)}, u32[]{:S(2)}, u32[]{:S(2)}) collective-permute-start(bf16[2,768,128]{2,1,0:T(8,128)(2,1)S(1)} %collective-permute-done.99.refs_4_), channel_id=1, source_target_pairs={{0,4},{1,5},{4,8},{5,9},{8,12},{9,13},{12,14},{13,15},{14,10},{15,... | collective-permute-start | bytes 1179656 | tf_op jit(solution)/shard_map/ppermute | solution.py:887
  291.4 11.6 %collective-permute-start.103 = (bf16[2,768,128]{2,1,0:T(8,128)(2,1)S(1)}, bf16[2,768,128]{2,1,0:T(8,128)(2,1)S(1)}, u32[]{:S(2)}, u32[]{:S(2)}) collective-permute-start(bf16[2,768,128]{2,1,0:T(8,128)(2,1)S(1)} %collective-permute-done.100.refs_5_), channel_id=1, source_target_pairs={{0,2},{1,3},{4,0},{5,1},{8,4},{9,5},{12,8},{13,9},{14,12},{15,13},... | collective-permute-start | bytes 1179656 | tf_op jit(solution)/shard_map/ppermute | solution.py:890
  303.5 12.4 %collective-permute-start.111 = (bf16[2,816,128]{2,1,0:T(8,128)(2,1)S(1)}, bf16[2,816,128]{2,1,0:T(8,128)(2,1)S(1)}, u32[]{:S(2)}, u32[]{:S(2)}) collective-permute-start(bf16[2,816,128]{2,1,0:T(8,128)(2,1)S(1)} %get-tuple-element.608), channel_id=1, source_target_pairs={{0,1},{1,0},{2,3},{3,2},{4,5},{5,4},{6,7},{7,6},{8,9},{9,8},{10,11... | collective-permute-start | bytes 1253384 | tf_op jit(solution)/shard_map/ppermute | solution.py:893
  303.5 12.4 %collective-permute-start.112 = (bf16[2,816,128]{2,1,0:T(8,128)(2,1)S(1)}, bf16[2,816,128]{2,1,0:T(8,128)(2,1)S(1)}, u32[]{:S(2)}, u32[]{:S(2)}) collective-permute-start(bf16[2,816,128]{2,1,0:T(8,128)(2,1)S(1)} %get-tuple-element.610), channel_id=1, source_target_pairs={{0,1},{1,0},{2,3},{3,2},{4,5},{5,4},{6,7},{7,6},{8,9},{9,8},{10,11... | collective-permute-start | bytes 1253384 | tf_op jit(solution)/shard_map/ppermute | solution.py:893
  304.0 11.0 %collective-permute-start.107 = (bf16[2,768,128]{2,1,0:T(8,128)(2,1)S(1)}, bf16[2,768,128]{2,1,0:T(8,128)(2,1)S(1)}, u32[]{:S(2)}, u32[]{:S(2)}) collective-permute-start(bf16[2,768,128]{2,1,0:T(8,128)(2,1)S(1)} %collective-permute-done.102.refs_4_), channel_id=1, source_target_pairs={{0,4},{1,5},{4,8},{5,9},{8,12},{9,13},{12,14},{13,15},{14,10},{15,... | collective-permute-start | bytes 1179656 | tf_op jit(solution)/shard_map/ppermute | solution.py:887
  304.7 11.2 %collective-permute-start.108 = (bf16[2,768,128]{2,1,0:T(8,128)(2,1)S(1)}, bf16[2,768,128]{2,1,0:T(8,128)(2,1)S(1)}, u32[]{:S(2)}, u32[]{:S(2)}) collective-permute-start(bf16[2,768,128]{2,1,0:T(8,128)(2,1)S(1)} %collective-permute-done.103.refs_5_), channel_id=1, source_target_pairs={{0,2},{1,3},{4,0},{5,1},{8,4},{9,5},{12,8},{13,9},{14,12},{15,13},... | collective-permute-start | bytes 1179656 | tf_op jit(solution)/shard_map/ppermute | solution.py:890
  333.4 10.4 %collective-permute-start.119 = (bf16[2,816,128]{2,1,0:T(8,128)(2,1)S(1)}, bf16[2,816,128]{2,1,0:T(8,128)(2,1)S(1)}, u32[]{:S(2)}, u32[]{:S(2)}) collective-permute-start(bf16[2,816,128]{2,1,0:T(8,128)(2,1)S(1)} %get-tuple-element.639), channel_id=1, source_target_pairs={{0,1},{1,0},{2,3},{3,2},{4,5},{5,4},{6,7},{7,6},{8,9},{9,8},{10,11... | collective-permute-start | bytes 1253384 | tf_op jit(solution)/shard_map/ppermute | solution.py:893
  333.7 10.2 %collective-permute-start.125 = (bf16[2,816,128]{2,1,0:T(8,128)(2,1)S(1)}, bf16[2,816,128]{2,1,0:T(8,128)(2,1)S(1)}, u32[]{:S(2)}, u32[]{:S(2)}) collective-permute-start(bf16[2,816,128]{2,1,0:T(8,128)(2,1)S(1)} %get-tuple-element.675), channel_id=1, source_target_pairs={{0,1},{1,0},{2,3},{3,2},{4,5},{5,4},{6,7},{7,6},{8,9},{9,8},{10,11... | collective-permute-start | bytes 1253384 | tf_op jit(solution)/shard_map/ppermute | solution.py:893
  346.2 10.4 %collective-permute-start.131 = (bf16[1,816,128]{2,1,0:T(8,128)(2,1)S(1)}, bf16[1,816,128]{2,1,0:T(8,128)(2,1)S(1)}, u32[]{:S(2)}, u32[]{:S(2)}) collective-permute-start(bf16[1,816,128]{2,1,0:T(8,128)(2,1)S(1)} %get-tuple-element.679), channel_id=1, source_target_pairs={{0,2},{1,3},{4,0},{5,1},{8,4},{9,5},{12,8},{13,9},{14,12},{15,13},... | collective-permute-start | bytes 626696 | tf_op jit(solution)/shard_map/ppermute | solution.py:890
  348.0 10.4 %collective-permute-start.132 = (bf16[1,816,128]{2,1,0:T(8,128)(2,1)S(1)}, bf16[1,816,128]{2,1,0:T(8,128)(2,1)S(1)}, u32[]{:S(2)}, u32[]{:S(2)}) collective-permute-start(bf16[1,816,128]{2,1,0:T(8,128)(2,1)S(1)} %get-tuple-element.680), channel_id=1, source_target_pairs={{0,4},{1,5},{4,8},{5,9},{8,12},{9,13},{12,14},{13,15},{14,10},{15,... | collective-permute-start | bytes 626696 | tf_op jit(solution)/shard_map/ppermute | solution.py:887
  391.7 11.5 %collective-permute-start.147 = (bf16[32,3200]{1,0:T(8,128)(2,1)S(1)}, bf16[32,3200]{1,0:T(8,128)(2,1)S(1)}, u32[]{:S(2)}, u32[]{:S(2)}) collective-permute-start(bf16[32,3200]{1,0:T(8,128)(2,1)S(1)} %add.225), channel_id=1, source_target_pairs={{0,4},{1,5},{4,8},{5,9},{8,12},{9,13},{12,14},{13,15},{14,10},{15,... | collective-permute-start | bytes 614408 | tf_op jit(solution)/shard_map/ppermute | solution.py:887
  417.9 14.3 %collective-permute-start.143 = (bf16[64,3200]{1,0:T(8,128)(2,1)S(1)}, bf16[64,3200]{1,0:T(8,128)(2,1)S(1)}, u32[]{:S(2)}, u32[]{:S(2)}) collective-permute-start(bf16[64,3200]{1,0:T(8,128)(2,1)S(1)} %get-tuple-element.712), channel_id=1, source_target_pairs={{0,1},{1,0},{2,3},{3,2},{4,5},{5,4},{6,7},{7,6},{8,9},{9,8},{10,11... | collective-permute-start | bytes 1228808 | tf_op jit(solution)/shard_map/ppermute | solution.py:893
  (137 other events, 973.9 us)
